TPU v7x, 32 devices: a whole 2x2x4 slice. The times are simulated.
32 devices in a mesh: dp: 4 (over y, x), expert: 8 (over z, core).
Axes of the slice: x: 2, y: 2, z: 4, core: 2. Of those that a mesh axis runs over, the one named last changes fastest.
Arguments:
- output_gradient: bfloat16 [4096, 2048], P(('dp', 'expert')), may hold values from -3 to 3
- chosen_expert_index: int32 [4096, 8], P(('dp', 'expert')), may hold values from 0 to 127, all different within a row; in each aligned block of 64 rows (0 to 63, 64 to 127, ...) at most 5 rows name the same one
- routing_gate_weight: bfloat16 [4096, 8], P(('dp', 'expert')), may hold values from 0.049804688 to 1
- hidden: bfloat16 [2, 512, 40, 384], P(None, ('dp', 'expert')), may hold values from -2 to 2
- frozen_down_weight: bfloat16 [128, 384, 2048], P('expert'), may hold values from -0.3125 to 0.3125
- adapter_input_map: bfloat16 [128, 384, 64], P('expert'), may hold values from -0.3125 to 0.3125
- adapter_output_map: bfloat16 [128, 64, 2048], P('expert'), may hold values from -0.125 to 0.125
Outputs:
- hidden_grad: bfloat16 [2, 512, 40, 384], P(None, ('dp', 'expert'))
- router_grad: float32 [4096, 8], P(('dp', 'expert'))
- lora_a_grad: float32 [128, 64, 384], P('expert', None, 'dp')
- lora_b_grad: float32 [128, 64, 2048], P('expert', None, 'dp')
Inputs may be any that keep to these rules, and one draw needn't show every extreme that they name: `chosen_expert_index`: each row names 8 different experts; within each aligned block of 64 rows (one device's microbatch) no expert is named more than 5 times, a bound that some block reaches.
All inputs are finite; a program needn't handle non-finite values.
Results may differ from a plain program's by a relative error of at most 0.0049.
Values may be sent and summed in bfloat16 or wider, within the bound.
No kernel may reach another device: no remote copies, remote signals or barrier semaphores. Data moves between devices by JAX's collectives and lax.ppermute only.
A program may use at most 128 MiB of HBM per device.

v0:
```python
import jax
import jax.numpy as jnp
from jax import lax
from jax.sharding import PartitionSpec as P

adapter_scale = 2.0


def slot_rows(id_rows, experts, per_device, sources, capacity):
    onehot = (id_rows[:, :, None] == jnp.arange(experts, dtype=jnp.int32)[None, None, :]).astype(
        jnp.int32
    )
    before = jnp.sum(jnp.cumsum(onehot, axis=1) * onehot, axis=2) - 1
    target_dev = id_rows // per_device
    target_slot = id_rows % per_device
    return (target_slot * sources + target_dev) * capacity + before


def pick_rows(source, indices):
    return source[indices]


def dispatch_buffers(grad_rows, weight_rows, send_rows, top_count, buffer_len):
    entry_count = send_rows.shape[1]
    token_count = grad_rows.shape[1]
    filler = jnp.full((buffer_len,), entry_count, jnp.int32)

    def invert(rows):
        return filler.at[rows].set(jnp.arange(entry_count, dtype=jnp.int32))

    table = jax.vmap(invert)(send_rows)
    padded_grad = jnp.concatenate(
        [grad_rows, jnp.zeros((grad_rows.shape[0], 1, grad_rows.shape[2]), grad_rows.dtype)], axis=1
    )
    padded_weight = jnp.concatenate(
        [weight_rows, jnp.zeros((weight_rows.shape[0], 1), weight_rows.dtype)], axis=1
    )
    token_pick = jnp.where(table < entry_count, table // top_count, token_count)
    sent_grad = jax.vmap(pick_rows)(padded_grad, token_pick)
    sent_weight = jax.vmap(pick_rows)(padded_weight, table)
    return (sent_grad, sent_weight)


def expert_rows_view(
    received_gradient,
    received_weight,
    retained_rows,
    frozen_down_weight,
    adapter_input_map,
    adapter_output_map,
):
    frozen_term = jnp.einsum(
        "mesd,efd->mesf", received_gradient, frozen_down_weight, preferred_element_type=jnp.float32
    )
    across_product = jnp.einsum(
        "hati,aki->hatk", received_gradient, adapter_output_map, preferred_element_type=jnp.float32
    ).astype(jnp.bfloat16)
    low_rank_state = jnp.einsum(
        "ptqv,tgv->ptqg", across_product, adapter_input_map, preferred_element_type=jnp.float32
    )
    capacity_slot_weight = received_weight.astype(jnp.float32)[..., None]
    hidden_state_gradient = (
        capacity_slot_weight * (frozen_term + adapter_scale * low_rank_state)
    ).astype(jnp.bfloat16)
    down_mapping = jnp.einsum(
        "lkgu,kup->lkgp", retained_rows, adapter_input_map, preferred_element_type=jnp.float32
    ).astype(jnp.bfloat16)
    complete_term = jnp.sum(frozen_term * retained_rows.astype(jnp.float32), axis=-1)
    adapter_term = jnp.einsum(
        "mesr,mesr->mes", down_mapping, across_product, preferred_element_type=jnp.float32
    )
    routing_rows = complete_term + adapter_scale * adapter_term
    scaled_gradient = (capacity_slot_weight * received_gradient).astype(jnp.bfloat16)
    scaled_across_product = (capacity_slot_weight * across_product.astype(jnp.float32)).astype(
        jnp.bfloat16
    )
    adapter_output_gradient = adapter_scale * jnp.einsum(
        "mesr,mesd->erd", down_mapping, scaled_gradient, preferred_element_type=jnp.float32
    )
    adapter_input_gradient = adapter_scale * jnp.einsum(
        "mesr,mesf->erf", scaled_across_product, retained_rows, preferred_element_type=jnp.float32
    )
    return (hidden_state_gradient, routing_rows, adapter_input_gradient, adapter_output_gradient)


def local(
    output_gradient,
    chosen_expert_index,
    routing_gate_weight,
    hidden,
    frozen_down_weight,
    adapter_input_map,
    adapter_output_map,
):
    sources = lax.axis_size("expert")
    per_device = frozen_down_weight.shape[0]
    experts = per_device * sources
    micro_count = hidden.shape[0]
    slot_count = hidden.shape[2]
    capacity = slot_count // sources
    top_count = chosen_expert_index.shape[1]
    model_width = output_gradient.shape[1]
    buffer_len = experts * capacity
    grad_rows = output_gradient.reshape(micro_count, -1, model_width)
    id_rows = chosen_expert_index.reshape(micro_count, -1)
    weight_rows = routing_gate_weight.reshape(micro_count, -1)
    send_rows = slot_rows(id_rows, experts, per_device, sources, capacity)
    sent_grad, sent_weight = dispatch_buffers(
        grad_rows, weight_rows, send_rows, top_count, buffer_len
    )
    sent_grad = sent_grad.reshape(micro_count, per_device, sources, capacity, model_width)
    sent_weight = sent_weight.reshape(micro_count, per_device, sources, capacity)
    received_gradient, received_weight = (
        lax.all_to_all(sent_grad, "expert", split_axis=2, concat_axis=2, tiled=True),
        lax.all_to_all(sent_weight, "expert", split_axis=2, concat_axis=2, tiled=True),
    )
    received_gradient = received_gradient.reshape(micro_count, per_device, slot_count, model_width)
    received_weight = received_weight.reshape(micro_count, per_device, slot_count)
    hidden_grad, routing_rows, adapter_input_gradient, adapter_output_gradient = expert_rows_view(
        received_gradient,
        received_weight,
        hidden,
        frozen_down_weight,
        adapter_input_map,
        adapter_output_map,
    )
    router_home = lax.all_to_all(
        routing_rows.reshape(micro_count, per_device, sources, capacity),
        "expert",
        split_axis=2,
        concat_axis=2,
        tiled=True,
    )
    router_flat = router_home.reshape(micro_count, buffer_len)
    router_grad = jax.vmap(pick_rows)(router_flat, send_rows).reshape(-1, top_count)
    share_a, share_b = (
        lax.psum_scatter(adapter_input_gradient, "dp", scatter_dimension=2, tiled=True),
        lax.psum_scatter(adapter_output_gradient, "dp", scatter_dimension=2, tiled=True),
    )
    return (hidden_grad, router_grad, share_a, share_b)


def solution(mesh):
    in_specs = (
        P(("dp", "expert"), None),
        P(("dp", "expert"), None),
        P(("dp", "expert"), None),
        P(None, ("dp", "expert"), None, None),
        P("expert", None, None),
        P("expert", None, None),
        P("expert", None, None),
    )
    out_specs = (
        P(None, ("dp", "expert"), None, None),
        P(("dp", "expert"), None),
        P("expert", None, "dp"),
        P("expert", None, "dp"),
    )
    return jax.shard_map(local, mesh=mesh, in_specs=in_specs, out_specs=out_specs, check_vma=False)
```

profile of v0, /device:TPU:0, one launch (start us, length us, event | category | flops | bytes accessed | tf_op | source)
XLA Modules:
  0.0 336.9 jit_solution(18004679260711959091)
XLA Ops:
  7.2 0.9 copy.39
  8.4 0.8 copy.38
  10.5 0.7 and_reduce_fusion
  11.2 0.7 multiply_reduce_fusion
  12.0 4.3 %scatter_custom_fusion = s32[1280]{0:T(1024)S(1)} fusion(s32[1024]{0:T(1024)S(1)} %bitcast.106, s32[1024]{0:T(1024)S(1)} %bitcast.105, s32[]{:T(128)} %constant.57.clone.1), kind=kCustom, calls=%fused_computation.73 | custom fusion | bytes 5124
  16.4 10.4 %gather_fusion = bf16[1280]{0:T(1024)(128)(2,1)S(1)} fusion(bf16[2,513]{1,0:T(2,128)(2,1)S(1)} %concatenate.6, s32[1280]{0:T(1024)S(1)} %reshape.195), kind=kCustom, calls=%fused_computation | custom fusion | bytes 15360 | tf_op jit(solution)/shard_map/vmap()/gather | solution.py:20
  27.0 0.8 copy.44
  27.8 6.3 %all-to-all-start = ((bf16[2,16,8,5]{1,0,3,2:T(2,128)(2,1)}), bf16[2,16,8,5]{1,0,3,2:T(2,128)(2,1)S(1)}, u32[]{:S(2)}, u32[]{:S(2)}) async-start(bf16[2,16,8,5]{1,0,3,2:T(2,128)(2,1)} %copy.44), calls=%async_computation | async-start | bytes 40960 | tf_op jit(solution)/shard_map/all_to_all | solution.py:115
  35.2 18.0 %gather_fusion.1 = bf16[1280,2048]{1,0:T(8,128)(2,1)} fusion(bf16[2,65,2048]{2,0,1:T(2,128)(2,1)S(1)} %concatenate.7, s32[1280]{0:T(1024)S(1)} %reshape.201), kind=kCustom, calls=%fused_computation.1 | custom fusion | bytes 10496000 | tf_op jit(solution)/shard_map/vmap()/gather | solution.py:20
  53.2 9.7 %reshape.185 = bf16[2,16,8,5,2048]{4,3,2,1,0:T(8,128)(2,1)} reshape(bf16[1280,2048]{1,0:T(8,128)(2,1)} %gather_fusion.1) | data formatting | bytes 10485760 | tf_op jit(solution)/shard_map/reshape | solution.py:111
  62.9 10.2 %copy.47 = bf16[2,16,8,5,2048]{4,1,3,0,2:T(8,128)(2,1)} copy(bf16[2,16,8,5,2048]{4,3,2,1,0:T(8,128)(2,1)} %reshape.185) | data formatting | bytes 10485760 | tf_op jit(solution)/shard_map/reshape | solution.py:111
  73.1 5.2 %all-to-all-start.1 = ((bf16[2,16,8,5,2048]{4,1,3,0,2:T(8,128)(2,1)}), bf16[2,16,8,5,2048]{4,1,3,0,2:T(8,128)(2,1)}, u32[]{:S(2)}, u32[]{:S(2)}) async-start(bf16[2,16,8,5,2048]{4,1,3,0,2:T(8,128)(2,1)} %copy.47), calls=%async_computation.1 | async-start | bytes 10485760 | tf_op jit(solution)/shard_map/all_to_all | solution.py:114
  79.2 115.7 %all-to-all-done.1 = bf16[2,16,8,5,2048]{4,1,3,0,2:T(8,128)(2,1)} async-done(((bf16[2,16,8,5,2048]{4,1,3,0,2:T(8,128)(2,1)}), bf16[2,16,8,5,2048]{4,1,3,0,2:T(8,128)(2,1)}, u32[]{:S(2)}, u32[]{:S(2)}) %all-to-all-start.1) | async-done | bytes 5242912 | tf_op jit(solution)/shard_map/all_to_all | solution.py:114
  194.9 3.1 copy.48
  198.6 4.0 %fusion.28 = (f32[2,16,40]{2,0,1:T(2,128)S(1)}, bf16[2,16,40,64]{3,2,0,1:T(8,128)(2,1)S(1)}) fusion(bf16[2,16,40,64]{3,2,0,1:T(8,128)(2,1)S(1)} %fusion.18, bf16[16,64,2048]{2,1,0:T(8,128)(2,1)S(1)} %copy-done.8, bf16[2,16,40,2048]{3,1,2,0:T(8,128)(2,1)S(1)} %bitcast.97), kind=kOutput, calls=%fused_computation.30 | convolution fusion | flops 335952640 | bytes 9769984 | tf_op jit(solution)/shard_map/hati,aki->hatk/dot_general | solution.py:55
  202.6 0.7 copy-done.3
  203.3 0.8 bitcast_multiply_fusion.2
  204.1 2.3 copy.71
  206.4 3.7 %reshape.240 = f32[384,1024]{1,0:T(8,128)} reshape(f32[384,16,64]{2,1,0:T(8,128)} %bitcast.100) | data formatting | bytes 3145728
  210.4 3.4 %multiply_convert_fusion = bf16[2,16,40,2048]{3,1,2,0:T(8,128)(2,1)S(1)} fusion(bf16[2,16,40,2048]{3,1,2,0:T(8,128)(2,1)} %bitcast.98, f32[2,16,40]{1,2,0:T(8,128)S(1)} %copy.57), kind=kLoop, calls=%fused_computation.6 | loop fusion | flops 7864320 | bytes 10490880 | tf_op jit(solution)/shard_map/convert_element_type | solution.py:73
  213.8 10.0 %bitcast_multiply_fusion = f32[16,64,2048]{2,1,0:T(8,128)} fusion(bf16[2,16,40,64]{3,2,0,1:T(8,128)(2,1)S(1)} %copy-done.7, bf16[2,16,40,2048]{3,1,2,0:T(8,128)(2,1)S(1)} %multiply_convert_fusion), kind=kOutput, calls=%fused_computation.7 | convolution fusion | flops 337641472 | bytes 13795328 | tf_op jit(solution)/shard_map/mesr,mesd->erd/dot_general | solution.py:77
  223.9 16.2 %fusion.12 = (f32[2,16,40]{2,0,1:T(2,128)S(1)}, f32[16,2,40,384]{3,2,1,0:T(8,128)S(1)}) fusion(bf16[2,16,40,384]{3,2,1,0:T(8,128)(2,1)} %param.10, bf16[16,384,2048]{2,1,0:T(8,128)(2,1)} %param.11, bf16[2,16,40,2048]{3,1,2,0:T(8,128)(2,1)} %bitcast.99), kind=kOutput, calls=%fused_computation.18 | convolution fusion | flops 2014739200 | bytes 33362944 | tf_op jit(solution)/shard_map/mesd,efd->mesf/dot_general | solution.py:52
  240.3 0.7 reshape.244
  241.0 3.3 all-to-all-start.2
  244.8 1.0 copy.59
  245.8 4.0 %all-to-all-done.2 = f32[8,1,160]{2,1,0:T(1,128)S(1)} async-done(((f32[8,1,160]{2,1,0:T(1,128)}), f32[8,1,160]{2,1,0:T(1,128)S(1)}, u32[]{:S(2)}, u32[]{:S(2)}) %all-to-all-start.2) | async-done | bytes 5152 | tf_op jit(solution)/shard_map/all_to_all | solution.py:127
  250.3 0.7 reduce.6
  251.4 9.1 %gather_fusion.2 = f32[1024]{0:T(1024)S(1)} fusion(f32[2,640]{1,0:T(2,128)S(1)} %reshape.188, s32[1024]{0:T(1024)S(1)} %bitcast.96), kind=kCustom, calls=%fused_computation.2 | custom fusion | bytes 16384 | tf_op jit(solution)/shard_map/vmap()/gather | solution.py:20
  260.7 0.7 copy.60
  261.3 1.2 reshape.241
  262.5 1.1 copy.72
  263.7 66.4 %reduce-scatter.5.cloned.1.call-done = f32[16,64,512]{2,1,0:T(8,128)} async-done(((f32[16,64,2048]{2,1,0:T(8,128)}), f32[16,64,512]{2,1,0:T(8,128)}) %reduce-scatter.5.cloned.1.call-update) | async-done | bytes 2097168 | tf_op jit(solution)/shard_map/reduce_scatter | solution.py:138
  (62 shorter events, 6.3 us)
Async XLA Ops:
  7.2 71.3 %copy-start = (bf16[16,384,64]{1,2,0:T(8,128)(2,1)S(1)}, bf16[16,384,64]{1,2,0:T(8,128)(2,1)}, u32[]{:S(2)}) copy-start(bf16[16,384,64]{1,2,0:T(8,128)(2,1)} %param.12) | copy-start | bytes 2359300
  7.2 27.0 %copy-start.5 = (bf16[128,2048]{1,0:T(8,128)(2,1)S(1)}, bf16[128,2048]{1,0:T(8,128)(2,1)}, u32[]{:S(2)}) copy-start(bf16[128,2048]{1,0:T(8,128)(2,1)} %param.7) | copy-start | bytes 1572868
  27.8 45.2 %all-to-all-start = ((bf16[2,16,8,5]{1,0,3,2:T(2,128)(2,1)}), bf16[2,16,8,5]{1,0,3,2:T(2,128)(2,1)S(1)}, u32[]{:S(2)}, u32[]{:S(2)}) async-start(bf16[2,16,8,5]{1,0,3,2:T(2,128)(2,1)} %copy.44), calls=%async_computation | async-start | bytes 40960 | tf_op jit(solution)/shard_map/all_to_all | solution.py:115
  73.0 5.5 %copy-start.2 = (bf16[2,16,40,384]{3,2,1,0:T(8,128)(2,1)S(1)}, bf16[2,16,40,384]{3,2,1,0:T(8,128)(2,1)}, u32[]{:S(2)}) copy-start(bf16[2,16,40,384]{3,2,1,0:T(8,128)(2,1)} %param.10) | copy-start | bytes 2949124
  73.1 121.8 %all-to-all-start.1 = ((bf16[2,16,8,5,2048]{4,1,3,0,2:T(8,128)(2,1)}), bf16[2,16,8,5,2048]{4,1,3,0,2:T(8,128)(2,1)}, u32[]{:S(2)}, u32[]{:S(2)}) async-start(bf16[2,16,8,5,2048]{4,1,3,0,2:T(8,128)(2,1)} %copy.47), calls=%async_computation.1 | async-start | bytes 10485760 | tf_op jit(solution)/shard_map/all_to_all | solution.py:114
  78.3 183.0 %reduce-scatter.7.cloned.1.call-start = ((), (), s32[]{:S(2)}) async-start(), calls=%async_computation.6 | async-start | bytes 1966080
  79.0 118.9 %copy-start.6 = (bf16[2,16,40,64]{3,2,0,1:T(8,128)(2,1)}, bf16[2,16,40,64]{3,2,0,1:T(8,128)(2,1)S(1)}, u32[]{:S(2)}) copy-start(bf16[2,16,40,64]{3,2,0,1:T(8,128)(2,1)S(1)} %fusion.18) | copy-start | bytes 491524
  194.9 3.7 %copy-start.8 = (bf16[16,64,2048]{2,1,0:T(8,128)(2,1)S(1)}, bf16[16,64,2048]{2,1,0:T(8,128)(2,1)}, u32[]{:S(2)}) copy-start(bf16[16,64,2048]{2,1,0:T(8,128)(2,1)} %param.13) | copy-start | bytes 12582916
  198.0 4.6 %copy-start.1 = (bf16[2,16,8,5,2048]{4,1,3,2,0:T(8,128)(2,1)}, bf16[2,16,8,5,2048]{4,1,3,2,0:T(8,128)(2,1)S(1)}, u32[]{:S(2)}) copy-start(bf16[2,16,8,5,2048]{4,1,3,2,0:T(8,128)(2,1)S(1)} %copy.48) | copy-start | bytes 15728644
  202.6 0.7 copy-start.3
  210.1 120.0 %reduce-scatter.5.cloned.1.call-start = ((), (), s32[]{:S(2)}) async-start(), calls=%async_computation.5 | async-start | bytes 10485760 | tf_op jit(solution)/shard_map/reduce_scatter | solution.py:138
  210.4 3.5 %copy-start.7 = (bf16[2,16,40,64]{3,2,0,1:T(8,128)(2,1)S(1)}, bf16[2,16,40,64]{3,2,0,1:T(8,128)(2,1)}, u32[]{:S(2)}) copy-start(bf16[2,16,40,64]{3,2,0,1:T(8,128)(2,1)} %copy-done.6) | copy-start | bytes 491524
  223.9 20.3 %copy-start.4 = (bf16[2,16,40,64]{3,2,0,1:T(8,128)(2,1)S(1)}, bf16[2,16,40,64]{3,2,0,1:T(8,128)(2,1)}, u32[]{:S(2)}) copy-start(bf16[2,16,40,64]{3,2,0,1:T(8,128)(2,1)} %copy-done.3) | copy-start | bytes 491524
  241.0 8.8 %all-to-all-start.2 = ((f32[8,1,160]{2,1,0:T(1,128)}), f32[8,1,160]{2,1,0:T(1,128)S(1)}, u32[]{:S(2)}, u32[]{:S(2)}) async-start(f32[8,1,160]{2,1,0:T(1,128)} %reshape.244), calls=%async_computation.2 | async-start | bytes 16384 | tf_op jit(solution)/shard_map/all_to_all | solution.py:127
Sparse Core Ops, SparseCore 0:
  210.2 29.8 reduce-scatter.6
  243.7 86.3 reduce-scatter.4
where the time goes:
time: 338 us; the launch traced here: 337 us
  waiting for transfers between devices  186 us (55%)
  local copies, waits for them, and re-layouts  82.4 us (24%)
  matrix products  32 us (9%)
  starting transfers between devices  15.3 us (5%)
  between operations  14.4 us (4%)
  other arithmetic  6.66 us (2%)
    all_to_all x1, waiting for transfers between devices, local(): lax.all_to_all(sent_grad, 'expert', split_axis=2, concat_axis=2, tiled=True)  116 us
    reduce_scatter x1, waiting for transfers between devices, local(): lax.psum_scatter(adapter_output_gradient, 'dp', scatter_dimension=2, tile...  66.4 us
    gather x5, local copies, waits for them, and re-layouts, pick_rows(): return source[indices]  37.5 us
    reshape x2, local copies, waits for them, and re-layouts, local(): sent_grad.reshape(micro_count, per_device, sources, capacity, model_width)  19.9 us
    unnamed x33, local copies, waits for them, and re-layouts  18.2 us
    dot_general x1, matrix products, expert_rows_view(): jnp.einsum('mesd,efd->mesf', received_gradient, frozen_down_weight, prefe...  16.2 us
    dot_general x1, matrix products, expert_rows_view(): jnp.einsum('mesr,mesd->erd', down_mapping, scaled_gradient, preferred_ele...  10 us
  transfers between devices with their start and end apart: 5, of which 3 were waited for; matrix products, arithmetic and copies ran while one was open for 25% of the time, Pallas kernels for 0%

commit v1 on v0

--- a/solution.py
+++ b/solution.py
@@ -1,6 +1,10 @@
+import functools
+
 import jax
 import jax.numpy as jnp
 from jax import lax
+from jax.experimental import pallas as pl
+from jax.experimental.pallas import tpu as pltpu
 from jax.sharding import PartitionSpec as P
 
 adapter_scale = 2.0
@@ -83,7 +87,7 @@
     return (hidden_state_gradient, routing_rows, adapter_input_gradient, adapter_output_gradient)
 
 
-def local(
+def local_by_slots(
     output_gradient,
     chosen_expert_index,
     routing_gate_weight,
@@ -140,6 +144,234 @@
     return (hidden_grad, router_grad, share_a, share_b)
 
 
+def pad_rows(count):
+    return -(-count // 16) * 16
+
+
+def expert_kernel(
+    capacity,
+    meta_ref,
+    dy_hbm,
+    hidden_ref,
+    weight_hbm,
+    amap_ref,
+    bmap_hbm,
+    hg_ref,
+    rk_ref,
+    la_ref,
+    lb_ref,
+    dy_s,
+    wb_s,
+    rows_s,
+    code_s,
+    gate_s,
+    back_s,
+    dy_sem,
+    w_sem,
+    b_sem,
+):
+    sources, twice_top, span = meta_ref.shape
+    top = twice_top // 2
+    micro, experts, slots, units = hidden_ref.shape
+    rank = la_ref.shape[1]
+    width = dy_hbm.shape[1]
+    block = span // micro
+    padded = rows_s.shape[1] // micro
+    base = (lax.axis_index("expert") * experts).astype(jnp.float32)
+
+    dy_copy = pltpu.make_async_copy(dy_hbm, dy_s, dy_sem)
+    dy_copy.start()
+
+    def weight_copies(x):
+        return (
+            pltpu.make_async_copy(weight_hbm.at[x], wb_s.at[x, pl.ds(0, units)], w_sem.at[x]),
+            pltpu.make_async_copy(bmap_hbm.at[x], wb_s.at[x, pl.ds(units, rank)], b_sem.at[x]),
+        )
+
+    for x in range(experts):
+        for copy in weight_copies(x):
+            copy.start()
+
+    number = lax.broadcasted_iota(jnp.int32, (experts, span), 0).astype(jnp.float32) + base
+    from_row = lax.broadcasted_iota(jnp.int32, (span, span), 0)
+    to_row = lax.broadcasted_iota(jnp.int32, (span, span), 1)
+    earlier = jnp.where(
+        (from_row // block == to_row // block) & (from_row < to_row), 1.0, 0.0
+    ).astype(jnp.bfloat16)
+    codes, gates = [], []
+    for j in range(sources):
+        named = jnp.zeros((experts, span), jnp.float32)
+        gate = jnp.zeros((experts, span), jnp.float32)
+        for k in range(top):
+            hit = meta_ref[j, k : k + 1, :] == number
+            named = jnp.where(hit, 1.0, named)
+            gate = jnp.where(hit, meta_ref[j, top + k : top + k + 1, :], gate)
+        before = jnp.dot(named.astype(jnp.bfloat16), earlier, preferred_element_type=jnp.float32)
+        codes.append(jnp.where(named > 0.0, before + float(j * capacity), -1.0))
+        gates.append(gate)
+
+    slot_of = lax.broadcasted_iota(jnp.int32, (padded, sources * block), 0).astype(jnp.float32)
+    picks = []
+    for m in range(micro):
+        part = slice(m * block, (m + 1) * block)
+        code_m = jnp.concatenate([c[:, part] for c in codes], axis=1)
+        gate_m = jnp.concatenate([g[:, part] for g in gates], axis=1)
+        code_s[m] = code_m
+        chosen = []
+        for x in range(experts):
+            hit = code_m[x : x + 1, :] == slot_of
+            chosen.append(jnp.where(hit, 1.0, 0.0).astype(jnp.bfloat16))
+            gate_s[x, m * padded : (m + 1) * padded, :] = jnp.sum(
+                jnp.where(hit, gate_m[x : x + 1, :], 0.0), axis=1, keepdims=True
+            )
+        picks.append(jnp.concatenate(chosen, axis=0))
+
+    dy_copy.wait()
+    tile = 512 if width % 512 == 0 else width
+    for m in range(micro):
+        for n in range(width // tile):
+            cols = slice(n * tile, (n + 1) * tile)
+            tokens = jnp.concatenate(
+                [
+                    dy_s[j * span + m * block : j * span + (m + 1) * block, cols]
+                    for j in range(sources)
+                ],
+                axis=0,
+            )
+            rows = jnp.dot(picks[m], tokens, preferred_element_type=jnp.float32)
+            rows_s[:, m * padded : (m + 1) * padded, cols] = rows.astype(jnp.bfloat16).reshape(
+                experts, padded, tile
+            )
+
+    contract_last = (((1,), (1,)), ((), ()))
+    contract_first = (((0,), (0,)), ((), ()))
+
+    def one_expert(x, carry):
+        for copy in weight_copies(x):
+            copy.wait()
+        rows = rows_s[x]
+        both = lax.dot_general(rows, wb_s[x], contract_last, preferred_element_type=jnp.float32)
+        main = both[:, :units]
+        v = both[:, units:].astype(jnp.bfloat16)
+        amap = amap_ref[x]
+        low = lax.dot_general(v, amap, contract_last, preferred_element_type=jnp.float32)
+        gate = gate_s[x]
+        grad = (gate * (main + adapter_scale * low)).astype(jnp.bfloat16)
+        filler = jnp.zeros((padded - slots, units), jnp.float32)
+        pieces = []
+        for m in range(micro):
+            hg_ref[m, x] = grad[m * padded : m * padded + slots]
+            pieces.append(hidden_ref[m, x].astype(jnp.float32))
+            pieces.append(filler)
+        held_wide = jnp.concatenate(pieces, axis=0)
+        held = held_wide.astype(jnp.bfloat16)
+        u = jnp.dot(held, amap, preferred_element_type=jnp.float32).astype(jnp.bfloat16)
+        v_wide = v.astype(jnp.float32)
+        routed = jnp.sum(main * held_wide, axis=1, keepdims=True) + adapter_scale * jnp.sum(
+            u.astype(jnp.float32) * v_wide, axis=1, keepdims=True
+        )
+        for m in range(micro):
+            hit = code_s[m, pl.ds(x, 1), :] == slot_of
+            back_s[m, pl.ds(x, 1), :] = jnp.sum(
+                jnp.where(hit, routed[m * padded : (m + 1) * padded], 0.0), axis=0, keepdims=True
+            )
+        q = (gate * rows.astype(jnp.float32)).astype(jnp.bfloat16)
+        w = (gate * v_wide).astype(jnp.bfloat16)
+        lb_ref[x] = (
+            adapter_scale
+            * lax.dot_general(u, q, contract_first, preferred_element_type=jnp.float32)
+        ).astype(lb_ref.dtype)
+        la_ref[x] = (
+            adapter_scale
+            * lax.dot_general(w, held, contract_first, preferred_element_type=jnp.float32)
+        ).astype(la_ref.dtype)
+        return carry
+
+    lax.fori_loop(0, experts, one_expert, 0)
+
+    for j in range(sources):
+        back = jnp.concatenate(
+            [back_s[m, :, j * block : (j + 1) * block] for m in range(micro)], axis=1
+        )
+        for k in range(top):
+            rk_ref[j, k : k + 1, :] = jnp.sum(
+                jnp.where(meta_ref[j, k : k + 1, :] == number, back, 0.0), axis=0, keepdims=True
+            )
+
+
+def local_by_tokens(
+    output_gradient,
+    chosen_expert_index,
+    routing_gate_weight,
+    hidden,
+    frozen_down_weight,
+    adapter_input_map,
+    adapter_output_map,
+):
+    sources = lax.axis_size("expert")
+    micro, experts, slots, units = hidden.shape
+    span, top = chosen_expert_index.shape
+    width = output_gradient.shape[1]
+    rank = adapter_input_map.shape[2]
+    capacity = slots // sources
+    block = span // micro
+    padded = pad_rows(slots)
+    meta = jnp.concatenate(
+        [
+            chosen_expert_index.T.astype(jnp.float32),
+            routing_gate_weight.T.astype(jnp.float32),
+        ],
+        axis=0,
+    )
+    meta = lax.all_gather(meta, "expert", axis=0)
+    tokens = lax.all_gather(output_gradient, "expert", axis=0, tiled=True)
+    vmem = pl.BlockSpec(memory_space=pltpu.VMEM)
+    anywhere = pl.BlockSpec(memory_space=pl.ANY)
+    hidden_grad, routed, share_a, share_b = pl.pallas_call(
+        functools.partial(expert_kernel, capacity),
+        out_shape=(
+            jax.ShapeDtypeStruct(hidden.shape, jnp.bfloat16),
+            jax.ShapeDtypeStruct((sources, top, span), jnp.float32),
+            jax.ShapeDtypeStruct((experts, rank, units), jnp.bfloat16),
+            jax.ShapeDtypeStruct((experts, rank, width), jnp.bfloat16),
+        ),
+        in_specs=[vmem, anywhere, vmem, anywhere, vmem, anywhere],
+        out_specs=(vmem, vmem, vmem, vmem),
+        scratch_shapes=[
+            pltpu.VMEM((sources * span, width), jnp.bfloat16),
+            pltpu.VMEM((experts, units + rank, width), jnp.bfloat16),
+            pltpu.VMEM((experts, micro * padded, width), jnp.bfloat16),
+            pltpu.VMEM((micro, experts, sources * block), jnp.float32),
+            pltpu.VMEM((experts, micro * padded, 1), jnp.float32),
+            pltpu.VMEM((micro, experts, sources * block), jnp.float32),
+            pltpu.SemaphoreType.DMA,
+            pltpu.SemaphoreType.DMA((experts,)),
+            pltpu.SemaphoreType.DMA((experts,)),
+        ],
+        compiler_params=pltpu.CompilerParams(vmem_limit_bytes=58 * 1024 * 1024),
+        cost_estimate=pl.CostEstimate(
+            flops=2 * experts * micro * padded * width * (2 * (units + rank) + sources * block),
+            bytes_accessed=2 * experts * width * (units + 3 * rank),
+            transcendentals=0,
+        ),
+        name="expert_rows",
+    )(meta, tokens, hidden, frozen_down_weight, adapter_input_map, adapter_output_map)
+    home = lax.all_to_all(routed, "expert", split_axis=0, concat_axis=0, tiled=True)
+    router_grad = jnp.sum(home, axis=0).T
+    lora_a = lax.psum_scatter(share_a, "dp", scatter_dimension=2, tiled=True)
+    lora_b = lax.psum_scatter(share_b, "dp", scatter_dimension=2, tiled=True)
+    return (hidden_grad, router_grad, lora_a.astype(jnp.float32), lora_b.astype(jnp.float32))
+
+
+def local(*arrays):
+    sources = lax.axis_size("expert")
+    gathered = sources * arrays[0].shape[0]
+    by_slot = arrays[3].shape[0] * arrays[4].shape[0] * arrays[3].shape[2]
+    if gathered <= by_slot:
+        return local_by_tokens(*arrays)
+    return local_by_slots(*arrays)
+
+
 def solution(mesh):
     in_specs = (
         P(("dp", "expert"), None),

time: 338 us -> 190 us (0.56)
  waiting for transfers between devices: 186 us -> 102 us
  local copies, waits for them, and re-layouts: 82.4 us -> 8.11 us
  Pallas kernels: 0 us -> 35.3 us
  matrix products: 32 us -> 0 us
  blocking collectives: 0 us -> 24.7 us
  starting transfers between devices: 15.3 us -> 0.12 us
    all_to_all x3 -> x0, waiting for transfers between devices: 120 us -> none  [the longest x1 116 us: local(): lax.all_to_all(sent_grad, 'expert', split_axis=2, concat_axis=2, tiled=True)]
    gather x5 -> x0, local copies, waits for them, and re-layouts: 37.5 us -> none  [pick_rows(): return source[indices]]
    pallas_call x0 -> x1, Pallas kernels: none -> 35.3 us  [local_by_tokens(): pl.pallas_call(functools.partial(expert_kernel, capacity), out_shape=(jax...]
    dot_general x6 -> x0, matrix products: 32 us -> none  [the longest x1 16.2 us: expert_rows_view(): jnp.einsum('mesd,efd->mesf', received_gradient, frozen_down_weight, prefe...]
    all_gather x0 -> x1, waiting for transfers between devices: none -> 31.5 us  [local_by_tokens(): tokens = lax.all_gather(output_gradient, 'expert', axis=0, tiled=True)]
    reshape x9 -> x0, local copies, waits for them, and re-layouts: 21.9 us -> none  [the longest x2 19.9 us: local(): sent_grad.reshape(micro_count, per_device, sources, capacity, model_width)]
    unnamed x3 -> x4, waiting for transfers between devices: 0.03 us -> 17 us
    all_gather x0 -> x1, blocking collectives: none -> 16.6 us  [local_by_tokens(): meta = lax.all_gather(meta, 'expert', axis=0)]
  transfers between devices with their start and end apart: 5 -> 3, of which waited for: 3 -> 3; matrix products, arithmetic and copies ran while one was open for 25% -> 4% of each run, Pallas kernels for 0% -> 0%
where the time goes in v1:
time: 190 us; the launch traced here: 189 us
  waiting for transfers between devices  102 us (54%)
  Pallas kernels  35.3 us (19%)
  blocking collectives  24.7 us (13%)
  between operations  13.8 us (7%)
  local copies, waits for them, and re-layouts  8.11 us (4%)
  other arithmetic  5.65 us (3%)
    reduce_scatter x1, waiting for transfers between devices, local_by_tokens(): lora_b = lax.psum_scatter(share_b, 'dp', scatter_dimension=2, tiled=True)  53.2 us
    pallas_call x1, Pallas kernels, local_by_tokens(): pl.pallas_call(functools.partial(expert_kernel, capacity), out_shape=(jax...  35.3 us
    all_gather x1, waiting for transfers between devices, local_by_tokens(): tokens = lax.all_gather(output_gradient, 'expert', axis=0, tiled=True)  31.5 us
    unnamed x4, waiting for transfers between devices  17 us
    all_gather x1, blocking collectives, local_by_tokens(): meta = lax.all_gather(meta, 'expert', axis=0)  16.6 us
    all_to_all x1, blocking collectives, local_by_tokens(): lax.all_to_all(routed, 'expert', split_axis=0, concat_axis=0, tiled=True)  8.13 us
    unnamed x7, local copies, waits for them, and re-layouts  8.11 us
  transfers between devices with their start and end apart: 3, of which 3 were waited for; matrix products, arithmetic and copies ran while one was open for 4% of the time, Pallas kernels for 0%

profile of v1, /device:TPU:0, one launch (start us, length us, event | category | flops | bytes accessed | tf_op | source)
XLA Modules:
  0.0 189.5 jit_solution(2169454985950178159)
XLA Ops:
  7.2 0.0 all-gather.3.cloned.1.call-start
  7.2 0.7 all-gather.3.cloned.1.call-update
  7.9 0.0 reduce-scatter.7.cloned.1.call-start
  7.9 2.5 %copy.12.amap_ref = bf16[16,384,64]{2,1,0:T(8,128)(2,1)} copy(bf16[16,384,64]{1,2,0:T(8,128)(2,1)} %param.12) | data formatting | bytes 1572864 | tf_op args[5]
  10.4 0.7 convert_bitcast_fusion
  11.1 0.7 convert_bitcast_fusion.1
  11.8 16.6 %all-gather = f32[128,128]{1,0:T(8,128)} all-gather(f32[16,128]{1,0:T(8,128)S(1)} %pad_maximum_fusion), channel_id=2, replica_groups=mesh['dp'=4,'expert'=8] {'expert'}, dimensions={0}, use_global_device_ids=true | all-gather | bytes 73728 | tf_op jit(solution)/shard_map/all_gather | solution.py:326
  28.3 31.5 %all-gather.3.cloned.1.call-done.dy_hbm = bf16[1024,2048]{1,0:T(8,128)(2,1)} async-done(((bf16[128,2048]{1,0:T(8,128)(2,1)}), bf16[1024,2048]{1,0:T(8,128)(2,1)}) %all-gather.3.cloned.1.call-update) | async-done | bytes 4194320 | tf_op jit(solution)/shard_map/all_gather | solution.py:327
  59.9 35.3 %expert_rows.1 = (bf16[2,16,40,384]{3,2,1,0:T(8,128)(2,1)}, f32[8,8,128]{2,1,0:T(8,128)}, bf16[16,64,384]{2,1,0:T(8,128)(2,1)}, bf16[16,64,2048]{2,1,0:T(8,128)(2,1)}) custom-call(f32[8,16,128]{2,1,0:T(8,128)} %bitcast.10, bf16[1024,2048]{1,0:T(8,128)(2,1)} %all-gather.3.cloned.1.call-done.dy_hbm, bf16[2,16,40,384]{3,2,1,0:T(8,128)(2,1)} %hidden_ref.1, ...), custom_call_target="tpu_custom_call" | custom-call | flops 8858370048 | bytes 37748736 | tf_op jit(solution)/shard_map/expert_rows/pallas_call | solution.py:330
  95.2 2.2 %copy.13 = bf16[16,64,384]{1,0,2:T(8,128)(2,1)S(1)} copy(bf16[16,64,384]{2,1,0:T(8,128)(2,1)} %get-tuple-element.10) | data formatting | bytes 1572864
  97.4 0.0 copy-start
  97.4 1.9 reshape.9
  99.3 0.0 reduce-scatter.7.cloned.1.call-update
  99.3 0.0 reduce-scatter.5.cloned.1.call-start
  99.4 0.7 reduce-scatter.5.cloned.1.call-update
  100.0 0.0 copy-done
  100.1 8.1 %all_to_all.5 = f32[8,8,128]{2,1,0:T(8,128)S(1)} all-to-all(f32[8,8,128]{2,1,0:T(8,128)S(1)} %copy-done), channel_id=1, replica_groups=mesh['dp'=4,'expert'=8] {'expert'}, dimensions={0} | all-to-all | bytes 65536 | tf_op jit(solution)/shard_map/all_to_all | solution.py:359
  108.2 0.6 reduce_sum.9
  108.8 15.6 %reduce-scatter.7.cloned.1.call-done = bf16[96,1024]{1,0:T(8,128)(2,1)} async-done(((bf16[384,1024]{1,0:T(8,128)(2,1)}), bf16[96,1024]{1,0:T(8,128)(2,1)}) %reduce-scatter.7.cloned.1.call-update) | async-done | bytes 196624
  124.4 1.2 reshape.10
  125.7 0.4 copy.14
  126.0 0.8 convert_element_type.22
  126.9 53.2 %reduce-scatter.5.cloned.1.call-done = bf16[16,64,512]{2,1,0:T(8,128)(2,1)} async-done(((bf16[16,64,2048]{2,1,0:T(8,128)(2,1)}), bf16[16,64,512]{2,1,0:T(8,128)(2,1)}) %reduce-scatter.5.cloned.1.call-update) | async-done | bytes 1048592 | tf_op jit(solution)/shard_map/reduce_scatter | solution.py:362
  180.1 2.8 %convert_element_type.23 = f32[16,64,512]{2,1,0:T(8,128)} convert(bf16[16,64,512]{2,1,0:T(8,128)(2,1)} %reduce-scatter.5.cloned.1.call-done) | non-fusion elementwise | flops 524288 | bytes 3145728 | tf_op jit(solution)/shard_map/convert_element_type | solution.py:363
  (1 shorter events, 0.0 us)
Async XLA Ops:
  7.2 52.7 %all-gather.3.cloned.1.call-start = ((), (), s32[]{:S(2)}) async-start(), calls=%async_computation.3 | async-start | bytes 4718592 | tf_op jit(solution)/shard_map/all_gather | solution.py:327
  7.9 116.5 %reduce-scatter.7.cloned.1.call-start = ((), (), s32[]{:S(2)}) async-start(), calls=%async_computation.5 | async-start | bytes 983040
  97.4 2.6 %copy-start = (f32[8,8,128]{2,1,0:T(8,128)S(1)}, f32[8,8,128]{2,1,0:T(8,128)}, u32[]{:S(2)}) copy-start(f32[8,8,128]{2,1,0:T(8,128)} %get-tuple-element.9) | copy-start | bytes 98308
  99.3 80.8 %reduce-scatter.5.cloned.1.call-start = ((), (), s32[]{:S(2)}) async-start(), calls=%async_computation.4 | async-start | bytes 5242880 | tf_op jit(solution)/shard_map/reduce_scatter | solution.py:362
Sparse Core Ops, SparseCore 0:
  9.6 50.2 all-gather.2
  99.4 24.9 reduce-scatter.6
  127.4 52.6 reduce-scatter.4

commit v2 on v1

--- a/solution.py
+++ b/solution.py
@@ -148,113 +148,109 @@
     return -(-count // 16) * 16
 
 
-def expert_kernel(
-    capacity,
-    meta_ref,
-    dy_hbm,
-    hidden_ref,
-    weight_hbm,
-    amap_ref,
-    bmap_hbm,
-    hg_ref,
-    rk_ref,
-    la_ref,
-    lb_ref,
-    dy_s,
-    wb_s,
-    rows_s,
-    code_s,
-    gate_s,
-    back_s,
-    dy_sem,
-    w_sem,
-    b_sem,
-):
-    sources, twice_top, span = meta_ref.shape
-    top = twice_top // 2
-    micro, experts, slots, units = hidden_ref.shape
-    rank = la_ref.shape[1]
-    width = dy_hbm.shape[1]
+def slot_codes(meta, owners_ref, first, capacity, experts, micro):
+    shards = meta.shape[0]
+    top, span = meta.shape[1] // 2, meta.shape[2]
     block = span // micro
-    padded = rows_s.shape[1] // micro
-    base = (lax.axis_index("expert") * experts).astype(jnp.float32)
-
-    dy_copy = pltpu.make_async_copy(dy_hbm, dy_s, dy_sem)
-    dy_copy.start()
-
-    def weight_copies(x):
-        return (
-            pltpu.make_async_copy(weight_hbm.at[x], wb_s.at[x, pl.ds(0, units)], w_sem.at[x]),
-            pltpu.make_async_copy(bmap_hbm.at[x], wb_s.at[x, pl.ds(units, rank)], b_sem.at[x]),
-        )
-
-    for x in range(experts):
-        for copy in weight_copies(x):
-            copy.start()
-
-    number = lax.broadcasted_iota(jnp.int32, (experts, span), 0).astype(jnp.float32) + base
+    number = lax.broadcasted_iota(jnp.int32, (experts, span), 0).astype(jnp.float32) + first
     from_row = lax.broadcasted_iota(jnp.int32, (span, span), 0)
     to_row = lax.broadcasted_iota(jnp.int32, (span, span), 1)
     earlier = jnp.where(
         (from_row // block == to_row // block) & (from_row < to_row), 1.0, 0.0
     ).astype(jnp.bfloat16)
     codes, gates = [], []
-    for j in range(sources):
+    for j in range(shards):
         named = jnp.zeros((experts, span), jnp.float32)
         gate = jnp.zeros((experts, span), jnp.float32)
         for k in range(top):
-            hit = meta_ref[j, k : k + 1, :] == number
+            hit = meta[j, k : k + 1, :] == number
             named = jnp.where(hit, 1.0, named)
-            gate = jnp.where(hit, meta_ref[j, top + k : top + k + 1, :], gate)
+            gate = jnp.where(hit, meta[j, top + k : top + k + 1, :], gate)
         before = jnp.dot(named.astype(jnp.bfloat16), earlier, preferred_element_type=jnp.float32)
-        codes.append(jnp.where(named > 0.0, before + float(j * capacity), -1.0))
+        offset = (owners_ref[j] * capacity).astype(jnp.float32)
+        codes.append(jnp.where(named > 0.0, before + offset, -1.0))
         gates.append(gate)
-
-    slot_of = lax.broadcasted_iota(jnp.int32, (padded, sources * block), 0).astype(jnp.float32)
+    parts = [slice(m * block, (m + 1) * block) for m in range(micro)]
+    return (
+        [jnp.concatenate([c[:, part] for c in codes], axis=1) for part in parts],
+        [jnp.concatenate([g[:, part] for g in gates], axis=1) for part in parts],
+    )
+
+
+contract_last = (((1,), (1,)), ((), ()))
+contract_first = (((0,), (0,)), ((), ()))
+
+
+def expert_kernel(capacity, group_count, shards, *refs):
+    owners_ref, meta_ref = refs[:2]
+    token_refs = refs[2 : 2 + shards]
+    hidden_ref, u_ref, weight_hbm, amap_ref, bmap_hbm = refs[2 + shards : 7 + shards]
+    hg_ref, rk_ref = refs[7 + shards : 9 + shards]
+    la_refs = refs[9 + shards : 9 + shards + group_count]
+    dy_s, wb_s, rows_s, code_s, gate_s, back_s, dy_sem, w_sem, b_sem = refs[
+        9 + shards + group_count :
+    ]
+    twice_top, span = meta_ref.shape[1:]
+    top = twice_top // 2
+    micro, experts, slots, units = hidden_ref.shape
+    rank = amap_ref.shape[1]
+    width = dy_s.shape[2]
+    block = span // micro
+    padded = rows_s.shape[1] // micro
+    first = (lax.axis_index("expert") * experts).astype(jnp.float32)
+    group = lax.axis_index("dp")
+
+    token_copies = [
+        pltpu.make_async_copy(token_refs[i].at[pl.ds(0, span)], dy_s.at[i], dy_sem.at[i])
+        for i in range(shards)
+    ]
+    for copy in token_copies:
+        copy.start()
+
+    def weight_copies(x):
+        return (
+            pltpu.make_async_copy(weight_hbm.at[x], wb_s.at[x, pl.ds(0, units)], w_sem.at[x]),
+            pltpu.make_async_copy(bmap_hbm.at[x], wb_s.at[x, pl.ds(units, rank)], b_sem.at[x]),
+        )
+
+    for x in range(experts):
+        for copy in weight_copies(x):
+            copy.start()
+
+    codes, gates = slot_codes(meta_ref[...], owners_ref, first, capacity, experts, micro)
+    slot_of = lax.broadcasted_iota(jnp.int32, (padded, shards * block), 0).astype(jnp.float32)
     picks = []
     for m in range(micro):
-        part = slice(m * block, (m + 1) * block)
-        code_m = jnp.concatenate([c[:, part] for c in codes], axis=1)
-        gate_m = jnp.concatenate([g[:, part] for g in gates], axis=1)
-        code_s[m] = code_m
+        code_s[m] = codes[m]
         chosen = []
         for x in range(experts):
-            hit = code_m[x : x + 1, :] == slot_of
+            hit = codes[m][x : x + 1, :] == slot_of
             chosen.append(jnp.where(hit, 1.0, 0.0).astype(jnp.bfloat16))
             gate_s[x, m * padded : (m + 1) * padded, :] = jnp.sum(
-                jnp.where(hit, gate_m[x : x + 1, :], 0.0), axis=1, keepdims=True
+                jnp.where(hit, gates[m][x : x + 1, :], 0.0), axis=1, keepdims=True
             )
         picks.append(jnp.concatenate(chosen, axis=0))
 
-    dy_copy.wait()
+    for copy in token_copies:
+        copy.wait()
     tile = 512 if width % 512 == 0 else width
     for m in range(micro):
         for n in range(width // tile):
             cols = slice(n * tile, (n + 1) * tile)
             tokens = jnp.concatenate(
-                [
-                    dy_s[j * span + m * block : j * span + (m + 1) * block, cols]
-                    for j in range(sources)
-                ],
-                axis=0,
+                [dy_s[i, m * block : (m + 1) * block, cols] for i in range(shards)], axis=0
             )
             rows = jnp.dot(picks[m], tokens, preferred_element_type=jnp.float32)
             rows_s[:, m * padded : (m + 1) * padded, cols] = rows.astype(jnp.bfloat16).reshape(
                 experts, padded, tile
             )
 
-    contract_last = (((1,), (1,)), ((), ()))
-    contract_first = (((0,), (0,)), ((), ()))
-
-    def one_expert(x, carry):
-        for copy in weight_copies(x):
-            copy.wait()
+    def one_expert(x):
         rows = rows_s[x]
         both = lax.dot_general(rows, wb_s[x], contract_last, preferred_element_type=jnp.float32)
         main = both[:, :units]
         v = both[:, units:].astype(jnp.bfloat16)
-        amap = amap_ref[x]
-        low = lax.dot_general(v, amap, contract_last, preferred_element_type=jnp.float32)
+        low = jnp.dot(v, amap_ref[x], preferred_element_type=jnp.float32)
         gate = gate_s[x]
         grad = (gate * (main + adapter_scale * low)).astype(jnp.bfloat16)
         filler = jnp.zeros((padded - slots, units), jnp.float32)
@@ -265,38 +261,111 @@
             pieces.append(filler)
         held_wide = jnp.concatenate(pieces, axis=0)
         held = held_wide.astype(jnp.bfloat16)
-        u = jnp.dot(held, amap, preferred_element_type=jnp.float32).astype(jnp.bfloat16)
         v_wide = v.astype(jnp.float32)
         routed = jnp.sum(main * held_wide, axis=1, keepdims=True) + adapter_scale * jnp.sum(
-            u.astype(jnp.float32) * v_wide, axis=1, keepdims=True
+            u_ref[x].astype(jnp.float32) * v_wide, axis=1, keepdims=True
         )
         for m in range(micro):
             hit = code_s[m, pl.ds(x, 1), :] == slot_of
             back_s[m, pl.ds(x, 1), :] = jnp.sum(
                 jnp.where(hit, routed[m * padded : (m + 1) * padded], 0.0), axis=0, keepdims=True
             )
-        q = (gate * rows.astype(jnp.float32)).astype(jnp.bfloat16)
         w = (gate * v_wide).astype(jnp.bfloat16)
-        lb_ref[x] = (
-            adapter_scale
-            * lax.dot_general(u, q, contract_first, preferred_element_type=jnp.float32)
-        ).astype(lb_ref.dtype)
-        la_ref[x] = (
-            adapter_scale
-            * lax.dot_general(w, held, contract_first, preferred_element_type=jnp.float32)
-        ).astype(la_ref.dtype)
+        la = adapter_scale * lax.dot_general(
+            w, held, contract_first, preferred_element_type=jnp.float32
+        )
+        share = units // group_count
+        for s in range(group_count):
+            aim = lax.rem(group + s, group_count)
+            mine = la[:, :share]
+            for k in range(1, group_count):
+                mine = jnp.where(aim == k, la[:, k * share : (k + 1) * share], mine)
+            la_refs[s][x] = mine.astype(la_refs[s].dtype)
+
+    batch = 2 if experts % 2 == 0 else 1
+
+    def some_experts(step, carry):
+        for i in range(batch):
+            for copy in weight_copies(step * batch + i):
+                copy.wait()
+        for i in range(batch):
+            one_expert(step * batch + i)
         return carry
 
-    lax.fori_loop(0, experts, one_expert, 0)
-
-    for j in range(sources):
+    lax.fori_loop(0, experts // batch, some_experts, 0)
+
+    number = lax.broadcasted_iota(jnp.int32, (experts, span), 0).astype(jnp.float32) + first
+    for i in range(shards):
         back = jnp.concatenate(
-            [back_s[m, :, j * block : (j + 1) * block] for m in range(micro)], axis=1
-        )
-        for k in range(top):
-            rk_ref[j, k : k + 1, :] = jnp.sum(
-                jnp.where(meta_ref[j, k : k + 1, :] == number, back, 0.0), axis=0, keepdims=True
-            )
+            [back_s[m, :, i * block : (i + 1) * block] for m in range(micro)], axis=1
+        )
+        found = [
+            jnp.sum(
+                jnp.where(meta_ref[i, k : k + 1, :] == number, back, 0.0), axis=0, keepdims=True
+            )
+            for k in range(top)
+        ]
+        rk_ref[owners_ref[i]] = jnp.concatenate(found, axis=0)
+
+
+def adapter_kernel(capacity, micro, group_count, shards, *refs):
+    owners_ref, meta_ref = refs[:2]
+    token_refs = refs[2 : 2 + shards]
+    near_refs = refs[2 + shards : 1 + shards + group_count]
+    far_refs = refs[1 + shards + group_count : shards + 2 * group_count]
+    u_refs = refs[shards + 2 * group_count : shards + 3 * group_count]
+    lb_ref, tok_s, q_s, u_s, sem = refs[shards + 3 * group_count :]
+    span = meta_ref.shape[3]
+    experts, tall, rank = u_refs[0].shape
+    share = lb_ref.shape[2]
+    half = shards // 2
+    padded = tall // micro
+    block = span // micro
+    first = (lax.axis_index("expert") * experts).astype(jnp.float32)
+    group = lax.axis_index("dp")
+    cols = pl.ds(pl.multiple_of(group * share, share), share)
+    copies = []
+    for g in range(group_count):
+        for i in range(shards):
+            if g == 0:
+                source = token_refs[i].at[pl.ds(0, span), cols]
+            elif i < half:
+                source = near_refs[g - 1].at[i, pl.ds(0, span)]
+            else:
+                source = far_refs[g - 1].at[i - half, pl.ds(0, span)]
+            copies.append(pltpu.make_async_copy(source, tok_s.at[g, i], sem.at[g, i]))
+    for copy in copies:
+        copy.start()
+    slot_of = lax.broadcasted_iota(jnp.int32, (padded, shards * block), 0).astype(jnp.float32)
+    for g in range(group_count):
+        u_s[:, g * tall : (g + 1) * tall, :] = u_refs[g][...]
+        codes, gates = slot_codes(meta_ref[g], owners_ref, first, capacity, experts, micro)
+        for i in range(shards):
+            copies[g * shards + i].wait()
+        for m in range(micro):
+            picks = jnp.concatenate(
+                [
+                    jnp.where(
+                        codes[m][x : x + 1, :] == slot_of, gates[m][x : x + 1, :], 0.0
+                    ).astype(jnp.bfloat16)
+                    for x in range(experts)
+                ],
+                axis=0,
+            )
+            tokens = jnp.concatenate(
+                [tok_s[g, i, m * block : (m + 1) * block, :] for i in range(shards)], axis=0
+            )
+            q = jnp.dot(picks, tokens, preferred_element_type=jnp.float32).astype(jnp.bfloat16)
+            at = g * tall + m * padded
+            q_s[:, at : at + padded, :] = q.reshape(experts, padded, share)
+    for x in range(experts):
+        lb_ref[x] = adapter_scale * lax.dot_general(
+            u_s[x], q_s[x], contract_first, preferred_element_type=jnp.float32
+        )
+
+
+def ring_order(count):
+    return list(range(0, count, 2)) + list(range(1, count, 2))[::-1]
 
 
 def local_by_tokens(
@@ -309,6 +378,7 @@
     adapter_output_map,
 ):
     sources = lax.axis_size("expert")
+    group_count = lax.axis_size("dp")
     micro, experts, slots, units = hidden.shape
     span, top = chosen_expert_index.shape
     width = output_gradient.shape[1]
@@ -316,58 +386,153 @@
     capacity = slots // sources
     block = span // micro
     padded = pad_rows(slots)
-    meta = jnp.concatenate(
+    share = width // group_count
+    pairs = sources // 2
+    me = lax.axis_index("expert")
+    group = lax.axis_index("dp")
+
+    order = ring_order(pairs)
+    place = {z: i for i, z in enumerate(order)}
+    ring = [
+        (2 * z + c, 2 * order[(place[z] + 1) % pairs] + c) for z in range(pairs) for c in range(2)
+    ]
+    swap = [(e, e ^ 1) for e in range(sources)]
+    owner_table = [
         [
-            chosen_expert_index.T.astype(jnp.float32),
-            routing_gate_weight.T.astype(jnp.float32),
+            2 * order[(place[e // 2] - i) % pairs] + (e % 2 if near else 1 - e % 2)
+            for near in (True, False)
+            for i in range(pairs)
+        ]
+        for e in range(sources)
+    ]
+    owners = jnp.asarray(owner_table, jnp.int32)[me]
+
+    amap = jnp.swapaxes(adapter_input_map, 1, 2)
+    u = jnp.einsum("mesk,exk->emsx", hidden, amap, preferred_element_type=jnp.float32)
+    u = u.astype(jnp.bfloat16)
+    u = jnp.pad(u, ((0, 0), (0, 0), (0, padded - slots), (0, 0))).reshape(
+        experts, micro * padded, rank
+    )
+
+    def shift_groups(array, by):
+        return lax.ppermute(
+            array, "dp", [(d, (d + by) % group_count) for d in range(group_count)]
+        )
+
+    u_all = [u] + [shift_groups(u, s) for s in range(1, group_count)]
+
+    names = jnp.concatenate(
+        [chosen_expert_index.T.astype(jnp.bfloat16), routing_gate_weight.T], axis=0
+    )
+    lines = 2 * top * span // share
+    names = jnp.tile(names.reshape(lines, share), (1, group_count))
+    extra = -(-lines // 8) * 8
+    sent = jnp.concatenate(
+        [output_gradient, jnp.pad(names, ((0, extra - lines), (0, 0)))], axis=0
+    )
+
+    near = [sent]
+    for _ in range(pairs - 1):
+        near.append(lax.ppermute(near[-1], "expert", ring))
+    far = [lax.ppermute(piece, "expert", swap) for piece in near]
+    pieces = near + far
+
+    def names_of(piece):
+        return piece[..., span : span + lines, :share].reshape(
+            piece.shape[:-2] + (2 * top, span)
+        )
+
+    own_meta = jnp.stack([names_of(piece) for piece in pieces]).astype(jnp.float32)
+
+    crossing, returned = [], []
+    for s in range(1, group_count):
+        aim = lax.rem(group + s, group_count) * share
+        columns = jnp.stack(
+            [lax.dynamic_slice_in_dim(piece, aim, share, axis=1) for piece in near]
+        )
+        crossing.append(shift_groups(columns, s))
+    for columns in crossing:
+        returned.append(lax.ppermute(columns, "expert", swap))
+    all_meta = jnp.concatenate(
+        [own_meta[None]]
+        + [
+            jnp.concatenate([names_of(a), names_of(b)], axis=0)[None].astype(jnp.float32)
+            for a, b in zip(crossing, returned)
         ],
         axis=0,
     )
-    meta = lax.all_gather(meta, "expert", axis=0)
-    tokens = lax.all_gather(output_gradient, "expert", axis=0, tiled=True)
+
     vmem = pl.BlockSpec(memory_space=pltpu.VMEM)
+    smem = pl.BlockSpec(memory_space=pltpu.SMEM)
     anywhere = pl.BlockSpec(memory_space=pl.ANY)
-    hidden_grad, routed, share_a, share_b = pl.pallas_call(
-        functools.partial(expert_kernel, capacity),
+    part_a = jax.ShapeDtypeStruct((experts, rank, units // group_count), jnp.bfloat16)
+    hidden_grad, routed, *parts = pl.pallas_call(
+        functools.partial(expert_kernel, capacity, group_count, sources),
         out_shape=(
             jax.ShapeDtypeStruct(hidden.shape, jnp.bfloat16),
             jax.ShapeDtypeStruct((sources, top, span), jnp.float32),
-            jax.ShapeDtypeStruct((experts, rank, units), jnp.bfloat16),
-            jax.ShapeDtypeStruct((experts, rank, width), jnp.bfloat16),
-        ),
-        in_specs=[vmem, anywhere, vmem, anywhere, vmem, anywhere],
-        out_specs=(vmem, vmem, vmem, vmem),
+        )
+        + (part_a,) * group_count,
+        in_specs=[smem, vmem] + [anywhere] * sources + [vmem, vmem, anywhere, vmem, anywhere],
+        out_specs=(vmem,) * (2 + group_count),
         scratch_shapes=[
-            pltpu.VMEM((sources * span, width), jnp.bfloat16),
+            pltpu.VMEM((sources, span, width), jnp.bfloat16),
             pltpu.VMEM((experts, units + rank, width), jnp.bfloat16),
             pltpu.VMEM((experts, micro * padded, width), jnp.bfloat16),
             pltpu.VMEM((micro, experts, sources * block), jnp.float32),
             pltpu.VMEM((experts, micro * padded, 1), jnp.float32),
             pltpu.VMEM((micro, experts, sources * block), jnp.float32),
-            pltpu.SemaphoreType.DMA,
+            pltpu.SemaphoreType.DMA((sources,)),
             pltpu.SemaphoreType.DMA((experts,)),
             pltpu.SemaphoreType.DMA((experts,)),
         ],
         compiler_params=pltpu.CompilerParams(vmem_limit_bytes=58 * 1024 * 1024),
         cost_estimate=pl.CostEstimate(
-            flops=2 * experts * micro * padded * width * (2 * (units + rank) + sources * block),
-            bytes_accessed=2 * experts * width * (units + 3 * rank),
+            flops=2 * experts * micro * padded * width * (units + rank + sources * block),
+            bytes_accessed=2 * experts * width * (units + rank) + 2 * sources * span * width,
             transcendentals=0,
         ),
         name="expert_rows",
-    )(meta, tokens, hidden, frozen_down_weight, adapter_input_map, adapter_output_map)
+    )(owners, own_meta, *pieces, hidden, u, frozen_down_weight, amap, adapter_output_map)
+
     home = lax.all_to_all(routed, "expert", split_axis=0, concat_axis=0, tiled=True)
     router_grad = jnp.sum(home, axis=0).T
-    lora_a = lax.psum_scatter(share_a, "dp", scatter_dimension=2, tiled=True)
-    lora_b = lax.psum_scatter(share_b, "dp", scatter_dimension=2, tiled=True)
-    return (hidden_grad, router_grad, lora_a.astype(jnp.float32), lora_b.astype(jnp.float32))
+    lora_a = parts[0].astype(jnp.float32)
+    for s in range(1, group_count):
+        lora_a = lora_a + shift_groups(parts[s], s).astype(jnp.float32)
+
+    lora_b = pl.pallas_call(
+        functools.partial(adapter_kernel, capacity, micro, group_count, sources),
+        out_shape=jax.ShapeDtypeStruct((experts, rank, share), jnp.float32),
+        in_specs=[smem, vmem]
+        + [anywhere] * (sources + 2 * (group_count - 1))
+        + [vmem] * group_count,
+        out_specs=vmem,
+        scratch_shapes=[
+            pltpu.VMEM((group_count, sources, span, share), jnp.bfloat16),
+            pltpu.VMEM((experts, group_count * micro * padded, share), jnp.bfloat16),
+            pltpu.VMEM((experts, group_count * micro * padded, rank), jnp.bfloat16),
+            pltpu.SemaphoreType.DMA((group_count, sources)),
+        ],
+        compiler_params=pltpu.CompilerParams(vmem_limit_bytes=40 * 1024 * 1024),
+        cost_estimate=pl.CostEstimate(
+            flops=2 * experts * micro * padded * share * group_count * (rank + sources * block),
+            bytes_accessed=2 * group_count * sources * span * share + 4 * experts * rank * share,
+            transcendentals=0,
+        ),
+        name="adapter_columns",
+    )(owners, all_meta, *pieces, *crossing, *returned, *u_all)
+    return (hidden_grad, router_grad, lora_a, lora_b)
 
 
 def local(*arrays):
-    sources = lax.axis_size("expert")
-    gathered = sources * arrays[0].shape[0]
-    by_slot = arrays[3].shape[0] * arrays[4].shape[0] * arrays[3].shape[2]
-    if gathered <= by_slot:
+    sources, groups = lax.axis_size("expert"), lax.axis_size("dp")
+    span, width = arrays[0].shape
+    top, (micro, experts, slots, units) = arrays[1].shape[1], arrays[3].shape
+    even = sources % 2 == 0 and width % (128 * groups) == 0 and units % groups == 0
+    packs = 2 * top * span % (width // groups) == 0 and (width // groups) % span == 0
+    exact = experts * sources <= 256
+    if even and packs and exact and sources * span <= micro * experts * slots:
         return local_by_tokens(*arrays)
     return local_by_slots(*arrays)
 

time: 190 us -> 157 us (0.83)
  waiting for transfers between devices: 102 us -> 56.3 us
  starting transfers between devices: 0.12 us -> 27.3 us
  blocking collectives: 24.7 us -> 0 us
  between operations: 13.8 us -> 1.23 us
  local copies, waits for them, and re-layouts: 8.11 us -> 18.9 us
  Pallas kernels: 35.3 us -> 42 us
  other arithmetic: 5.65 us -> 8.63 us
    reduce_scatter x1 -> x0, waiting for transfers between devices: 53.2 us -> none  [local_by_tokens(): lora_b = lax.psum_scatter(share_b, 'dp', scatter_dimension=2, tiled=True)]
    ppermute x0 -> x19, waiting for transfers between devices: none -> 51.2 us  [the longest x9 26.8 us: shift_groups(): lax.ppermute(array, 'dp', [(d, (d + by) % group_count) for d in range(gro...]
    all_gather x1 -> x0, waiting for transfers between devices: 31.5 us -> none  [local_by_tokens(): tokens = lax.all_gather(output_gradient, 'expert', axis=0, tiled=True)]
    ppermute x0 -> x19, starting transfers between devices: none -> 22.5 us  [the longest x9 11.2 us: shift_groups(): lax.ppermute(array, 'dp', [(d, (d + by) % group_count) for d in range(gro...]
    unnamed x4 -> x0, waiting for transfers between devices: 17 us -> none
    all_gather x1 -> x0, blocking collectives: 16.6 us -> none  [local_by_tokens(): meta = lax.all_gather(meta, 'expert', axis=0)]
    all_to_all x1 -> x0, blocking collectives: 8.13 us -> none  [local_by_tokens(): lax.all_to_all(routed, 'expert', split_axis=0, concat_axis=0, tiled=True)]
    another operation x0 -> x23, local copies, waits for them, and re-layouts: none -> 7.73 us  [the longest x18 6.21 us: local_by_tokens(): jnp.stack([names_of(piece) for piece in pieces]).astype(jnp.float32)]
  transfers between devices with their start and end apart: 3 -> 20, of which waited for: 3 -> 9; matrix products, arithmetic and copies ran while one was open for 4% -> 14% of each run, Pallas kernels for 0% -> 21%
where the time goes in v2:
time: 157 us; the launch traced here: 156 us
  waiting for transfers between devices  56.3 us (36%)
  Pallas kernels  42 us (27%)
  starting transfers between devices  27.3 us (17%)
  local copies, waits for them, and re-layouts  18.9 us (12%)
  other arithmetic  8.63 us (5%)
  matrix products  1.62 us (1%)
    pallas_call x1, Pallas kernels, local_by_tokens(): pl.pallas_call(functools.partial(expert_kernel, capacity, group_count, so...  32.4 us
    ppermute x9, waiting for transfers between devices, shift_groups(): lax.ppermute(array, 'dp', [(d, (d + by) % group_count) for d in range(gro...  26.8 us
    ppermute x3, waiting for transfers between devices, local_by_tokens(): near.append(lax.ppermute(near[-1], 'expert', ring))  22.5 us
    ppermute x9, starting transfers between devices, shift_groups(): lax.ppermute(array, 'dp', [(d, (d + by) % group_count) for d in range(gro...  11.2 us
    ppermute x3, starting transfers between devices, local_by_tokens(): near.append(lax.ppermute(near[-1], 'expert', ring))  10.8 us
    pallas_call x1, Pallas kernels, local_by_tokens(): pl.pallas_call(functools.partial(adapter_kernel, capacity, micro, group_c...  9.59 us
    another operation x18, local copies, waits for them, and re-layouts, local_by_tokens(): jnp.stack([names_of(piece) for piece in pieces]).astype(jnp.float32)  6.21 us
    slice x14, local copies, waits for them, and re-layouts, names_of(): piece[..., span:span + lines, :share]  5.34 us
  transfers between devices with their start and end apart: 20, of which 9 were waited for; matrix products, arithmetic and copies ran while one was open for 14% of the time, Pallas kernels for 21%

profile of v2, /device:TPU:0, one launch (start us, length us, event | category | flops | bytes accessed | tf_op | source)
XLA Modules:
  0.0 156.0 jit_solution(10890607710697935582)
XLA Ops:
  2.1 1.1 fusion.3.refs_2_
  3.2 4.1 %collective-permute-start = (bf16[136,2048]{1,0:T(8,128)(2,1)S(1)}, bf16[136,2048]{1,0:T(8,128)(2,1)S(1)}, u32[]{:S(2)}, u32[]{:S(2)}) collective-permute-start(bf16[136,2048]{1,0:T(8,128)(2,1)S(1)} %fusion.3.refs_2_), channel_id=1, source_target_pairs={{0,4},{1,5},{2,0},{3,1},{4,6},{5,7},{6,2},{7,3},{8,12},{9,13},{10,... | collective-permute-start | bytes 1671176 | tf_op jit(solution)/shard_map/ppermute | solution.py:436
  7.3 1.6 %convolution_convert_fusion = bf16[16,2,40,64]{3,2,1,0:T(8,128)(2,1)S(1)} fusion(bf16[2,16,40,384]{3,2,1,0:T(8,128)(2,1)S(1)} %copy-done.16, bf16[16,384,64]{1,2,0:T(8,128)(2,1)} %param.13), kind=kOutput, calls=%fused_computation | convolution fusion | flops 62996480 | bytes 1933312 | tf_op jit(solution)/shard_map/mesk,exk->emsx/dot_general | solution.py:411
  9.0 0.8 pad.9
  9.9 9.4 %collective-permute-done.refs_3_ = bf16[136,2048]{1,0:T(8,128)(2,1)S(1)} collective-permute-done((bf16[136,2048]{1,0:T(8,128)(2,1)S(1)}, bf16[136,2048]{1,0:T(8,128)(2,1)S(1)}, u32[]{:S(2)}, u32[]{:S(2)}) %collective-permute-start) | collective-permute-done | bytes 557088 | tf_op jit(solution)/shard_map/ppermute | solution.py:436
  19.2 3.4 %collective-permute-start.1 = (bf16[136,2048]{1,0:T(8,128)(2,1)S(1)}, bf16[136,2048]{1,0:T(8,128)(2,1)S(1)}, u32[]{:S(2)}, u32[]{:S(2)}) collective-permute-start(bf16[136,2048]{1,0:T(8,128)(2,1)S(1)} %collective-permute-done.refs_3_), channel_id=1, source_target_pairs={{0,4},{1,5},{2,0},{3,1},{4,6},{5,7},{6,2},{7,3},{8,12},{9,13},{10,... | collective-permute-start | bytes 1671176 | tf_op jit(solution)/shard_map/ppermute | solution.py:436
  22.6 1.2 fusion.4.refs_0_
  24.6 9.0 %collective-permute-done.1.refs_4_ = bf16[136,2048]{1,0:T(8,128)(2,1)S(1)} collective-permute-done((bf16[136,2048]{1,0:T(8,128)(2,1)S(1)}, bf16[136,2048]{1,0:T(8,128)(2,1)S(1)}, u32[]{:S(2)}, u32[]{:S(2)}) %collective-permute-start.1) | collective-permute-done | bytes 557088 | tf_op jit(solution)/shard_map/ppermute | solution.py:436
  33.6 3.4 %collective-permute-start.2 = (bf16[136,2048]{1,0:T(8,128)(2,1)S(1)}, bf16[136,2048]{1,0:T(8,128)(2,1)S(1)}, u32[]{:S(2)}, u32[]{:S(2)}) collective-permute-start(bf16[136,2048]{1,0:T(8,128)(2,1)S(1)} %collective-permute-done.1.refs_4_), channel_id=1, source_target_pairs={{0,4},{1,5},{2,0},{3,1},{4,6},{5,7},{6,2},{7,3},{8,12},{9,13},{10,... | collective-permute-start | bytes 1671176 | tf_op jit(solution)/shard_map/ppermute | solution.py:436
  43.0 4.1 %collective-permute-done.2.refs_5_ = bf16[136,2048]{1,0:T(8,128)(2,1)S(1)} collective-permute-done((bf16[136,2048]{1,0:T(8,128)(2,1)S(1)}, bf16[136,2048]{1,0:T(8,128)(2,1)S(1)}, u32[]{:S(2)}, u32[]{:S(2)}) %collective-permute-start.2) | collective-permute-done | bytes 557088 | tf_op jit(solution)/shard_map/ppermute | solution.py:436
  49.6 1.0 pad_maximum_fusion
  50.7 1.5 collective-permute-start.10
  52.2 0.9 pad_maximum_fusion.1
  53.1 1.5 collective-permute-start.12
  54.7 1.5 collective-permute-start.14
  56.3 1.8 %collective-permute-done.6.refs_9_ = bf16[136,2048]{1,0:T(8,128)(2,1)S(1)} collective-permute-done((bf16[136,2048]{1,0:T(8,128)(2,1)S(1)}, bf16[136,2048]{1,0:T(8,128)(2,1)S(1)}, u32[]{:S(2)}, u32[]{:S(2)}) %collective-permute-start.6) | collective-permute-done | bytes 557088 | tf_op jit(solution)/shard_map/ppermute | solution.py:437
  58.9 8.4 %collective-permute-done.10.refs_10_ = bf16[4,136,512]{2,1,0:T(8,128)(2,1)} collective-permute-done((bf16[4,136,512]{2,1,0:T(8,128)(2,1)S(1)}, bf16[4,136,512]{2,1,0:T(8,128)(2,1)}, u32[]{:S(2)}, u32[]{:S(2)}) %collective-permute-start.10) | collective-permute-done | bytes 557088 | tf_op jit(solution)/shard_map/ppermute | solution.py:418
  67.3 32.4 %expert_rows.1 = (bf16[2,16,40,384]{3,2,1,0:T(8,128)(2,1)}, f32[8,8,128]{2,1,0:T(8,128)}, bf16[16,64,96]{2,1,0:T(8,128)(2,1)}, bf16[16,64,96]{2,1,0:T(8,128)(2,1...) custom-call(s32[8]{0:T(128)} %fusion.4.refs_0_, f32[8,16,128]{2,1,0:T(8,128)} %convert_element_type.57.refs_1_, ...), custom_call_target="tpu_custom_call" | custom-call | flops 6039797760 | bytes 33554432 | tf_op jit(solution)/shard_map/expert_rows/pallas_call | solution.py:469
  100.9 1.5 collective-permute-start.8
  102.4 7.4 %collective-permute-done.7 = bf16[16,64,96]{2,1,0:T(8,128)(2,1)} collective-permute-done((bf16[16,64,96]{2,1,0:T(8,128)(2,1)}, bf16[16,64,96]{2,1,0:T(8,128)(2,1)}, u32[]{:S(2)}, u32[]{:S(2)}) %collective-permute-start.7) | collective-permute-done | bytes 196640 | tf_op jit(solution)/shard_map/ppermute | solution.py:418
  112.7 4.8 %all-to-all-start = ((f32[8,8,128]{2,1,0:T(8,128)}), f32[8,8,128]{2,1,0:T(8,128)S(1)}, u32[]{:S(2)}, u32[]{:S(2)}) async-start(f32[8,8,128]{2,1,0:T(8,128)} %get-tuple-element.11), calls=%async_computation | async-start | bytes 65536 | tf_op jit(solution)/shard_map/all_to_all | solution.py:498
  118.2 5.1 %all-to-all-done = f32[8,8,128]{2,1,0:T(8,128)S(1)} async-done(((f32[8,8,128]{2,1,0:T(8,128)}), f32[8,8,128]{2,1,0:T(8,128)S(1)}, u32[]{:S(2)}, u32[]{:S(2)}) %all-to-all-start) | async-done | bytes 32800 | tf_op jit(solution)/shard_map/all_to_all | solution.py:498
  123.9 1.5 collective-permute-start.16
  125.4 1.5 collective-permute-start.17
  126.9 0.9 collective-permute-start.18
  127.8 2.1 %convert_add_fusion = f32[16,64,96]{2,1,0:T(8,128)} fusion(bf16[16,64,96]{2,1,0:T(8,128)(2,1)} %collective-permute-done.9, bf16[16,64,96]{2,1,0:T(8,128)(2,1)S(1)} %collective-permute-done.8, bf16[16,64,96]{2,1,0:T(8,128)(2,1)} %collective-permute-done.7, bf16[16,64,96]{2,1,0:T(8,128)(2,1)} %get-tuple-element.12), kind=kLoop, calls=%fused_computation.9 | loop fusion | flops 688128 | bytes 1179648 | tf_op jit(solution)/shard_map/add | solution.py:502
  132.2 0.8 maximum_convert_fusion.refs_1_
  133.0 3.9 %collective-permute-done.16.refs_17_ = bf16[16,96,64]{2,1,0:T(8,128)(2,1)} collective-permute-done((bf16[16,96,64]{2,1,0:T(8,128)(2,1)S(1)}, bf16[16,96,64]{2,1,0:T(8,128)(2,1)}, u32[]{:S(2)}, u32[]{:S(2)}) %collective-permute-start.16) | collective-permute-done | bytes 196640 | tf_op jit(solution)/shard_map/ppermute | solution.py:418
  137.0 7.1 %collective-permute-done.17.refs_18_ = bf16[16,96,64]{2,1,0:T(8,128)(2,1)} collective-permute-done((bf16[16,96,64]{2,1,0:T(8,128)(2,1)S(1)}, bf16[16,96,64]{2,1,0:T(8,128)(2,1)}, u32[]{:S(2)}, u32[]{:S(2)}) %collective-permute-start.17) | collective-permute-done | bytes 196640 | tf_op jit(solution)/shard_map/ppermute | solution.py:418
  144.1 1.0 copy-done.12
  145.2 1.1 copy-done.14
  146.2 9.6 %adapter_columns.1 = f32[16,64,512]{2,1,0:T(8,128)} custom-call(s32[8]{0:T(128)S(1)} %copy-done.15, f32[4,8,16,128]{3,2,1,0:T(8,128)S(1)} %maximum_convert_fusion.refs_1_, bf16[136,2048]{1,0:T(8,128)(2,1)S(1)} %copy-done.1, bf16[136,2048]{1,0:T(8,128)(2,1)S(1)} %copy-done.3, bf16[136,2048]{1,0:T(8,128)(2,1)S(1)} %copy-done.5, ...), custom_call_target="tpu_custom_call" | custom-call | flops 3623878656 | bytes 6291456 | tf_op jit(solution)/shard_map/adapter_columns/pallas_call | solution.py:504
  (138 shorter events, 19.3 us)
Async XLA Ops:
  3.2 20.5 %copy-start = (bf16[136,2048]{1,0:T(8,128)(2,1)}, bf16[136,2048]{1,0:T(8,128)(2,1)S(1)}, u32[]{:S(2)}) copy-start(bf16[136,2048]{1,0:T(8,128)(2,1)S(1)} %fusion.3.refs_2_) | copy-start | bytes 1671172
  3.2 16.0 %collective-permute-start = (bf16[136,2048]{1,0:T(8,128)(2,1)S(1)}, bf16[136,2048]{1,0:T(8,128)(2,1)S(1)}, u32[]{:S(2)}, u32[]{:S(2)}) collective-permute-start(bf16[136,2048]{1,0:T(8,128)(2,1)S(1)} %fusion.3.refs_2_), channel_id=1, source_target_pairs={{0,4},{1,5},{2,0},{3,1},{4,6},{5,7},{6,2},{7,3},{8,12},{9,13},{10,... | collective-permute-start | bytes 1671176 | tf_op jit(solution)/shard_map/ppermute | solution.py:436
  7.3 16.5 %collective-permute-start.3 = (bf16[136,2048]{1,0:T(8,128)(2,1)S(1)}, bf16[136,2048]{1,0:T(8,128)(2,1)S(1)}, u32[]{:S(2)}, u32[]{:S(2)}) collective-permute-start(bf16[136,2048]{1,0:T(8,128)(2,1)S(1)} %fusion.3.refs_2_), channel_id=1, source_target_pairs={{0,1},{1,0},{2,3},{3,2},{4,5},{5,4},{6,7},{7,6},{8,9},{9,8},{10,11... | collective-permute-start | bytes 1671176 | tf_op jit(solution)/shard_map/ppermute | solution.py:437
  19.2 23.7 %copy-start.2 = (bf16[136,2048]{1,0:T(8,128)(2,1)}, bf16[136,2048]{1,0:T(8,128)(2,1)S(1)}, u32[]{:S(2)}) copy-start(bf16[136,2048]{1,0:T(8,128)(2,1)S(1)} %collective-permute-done.refs_3_) | copy-start | bytes 1671172
  19.2 14.4 %collective-permute-start.1 = (bf16[136,2048]{1,0:T(8,128)(2,1)S(1)}, bf16[136,2048]{1,0:T(8,128)(2,1)S(1)}, u32[]{:S(2)}, u32[]{:S(2)}) collective-permute-start(bf16[136,2048]{1,0:T(8,128)(2,1)S(1)} %collective-permute-done.refs_3_), channel_id=1, source_target_pairs={{0,4},{1,5},{2,0},{3,1},{4,6},{5,7},{6,2},{7,3},{8,12},{9,13},{10,... | collective-permute-start | bytes 1671176 | tf_op jit(solution)/shard_map/ppermute | solution.py:436
  22.6 16.3 %collective-permute-start.4 = (bf16[136,2048]{1,0:T(8,128)(2,1)S(1)}, bf16[136,2048]{1,0:T(8,128)(2,1)}, u32[]{:S(2)}, u32[]{:S(2)}) collective-permute-start(bf16[136,2048]{1,0:T(8,128)(2,1)S(1)} %collective-permute-done.refs_3_), channel_id=1, source_target_pairs={{0,1},{1,0},{2,3},{3,2},{4,5},{5,4},{6,7},{7,6},{8,9},{9,8},{10,11... | collective-permute-start | bytes 1671176 | tf_op jit(solution)/shard_map/ppermute | solution.py:437
  23.9 25.7 %copy-start.9 = (bf16[136,2048]{1,0:T(8,128)(2,1)}, bf16[136,2048]{1,0:T(8,128)(2,1)S(1)}, u32[]{:S(2)}) copy-start(bf16[136,2048]{1,0:T(8,128)(2,1)S(1)} %collective-permute-done.3.refs_6_) | copy-start | bytes 1671172
  33.6 13.5 %collective-permute-start.2 = (bf16[136,2048]{1,0:T(8,128)(2,1)S(1)}, bf16[136,2048]{1,0:T(8,128)(2,1)S(1)}, u32[]{:S(2)}, u32[]{:S(2)}) collective-permute-start(bf16[136,2048]{1,0:T(8,128)(2,1)S(1)} %collective-permute-done.1.refs_4_), channel_id=1, source_target_pairs={{0,4},{1,5},{2,0},{3,1},{4,6},{5,7},{6,2},{7,3},{8,12},{9,13},{10,... | collective-permute-start | bytes 1671176 | tf_op jit(solution)/shard_map/ppermute | solution.py:436
  37.0 11.3 %collective-permute-start.5 = (bf16[136,2048]{1,0:T(8,128)(2,1)S(1)}, bf16[136,2048]{1,0:T(8,128)(2,1)S(1)}, u32[]{:S(2)}, u32[]{:S(2)}) collective-permute-start(bf16[136,2048]{1,0:T(8,128)(2,1)S(1)} %collective-permute-done.1.refs_4_), channel_id=1, source_target_pairs={{0,1},{1,0},{2,3},{3,2},{4,5},{5,4},{6,7},{7,6},{8,9},{9,8},{10,11... | collective-permute-start | bytes 1671176 | tf_op jit(solution)/shard_map/ppermute | solution.py:437
  50.7 16.6 %collective-permute-start.10 = (bf16[4,136,512]{2,1,0:T(8,128)(2,1)S(1)}, bf16[4,136,512]{2,1,0:T(8,128)(2,1)}, u32[]{:S(2)}, u32[]{:S(2)}) collective-permute-start(bf16[4,136,512]{2,1,0:T(8,128)(2,1)S(1)} %pad_maximum_fusion), channel_id=1, source_target_pairs={{0,8},{8,16},{16,24},{24,0},{1,9},{9,17},{17,25},{25,1},{2,10},{10... | collective-permute-start | bytes 1671176 | tf_op jit(solution)/shard_map/ppermute | solution.py:418
  53.1 47.2 %collective-permute-start.12 = (bf16[4,136,512]{2,1,0:T(8,128)(2,1)}, bf16[4,136,512]{2,1,0:T(8,128)(2,1)}, u32[]{:S(2)}, u32[]{:S(2)}) collective-permute-start(bf16[4,136,512]{2,1,0:T(8,128)(2,1)} %pad_maximum_fusion.1), channel_id=1, source_target_pairs={{0,16},{8,24},{16,0},{24,8},{1,17},{9,25},{17,1},{25,9},{2,18},{10... | collective-permute-start | bytes 1671176 | tf_op jit(solution)/shard_map/ppermute | solution.py:418
  54.7 45.9 %collective-permute-start.14 = (bf16[4,136,512]{2,1,0:T(8,128)(2,1)S(1)}, bf16[4,136,512]{2,1,0:T(8,128)(2,1)}, u32[]{:S(2)}, u32[]{:S(2)}) collective-permute-start(bf16[4,136,512]{2,1,0:T(8,128)(2,1)S(1)} %pad_maximum_fusion.2), channel_id=1, source_target_pairs={{0,24},{8,0},{16,8},{24,16},{1,25},{9,1},{17,9},{25,17},{2,26},{10... | collective-permute-start | bytes 1671176 | tf_op jit(solution)/shard_map/ppermute | solution.py:418
  56.2 2.0 %collective-permute-start.6 = (bf16[136,2048]{1,0:T(8,128)(2,1)S(1)}, bf16[136,2048]{1,0:T(8,128)(2,1)S(1)}, u32[]{:S(2)}, u32[]{:S(2)}) collective-permute-start(bf16[136,2048]{1,0:T(8,128)(2,1)S(1)} %collective-permute-done.2.refs_5_), channel_id=1, source_target_pairs={{0,1},{1,0},{2,3},{3,2},{4,5},{5,4},{6,7},{7,6},{8,9},{9,8},{10,11... | collective-permute-start | bytes 1671176 | tf_op jit(solution)/shard_map/ppermute | solution.py:437
  67.3 59.6 %collective-permute-start.11 = (bf16[4,136,512]{2,1,0:T(8,128)(2,1)}, bf16[4,136,512]{2,1,0:T(8,128)(2,1)}, u32[]{:S(2)}, u32[]{:S(2)}) collective-permute-start(bf16[4,136,512]{2,1,0:T(8,128)(2,1)} %collective-permute-done.10.refs_10_), channel_id=1, source_target_pairs={{0,1},{1,0},{2,3},{3,2},{4,5},{5,4},{6,7},{7,6},{8,9},{9,8},{10,11... | collective-permute-start | bytes 1671176 | tf_op jit(solution)/shard_map/ppermute | solution.py:455
  67.3 33.6 %copy-start.21 = (bf16[1,1,16,128]{3,2,1,0:T(8,128)(2,1)S(1)}, bf16[1,1,16,128]{3,2,1,0:T(8,128)(2,1)}, u32[]{:S(2)}) copy-start(bf16[1,1,16,128]{3,2,1,0:T(8,128)(2,1)} %stack.72) | copy-start | bytes 12292
  67.3 43.0 %copy-start.22 = (bf16[1,1,16,128]{3,2,1,0:T(8,128)(2,1)S(1)}, bf16[1,1,16,128]{3,2,1,0:T(8,128)(2,1)}, u32[]{:S(2)}) copy-start(bf16[1,1,16,128]{3,2,1,0:T(8,128)(2,1)} %stack.73) | copy-start | bytes 12292
  67.3 56.6 %copy-start.8 = (bf16[16,2,48,64]{3,2,1,0:T(8,128)(2,1)S(1)}, bf16[16,2,48,64]{3,2,1,0:T(8,128)(2,1)}, u32[]{:S(2)}) copy-start(bf16[16,2,48,64]{3,2,1,0:T(8,128)(2,1)} %pad.9) | copy-start | bytes 589828
  67.3 76.8 %copy-start.10 = (bf16[136,2048]{1,0:T(8,128)(2,1)S(1)}, bf16[136,2048]{1,0:T(8,128)(2,1)}, u32[]{:S(2)}) copy-start(bf16[136,2048]{1,0:T(8,128)(2,1)} %copy-done.9) | copy-start | bytes 1671172
  99.7 10.1 %collective-permute-start.7 = (bf16[16,64,96]{2,1,0:T(8,128)(2,1)}, bf16[16,64,96]{2,1,0:T(8,128)(2,1)}, u32[]{:S(2)}, u32[]{:S(2)}) collective-permute-start(bf16[16,64,96]{2,1,0:T(8,128)(2,1)} %get-tuple-element.13), channel_id=1, source_target_pairs={{0,8},{8,16},{16,24},{24,0},{1,9},{9,17},{17,25},{25,1},{2,10},{10... | collective-permute-start | bytes 589832 | tf_op jit(solution)/shard_map/ppermute | solution.py:418
  100.4 30.3 %collective-permute-start.13 = (bf16[4,136,512]{2,1,0:T(8,128)(2,1)}, bf16[4,136,512]{2,1,0:T(8,128)(2,1)}, u32[]{:S(2)}, u32[]{:S(2)}) collective-permute-start(bf16[4,136,512]{2,1,0:T(8,128)(2,1)} %collective-permute-done.12.refs_11_), channel_id=1, source_target_pairs={{0,1},{1,0},{2,3},{3,2},{4,5},{5,4},{6,7},{7,6},{8,9},{9,8},{10,11... | collective-permute-start | bytes 1671176 | tf_op jit(solution)/shard_map/ppermute | solution.py:455
  100.6 30.9 %collective-permute-start.15 = (bf16[4,136,512]{2,1,0:T(8,128)(2,1)}, bf16[4,136,512]{2,1,0:T(8,128)(2,1)}, u32[]{:S(2)}, u32[]{:S(2)}) collective-permute-start(bf16[4,136,512]{2,1,0:T(8,128)(2,1)} %collective-permute-done.14.refs_12_), channel_id=1, source_target_pairs={{0,1},{1,0},{2,3},{3,2},{4,5},{5,4},{6,7},{7,6},{8,9},{9,8},{10,11... | collective-permute-start | bytes 1671176 | tf_op jit(solution)/shard_map/ppermute | solution.py:455
  100.9 23.0 %collective-permute-start.8 = (bf16[16,64,96]{2,1,0:T(8,128)(2,1)}, bf16[16,64,96]{2,1,0:T(8,128)(2,1)S(1)}, u32[]{:S(2)}, u32[]{:S(2)}) collective-permute-start(bf16[16,64,96]{2,1,0:T(8,128)(2,1)} %get-tuple-element.14), channel_id=1, source_target_pairs={{0,16},{8,24},{16,0},{24,8},{1,17},{9,25},{17,1},{25,9},{2,18},{10... | collective-permute-start | bytes 589832 | tf_op jit(solution)/shard_map/ppermute | solution.py:418
  109.8 15.6 %collective-permute-start.9 = (bf16[16,64,96]{2,1,0:T(8,128)(2,1)}, bf16[16,64,96]{2,1,0:T(8,128)(2,1)}, u32[]{:S(2)}, u32[]{:S(2)}) collective-permute-start(bf16[16,64,96]{2,1,0:T(8,128)(2,1)} %get-tuple-element.15), channel_id=1, source_target_pairs={{0,24},{8,0},{16,8},{24,16},{1,25},{9,1},{17,9},{25,17},{2,26},{10... | collective-permute-start | bytes 589832 | tf_op jit(solution)/shard_map/ppermute | solution.py:418
  112.7 31.4 %copy-start.7 = (bf16[136,2048]{1,0:T(8,128)(2,1)S(1)}, bf16[136,2048]{1,0:T(8,128)(2,1)}, u32[]{:S(2)}) copy-start(bf16[136,2048]{1,0:T(8,128)(2,1)} %copy-done.6) | copy-start | bytes 1671172
  112.7 10.5 %all-to-all-start = ((f32[8,8,128]{2,1,0:T(8,128)}), f32[8,8,128]{2,1,0:T(8,128)S(1)}, u32[]{:S(2)}, u32[]{:S(2)}) async-start(f32[8,8,128]{2,1,0:T(8,128)} %get-tuple-element.11), calls=%async_computation | async-start | bytes 65536 | tf_op jit(solution)/shard_map/all_to_all | solution.py:498
  117.5 26.5 %copy-start.1 = (bf16[136,2048]{1,0:T(8,128)(2,1)S(1)}, bf16[136,2048]{1,0:T(8,128)(2,1)}, u32[]{:S(2)}) copy-start(bf16[136,2048]{1,0:T(8,128)(2,1)} %copy-done) | copy-start | bytes 1671172
  117.5 26.6 %copy-start.3 = (bf16[136,2048]{1,0:T(8,128)(2,1)S(1)}, bf16[136,2048]{1,0:T(8,128)(2,1)}, u32[]{:S(2)}) copy-start(bf16[136,2048]{1,0:T(8,128)(2,1)} %copy-done.2) | copy-start | bytes 1671172
  117.6 26.6 %copy-start.5 = (bf16[136,2048]{1,0:T(8,128)(2,1)S(1)}, bf16[136,2048]{1,0:T(8,128)(2,1)}, u32[]{:S(2)}) copy-start(bf16[136,2048]{1,0:T(8,128)(2,1)} %copy-done.4) | copy-start | bytes 1671172
  117.6 26.6 %copy-start.15 = (s32[8]{0:T(128)S(1)}, s32[8]{0:T(128)}, u32[]{:S(2)}) copy-start(s32[8]{0:T(128)} %fusion.4.refs_0_) | copy-start | bytes 100
  123.9 13.1 %collective-permute-start.16 = (bf16[16,96,64]{2,1,0:T(8,128)(2,1)S(1)}, bf16[16,96,64]{2,1,0:T(8,128)(2,1)}, u32[]{:S(2)}, u32[]{:S(2)}) collective-permute-start(bf16[16,96,64]{2,1,0:T(8,128)(2,1)S(1)} %bitcast.41), channel_id=1, source_target_pairs={{0,8},{8,16},{16,24},{24,0},{1,9},{9,17},{17,25},{25,1},{2,10},{10... | collective-permute-start | bytes 589832 | tf_op jit(solution)/shard_map/ppermute | solution.py:418
  125.4 18.7 %collective-permute-start.17 = (bf16[16,96,64]{2,1,0:T(8,128)(2,1)S(1)}, bf16[16,96,64]{2,1,0:T(8,128)(2,1)}, u32[]{:S(2)}, u32[]{:S(2)}) collective-permute-start(bf16[16,96,64]{2,1,0:T(8,128)(2,1)S(1)} %bitcast.42), channel_id=1, source_target_pairs={{0,16},{8,24},{16,0},{24,8},{1,17},{9,25},{17,1},{25,9},{2,18},{10... | collective-permute-start | bytes 589832 | tf_op jit(solution)/shard_map/ppermute | solution.py:418
  126.9 17.2 %collective-permute-start.18 = (bf16[16,96,64]{2,1,0:T(8,128)(2,1)S(1)}, bf16[16,96,64]{2,1,0:T(8,128)(2,1)}, u32[]{:S(2)}, u32[]{:S(2)}) collective-permute-start(bf16[16,96,64]{2,1,0:T(8,128)(2,1)S(1)} %bitcast.43), channel_id=1, source_target_pairs={{0,24},{8,0},{16,8},{24,16},{1,25},{9,1},{17,9},{25,17},{2,26},{10... | collective-permute-start | bytes 589832 | tf_op jit(solution)/shard_map/ppermute | solution.py:418
  (16 other events, 84.9 us)

commit v3 on v2

--- a/solution.py
+++ b/solution.py
@@ -148,9 +148,19 @@
     return -(-count // 16) * 16
 
 
-def slot_codes(meta, owners_ref, first, capacity, experts, micro):
-    shards = meta.shape[0]
-    top, span = meta.shape[1] // 2, meta.shape[2]
+def read_names(rows, span, top):
+    wide = rows.astype(jnp.float32)
+    per = wide.shape[1] // span
+    lines = [
+        wide[k // per : k // per + 1, (k % per) * span : (k % per + 1) * span]
+        for k in range(2 * top)
+    ]
+    return lines[:top], lines[top:]
+
+
+def slot_codes(names, owners_ref, first, capacity, experts, micro):
+    shards = len(names)
+    span = names[0][0][0].shape[1]
     block = span // micro
     number = lax.broadcasted_iota(jnp.int32, (experts, span), 0).astype(jnp.float32) + first
     from_row = lax.broadcasted_iota(jnp.int32, (span, span), 0)
@@ -162,10 +172,10 @@
     for j in range(shards):
         named = jnp.zeros((experts, span), jnp.float32)
         gate = jnp.zeros((experts, span), jnp.float32)
-        for k in range(top):
-            hit = meta[j, k : k + 1, :] == number
+        for name, weight in zip(*names[j]):
+            hit = name == number
             named = jnp.where(hit, 1.0, named)
-            gate = jnp.where(hit, meta[j, top + k : top + k + 1, :], gate)
+            gate = jnp.where(hit, weight, gate)
         before = jnp.dot(named.astype(jnp.bfloat16), earlier, preferred_element_type=jnp.float32)
         offset = (owners_ref[j] * capacity).astype(jnp.float32)
         codes.append(jnp.where(named > 0.0, before + offset, -1.0))
@@ -182,16 +192,15 @@
 
 
 def expert_kernel(capacity, group_count, shards, *refs):
-    owners_ref, meta_ref = refs[:2]
-    token_refs = refs[2 : 2 + shards]
-    hidden_ref, u_ref, weight_hbm, amap_ref, bmap_hbm = refs[2 + shards : 7 + shards]
-    hg_ref, rk_ref = refs[7 + shards : 9 + shards]
-    la_refs = refs[9 + shards : 9 + shards + group_count]
+    owners_ref = refs[0]
+    token_refs = refs[1 : 1 + shards]
+    hidden_ref, u_ref, weight_hbm, amap_ref, bmap_hbm = refs[1 + shards : 6 + shards]
+    hg_ref, rk_ref = refs[6 + shards : 8 + shards]
+    la_refs = refs[8 + shards : 8 + shards + group_count]
     dy_s, wb_s, rows_s, code_s, gate_s, back_s, dy_sem, w_sem, b_sem = refs[
-        9 + shards + group_count :
-    ]
-    twice_top, span = meta_ref.shape[1:]
-    top = twice_top // 2
+        8 + shards + group_count :
+    ]
+    top, span = rk_ref.shape[1:]
     micro, experts, slots, units = hidden_ref.shape
     rank = amap_ref.shape[1]
     width = dy_s.shape[2]
@@ -201,7 +210,7 @@
     group = lax.axis_index("dp")
 
     token_copies = [
-        pltpu.make_async_copy(token_refs[i].at[pl.ds(0, span)], dy_s.at[i], dy_sem.at[i])
+        pltpu.make_async_copy(token_refs[i], dy_s.at[i], dy_sem.at[i])
         for i in range(shards)
     ]
     for copy in token_copies:
@@ -217,7 +226,12 @@
         for copy in weight_copies(x):
             copy.start()
 
-    codes, gates = slot_codes(meta_ref[...], owners_ref, first, capacity, experts, micro)
+    for copy in token_copies:
+        copy.wait()
+    names = [
+        read_names(dy_s[i, span:, : width // group_count], span, top) for i in range(shards)
+    ]
+    codes, gates = slot_codes(names, owners_ref, first, capacity, experts, micro)
     slot_of = lax.broadcasted_iota(jnp.int32, (padded, shards * block), 0).astype(jnp.float32)
     picks = []
     for m in range(micro):
@@ -231,8 +245,6 @@
             )
         picks.append(jnp.concatenate(chosen, axis=0))
 
-    for copy in token_copies:
-        copy.wait()
     tile = 512 if width % 512 == 0 else width
     for m in range(micro):
         for n in range(width // tile):
@@ -245,9 +257,10 @@
                 experts, padded, tile
             )
 
-    def one_expert(x):
-        rows = rows_s[x]
-        both = lax.dot_general(rows, wb_s[x], contract_last, preferred_element_type=jnp.float32)
+    def one_expert(x, lanes):
+        both = lax.dot_general(
+            wb_s[x], rows_s[x], contract_last, preferred_element_type=jnp.float32
+        ).T
         main = both[:, :units]
         v = both[:, units:].astype(jnp.bfloat16)
         low = jnp.dot(v, amap_ref[x], preferred_element_type=jnp.float32)
@@ -263,7 +276,7 @@
         held = held_wide.astype(jnp.bfloat16)
         v_wide = v.astype(jnp.float32)
         routed = jnp.sum(main * held_wide, axis=1, keepdims=True) + adapter_scale * jnp.sum(
-            u_ref[x].astype(jnp.float32) * v_wide, axis=1, keepdims=True
+            u_ref[lax.rem(x, experts // 2), :, lanes].astype(jnp.float32) * v_wide, axis=1, keepdims=True
         )
         for m in range(micro):
             hit = code_s[m, pl.ds(x, 1), :] == slot_of
@@ -282,17 +295,16 @@
                 mine = jnp.where(aim == k, la[:, k * share : (k + 1) * share], mine)
             la_refs[s][x] = mine.astype(la_refs[s].dtype)
 
-    batch = 2 if experts % 2 == 0 else 1
-
-    def some_experts(step, carry):
-        for i in range(batch):
-            for copy in weight_copies(step * batch + i):
-                copy.wait()
-        for i in range(batch):
-            one_expert(step * batch + i)
+    half = experts // 2
+
+    def two_experts(x, carry):
+        for copy in weight_copies(x) + weight_copies(x + half):
+            copy.wait()
+        one_expert(x, slice(0, rank))
+        one_expert(x + half, slice(rank, 2 * rank))
         return carry
 
-    lax.fori_loop(0, experts // batch, some_experts, 0)
+    lax.fori_loop(0, half, two_experts, 0)
 
     number = lax.broadcasted_iota(jnp.int32, (experts, span), 0).astype(jnp.float32) + first
     for i in range(shards):
@@ -301,24 +313,26 @@
         )
         found = [
             jnp.sum(
-                jnp.where(meta_ref[i, k : k + 1, :] == number, back, 0.0), axis=0, keepdims=True
-            )
-            for k in range(top)
+                jnp.where(name == number, back, 0.0), axis=0, keepdims=True
+            )
+            for name in names[i][0]
         ]
         rk_ref[owners_ref[i]] = jnp.concatenate(found, axis=0)
 
 
-def adapter_kernel(capacity, micro, group_count, shards, *refs):
-    owners_ref, meta_ref = refs[:2]
-    token_refs = refs[2 : 2 + shards]
-    near_refs = refs[2 + shards : 1 + shards + group_count]
-    far_refs = refs[1 + shards + group_count : shards + 2 * group_count]
-    u_refs = refs[shards + 2 * group_count : shards + 3 * group_count]
-    lb_ref, tok_s, q_s, u_s, sem = refs[shards + 3 * group_count :]
-    span = meta_ref.shape[3]
-    experts, tall, rank = u_refs[0].shape
-    share = lb_ref.shape[2]
-    half = shards // 2
+def adapter_kernel(capacity, micro, span, top, group_count, shards, *refs):
+    others = group_count - 1
+    pairs = shards // 2
+    early = pairs // 2
+    owners_ref = refs[0]
+    token_refs = refs[1 : 1 + shards]
+    early_refs = refs[1 + shards : 1 + shards + others]
+    late_refs = refs[1 + shards + others : 1 + shards + 2 * others]
+    swapped_refs = refs[1 + shards + 2 * others : 1 + shards + 3 * others]
+    u_refs = refs[1 + shards + 3 * others : 2 + shards + 4 * others]
+    lb_ref, tok_s, q_s, sem = refs[2 + shards + 4 * others :]
+    experts, rank, share = lb_ref.shape
+    tall = u_refs[0].shape[1]
     padded = tall // micro
     block = span // micro
     first = (lax.axis_index("expert") * experts).astype(jnp.float32)
@@ -327,21 +341,22 @@
     copies = []
     for g in range(group_count):
         for i in range(shards):
+            far, k = i // pairs, i % pairs
             if g == 0:
-                source = token_refs[i].at[pl.ds(0, span), cols]
-            elif i < half:
-                source = near_refs[g - 1].at[i, pl.ds(0, span)]
+                source = token_refs[i].at[:, cols]
+            elif k < early:
+                source = early_refs[g - 1].at[far * early + k]
             else:
-                source = far_refs[g - 1].at[i - half, pl.ds(0, span)]
+                source = (swapped_refs if far else late_refs)[g - 1].at[k - early]
             copies.append(pltpu.make_async_copy(source, tok_s.at[g, i], sem.at[g, i]))
     for copy in copies:
         copy.start()
     slot_of = lax.broadcasted_iota(jnp.int32, (padded, shards * block), 0).astype(jnp.float32)
     for g in range(group_count):
-        u_s[:, g * tall : (g + 1) * tall, :] = u_refs[g][...]
-        codes, gates = slot_codes(meta_ref[g], owners_ref, first, capacity, experts, micro)
         for i in range(shards):
             copies[g * shards + i].wait()
+        names = [read_names(tok_s[g, i, span:, :], span, top) for i in range(shards)]
+        codes, gates = slot_codes(names, owners_ref, first, capacity, experts, micro)
         for m in range(micro):
             picks = jnp.concatenate(
                 [
@@ -358,9 +373,14 @@
             q = jnp.dot(picks, tokens, preferred_element_type=jnp.float32).astype(jnp.bfloat16)
             at = g * tall + m * padded
             q_s[:, at : at + padded, :] = q.reshape(experts, padded, share)
-    for x in range(experts):
+    half = experts // 2
+    for x in range(half):
+        both = jnp.concatenate([u_refs[g][x] for g in range(group_count)], axis=0)
         lb_ref[x] = adapter_scale * lax.dot_general(
-            u_s[x], q_s[x], contract_first, preferred_element_type=jnp.float32
+            both[:, :rank], q_s[x], contract_first, preferred_element_type=jnp.float32
+        )
+        lb_ref[x + half] = adapter_scale * lax.dot_general(
+            both[:, rank:], q_s[x + half], contract_first, preferred_element_type=jnp.float32
         )
 
 
@@ -411,15 +431,26 @@
     u = jnp.einsum("mesk,exk->emsx", hidden, amap, preferred_element_type=jnp.float32)
     u = u.astype(jnp.bfloat16)
     u = jnp.pad(u, ((0, 0), (0, 0), (0, padded - slots), (0, 0))).reshape(
-        experts, micro * padded, rank
-    )
+        2, experts // 2, micro * padded, rank
+    )
+    u = jnp.concatenate([u[0], u[1]], axis=-1)
 
     def shift_groups(array, by):
         return lax.ppermute(
             array, "dp", [(d, (d + by) % group_count) for d in range(group_count)]
         )
 
-    u_all = [u] + [shift_groups(u, s) for s in range(1, group_count)]
+    def swap_partners(array):
+        return lax.ppermute(array, "expert", swap)
+
+    def columns_for(group_shift, chosen):
+        aim = lax.rem(group + group_shift, group_count) * share
+        return jnp.stack(
+            [lax.dynamic_slice_in_dim(piece, aim, share, axis=1) for piece in chosen]
+        )
+
+    others = range(1, group_count)
+    u_all = [u] + [shift_groups(u, s) for s in others]
 
     names = jnp.concatenate(
         [chosen_expert_index.T.astype(jnp.bfloat16), routing_gate_weight.T], axis=0
@@ -431,36 +462,20 @@
         [output_gradient, jnp.pad(names, ((0, extra - lines), (0, 0)))], axis=0
     )
 
-    near = [sent]
-    for _ in range(pairs - 1):
-        near.append(lax.ppermute(near[-1], "expert", ring))
-    far = [lax.ppermute(piece, "expert", swap) for piece in near]
+    early = pairs // 2
+    near, far = [sent], []
+    for step in range(pairs - 1):
+        ahead = near[-1]
+        if step == pairs - 2:
+            ahead, *u_all = lax.optimization_barrier((ahead, *u_all))
+        near.append(lax.ppermute(ahead, "expert", ring))
+        far.append(swap_partners(near[step]))
+    far.append(swap_partners(near[-1]))
+    early_columns = [
+        shift_groups(columns_for(s, near[:early] + far[:early]), s) for s in others
+    ]
+    late_columns = [shift_groups(columns_for(s, near[early:]), s) for s in others]
     pieces = near + far
-
-    def names_of(piece):
-        return piece[..., span : span + lines, :share].reshape(
-            piece.shape[:-2] + (2 * top, span)
-        )
-
-    own_meta = jnp.stack([names_of(piece) for piece in pieces]).astype(jnp.float32)
-
-    crossing, returned = [], []
-    for s in range(1, group_count):
-        aim = lax.rem(group + s, group_count) * share
-        columns = jnp.stack(
-            [lax.dynamic_slice_in_dim(piece, aim, share, axis=1) for piece in near]
-        )
-        crossing.append(shift_groups(columns, s))
-    for columns in crossing:
-        returned.append(lax.ppermute(columns, "expert", swap))
-    all_meta = jnp.concatenate(
-        [own_meta[None]]
-        + [
-            jnp.concatenate([names_of(a), names_of(b)], axis=0)[None].astype(jnp.float32)
-            for a, b in zip(crossing, returned)
-        ],
-        axis=0,
-    )
 
     vmem = pl.BlockSpec(memory_space=pltpu.VMEM)
     smem = pl.BlockSpec(memory_space=pltpu.SMEM)
@@ -473,10 +488,10 @@
             jax.ShapeDtypeStruct((sources, top, span), jnp.float32),
         )
         + (part_a,) * group_count,
-        in_specs=[smem, vmem] + [anywhere] * sources + [vmem, vmem, anywhere, vmem, anywhere],
+        in_specs=[smem] + [anywhere] * sources + [vmem, vmem, anywhere, vmem, anywhere],
         out_specs=(vmem,) * (2 + group_count),
         scratch_shapes=[
-            pltpu.VMEM((sources, span, width), jnp.bfloat16),
+            pltpu.VMEM((sources, span + extra, width), jnp.bfloat16),
             pltpu.VMEM((experts, units + rank, width), jnp.bfloat16),
             pltpu.VMEM((experts, micro * padded, width), jnp.bfloat16),
             pltpu.VMEM((micro, experts, sources * block), jnp.float32),
@@ -493,25 +508,23 @@
             transcendentals=0,
         ),
         name="expert_rows",
-    )(owners, own_meta, *pieces, hidden, u, frozen_down_weight, amap, adapter_output_map)
-
+    )(owners, *pieces, hidden, u, frozen_down_weight, amap, adapter_output_map)
+
+    late_columns, parts = lax.optimization_barrier((late_columns, parts))
+    swapped = [swap_partners(columns) for columns in late_columns]
     home = lax.all_to_all(routed, "expert", split_axis=0, concat_axis=0, tiled=True)
-    router_grad = jnp.sum(home, axis=0).T
-    lora_a = parts[0].astype(jnp.float32)
-    for s in range(1, group_count):
-        lora_a = lora_a + shift_groups(parts[s], s).astype(jnp.float32)
+    arrived = [shift_groups(parts[s], s) for s in others]
 
     lora_b = pl.pallas_call(
-        functools.partial(adapter_kernel, capacity, micro, group_count, sources),
+        functools.partial(adapter_kernel, capacity, micro, span, top, group_count, sources),
         out_shape=jax.ShapeDtypeStruct((experts, rank, share), jnp.float32),
-        in_specs=[smem, vmem]
-        + [anywhere] * (sources + 2 * (group_count - 1))
+        in_specs=[smem]
+        + [anywhere] * (sources + 3 * (group_count - 1))
         + [vmem] * group_count,
         out_specs=vmem,
         scratch_shapes=[
-            pltpu.VMEM((group_count, sources, span, share), jnp.bfloat16),
+            pltpu.VMEM((group_count, sources, span + extra, share), jnp.bfloat16),
             pltpu.VMEM((experts, group_count * micro * padded, share), jnp.bfloat16),
-            pltpu.VMEM((experts, group_count * micro * padded, rank), jnp.bfloat16),
             pltpu.SemaphoreType.DMA((group_count, sources)),
         ],
         compiler_params=pltpu.CompilerParams(vmem_limit_bytes=40 * 1024 * 1024),
@@ -521,7 +534,13 @@
             transcendentals=0,
         ),
         name="adapter_columns",
-    )(owners, all_meta, *pieces, *crossing, *returned, *u_all)
+    )(owners, *pieces, *early_columns, *late_columns, *swapped, *u_all)
+
+    home, arrived, lora_b = lax.optimization_barrier((home, arrived, lora_b))
+    router_grad = jnp.sum(home, axis=0).T
+    lora_a = parts[0].astype(jnp.float32)
+    for part in arrived:
+        lora_a = lora_a + part.astype(jnp.float32)
     return (hidden_grad, router_grad, lora_a, lora_b)
 
 
@@ -529,7 +548,7 @@
     sources, groups = lax.axis_size("expert"), lax.axis_size("dp")
     span, width = arrays[0].shape
     top, (micro, experts, slots, units) = arrays[1].shape[1], arrays[3].shape
-    even = sources % 2 == 0 and width % (128 * groups) == 0 and units % groups == 0
+    even = sources % 4 == 0 and experts % 2 == 0 and width % (128 * groups) == 0 and units % groups == 0
     packs = 2 * top * span % (width // groups) == 0 and (width // groups) % span == 0
     exact = experts * sources <= 256
     if even and packs and exact and sources * span <= micro * experts * slots:

time: 157 us -> 135 us (0.86)
  waiting for transfers between devices: 56.3 us -> 33.5 us
  local copies, waits for them, and re-layouts: 18.9 us -> 9.34 us
  Pallas kernels: 42 us -> 50.2 us
  starting transfers between devices: 27.3 us -> 29.2 us
    ppermute x9 -> x12, waiting for transfers between devices: 26.8 us -> 14.6 us  [shift_groups(): lax.ppermute(array, 'dp', [(d, (d + by) % group_count) for d in range(gro...]
    pallas_call x1, Pallas kernels: 32.4 us -> 41.3 us  [local_by_tokens(): pl.pallas_call(functools.partial(expert_kernel, capacity, group_count, so...]
    another operation x22 -> x6, local copies, waits for them, and re-layouts: 7.71 us -> 0.18 us  [columns_for(): jnp.stack([lax.dynamic_slice_in_dim(piece, aim, share, axis=1) for piece...]
    ppermute x10, waiting for transfers between devices: 24.4 us -> 18.8 us  [the longest x3 18.8 us: local_by_tokens(): near.append(lax.ppermute(ahead, 'expert', ring))]
    slice x14 -> x1, local copies, waits for them, and re-layouts: 5.34 us -> 0.07 us  [local_by_tokens(): u = jnp.concatenate([u[0], u[1]], axis=-1)]
    ppermute x9 -> x12, starting transfers between devices: 11.2 us -> 16.3 us  [shift_groups(): lax.ppermute(array, 'dp', [(d, (d + by) % group_count) for d in range(gro...]
    all_to_all x1, waiting for transfers between devices: 5.12 us -> 0.01 us  [local_by_tokens(): lax.all_to_all(routed, 'expert', split_axis=0, concat_axis=0, tiled=True)]
    unnamed x72 -> x58, local copies, waits for them, and re-layouts: 3.7 us -> 7.88 us
  transfers between devices with their start and end apart: 20 -> 23, of which waited for: 9 -> 5; matrix products, arithmetic and copies ran while one was open for 14% -> 5% of each run, Pallas kernels for 21% -> 38%
where the time goes in v3:
time: 135 us; the launch traced here: 134 us
  Pallas kernels  50.2 us (37%)
  waiting for transfers between devices  33.5 us (25%)
  starting transfers between devices  29.2 us (22%)
  local copies, waits for them, and re-layouts  9.34 us (7%)
  other arithmetic  9.05 us (7%)
  matrix products  1.62 us (1%)
    pallas_call x1, Pallas kernels, local_by_tokens(): pl.pallas_call(functools.partial(expert_kernel, capacity, group_count, so...  41.3 us
    ppermute x3, waiting for transfers between devices, local_by_tokens(): near.append(lax.ppermute(ahead, 'expert', ring))  18.8 us
    ppermute x12, starting transfers between devices, shift_groups(): lax.ppermute(array, 'dp', [(d, (d + by) % group_count) for d in range(gro...  16.3 us
    ppermute x12, waiting for transfers between devices, shift_groups(): lax.ppermute(array, 'dp', [(d, (d + by) % group_count) for d in range(gro...  14.6 us
    pallas_call x1, Pallas kernels, local_by_tokens(): pl.pallas_call(functools.partial(adapter_kernel, capacity, micro, span, t...  8.92 us
    ppermute x3, starting transfers between devices, local_by_tokens(): near.append(lax.ppermute(ahead, 'expert', ring))  8.2 us
    unnamed x58, local copies, waits for them, and re-layouts  7.88 us
    all_to_all x1, starting transfers between devices, local_by_tokens(): lax.all_to_all(routed, 'expert', split_axis=0, concat_axis=0, tiled=True)  3.94 us
  transfers between devices with their start and end apart: 23, of which 5 were waited for; matrix products, arithmetic and copies ran while one was open for 5% of the time, Pallas kernels for 38%

profile of v3, /device:TPU:0, one launch (start us, length us, event | category | flops | bytes accessed | tf_op | source)
XLA Modules:
  0.0 133.9 jit_solution(10925552724276324786)
XLA Ops:
  2.1 1.1 fusion.3.refs_1_
  3.2 4.1 %collective-permute-start = (bf16[136,2048]{1,0:T(8,128)(2,1)S(1)}, bf16[136,2048]{1,0:T(8,128)(2,1)S(1)}, u32[]{:S(2)}, u32[]{:S(2)}) collective-permute-start(bf16[136,2048]{1,0:T(8,128)(2,1)S(1)} %fusion.3.refs_1_), channel_id=1, source_target_pairs={{0,4},{1,5},{2,0},{3,1},{4,6},{5,7},{6,2},{7,3},{8,12},{9,13},{10,... | collective-permute-start | bytes 1671176 | tf_op jit(solution)/shard_map/ppermute | solution.py:471
  7.3 1.6 %convolution_convert_fusion = bf16[16,2,40,64]{3,2,1,0:T(8,128)(2,1)S(1)} fusion(bf16[2,16,40,384]{3,2,1,0:T(8,128)(2,1)S(1)} %copy-done.27, bf16[16,384,64]{1,2,0:T(8,128)(2,1)} %param.13), kind=kOutput, calls=%fused_computation | convolution fusion | flops 62996480 | bytes 1933312 | tf_op jit(solution)/shard_map/mesk,exk->emsx/dot_general | solution.py:431
  9.0 10.3 %collective-permute-done.refs_2_ = bf16[136,2048]{1,0:T(8,128)(2,1)S(1)} collective-permute-done((bf16[136,2048]{1,0:T(8,128)(2,1)S(1)}, bf16[136,2048]{1,0:T(8,128)(2,1)S(1)}, u32[]{:S(2)}, u32[]{:S(2)}) %collective-permute-start) | collective-permute-done | bytes 557088 | tf_op jit(solution)/shard_map/ppermute | solution.py:471
  19.2 3.4 %collective-permute-start.1 = (bf16[136,2048]{1,0:T(8,128)(2,1)S(1)}, bf16[136,2048]{1,0:T(8,128)(2,1)S(1)}, u32[]{:S(2)}, u32[]{:S(2)}) collective-permute-start(bf16[136,2048]{1,0:T(8,128)(2,1)S(1)} %collective-permute-done.refs_2_), channel_id=1, source_target_pairs={{0,4},{1,5},{2,0},{3,1},{4,6},{5,7},{6,2},{7,3},{8,12},{9,13},{10,... | collective-permute-start | bytes 1671176 | tf_op jit(solution)/shard_map/ppermute | solution.py:471
  22.9 2.5 %collective-permute-start.4 = (bf16[8,96,128]{2,1,0:T(8,128)(2,1)S(1)}, bf16[8,96,128]{2,1,0:T(8,128)(2,1)S(1)}, u32[]{:S(2)}, u32[]{:S(2)}) collective-permute-start(bf16[8,96,128]{2,1,0:T(8,128)(2,1)S(1)} %pad_maximum_fusion.6.refs_10_.refs_18_), channel_id=1, source_target_pairs={{0,24},{8,0},{16,8},{24,16},{1,25},{9,1},{17,9},{25,17},{2,26},{10... | collective-permute-start | bytes 589832 | tf_op jit(solution)/shard_map/ppermute | solution.py:439
  25.9 4.3 %collective-permute-done.4.refs_21_ = bf16[8,96,128]{2,1,0:T(8,128)(2,1)S(1)} collective-permute-done((bf16[8,96,128]{2,1,0:T(8,128)(2,1)S(1)}, bf16[8,96,128]{2,1,0:T(8,128)(2,1)S(1)}, u32[]{:S(2)}, u32[]{:S(2)}) %collective-permute-start.4) | collective-permute-done | bytes 196640 | tf_op jit(solution)/shard_map/ppermute | solution.py:439
  30.3 2.5 %collective-permute-start.2 = (bf16[8,96,128]{2,1,0:T(8,128)(2,1)S(1)}, bf16[8,96,128]{2,1,0:T(8,128)(2,1)S(1)}, u32[]{:S(2)}, u32[]{:S(2)}) collective-permute-start(bf16[8,96,128]{2,1,0:T(8,128)(2,1)S(1)} %pad_maximum_fusion.6.refs_10_.refs_18_), channel_id=1, source_target_pairs={{0,8},{8,16},{16,24},{24,0},{1,9},{9,17},{17,25},{25,1},{2,10},{10... | collective-permute-start | bytes 589832 | tf_op jit(solution)/shard_map/ppermute | solution.py:439
  32.7 1.2 fusion.4.refs_0_
  34.7 3.7 %collective-permute-done.2.refs_19_ = bf16[8,96,128]{2,1,0:T(8,128)(2,1)S(1)} collective-permute-done((bf16[8,96,128]{2,1,0:T(8,128)(2,1)S(1)}, bf16[8,96,128]{2,1,0:T(8,128)(2,1)S(1)}, u32[]{:S(2)}, u32[]{:S(2)}) %collective-permute-start.2) | collective-permute-done | bytes 196640 | tf_op jit(solution)/shard_map/ppermute | solution.py:439
  39.3 1.0 pad_maximum_fusion
  41.1 0.9 pad_maximum_fusion.1
  42.0 1.5 %collective-permute-start.17 = (bf16[4,136,512]{2,1,0:T(8,128)(2,1)}, bf16[4,136,512]{2,1,0:T(8,128)(2,1)}, u32[]{:S(2)}, u32[]{:S(2)}) collective-permute-start(bf16[4,136,512]{2,1,0:T(8,128)(2,1)} %pad_maximum_fusion.1), channel_id=1, source_target_pairs={{0,16},{8,24},{16,0},{24,8},{1,17},{9,25},{17,1},{25,9},{2,18},{10... | collective-permute-start | bytes 1671176 | tf_op jit(solution)/shard_map/ppermute | solution.py:439
  43.6 8.5 %collective-permute-done.5.refs_4_ = bf16[136,2048]{1,0:T(8,128)(2,1)S(1)} collective-permute-done((bf16[136,2048]{1,0:T(8,128)(2,1)S(1)}, bf16[136,2048]{1,0:T(8,128)(2,1)S(1)}, u32[]{:S(2)}, u32[]{:S(2)}) %collective-permute-start.5) | collective-permute-done | bytes 557088 | tf_op jit(solution)/shard_map/ppermute | solution.py:471
  52.7 0.9 pad_maximum_fusion.2
  53.7 2.5 %collective-permute-start.18 = (bf16[4,136,512]{2,1,0:T(8,128)(2,1)}, bf16[4,136,512]{2,1,0:T(8,128)(2,1)}, u32[]{:S(2)}, u32[]{:S(2)}) collective-permute-start(bf16[4,136,512]{2,1,0:T(8,128)(2,1)} %pad_maximum_fusion.2), channel_id=1, source_target_pairs={{0,24},{8,0},{16,8},{24,16},{1,25},{9,1},{17,9},{25,17},{2,26},{10... | collective-permute-start | bytes 1671176 | tf_op jit(solution)/shard_map/ppermute | solution.py:439
  56.2 6.5 %collective-permute-done.10.refs_12_ = bf16[2,136,512]{2,1,0:T(8,128)(2,1)} collective-permute-done((bf16[2,136,512]{2,1,0:T(8,128)(2,1)S(1)}, bf16[2,136,512]{2,1,0:T(8,128)(2,1)}, u32[]{:S(2)}, u32[]{:S(2)}) %collective-permute-start.10) | collective-permute-done | bytes 278560 | tf_op jit(solution)/shard_map/ppermute | solution.py:439
  64.1 41.3 %expert_rows.1 = (bf16[2,16,40,384]{3,2,1,0:T(8,128)(2,1)}, f32[8,8,128]{2,1,0:T(8,128)}, bf16[16,64,96]{2,1,0:T(8,128)(2,1)}, bf16[16,64,96]{2,1,0:T(8,128)(2,1...) custom-call(s32[8]{0:T(128)} %fusion.4.refs_0_, bf16[136,2048]{1,0:T(8,128)(2,1)} %copy-done, ...), custom_call_target="tpu_custom_call" | custom-call | flops 6039797760 | bytes 33554432 | tf_op jit(solution)/shard_map/expert_rows/pallas_call | solution.py:484
  106.1 0.8 copy-done.19
  107.0 3.9 %all-to-all-start = ((f32[8,8,128]{2,1,0:T(8,128)}), f32[8,8,128]{2,1,0:T(8,128)}, u32[]{:S(2)}, u32[]{:S(2)}) async-start(f32[8,8,128]{2,1,0:T(8,128)} %get-tuple-element.29), calls=%async_computation | async-start | bytes 65536 | tf_op jit(solution)/shard_map/all_to_all | solution.py:515
  110.9 1.2 collective-permute-start.13
  112.1 1.5 %collective-permute-start.14 = (bf16[16,64,96]{2,1,0:T(8,128)(2,1)}, bf16[16,64,96]{2,1,0:T(8,128)(2,1)}, u32[]{:S(2)}, u32[]{:S(2)}) collective-permute-start(bf16[16,64,96]{2,1,0:T(8,128)(2,1)} %get-tuple-element.35), channel_id=1, source_target_pairs={{0,16},{8,24},{16,0},{24,8},{1,17},{9,25},{17,1},{25,9},{2,18},{10... | collective-permute-start | bytes 589832 | tf_op jit(solution)/shard_map/ppermute | solution.py:439
  113.7 1.8 %collective-permute-start.15 = (bf16[16,64,96]{2,1,0:T(8,128)(2,1)}, bf16[16,64,96]{2,1,0:T(8,128)(2,1)}, u32[]{:S(2)}, u32[]{:S(2)}) collective-permute-start(bf16[16,64,96]{2,1,0:T(8,128)(2,1)} %get-tuple-element.36), channel_id=1, source_target_pairs={{0,24},{8,0},{16,8},{24,16},{1,25},{9,1},{17,9},{25,17},{2,26},{10... | collective-permute-start | bytes 589832 | tf_op jit(solution)/shard_map/ppermute | solution.py:439
  115.5 1.0 copy-done.15
  116.6 1.1 copy-done.17
  117.6 1.1 copy-done.20
  118.7 0.9 copy-done.22
  119.6 0.9 copy-done.24
  120.5 0.9 copy-done.26
  121.5 8.9 %adapter_columns.1 = f32[16,64,512]{2,1,0:T(8,128)} custom-call(s32[8]{0:T(128)S(1)} %copy-done.18, bf16[136,2048]{1,0:T(8,128)(2,1)S(1)} %copy-done.1, bf16[136,2048]{1,0:T(8,128)(2,1)S(1)} %copy-done.3, bf16[136,2048]{1,0:T(8,128)(2,1)S(1)} %copy-done.7, bf16[136,2048]{1,0:T(8,128)(2,1)S(1)} %copy-done.11, bf16[136,2048]{1,0:T(8,128)(2,1)S(1)} %copy-done.5, ...), custom_call_target="tpu_custom_call" | custom-call | flops 3623878656 | bytes 6291456 | tf_op jit(solution)/shard_map/adapter_columns/pallas_call | solution.py:518
  130.4 1.4 %reduce_sum.9 = f32[8,128]{1,0:T(8,128)} reduce(f32[8,8,128]{2,1,0:T(8,128)} %all-to-all-done, f32[]{:T(128)} %constant.34.clone.1), dimensions={0}, to_apply=%region_0.1 | reduce | flops 7168 | bytes 36868 | tf_op jit(solution)/shard_map/reduce_sum | solution.py:540
  131.8 2.1 %convert_add_fusion = f32[16,64,96]{2,1,0:T(8,128)} fusion(bf16[16,64,96]{2,1,0:T(8,128)(2,1)} %collective-permute-done.15, bf16[16,64,96]{2,1,0:T(8,128)(2,1)} %collective-permute-done.14, bf16[16,64,96]{2,1,0:T(8,128)(2,1)} %collective-permute-done.13, bf16[16,64,96]{2,1,0:T(8,128)(2,1)} %get-tuple-element.45), kind=kLoop, calls=%fused_computation.9 | loop fusion | flops 688128 | bytes 1179648 | tf_op jit(solution)/shard_map/add | solution.py:543
  (96 shorter events, 7.4 us)
Async XLA Ops:
  3.2 22.7 %copy-start = (bf16[136,2048]{1,0:T(8,128)(2,1)}, bf16[136,2048]{1,0:T(8,128)(2,1)S(1)}, u32[]{:S(2)}) copy-start(bf16[136,2048]{1,0:T(8,128)(2,1)S(1)} %fusion.3.refs_1_) | copy-start | bytes 1671172
  3.2 16.0 %collective-permute-start = (bf16[136,2048]{1,0:T(8,128)(2,1)S(1)}, bf16[136,2048]{1,0:T(8,128)(2,1)S(1)}, u32[]{:S(2)}, u32[]{:S(2)}) collective-permute-start(bf16[136,2048]{1,0:T(8,128)(2,1)S(1)} %fusion.3.refs_1_), channel_id=1, source_target_pairs={{0,4},{1,5},{2,0},{3,1},{4,6},{5,7},{6,2},{7,3},{8,12},{9,13},{10,... | collective-permute-start | bytes 1671176 | tf_op jit(solution)/shard_map/ppermute | solution.py:471
  7.3 31.8 %collective-permute-start.6 = (bf16[136,2048]{1,0:T(8,128)(2,1)S(1)}, bf16[136,2048]{1,0:T(8,128)(2,1)S(1)}, u32[]{:S(2)}, u32[]{:S(2)}) collective-permute-start(bf16[136,2048]{1,0:T(8,128)(2,1)S(1)} %fusion.3.refs_1_), channel_id=1, source_target_pairs={{0,1},{1,0},{2,3},{3,2},{4,5},{5,4},{6,7},{7,6},{8,9},{9,8},{10,11... | collective-permute-start | bytes 1671176 | tf_op jit(solution)/shard_map/ppermute | solution.py:444
  19.2 19.2 %collective-permute-start.1 = (bf16[136,2048]{1,0:T(8,128)(2,1)S(1)}, bf16[136,2048]{1,0:T(8,128)(2,1)S(1)}, u32[]{:S(2)}, u32[]{:S(2)}) collective-permute-start(bf16[136,2048]{1,0:T(8,128)(2,1)S(1)} %collective-permute-done.refs_2_), channel_id=1, source_target_pairs={{0,4},{1,5},{2,0},{3,1},{4,6},{5,7},{6,2},{7,3},{8,12},{9,13},{10,... | collective-permute-start | bytes 1671176 | tf_op jit(solution)/shard_map/ppermute | solution.py:471
  22.7 16.6 %collective-permute-start.7 = (bf16[136,2048]{1,0:T(8,128)(2,1)S(1)}, bf16[136,2048]{1,0:T(8,128)(2,1)S(1)}, u32[]{:S(2)}, u32[]{:S(2)}) collective-permute-start(bf16[136,2048]{1,0:T(8,128)(2,1)S(1)} %collective-permute-done.refs_2_), channel_id=1, source_target_pairs={{0,1},{1,0},{2,3},{3,2},{4,5},{5,4},{6,7},{7,6},{8,9},{9,8},{10,11... | collective-permute-start | bytes 1671176 | tf_op jit(solution)/shard_map/ppermute | solution.py:444
  22.9 7.4 %collective-permute-start.4 = (bf16[8,96,128]{2,1,0:T(8,128)(2,1)S(1)}, bf16[8,96,128]{2,1,0:T(8,128)(2,1)S(1)}, u32[]{:S(2)}, u32[]{:S(2)}) collective-permute-start(bf16[8,96,128]{2,1,0:T(8,128)(2,1)S(1)} %pad_maximum_fusion.6.refs_10_.refs_18_), channel_id=1, source_target_pairs={{0,24},{8,0},{16,8},{24,16},{1,25},{9,1},{17,9},{25,17},{2,26},{10... | collective-permute-start | bytes 589832 | tf_op jit(solution)/shard_map/ppermute | solution.py:439
  25.4 8.6 %collective-permute-start.3 = (bf16[8,96,128]{2,1,0:T(8,128)(2,1)S(1)}, bf16[8,96,128]{2,1,0:T(8,128)(2,1)S(1)}, u32[]{:S(2)}, u32[]{:S(2)}) collective-permute-start(bf16[8,96,128]{2,1,0:T(8,128)(2,1)S(1)} %pad_maximum_fusion.6.refs_10_.refs_18_), channel_id=1, source_target_pairs={{0,16},{8,24},{16,0},{24,8},{1,17},{9,25},{17,1},{25,9},{2,18},{10... | collective-permute-start | bytes 589832 | tf_op jit(solution)/shard_map/ppermute | solution.py:439
  30.3 8.2 %collective-permute-start.2 = (bf16[8,96,128]{2,1,0:T(8,128)(2,1)S(1)}, bf16[8,96,128]{2,1,0:T(8,128)(2,1)S(1)}, u32[]{:S(2)}, u32[]{:S(2)}) collective-permute-start(bf16[8,96,128]{2,1,0:T(8,128)(2,1)S(1)} %pad_maximum_fusion.6.refs_10_.refs_18_), channel_id=1, source_target_pairs={{0,8},{8,16},{16,24},{24,0},{1,9},{9,17},{17,25},{25,1},{2,10},{10... | collective-permute-start | bytes 589832 | tf_op jit(solution)/shard_map/ppermute | solution.py:439
  38.4 13.7 %collective-permute-start.5 = (bf16[136,2048]{1,0:T(8,128)(2,1)S(1)}, bf16[136,2048]{1,0:T(8,128)(2,1)S(1)}, u32[]{:S(2)}, u32[]{:S(2)}) collective-permute-start(bf16[136,2048]{1,0:T(8,128)(2,1)S(1)} %collective-permute-done.1.refs_3_), channel_id=1, source_target_pairs={{0,4},{1,5},{2,0},{3,1},{4,6},{5,7},{6,2},{7,3},{8,12},{9,13},{10,... | collective-permute-start | bytes 1671176 | tf_op jit(solution)/shard_map/ppermute | solution.py:471
  40.3 65.8 %collective-permute-start.16 = (bf16[4,136,512]{2,1,0:T(8,128)(2,1)}, bf16[4,136,512]{2,1,0:T(8,128)(2,1)S(1)}, u32[]{:S(2)}, u32[]{:S(2)}) collective-permute-start(bf16[4,136,512]{2,1,0:T(8,128)(2,1)} %pad_maximum_fusion), channel_id=1, source_target_pairs={{0,8},{8,16},{16,24},{24,0},{1,9},{9,17},{17,25},{25,1},{2,10},{10... | collective-permute-start | bytes 1671176 | tf_op jit(solution)/shard_map/ppermute | solution.py:439
  42.0 68.9 %collective-permute-start.17 = (bf16[4,136,512]{2,1,0:T(8,128)(2,1)}, bf16[4,136,512]{2,1,0:T(8,128)(2,1)}, u32[]{:S(2)}, u32[]{:S(2)}) collective-permute-start(bf16[4,136,512]{2,1,0:T(8,128)(2,1)} %pad_maximum_fusion.1), channel_id=1, source_target_pairs={{0,16},{8,24},{16,0},{24,8},{1,17},{9,25},{17,1},{25,9},{2,18},{10... | collective-permute-start | bytes 1671176 | tf_op jit(solution)/shard_map/ppermute | solution.py:439
  43.5 10.1 %collective-permute-start.8 = (bf16[136,2048]{1,0:T(8,128)(2,1)S(1)}, bf16[136,2048]{1,0:T(8,128)(2,1)S(1)}, u32[]{:S(2)}, u32[]{:S(2)}) collective-permute-start(bf16[136,2048]{1,0:T(8,128)(2,1)S(1)} %collective-permute-done.1.refs_3_), channel_id=1, source_target_pairs={{0,1},{1,0},{2,3},{3,2},{4,5},{5,4},{6,7},{7,6},{8,9},{9,8},{10,11... | collective-permute-start | bytes 1671176 | tf_op jit(solution)/shard_map/ppermute | solution.py:444
  52.1 11.2 %collective-permute-start.9 = (bf16[136,2048]{1,0:T(8,128)(2,1)S(1)}, bf16[136,2048]{1,0:T(8,128)(2,1)S(1)}, u32[]{:S(2)}, u32[]{:S(2)}) collective-permute-start(bf16[136,2048]{1,0:T(8,128)(2,1)S(1)} %collective-permute-done.5.refs_4_), channel_id=1, source_target_pairs={{0,1},{1,0},{2,3},{3,2},{4,5},{5,4},{6,7},{7,6},{8,9},{9,8},{10,11... | collective-permute-start | bytes 1671176 | tf_op jit(solution)/shard_map/ppermute | solution.py:444
  52.2 10.6 %collective-permute-start.10 = (bf16[2,136,512]{2,1,0:T(8,128)(2,1)S(1)}, bf16[2,136,512]{2,1,0:T(8,128)(2,1)}, u32[]{:S(2)}, u32[]{:S(2)}) collective-permute-start(bf16[2,136,512]{2,1,0:T(8,128)(2,1)S(1)} %pad_maximum_fusion.3), channel_id=1, source_target_pairs={{0,8},{8,16},{16,24},{24,0},{1,9},{9,17},{17,25},{25,1},{2,10},{10... | collective-permute-start | bytes 835592 | tf_op jit(solution)/shard_map/ppermute | solution.py:439
  53.7 58.5 %collective-permute-start.18 = (bf16[4,136,512]{2,1,0:T(8,128)(2,1)}, bf16[4,136,512]{2,1,0:T(8,128)(2,1)}, u32[]{:S(2)}, u32[]{:S(2)}) collective-permute-start(bf16[4,136,512]{2,1,0:T(8,128)(2,1)} %pad_maximum_fusion.2), channel_id=1, source_target_pairs={{0,24},{8,0},{16,8},{24,16},{1,25},{9,1},{17,9},{25,17},{2,26},{10... | collective-permute-start | bytes 1671176 | tf_op jit(solution)/shard_map/ppermute | solution.py:439
  62.7 42.8 %collective-permute-start.11 = (bf16[2,136,512]{2,1,0:T(8,128)(2,1)S(1)}, bf16[2,136,512]{2,1,0:T(8,128)(2,1)}, u32[]{:S(2)}, u32[]{:S(2)}) collective-permute-start(bf16[2,136,512]{2,1,0:T(8,128)(2,1)S(1)} %pad_maximum_fusion.4), channel_id=1, source_target_pairs={{0,16},{8,24},{16,0},{24,8},{1,17},{9,25},{17,1},{25,9},{2,18},{10... | collective-permute-start | bytes 835592 | tf_op jit(solution)/shard_map/ppermute | solution.py:439
  63.3 42.2 %collective-permute-start.12 = (bf16[2,136,512]{2,1,0:T(8,128)(2,1)S(1)}, bf16[2,136,512]{2,1,0:T(8,128)(2,1)}, u32[]{:S(2)}, u32[]{:S(2)}) collective-permute-start(bf16[2,136,512]{2,1,0:T(8,128)(2,1)S(1)} %pad_maximum_fusion.5), channel_id=1, source_target_pairs={{0,24},{8,0},{16,8},{24,16},{1,25},{9,1},{17,9},{25,17},{2,26},{10... | collective-permute-start | bytes 835592 | tf_op jit(solution)/shard_map/ppermute | solution.py:439
  64.1 51.3 %copy-start.1 = (bf16[136,2048]{1,0:T(8,128)(2,1)S(1)}, bf16[136,2048]{1,0:T(8,128)(2,1)}, u32[]{:S(2)}) copy-start(bf16[136,2048]{1,0:T(8,128)(2,1)} %copy-done) | copy-start | bytes 1671172
  64.1 51.3 %copy-start.3 = (bf16[136,2048]{1,0:T(8,128)(2,1)S(1)}, bf16[136,2048]{1,0:T(8,128)(2,1)}, u32[]{:S(2)}) copy-start(bf16[136,2048]{1,0:T(8,128)(2,1)} %copy-done.2) | copy-start | bytes 1671172
  64.1 51.4 %copy-start.5 = (bf16[136,2048]{1,0:T(8,128)(2,1)S(1)}, bf16[136,2048]{1,0:T(8,128)(2,1)}, u32[]{:S(2)}) copy-start(bf16[136,2048]{1,0:T(8,128)(2,1)} %copy-done.4) | copy-start | bytes 1671172
  64.1 51.4 %copy-start.7 = (bf16[136,2048]{1,0:T(8,128)(2,1)S(1)}, bf16[136,2048]{1,0:T(8,128)(2,1)}, u32[]{:S(2)}) copy-start(bf16[136,2048]{1,0:T(8,128)(2,1)} %copy-done.6) | copy-start | bytes 1671172
  64.1 51.4 %copy-start.9 = (bf16[136,2048]{1,0:T(8,128)(2,1)S(1)}, bf16[136,2048]{1,0:T(8,128)(2,1)}, u32[]{:S(2)}) copy-start(bf16[136,2048]{1,0:T(8,128)(2,1)} %copy-done.8) | copy-start | bytes 1671172
  64.1 51.4 %copy-start.11 = (bf16[136,2048]{1,0:T(8,128)(2,1)S(1)}, bf16[136,2048]{1,0:T(8,128)(2,1)}, u32[]{:S(2)}) copy-start(bf16[136,2048]{1,0:T(8,128)(2,1)} %copy-done.10) | copy-start | bytes 1671172
  64.1 51.4 %copy-start.13 = (bf16[8,96,128]{2,1,0:T(8,128)(2,1)S(1)}, bf16[8,96,128]{2,1,0:T(8,128)(2,1)}, u32[]{:S(2)}) copy-start(bf16[8,96,128]{2,1,0:T(8,128)(2,1)} %copy-done.12) | copy-start | bytes 589828
  64.1 51.4 %copy-start.18 = (s32[8]{0:T(128)S(1)}, s32[8]{0:T(128)}, u32[]{:S(2)}) copy-start(s32[8]{0:T(128)} %fusion.4.refs_0_) | copy-start | bytes 100
  105.5 8.2 %collective-permute-start.19 = (bf16[2,136,512]{2,1,0:T(8,128)(2,1)}, bf16[2,136,512]{2,1,0:T(8,128)(2,1)}, u32[]{:S(2)}, u32[]{:S(2)}) collective-permute-start(bf16[2,136,512]{2,1,0:T(8,128)(2,1)} %collective-permute-done.10.refs_12_), channel_id=1, source_target_pairs={{0,1},{1,0},{2,3},{3,2},{4,5},{5,4},{6,7},{7,6},{8,9},{9,8},{10,11... | collective-permute-start | bytes 835592 | tf_op jit(solution)/shard_map/ppermute | solution.py:444
  105.6 9.8 %collective-permute-start.20 = (bf16[2,136,512]{2,1,0:T(8,128)(2,1)}, bf16[2,136,512]{2,1,0:T(8,128)(2,1)}, u32[]{:S(2)}, u32[]{:S(2)}) collective-permute-start(bf16[2,136,512]{2,1,0:T(8,128)(2,1)} %collective-permute-done.11.refs_13_), channel_id=1, source_target_pairs={{0,1},{1,0},{2,3},{3,2},{4,5},{5,4},{6,7},{7,6},{8,9},{9,8},{10,11... | collective-permute-start | bytes 835592 | tf_op jit(solution)/shard_map/ppermute | solution.py:444
  106.9 8.6 %collective-permute-start.21 = (bf16[2,136,512]{2,1,0:T(8,128)(2,1)}, bf16[2,136,512]{2,1,0:T(8,128)(2,1)}, u32[]{:S(2)}, u32[]{:S(2)}) collective-permute-start(bf16[2,136,512]{2,1,0:T(8,128)(2,1)} %collective-permute-done.12.refs_14_), channel_id=1, source_target_pairs={{0,1},{1,0},{2,3},{3,2},{4,5},{5,4},{6,7},{7,6},{8,9},{9,8},{10,11... | collective-permute-start | bytes 835592 | tf_op jit(solution)/shard_map/ppermute | solution.py:444
  107.0 23.4 %all-to-all-start = ((f32[8,8,128]{2,1,0:T(8,128)}), f32[8,8,128]{2,1,0:T(8,128)}, u32[]{:S(2)}, u32[]{:S(2)}) async-start(f32[8,8,128]{2,1,0:T(8,128)} %get-tuple-element.29), calls=%async_computation | async-start | bytes 65536 | tf_op jit(solution)/shard_map/all_to_all | solution.py:515
  110.9 19.5 %collective-permute-start.13 = (bf16[16,64,96]{2,1,0:T(8,128)(2,1)}, bf16[16,64,96]{2,1,0:T(8,128)(2,1)}, u32[]{:S(2)}, u32[]{:S(2)}) collective-permute-start(bf16[16,64,96]{2,1,0:T(8,128)(2,1)} %get-tuple-element.34), channel_id=1, source_target_pairs={{0,8},{8,16},{16,24},{24,0},{1,9},{9,17},{17,25},{25,1},{2,10},{10... | collective-permute-start | bytes 589832 | tf_op jit(solution)/shard_map/ppermute | solution.py:439
  112.1 18.2 %collective-permute-start.14 = (bf16[16,64,96]{2,1,0:T(8,128)(2,1)}, bf16[16,64,96]{2,1,0:T(8,128)(2,1)}, u32[]{:S(2)}, u32[]{:S(2)}) collective-permute-start(bf16[16,64,96]{2,1,0:T(8,128)(2,1)} %get-tuple-element.35), channel_id=1, source_target_pairs={{0,16},{8,24},{16,0},{24,8},{1,17},{9,25},{17,1},{25,9},{2,18},{10... | collective-permute-start | bytes 589832 | tf_op jit(solution)/shard_map/ppermute | solution.py:439
  113.7 16.7 %collective-permute-start.15 = (bf16[16,64,96]{2,1,0:T(8,128)(2,1)}, bf16[16,64,96]{2,1,0:T(8,128)(2,1)}, u32[]{:S(2)}, u32[]{:S(2)}) collective-permute-start(bf16[16,64,96]{2,1,0:T(8,128)(2,1)} %get-tuple-element.36), channel_id=1, source_target_pairs={{0,24},{8,0},{16,8},{24,16},{1,25},{9,1},{17,9},{25,17},{2,26},{10... | collective-permute-start | bytes 589832 | tf_op jit(solution)/shard_map/ppermute | solution.py:439
  (19 other events, 75.6 us)

commit v4 on v3

--- a/solution.py
+++ b/solution.py
@@ -195,11 +195,8 @@
     owners_ref = refs[0]
     token_refs = refs[1 : 1 + shards]
     hidden_ref, u_ref, weight_hbm, amap_ref, bmap_hbm = refs[1 + shards : 6 + shards]
-    hg_ref, rk_ref = refs[6 + shards : 8 + shards]
-    la_refs = refs[8 + shards : 8 + shards + group_count]
-    dy_s, wb_s, rows_s, code_s, gate_s, back_s, dy_sem, w_sem, b_sem = refs[
-        8 + shards + group_count :
-    ]
+    hg_ref, rk_ref, la_ref = refs[6 + shards : 9 + shards]
+    dy_s, wb_s, rows_s, y_s, code_s, gate_s, back_s, dy_sem, w_sem, b_sem = refs[9 + shards :]
     top, span = rk_ref.shape[1:]
     micro, experts, slots, units = hidden_ref.shape
     rank = amap_ref.shape[1]
@@ -207,7 +204,6 @@
     block = span // micro
     padded = rows_s.shape[1] // micro
     first = (lax.axis_index("expert") * experts).astype(jnp.float32)
-    group = lax.axis_index("dp")
 
     token_copies = [
         pltpu.make_async_copy(token_refs[i], dy_s.at[i], dy_sem.at[i])
@@ -257,54 +253,82 @@
                 experts, padded, tile
             )
 
-    def one_expert(x, lanes):
-        both = lax.dot_general(
-            wb_s[x], rows_s[x], contract_last, preferred_element_type=jnp.float32
-        ).T
-        main = both[:, :units]
-        v = both[:, units:].astype(jnp.bfloat16)
-        low = jnp.dot(v, amap_ref[x], preferred_element_type=jnp.float32)
-        gate = gate_s[x]
-        grad = (gate * (main + adapter_scale * low)).astype(jnp.bfloat16)
-        filler = jnp.zeros((padded - slots, units), jnp.float32)
-        pieces = []
-        for m in range(micro):
-            hg_ref[m, x] = grad[m * padded : m * padded + slots]
-            pieces.append(hidden_ref[m, x].astype(jnp.float32))
-            pieces.append(filler)
-        held_wide = jnp.concatenate(pieces, axis=0)
-        held = held_wide.astype(jnp.bfloat16)
-        v_wide = v.astype(jnp.float32)
-        routed = jnp.sum(main * held_wide, axis=1, keepdims=True) + adapter_scale * jnp.sum(
-            u_ref[lax.rem(x, experts // 2), :, lanes].astype(jnp.float32) * v_wide, axis=1, keepdims=True
-        )
-        for m in range(micro):
-            hit = code_s[m, pl.ds(x, 1), :] == slot_of
-            back_s[m, pl.ds(x, 1), :] = jnp.sum(
-                jnp.where(hit, routed[m * padded : (m + 1) * padded], 0.0), axis=0, keepdims=True
-            )
-        w = (gate * v_wide).astype(jnp.bfloat16)
-        la = adapter_scale * lax.dot_general(
-            w, held, contract_first, preferred_element_type=jnp.float32
-        )
-        share = units // group_count
-        for s in range(group_count):
-            aim = lax.rem(group + s, group_count)
-            mine = la[:, :share]
-            for k in range(1, group_count):
-                mine = jnp.where(aim == k, la[:, k * share : (k + 1) * share], mine)
-            la_refs[s][x] = mine.astype(la_refs[s].dtype)
-
     half = experts // 2
 
-    def two_experts(x, carry):
-        for copy in weight_copies(x) + weight_copies(x + half):
+    def main_products(x, carry):
+        for copy in weight_copies(2 * x) + weight_copies(2 * x + 1):
             copy.wait()
-        one_expert(x, slice(0, rank))
-        one_expert(x + half, slice(rank, 2 * rank))
+        for i in range(2):
+            y_s[2 * x + i] = lax.dot_general(
+                rows_s[2 * x + i],
+                wb_s[2 * x + i],
+                contract_last,
+                preferred_element_type=jnp.float32,
+            )
         return carry
 
-    lax.fori_loop(0, half, two_experts, 0)
+    lax.fori_loop(0, half, main_products, 0)
+
+    share = units // group_count
+    filler = jnp.zeros((padded - slots, units), jnp.float32)
+    batch = 2 if half % 2 == 0 else 1
+
+    def small_steps(step, carry):
+        at = [step * batch + i for i in range(batch)]
+        picked = [(p, p, slice(0, rank)) for p in at]
+        picked += [(p + half, p, slice(rank, 2 * rank)) for p in at]
+        xs = [x for x, _, _ in picked]
+        mains = [y_s[x, :, :units] for x in xs]
+        vs = [y_s[x, :, units:].astype(jnp.bfloat16) for x in xs]
+        lows = [
+            jnp.dot(v, amap_ref[x], preferred_element_type=jnp.float32) for v, x in zip(vs, xs)
+        ]
+        gates_x = [gate_s[x] for x in xs]
+        wide = [
+            jnp.concatenate(
+                [
+                    part
+                    for m in range(micro)
+                    for part in (hidden_ref[m, x].astype(jnp.float32), filler)
+                ],
+                axis=0,
+            )
+            for x in xs
+        ]
+        v_wide = [v.astype(jnp.float32) for v in vs]
+        ws = [(gate * v).astype(jnp.bfloat16) for gate, v in zip(gates_x, v_wide)]
+        las = [
+            lax.dot_general(
+                w, held.astype(jnp.bfloat16), contract_first, preferred_element_type=jnp.float32
+            )
+            for w, held in zip(ws, wide)
+        ]
+        routed = [
+            jnp.sum(main * held, axis=1, keepdims=True)
+            + adapter_scale
+            * jnp.sum(u_ref[p, :, lanes].astype(jnp.float32) * v, axis=1, keepdims=True)
+            for main, held, v, (_, p, lanes) in zip(mains, wide, v_wide, picked)
+        ]
+        grads = [
+            (gate * (main + adapter_scale * low)).astype(jnp.bfloat16)
+            for gate, main, low in zip(gates_x, mains, lows)
+        ]
+        for x, grad, la, back in zip(xs, grads, las, routed):
+            for m in range(micro):
+                hg_ref[m, x] = grad[m * padded : m * padded + slots]
+                hit = code_s[m, pl.ds(x, 1), :] == slot_of
+                back_s[m, pl.ds(x, 1), :] = jnp.sum(
+                    jnp.where(hit, back[m * padded : (m + 1) * padded], 0.0),
+                    axis=0,
+                    keepdims=True,
+                )
+            for k in range(group_count):
+                la_ref[k, x] = (adapter_scale * la[:, k * share : (k + 1) * share]).astype(
+                    la_ref.dtype
+                )
+        return carry
+
+    lax.fori_loop(0, half // batch, small_steps, 0)
 
     number = lax.broadcasted_iota(jnp.int32, (experts, span), 0).astype(jnp.float32) + first
     for i in range(shards):
@@ -321,33 +345,26 @@
 
 
 def adapter_kernel(capacity, micro, span, top, group_count, shards, *refs):
-    others = group_count - 1
     pairs = shards // 2
     early = pairs // 2
-    owners_ref = refs[0]
-    token_refs = refs[1 : 1 + shards]
-    early_refs = refs[1 + shards : 1 + shards + others]
-    late_refs = refs[1 + shards + others : 1 + shards + 2 * others]
-    swapped_refs = refs[1 + shards + 2 * others : 1 + shards + 3 * others]
-    u_refs = refs[1 + shards + 3 * others : 2 + shards + 4 * others]
-    lb_ref, tok_s, q_s, sem = refs[2 + shards + 4 * others :]
+    owners_ref, early_ref, late_ref, swapped_ref = refs[:4]
+    u_refs = refs[4 : 4 + group_count]
+    lb_ref, tok_s, q_s, sem = refs[4 + group_count :]
     experts, rank, share = lb_ref.shape
     tall = u_refs[0].shape[1]
     padded = tall // micro
     block = span // micro
     first = (lax.axis_index("expert") * experts).astype(jnp.float32)
     group = lax.axis_index("dp")
-    cols = pl.ds(pl.multiple_of(group * share, share), share)
     copies = []
     for g in range(group_count):
+        home = lax.rem(group - g + group_count, group_count)
         for i in range(shards):
             far, k = i // pairs, i % pairs
-            if g == 0:
-                source = token_refs[i].at[:, cols]
-            elif k < early:
-                source = early_refs[g - 1].at[far * early + k]
+            if k < early:
+                source = early_ref.at[home, far * early + k]
             else:
-                source = (swapped_refs if far else late_refs)[g - 1].at[k - early]
+                source = (swapped_ref if far else late_ref).at[home, k - early]
             copies.append(pltpu.make_async_copy(source, tok_s.at[g, i], sem.at[g, i]))
     for copy in copies:
         copy.start()
@@ -443,11 +460,15 @@
     def swap_partners(array):
         return lax.ppermute(array, "expert", swap)
 
-    def columns_for(group_shift, chosen):
-        aim = lax.rem(group + group_shift, group_count) * share
-        return jnp.stack(
-            [lax.dynamic_slice_in_dim(piece, aim, share, axis=1) for piece in chosen]
-        )
+    def exchange_columns(chosen):
+        parts = [
+            jnp.stack([piece[:, g * share : (g + 1) * share] for piece in chosen])
+            for g in range(group_count)
+        ]
+        return jnp.stack(parts)
+
+    def across_groups(array):
+        return lax.all_to_all(array, "dp", split_axis=0, concat_axis=0, tiled=True)
 
     others = range(1, group_count)
     u_all = [u] + [shift_groups(u, s) for s in others]
@@ -465,35 +486,34 @@
     early = pairs // 2
     near, far = [sent], []
     for step in range(pairs - 1):
-        ahead = near[-1]
-        if step == pairs - 2:
-            ahead, *u_all = lax.optimization_barrier((ahead, *u_all))
-        near.append(lax.ppermute(ahead, "expert", ring))
+        near.append(lax.ppermute(near[-1], "expert", ring))
         far.append(swap_partners(near[step]))
+    early_columns = exchange_columns(near[:early] + far[:early])
+    early_columns, *u_all = lax.optimization_barrier((early_columns, *u_all))
+    early_columns = across_groups(early_columns)
+    late_columns = across_groups(exchange_columns(near[early:]))
     far.append(swap_partners(near[-1]))
-    early_columns = [
-        shift_groups(columns_for(s, near[:early] + far[:early]), s) for s in others
-    ]
-    late_columns = [shift_groups(columns_for(s, near[early:]), s) for s in others]
     pieces = near + far
 
     vmem = pl.BlockSpec(memory_space=pltpu.VMEM)
     smem = pl.BlockSpec(memory_space=pltpu.SMEM)
     anywhere = pl.BlockSpec(memory_space=pl.ANY)
-    part_a = jax.ShapeDtypeStruct((experts, rank, units // group_count), jnp.bfloat16)
-    hidden_grad, routed, *parts = pl.pallas_call(
+    hidden_grad, routed, part_a = pl.pallas_call(
         functools.partial(expert_kernel, capacity, group_count, sources),
         out_shape=(
             jax.ShapeDtypeStruct(hidden.shape, jnp.bfloat16),
             jax.ShapeDtypeStruct((sources, top, span), jnp.float32),
-        )
-        + (part_a,) * group_count,
+            jax.ShapeDtypeStruct(
+                (group_count, experts, rank, units // group_count), jnp.bfloat16
+            ),
+        ),
         in_specs=[smem] + [anywhere] * sources + [vmem, vmem, anywhere, vmem, anywhere],
-        out_specs=(vmem,) * (2 + group_count),
+        out_specs=(vmem,) * 3,
         scratch_shapes=[
             pltpu.VMEM((sources, span + extra, width), jnp.bfloat16),
             pltpu.VMEM((experts, units + rank, width), jnp.bfloat16),
             pltpu.VMEM((experts, micro * padded, width), jnp.bfloat16),
+            pltpu.VMEM((experts, micro * padded, units + rank), jnp.float32),
             pltpu.VMEM((micro, experts, sources * block), jnp.float32),
             pltpu.VMEM((experts, micro * padded, 1), jnp.float32),
             pltpu.VMEM((micro, experts, sources * block), jnp.float32),
@@ -510,37 +530,33 @@
         name="expert_rows",
     )(owners, *pieces, hidden, u, frozen_down_weight, amap, adapter_output_map)
 
-    late_columns, parts = lax.optimization_barrier((late_columns, parts))
-    swapped = [swap_partners(columns) for columns in late_columns]
+    late_columns, part_a, routed = lax.optimization_barrier((late_columns, part_a, routed))
+    swapped = swap_partners(late_columns)
+    arrived = across_groups(part_a)
     home = lax.all_to_all(routed, "expert", split_axis=0, concat_axis=0, tiled=True)
-    arrived = [shift_groups(parts[s], s) for s in others]
 
     lora_b = pl.pallas_call(
         functools.partial(adapter_kernel, capacity, micro, span, top, group_count, sources),
         out_shape=jax.ShapeDtypeStruct((experts, rank, share), jnp.float32),
-        in_specs=[smem]
-        + [anywhere] * (sources + 3 * (group_count - 1))
-        + [vmem] * group_count,
+        in_specs=[smem] + [anywhere] * 3 + [vmem] * group_count,
         out_specs=vmem,
         scratch_shapes=[
             pltpu.VMEM((group_count, sources, span + extra, share), jnp.bfloat16),
             pltpu.VMEM((experts, group_count * micro * padded, share), jnp.bfloat16),
             pltpu.SemaphoreType.DMA((group_count, sources)),
         ],
-        compiler_params=pltpu.CompilerParams(vmem_limit_bytes=40 * 1024 * 1024),
+        compiler_params=pltpu.CompilerParams(vmem_limit_bytes=58 * 1024 * 1024),
         cost_estimate=pl.CostEstimate(
             flops=2 * experts * micro * padded * share * group_count * (rank + sources * block),
             bytes_accessed=2 * group_count * sources * span * share + 4 * experts * rank * share,
             transcendentals=0,
         ),
         name="adapter_columns",
-    )(owners, *pieces, *early_columns, *late_columns, *swapped, *u_all)
+    )(owners, early_columns, late_columns, swapped, *u_all)
 
     home, arrived, lora_b = lax.optimization_barrier((home, arrived, lora_b))
     router_grad = jnp.sum(home, axis=0).T
-    lora_a = parts[0].astype(jnp.float32)
-    for part in arrived:
-        lora_a = lora_a + part.astype(jnp.float32)
+    lora_a = jnp.sum(arrived.astype(jnp.float32), axis=0)
     return (hidden_grad, router_grad, lora_a, lora_b)
 
 

time: 135 us -> 145 us (1.074)
  waiting for transfers between devices: 33.5 us -> 54.2 us
  Pallas kernels: 50.2 us -> 40.2 us
  starting transfers between devices: 29.2 us -> 33.3 us
  local copies, waits for them, and re-layouts: 9.34 us -> 6.99 us
  other arithmetic: 9.05 us -> 7.45 us
    all_to_all x0 -> x3, waiting for transfers between devices: none -> 29 us  [across_groups(): return lax.all_to_all(array, 'dp', split_axis=0, concat_axis=0, tiled=True)]
    ppermute x12 -> x3, waiting for transfers between devices: 14.6 us -> 0.01 us  [shift_groups(): lax.ppermute(array, 'dp', [(d, (d + by) % group_count) for d in range(gro...]
    all_to_all x0 -> x3, starting transfers between devices: none -> 12.1 us  [across_groups(): return lax.all_to_all(array, 'dp', split_axis=0, concat_axis=0, tiled=True)]
    pallas_call x1, Pallas kernels: 41.3 us -> 30.2 us  [local_by_tokens(): pl.pallas_call(functools.partial(expert_kernel, capacity, group_count, so...]
    ppermute x12 -> x3, starting transfers between devices: 16.3 us -> 5.56 us  [shift_groups(): lax.ppermute(array, 'dp', [(d, (d + by) % group_count) for d in range(gro...]
    unnamed x58 -> x40, local copies, waits for them, and re-layouts: 7.88 us -> 2.5 us
    all_to_all x1, waiting for transfers between devices: 0.01 us -> 4.08 us  [local_by_tokens(): lax.all_to_all(routed, 'expert', split_axis=0, concat_axis=0, tiled=True)]
    another operation x6, local copies, waits for them, and re-layouts: 0.18 us -> 3.2 us  [exchange_columns(): jnp.stack([piece[:, g * share:(g + 1) * share] for piece in chosen])]
  transfers between devices with their start and end apart: 23 -> 15, of which waited for: 5 -> 6; matrix products, arithmetic and copies ran while one was open for 5% -> 6% of each run, Pallas kernels for 38% -> 28%
where the time goes in v4:
time: 145 us
  waiting for transfers between devices  54.2 us (37%)
  Pallas kernels  40.2 us (28%)
  starting transfers between devices  33.3 us (23%)
  other arithmetic  7.45 us (5%)
  local copies, waits for them, and re-layouts  6.99 us (5%)
  matrix products  1.62 us (1%)
    pallas_call x1, Pallas kernels, local_by_tokens(): pl.pallas_call(functools.partial(expert_kernel, capacity, group_count, so...  30.2 us
    all_to_all x3, waiting for transfers between devices, across_groups(): return lax.all_to_all(array, 'dp', split_axis=0, concat_axis=0, tiled=True)  29 us
    ppermute x3, waiting for transfers between devices, local_by_tokens(): near.append(lax.ppermute(near[-1], 'expert', ring))  21.1 us
    all_to_all x3, starting transfers between devices, across_groups(): return lax.all_to_all(array, 'dp', split_axis=0, concat_axis=0, tiled=True)  12.1 us
    ppermute x3, starting transfers between devices, local_by_tokens(): near.append(lax.ppermute(near[-1], 'expert', ring))  10.8 us
    pallas_call x1, Pallas kernels, local_by_tokens(): pl.pallas_call(functools.partial(adapter_kernel, capacity, micro, span, t...  9.96 us
    ppermute x3, starting transfers between devices, shift_groups(): lax.ppermute(array, 'dp', [(d, (d + by) % group_count) for d in range(gro...  5.56 us
    all_to_all x1, starting transfers between devices, local_by_tokens(): lax.all_to_all(routed, 'expert', split_axis=0, concat_axis=0, tiled=True)  4.66 us
  transfers between devices with their start and end apart: 15, of which 6 were waited for; matrix products, arithmetic and copies ran while one was open for 6% of the time, Pallas kernels for 28%

profile of v4, /device:TPU:0, one launch (start us, length us, event | category | flops | bytes accessed | tf_op | source)
XLA Modules:
  0.0 144.7 jit_solution(17059741389666120560)
XLA Ops:
  0.6 0.8 convert_bitcast_fusion
  1.4 0.7 pad_maximum_fusion.3
  2.1 1.1 fusion.3.refs_1_
  3.2 4.1 %collective-permute-start = (bf16[136,2048]{1,0:T(8,128)(2,1)S(1)}, bf16[136,2048]{1,0:T(8,128)(2,1)S(1)}, u32[]{:S(2)}, u32[]{:S(2)}) collective-permute-start(bf16[136,2048]{1,0:T(8,128)(2,1)S(1)} %fusion.3.refs_1_), channel_id=1, source_target_pairs={{0,4},{1,5},{2,0},{3,1},{4,6},{5,7},{6,2},{7,3},{8,12},{9,13},{10,... | collective-permute-start | bytes 1671176 | tf_op jit(solution)/shard_map/ppermute | solution.py:489
  7.3 1.6 %convolution_convert_fusion = bf16[16,2,40,64]{3,2,1,0:T(8,128)(2,1)S(1)} fusion(bf16[2,16,40,384]{3,2,1,0:T(8,128)(2,1)S(1)} %copy-done.7, bf16[16,384,64]{1,2,0:T(8,128)(2,1)} %param.13), kind=kOutput, calls=%fused_computation.2 | convolution fusion | flops 62996480 | bytes 1933312 | tf_op jit(solution)/shard_map/mesk,exk->emsx/dot_general | solution.py:448
  9.2 1.5 %collective-permute-start.7 = (bf16[8,96,128]{2,1,0:T(8,128)(2,1)S(1)}, bf16[8,96,128]{2,1,0:T(8,128)(2,1)}, u32[]{:S(2)}, u32[]{:S(2)}) collective-permute-start(bf16[8,96,128]{2,1,0:T(8,128)(2,1)S(1)} %pad_maximum_fusion.2.refs_10_.refs_4_), channel_id=1, source_target_pairs={{0,8},{8,16},{16,24},{24,0},{1,9},{9,17},{17,25},{25,1},{2,10},{10... | collective-permute-start | bytes 589832 | tf_op jit(solution)/shard_map/ppermute | solution.py:456
  10.7 1.5 %collective-permute-start.8 = (bf16[8,96,128]{2,1,0:T(8,128)(2,1)S(1)}, bf16[8,96,128]{2,1,0:T(8,128)(2,1)}, u32[]{:S(2)}, u32[]{:S(2)}) collective-permute-start(bf16[8,96,128]{2,1,0:T(8,128)(2,1)S(1)} %pad_maximum_fusion.2.refs_10_.refs_4_), channel_id=1, source_target_pairs={{0,16},{8,24},{16,0},{24,8},{1,17},{9,25},{17,1},{25,9},{2,18},{10... | collective-permute-start | bytes 589832 | tf_op jit(solution)/shard_map/ppermute | solution.py:456
  12.2 7.0 %collective-permute-done.refs_2_ = bf16[136,2048]{1,0:T(8,128)(2,1)S(1)} collective-permute-done((bf16[136,2048]{1,0:T(8,128)(2,1)S(1)}, bf16[136,2048]{1,0:T(8,128)(2,1)S(1)}, u32[]{:S(2)}, u32[]{:S(2)}) %collective-permute-start) | collective-permute-done | bytes 557088 | tf_op jit(solution)/shard_map/ppermute | solution.py:489
  19.2 3.4 %collective-permute-start.1 = (bf16[136,2048]{1,0:T(8,128)(2,1)S(1)}, bf16[136,2048]{1,0:T(8,128)(2,1)S(1)}, u32[]{:S(2)}, u32[]{:S(2)}) collective-permute-start(bf16[136,2048]{1,0:T(8,128)(2,1)S(1)} %collective-permute-done.refs_2_), channel_id=1, source_target_pairs={{0,4},{1,5},{2,0},{3,1},{4,6},{5,7},{6,2},{7,3},{8,12},{9,13},{10,... | collective-permute-start | bytes 1671176 | tf_op jit(solution)/shard_map/ppermute | solution.py:489
  22.6 1.2 dynamic-slice_bitcast_fusion.refs_0_
  23.8 0.8 slice_bitcast_fusion.15
  24.6 0.8 slice_bitcast_fusion.14
  25.4 2.5 %collective-permute-start.9 = (bf16[8,96,128]{2,1,0:T(8,128)(2,1)S(1)}, bf16[8,96,128]{2,1,0:T(8,128)(2,1)}, u32[]{:S(2)}, u32[]{:S(2)}) collective-permute-start(bf16[8,96,128]{2,1,0:T(8,128)(2,1)S(1)} %pad_maximum_fusion.2.refs_10_.refs_4_), channel_id=1, source_target_pairs={{0,24},{8,0},{16,8},{24,16},{1,25},{9,1},{17,9},{25,17},{2,26},{10... | collective-permute-start | bytes 589832 | tf_op jit(solution)/shard_map/ppermute | solution.py:456
  27.9 5.7 %collective-permute-done.1.refs_3_ = bf16[136,2048]{1,0:T(8,128)(2,1)S(1)} collective-permute-done((bf16[136,2048]{1,0:T(8,128)(2,1)S(1)}, bf16[136,2048]{1,0:T(8,128)(2,1)S(1)}, u32[]{:S(2)}, u32[]{:S(2)}) %collective-permute-start.1) | collective-permute-done | bytes 557088 | tf_op jit(solution)/shard_map/ppermute | solution.py:489
  33.6 3.4 %collective-permute-start.2 = (bf16[136,2048]{1,0:T(8,128)(2,1)S(1)}, bf16[136,2048]{1,0:T(8,128)(2,1)S(1)}, u32[]{:S(2)}, u32[]{:S(2)}) collective-permute-start(bf16[136,2048]{1,0:T(8,128)(2,1)S(1)} %collective-permute-done.1.refs_3_), channel_id=1, source_target_pairs={{0,4},{1,5},{2,0},{3,1},{4,6},{5,7},{6,2},{7,3},{8,12},{9,13},{10,... | collective-permute-start | bytes 1671176 | tf_op jit(solution)/shard_map/ppermute | solution.py:489
  37.0 0.8 slice_bitcast_fusion.13
  37.9 0.8 slice_bitcast_fusion.12
  38.8 8.3 %collective-permute-done.2.refs_4_ = bf16[136,2048]{1,0:T(8,128)(2,1)S(1)} collective-permute-done((bf16[136,2048]{1,0:T(8,128)(2,1)S(1)}, bf16[136,2048]{1,0:T(8,128)(2,1)S(1)}, u32[]{:S(2)}, u32[]{:S(2)}) %collective-permute-start.2) | collective-permute-done | bytes 557088 | tf_op jit(solution)/shard_map/ppermute | solution.py:489
  47.2 0.7 copy-done.5
  48.0 1.1 pad_maximum_fusion.1
  49.1 4.3 %all-to-all-start = ((bf16[4,2,136,512]{3,2,1,0:T(8,128)(2,1)}), bf16[4,2,136,512]{3,2,1,0:T(8,128)(2,1)}, u32[]{:S(2)}, u32[]{:S(2)}) async-start(bf16[4,2,136,512]{3,2,1,0:T(8,128)(2,1)} %pad_maximum_fusion.1), calls=%async_computation | async-start | bytes 2228224 | tf_op jit(solution)/shard_map/all_to_all | solution.py:471
  53.6 0.7 copy-done.9
  54.9 30.2 %expert_rows.1 = (bf16[2,16,40,384]{3,2,1,0:T(8,128)(2,1)}, f32[8,8,128]{2,1,0:T(8,128)}, bf16[4,16,64,96]{3,2,1,0:T(8,128)(2,1)}) custom-call(s32[8]{0:T(128)} %dynamic-slice_bitcast_fusion.refs_0_, bf16[136,2048]{1,0:T(8,128)(2,1)} %copy-done, bf16[136,2048]{1,0:T(8,128)(2,1)} %copy-done.1, bf16[136,2048]{1,0:T(8,128)(2,1)} %copy-done.3, ...), custom_call_target="tpu_custom_call" | custom-call | flops 6039797760 | bytes 33554432 | tf_op jit(solution)/shard_map/expert_rows/pallas_call | solution.py:501
  85.1 4.7 %all-to-all-start.1 = ((f32[8,8,128]{2,1,0:T(8,128)}), f32[8,8,128]{2,1,0:T(8,128)S(1)}, u32[]{:S(2)}, u32[]{:S(2)}) async-start(f32[8,8,128]{2,1,0:T(8,128)} %get-tuple-element.21), calls=%async_computation.1 | async-start | bytes 65536 | tf_op jit(solution)/shard_map/all_to_all | solution.py:536
  89.8 1.7 %pad_maximum_fusion = bf16[4,4,136,512]{3,2,1,0:T(8,128)(2,1)} fusion(bf16[1,4,136,512]{3,2,1,0:T(8,128)(2,1)S(1)} %get-tuple-element.65, bf16[1,4,136,512]{3,2,1,0:T(8,128)(2,1)S(1)} %get-tuple-element.64, bf16[1,4,136,512]{3,2,1,0:T(8,128)(2,1)S(1)} %get-tuple-element.63, bf16[1,4,136,512]{3,2,1,0:T(8,128)(2,1)S(1)} %get-tuple-element.62), kind=kLoop, calls=%fused_computation | loop fusion | flops 3342336 | bytes 4456448 | tf_op jit(solution)/shard_map/stack | solution.py:468
  91.5 4.1 %all-to-all-done.1 = f32[8,8,128]{2,1,0:T(8,128)S(1)} async-done(((f32[8,8,128]{2,1,0:T(8,128)}), f32[8,8,128]{2,1,0:T(8,128)S(1)}, u32[]{:S(2)}, u32[]{:S(2)}) %all-to-all-start.1) | async-done | bytes 32800 | tf_op jit(solution)/shard_map/all_to_all | solution.py:536
  96.2 4.1 %all-to-all-start.3 = ((bf16[4,4,136,512]{3,2,1,0:T(8,128)(2,1)}), bf16[4,4,136,512]{3,2,1,0:T(8,128)(2,1)S(1)}, u32[]{:S(2)}, u32[]{:S(2)}) async-start(bf16[4,4,136,512]{3,2,1,0:T(8,128)(2,1)} %pad_maximum_fusion), calls=%async_computation.3 | async-start | bytes 4456448 | tf_op jit(solution)/shard_map/all_to_all | solution.py:471
  100.3 26.2 %all-to-all-done.3.refs_1_ = bf16[4,4,136,512]{3,2,1,0:T(8,128)(2,1)S(1)} async-done(((bf16[4,4,136,512]{3,2,1,0:T(8,128)(2,1)}), bf16[4,4,136,512]{3,2,1,0:T(8,128)(2,1)S(1)}, u32[]{:S(2)}, u32[]{:S(2)}) %all-to-all-start.3) | async-done | bytes 2228256 | tf_op jit(solution)/shard_map/all_to_all | solution.py:471
  126.5 3.7 %all-to-all-start.2 = ((bf16[4,16,64,96]{3,2,1,0:T(8,128)(2,1)}), bf16[4,16,64,96]{3,2,1,0:T(8,128)(2,1)S(1)}, u32[]{:S(2)}, u32[]{:S(2)}) async-start(bf16[4,16,64,96]{3,2,1,0:T(8,128)(2,1)} %get-tuple-element.22), calls=%async_computation.2 | async-start | bytes 2097152 | tf_op jit(solution)/shard_map/all_to_all | solution.py:471
  130.2 10.0 %adapter_columns.1 = f32[16,64,512]{2,1,0:T(8,128)} custom-call(s32[8]{0:T(128)} %dynamic-slice_bitcast_fusion.refs_0_, bf16[4,4,136,512]{3,2,1,0:T(8,128)(2,1)} %copy-done.6, bf16[4,2,136,512]{3,2,1,0:T(8,128)(2,1)} %all-to-all-done.refs_2_, bf16[4,2,136,512]{3,2,1,0:T(8,128)(2,1)} %collective-permute-done.10.refs_3_, bf16[8,96,128]{2,1,0:T(8,128)(2,1)} %copy-done.8, ...), custom_call_target="tpu_custom_call" | custom-call | flops 3623878656 | bytes 6291456 | tf_op jit(solution)/shard_map/adapter_columns/pallas_call | solution.py:538
  140.2 2.9 %all-to-all-done.2 = bf16[4,16,64,96]{3,2,1,0:T(8,128)(2,1)S(1)} async-done(((bf16[4,16,64,96]{3,2,1,0:T(8,128)(2,1)}), bf16[4,16,64,96]{3,2,1,0:T(8,128)(2,1)S(1)}, u32[]{:S(2)}, u32[]{:S(2)}) %all-to-all-start.2) | async-done | bytes 786464 | tf_op jit(solution)/shard_map/all_to_all | solution.py:471
  143.1 1.0 convert_reduce_fusion
  (62 shorter events, 2.5 us)
Async XLA Ops:
  0.6 6.7 %copy-start.7 = (bf16[2,16,40,384]{3,2,1,0:T(8,128)(2,1)S(1)}, bf16[2,16,40,384]{3,2,1,0:T(8,128)(2,1)}, u32[]{:S(2)}) copy-start(bf16[2,16,40,384]{3,2,1,0:T(8,128)(2,1)} %refs_9_.1) | copy-start | bytes 2949124
  3.2 20.6 %copy-start = (bf16[136,2048]{1,0:T(8,128)(2,1)}, bf16[136,2048]{1,0:T(8,128)(2,1)S(1)}, u32[]{:S(2)}) copy-start(bf16[136,2048]{1,0:T(8,128)(2,1)S(1)} %fusion.3.refs_1_) | copy-start | bytes 1671172
  3.2 16.0 %collective-permute-start = (bf16[136,2048]{1,0:T(8,128)(2,1)S(1)}, bf16[136,2048]{1,0:T(8,128)(2,1)S(1)}, u32[]{:S(2)}, u32[]{:S(2)}) collective-permute-start(bf16[136,2048]{1,0:T(8,128)(2,1)S(1)} %fusion.3.refs_1_), channel_id=1, source_target_pairs={{0,4},{1,5},{2,0},{3,1},{4,6},{5,7},{6,2},{7,3},{8,12},{9,13},{10,... | collective-permute-start | bytes 1671176 | tf_op jit(solution)/shard_map/ppermute | solution.py:489
  7.3 18.0 %collective-permute-start.3 = (bf16[136,2048]{1,0:T(8,128)(2,1)S(1)}, bf16[136,2048]{1,0:T(8,128)(2,1)S(1)}, u32[]{:S(2)}, u32[]{:S(2)}) collective-permute-start(bf16[136,2048]{1,0:T(8,128)(2,1)S(1)} %fusion.3.refs_1_), channel_id=1, source_target_pairs={{0,1},{1,0},{2,3},{3,2},{4,5},{5,4},{6,7},{7,6},{8,9},{9,8},{10,11... | collective-permute-start | bytes 1671176 | tf_op jit(solution)/shard_map/ppermute | solution.py:461
  9.2 16.2 %copy-start.8 = (bf16[8,96,128]{2,1,0:T(8,128)(2,1)}, bf16[8,96,128]{2,1,0:T(8,128)(2,1)S(1)}, u32[]{:S(2)}) copy-start(bf16[8,96,128]{2,1,0:T(8,128)(2,1)S(1)} %pad_maximum_fusion.2.refs_10_.refs_4_) | copy-start | bytes 589828
  9.2 82.3 %collective-permute-start.7 = (bf16[8,96,128]{2,1,0:T(8,128)(2,1)S(1)}, bf16[8,96,128]{2,1,0:T(8,128)(2,1)}, u32[]{:S(2)}, u32[]{:S(2)}) collective-permute-start(bf16[8,96,128]{2,1,0:T(8,128)(2,1)S(1)} %pad_maximum_fusion.2.refs_10_.refs_4_), channel_id=1, source_target_pairs={{0,8},{8,16},{16,24},{24,0},{1,9},{9,17},{17,25},{25,1},{2,10},{10... | collective-permute-start | bytes 589832 | tf_op jit(solution)/shard_map/ppermute | solution.py:456
  10.7 80.7 %collective-permute-start.8 = (bf16[8,96,128]{2,1,0:T(8,128)(2,1)S(1)}, bf16[8,96,128]{2,1,0:T(8,128)(2,1)}, u32[]{:S(2)}, u32[]{:S(2)}) collective-permute-start(bf16[8,96,128]{2,1,0:T(8,128)(2,1)S(1)} %pad_maximum_fusion.2.refs_10_.refs_4_), channel_id=1, source_target_pairs={{0,16},{8,24},{16,0},{24,8},{1,17},{9,25},{17,1},{25,9},{2,18},{10... | collective-permute-start | bytes 589832 | tf_op jit(solution)/shard_map/ppermute | solution.py:456
  19.2 6.1 %copy-start.1 = (bf16[136,2048]{1,0:T(8,128)(2,1)}, bf16[136,2048]{1,0:T(8,128)(2,1)S(1)}, u32[]{:S(2)}) copy-start(bf16[136,2048]{1,0:T(8,128)(2,1)S(1)} %collective-permute-done.refs_2_) | copy-start | bytes 1671172
  19.2 14.4 %collective-permute-start.1 = (bf16[136,2048]{1,0:T(8,128)(2,1)S(1)}, bf16[136,2048]{1,0:T(8,128)(2,1)S(1)}, u32[]{:S(2)}, u32[]{:S(2)}) collective-permute-start(bf16[136,2048]{1,0:T(8,128)(2,1)S(1)} %collective-permute-done.refs_2_), channel_id=1, source_target_pairs={{0,4},{1,5},{2,0},{3,1},{4,6},{5,7},{6,2},{7,3},{8,12},{9,13},{10,... | collective-permute-start | bytes 1671176 | tf_op jit(solution)/shard_map/ppermute | solution.py:489
  24.6 13.2 %collective-permute-start.4 = (bf16[136,2048]{1,0:T(8,128)(2,1)S(1)}, bf16[136,2048]{1,0:T(8,128)(2,1)S(1)}, u32[]{:S(2)}, u32[]{:S(2)}) collective-permute-start(bf16[136,2048]{1,0:T(8,128)(2,1)S(1)} %collective-permute-done.refs_2_), channel_id=1, source_target_pairs={{0,1},{1,0},{2,3},{3,2},{4,5},{5,4},{6,7},{7,6},{8,9},{9,8},{10,11... | collective-permute-start | bytes 1671176 | tf_op jit(solution)/shard_map/ppermute | solution.py:461
  25.4 12.5 %copy-start.2 = (bf16[136,2048]{1,0:T(8,128)(2,1)}, bf16[136,2048]{1,0:T(8,128)(2,1)S(1)}, u32[]{:S(2)}) copy-start(bf16[136,2048]{1,0:T(8,128)(2,1)S(1)} %collective-permute-done.3.refs_5_) | copy-start | bytes 1671172
  25.4 66.1 %collective-permute-start.9 = (bf16[8,96,128]{2,1,0:T(8,128)(2,1)S(1)}, bf16[8,96,128]{2,1,0:T(8,128)(2,1)}, u32[]{:S(2)}, u32[]{:S(2)}) collective-permute-start(bf16[8,96,128]{2,1,0:T(8,128)(2,1)S(1)} %pad_maximum_fusion.2.refs_10_.refs_4_), channel_id=1, source_target_pairs={{0,24},{8,0},{16,8},{24,16},{1,25},{9,1},{17,9},{25,17},{2,26},{10... | collective-permute-start | bytes 589832 | tf_op jit(solution)/shard_map/ppermute | solution.py:456
  33.6 4.2 %copy-start.3 = (bf16[136,2048]{1,0:T(8,128)(2,1)}, bf16[136,2048]{1,0:T(8,128)(2,1)S(1)}, u32[]{:S(2)}) copy-start(bf16[136,2048]{1,0:T(8,128)(2,1)S(1)} %collective-permute-done.1.refs_3_) | copy-start | bytes 1671172
  33.6 13.5 %collective-permute-start.2 = (bf16[136,2048]{1,0:T(8,128)(2,1)S(1)}, bf16[136,2048]{1,0:T(8,128)(2,1)S(1)}, u32[]{:S(2)}, u32[]{:S(2)}) collective-permute-start(bf16[136,2048]{1,0:T(8,128)(2,1)S(1)} %collective-permute-done.1.refs_3_), channel_id=1, source_target_pairs={{0,4},{1,5},{2,0},{3,1},{4,6},{5,7},{6,2},{7,3},{8,12},{9,13},{10,... | collective-permute-start | bytes 1671176 | tf_op jit(solution)/shard_map/ppermute | solution.py:489
  37.8 9.3 %copy-start.4 = (bf16[136,2048]{1,0:T(8,128)(2,1)}, bf16[136,2048]{1,0:T(8,128)(2,1)S(1)}, u32[]{:S(2)}) copy-start(bf16[136,2048]{1,0:T(8,128)(2,1)S(1)} %collective-permute-done.4.refs_6_) | copy-start | bytes 1671172
  37.9 17.0 %collective-permute-start.5 = (bf16[136,2048]{1,0:T(8,128)(2,1)S(1)}, bf16[136,2048]{1,0:T(8,128)(2,1)}, u32[]{:S(2)}, u32[]{:S(2)}) collective-permute-start(bf16[136,2048]{1,0:T(8,128)(2,1)S(1)} %collective-permute-done.1.refs_3_), channel_id=1, source_target_pairs={{0,1},{1,0},{2,3},{3,2},{4,5},{5,4},{6,7},{7,6},{8,9},{9,8},{10,11... | collective-permute-start | bytes 1671176 | tf_op jit(solution)/shard_map/ppermute | solution.py:461
  47.1 7.8 %collective-permute-start.6 = (bf16[136,2048]{1,0:T(8,128)(2,1)S(1)}, bf16[136,2048]{1,0:T(8,128)(2,1)}, u32[]{:S(2)}, u32[]{:S(2)}) collective-permute-start(bf16[136,2048]{1,0:T(8,128)(2,1)S(1)} %collective-permute-done.2.refs_4_), channel_id=1, source_target_pairs={{0,1},{1,0},{2,3},{3,2},{4,5},{5,4},{6,7},{7,6},{8,9},{9,8},{10,11... | collective-permute-start | bytes 1671176 | tf_op jit(solution)/shard_map/ppermute | solution.py:461
  49.1 36.0 %all-to-all-start = ((bf16[4,2,136,512]{3,2,1,0:T(8,128)(2,1)}), bf16[4,2,136,512]{3,2,1,0:T(8,128)(2,1)}, u32[]{:S(2)}, u32[]{:S(2)}) async-start(bf16[4,2,136,512]{3,2,1,0:T(8,128)(2,1)} %pad_maximum_fusion.1), calls=%async_computation | async-start | bytes 2228224 | tf_op jit(solution)/shard_map/all_to_all | solution.py:471
  53.4 0.9 copy-start.9
  53.4 1.0 copy-start.10
  53.4 1.0 copy-start.11
  53.4 1.1 copy-start.12
  53.4 1.1 copy-start.13
  53.4 1.2 copy-start.14
  53.5 1.2 copy-start.15
  53.5 1.2 copy-start.16
  85.1 10.4 %all-to-all-start.1 = ((f32[8,8,128]{2,1,0:T(8,128)}), f32[8,8,128]{2,1,0:T(8,128)S(1)}, u32[]{:S(2)}, u32[]{:S(2)}) async-start(f32[8,8,128]{2,1,0:T(8,128)} %get-tuple-element.21), calls=%async_computation.1 | async-start | bytes 65536 | tf_op jit(solution)/shard_map/all_to_all | solution.py:536
  96.2 30.3 %all-to-all-start.3 = ((bf16[4,4,136,512]{3,2,1,0:T(8,128)(2,1)}), bf16[4,4,136,512]{3,2,1,0:T(8,128)(2,1)S(1)}, u32[]{:S(2)}, u32[]{:S(2)}) async-start(bf16[4,4,136,512]{3,2,1,0:T(8,128)(2,1)} %pad_maximum_fusion), calls=%async_computation.3 | async-start | bytes 4456448 | tf_op jit(solution)/shard_map/all_to_all | solution.py:471
  100.3 29.9 %collective-permute-start.10 = (bf16[4,2,136,512]{3,2,1,0:T(8,128)(2,1)}, bf16[4,2,136,512]{3,2,1,0:T(8,128)(2,1)}, u32[]{:S(2)}, u32[]{:S(2)}) collective-permute-start(bf16[4,2,136,512]{3,2,1,0:T(8,128)(2,1)} %all-to-all-done.refs_2_), channel_id=1, source_target_pairs={{0,1},{1,0},{2,3},{3,2},{4,5},{5,4},{6,7},{7,6},{8,9},{9,8},{10,11... | collective-permute-start | bytes 3342344 | tf_op jit(solution)/shard_map/ppermute | solution.py:461
  126.5 3.7 %copy-start.6 = (bf16[4,4,136,512]{3,2,1,0:T(8,128)(2,1)}, bf16[4,4,136,512]{3,2,1,0:T(8,128)(2,1)S(1)}, u32[]{:S(2)}) copy-start(bf16[4,4,136,512]{3,2,1,0:T(8,128)(2,1)S(1)} %all-to-all-done.3.refs_1_) | copy-start | bytes 6684676
  126.5 16.6 %all-to-all-start.2 = ((bf16[4,16,64,96]{3,2,1,0:T(8,128)(2,1)}), bf16[4,16,64,96]{3,2,1,0:T(8,128)(2,1)S(1)}, u32[]{:S(2)}, u32[]{:S(2)}) async-start(bf16[4,16,64,96]{3,2,1,0:T(8,128)(2,1)} %get-tuple-element.22), calls=%async_computation.2 | async-start | bytes 2097152 | tf_op jit(solution)/shard_map/all_to_all | solution.py:471
  140.2 3.9 %copy-start.18 = (f32[8,8,128]{2,1,0:T(8,128)S(1)}, f32[8,8,128]{2,1,0:T(8,128)}, u32[]{:S(2)}) copy-start(f32[8,8,128]{2,1,0:T(8,128)} %copy-done.17) | copy-start | bytes 98308
  (2 other events, 1.5 us)

commit v5 on v4

--- a/solution.py
+++ b/solution.py
@@ -158,8 +158,8 @@
     return lines[:top], lines[top:]
 
 
-def slot_codes(names, owners_ref, first, capacity, experts, micro):
-    shards = len(names)
+def slot_codes(names, first, capacity, experts, micro):
+    sources = len(names)
     span = names[0][0][0].shape[1]
     block = span // micro
     number = lax.broadcasted_iota(jnp.int32, (experts, span), 0).astype(jnp.float32) + first
@@ -169,7 +169,7 @@
         (from_row // block == to_row // block) & (from_row < to_row), 1.0, 0.0
     ).astype(jnp.bfloat16)
     codes, gates = [], []
-    for j in range(shards):
+    for j in range(sources):
         named = jnp.zeros((experts, span), jnp.float32)
         gate = jnp.zeros((experts, span), jnp.float32)
         for name, weight in zip(*names[j]):
@@ -177,14 +177,50 @@
             named = jnp.where(hit, 1.0, named)
             gate = jnp.where(hit, weight, gate)
         before = jnp.dot(named.astype(jnp.bfloat16), earlier, preferred_element_type=jnp.float32)
-        offset = (owners_ref[j] * capacity).astype(jnp.float32)
-        codes.append(jnp.where(named > 0.0, before + offset, -1.0))
+        codes.append(jnp.where(named > 0.0, before + float(j * capacity), -1.0))
         gates.append(gate)
-    parts = [slice(m * block, (m + 1) * block) for m in range(micro)]
-    return (
-        [jnp.concatenate([c[:, part] for c in codes], axis=1) for part in parts],
-        [jnp.concatenate([g[:, part] for g in gates], axis=1) for part in parts],
-    )
+
+    def arrange(values):
+        half = sources // 2
+        return [
+            [
+                jnp.concatenate(
+                    [c[:, m * block : (m + 1) * block] for c in values[h * half : (h + 1) * half]],
+                    axis=1,
+                )
+                for h in range(2)
+            ]
+            for m in range(micro)
+        ]
+
+    return arrange(codes), arrange(gates)
+
+
+def slot_windows(slots):
+    half = slots // 2
+    return [(h * half // 8 * 8, -(-(h + 1) * half // 8) * 8) for h in range(2)]
+
+
+def slot_iota(window, lanes):
+    shape = (window[1] - window[0], lanes)
+    return lax.broadcasted_iota(jnp.int32, shape, 0).astype(jnp.float32) + float(window[0])
+
+
+def join_windows(first_part, second_part, windows, padded, axis):
+    (_, end), (start, last) = windows
+
+    def rows(values, low, high):
+        return lax.slice_in_dim(values, low, high, axis=axis)
+
+    parts = [rows(first_part, 0, start)]
+    if end > start:
+        parts.append(rows(first_part, start, end) + rows(second_part, 0, end - start))
+    parts.append(rows(second_part, end - start, last - start))
+    if padded > last:
+        shape = list(first_part.shape)
+        shape[axis] = padded - last
+        parts.append(jnp.zeros(shape, first_part.dtype))
+    return jnp.concatenate(parts, axis=axis)
 
 
 contract_last = (((1,), (1,)), ((), ()))
@@ -195,8 +231,11 @@
     owners_ref = refs[0]
     token_refs = refs[1 : 1 + shards]
     hidden_ref, u_ref, weight_hbm, amap_ref, bmap_hbm = refs[1 + shards : 6 + shards]
-    hg_ref, rk_ref, la_ref = refs[6 + shards : 9 + shards]
-    dy_s, wb_s, rows_s, y_s, code_s, gate_s, back_s, dy_sem, w_sem, b_sem = refs[9 + shards :]
+    hg_ref, rk_ref = refs[6 + shards : 8 + shards]
+    la_outs = refs[8 + shards : 8 + shards + group_count]
+    scratch = refs[8 + shards + group_count :]
+    dy_s, wb_s, rows_s, y_s, code_s, gate_s, back_s, la_s = scratch[:8]
+    dy_sem, w_sem, b_sem, la_sem = scratch[8:]
     top, span = rk_ref.shape[1:]
     micro, experts, slots, units = hidden_ref.shape
     rank = amap_ref.shape[1]
@@ -206,7 +245,7 @@
     first = (lax.axis_index("expert") * experts).astype(jnp.float32)
 
     token_copies = [
-        pltpu.make_async_copy(token_refs[i], dy_s.at[i], dy_sem.at[i])
+        pltpu.make_async_copy(token_refs[i], dy_s.at[owners_ref[i]], dy_sem.at[i])
         for i in range(shards)
     ]
     for copy in token_copies:
@@ -227,31 +266,48 @@
     names = [
         read_names(dy_s[i, span:, : width // group_count], span, top) for i in range(shards)
     ]
-    codes, gates = slot_codes(names, owners_ref, first, capacity, experts, micro)
-    slot_of = lax.broadcasted_iota(jnp.int32, (padded, shards * block), 0).astype(jnp.float32)
+    codes, gates = slot_codes(names, first, capacity, experts, micro)
+    windows = slot_windows(slots)
+    lanes_of = shards // 2 * block
+    slot_of = [slot_iota(window, lanes_of) for window in windows]
     picks = []
     for m in range(micro):
-        code_s[m] = codes[m]
-        chosen = []
+        chosen = [[], []]
+        for h in range(2):
+            code_s[m, h] = codes[m][h]
         for x in range(experts):
-            hit = codes[m][x : x + 1, :] == slot_of
-            chosen.append(jnp.where(hit, 1.0, 0.0).astype(jnp.bfloat16))
-            gate_s[x, m * padded : (m + 1) * padded, :] = jnp.sum(
-                jnp.where(hit, gates[m][x : x + 1, :], 0.0), axis=1, keepdims=True
+            sums = []
+            for h in range(2):
+                hit = codes[m][h][x : x + 1, :] == slot_of[h]
+                chosen[h].append(jnp.where(hit, 1.0, 0.0))
+                sums.append(
+                    jnp.sum(
+                        jnp.where(hit, gates[m][h][x : x + 1, :], 0.0), axis=1, keepdims=True
+                    )
+                )
+            gate_s[x, m * padded : (m + 1) * padded, :] = join_windows(
+                sums[0], sums[1], windows, padded, 0
             )
-        picks.append(jnp.concatenate(chosen, axis=0))
+        picks.append([jnp.concatenate(c, axis=0).astype(jnp.bfloat16) for c in chosen])
 
     tile = 512 if width % 512 == 0 else width
     for m in range(micro):
         for n in range(width // tile):
             cols = slice(n * tile, (n + 1) * tile)
-            tokens = jnp.concatenate(
-                [dy_s[i, m * block : (m + 1) * block, cols] for i in range(shards)], axis=0
-            )
-            rows = jnp.dot(picks[m], tokens, preferred_element_type=jnp.float32)
-            rows_s[:, m * padded : (m + 1) * padded, cols] = rows.astype(jnp.bfloat16).reshape(
-                experts, padded, tile
-            )
+            parts = []
+            for h in range(2):
+                tokens = jnp.concatenate(
+                    [
+                        dy_s[j, m * block : (m + 1) * block, cols]
+                        for j in range(h * shards // 2, (h + 1) * shards // 2)
+                    ],
+                    axis=0,
+                )
+                rows = jnp.dot(picks[m][h], tokens, preferred_element_type=jnp.float32)
+                parts.append(rows.reshape(experts, -1, tile))
+            rows_s[:, m * padded : (m + 1) * padded, cols] = join_windows(
+                parts[0], parts[1], windows, padded, 1
+            ).astype(jnp.bfloat16)
 
     half = experts // 2
 
@@ -316,40 +372,52 @@
         for x, grad, la, back in zip(xs, grads, las, routed):
             for m in range(micro):
                 hg_ref[m, x] = grad[m * padded : m * padded + slots]
-                hit = code_s[m, pl.ds(x, 1), :] == slot_of
-                back_s[m, pl.ds(x, 1), :] = jnp.sum(
-                    jnp.where(hit, back[m * padded : (m + 1) * padded], 0.0),
-                    axis=0,
-                    keepdims=True,
-                )
+                for h, (low, high) in enumerate(windows):
+                    hit = code_s[m, h, pl.ds(x, 1), :] == slot_of[h]
+                    rows = back[m * padded + low : m * padded + high]
+                    back_s[m, h, pl.ds(x, 1), :] = jnp.sum(
+                        jnp.where(hit, rows, 0.0), axis=0, keepdims=True
+                    )
             for k in range(group_count):
-                la_ref[k, x] = (adapter_scale * la[:, k * share : (k + 1) * share]).astype(
-                    la_ref.dtype
+                la_s[k, x] = (adapter_scale * la[:, k * share : (k + 1) * share]).astype(
+                    la_s.dtype
                 )
         return carry
 
     lax.fori_loop(0, half // batch, small_steps, 0)
 
+    group = lax.axis_index("dp")
+    la_copies = [
+        pltpu.make_async_copy(
+            la_s.at[lax.rem(group + s, group_count)], la_outs[s], la_sem.at[s]
+        )
+        for s in range(group_count)
+    ]
+    for copy in la_copies:
+        copy.start()
     number = lax.broadcasted_iota(jnp.int32, (experts, span), 0).astype(jnp.float32) + first
-    for i in range(shards):
+    for j in range(shards):
+        h, k = j // (shards // 2), j % (shards // 2)
         back = jnp.concatenate(
-            [back_s[m, :, i * block : (i + 1) * block] for m in range(micro)], axis=1
+            [back_s[m, h, :, k * block : (k + 1) * block] for m in range(micro)], axis=1
         )
         found = [
-            jnp.sum(
-                jnp.where(name == number, back, 0.0), axis=0, keepdims=True
-            )
-            for name in names[i][0]
-        ]
-        rk_ref[owners_ref[i]] = jnp.concatenate(found, axis=0)
+            jnp.sum(jnp.where(name == number, back, 0.0), axis=0, keepdims=True)
+            for name in names[j][0]
+        ]
+        rk_ref[j] = jnp.concatenate(found, axis=0)
+    for copy in la_copies:
+        copy.wait()
 
 
 def adapter_kernel(capacity, micro, span, top, group_count, shards, *refs):
     pairs = shards // 2
     early = pairs // 2
-    owners_ref, early_ref, late_ref, swapped_ref = refs[:4]
-    u_refs = refs[4 : 4 + group_count]
-    lb_ref, tok_s, q_s, sem = refs[4 + group_count :]
+    owners_ref = refs[0]
+    early_refs = refs[1 : 1 + early]
+    late_ref, swapped_ref = refs[1 + early : 3 + early]
+    u_refs = refs[3 + early : 3 + early + group_count]
+    lb_ref, tok_s, q_s, sem = refs[3 + early + group_count :]
     experts, rank, share = lb_ref.shape
     tall = u_refs[0].shape[1]
     padded = tall // micro
@@ -362,34 +430,46 @@
         for i in range(shards):
             far, k = i // pairs, i % pairs
             if k < early:
-                source = early_ref.at[home, far * early + k]
+                source = early_refs[k].at[home, far]
             else:
                 source = (swapped_ref if far else late_ref).at[home, k - early]
-            copies.append(pltpu.make_async_copy(source, tok_s.at[g, i], sem.at[g, i]))
+            copies.append(pltpu.make_async_copy(source, tok_s.at[g, owners_ref[i]], sem.at[g, i]))
     for copy in copies:
         copy.start()
-    slot_of = lax.broadcasted_iota(jnp.int32, (padded, shards * block), 0).astype(jnp.float32)
+    slots = capacity * shards
+    windows = slot_windows(slots)
+    slot_of = [slot_iota(window, shards // 2 * block) for window in windows]
     for g in range(group_count):
         for i in range(shards):
             copies[g * shards + i].wait()
         names = [read_names(tok_s[g, i, span:, :], span, top) for i in range(shards)]
-        codes, gates = slot_codes(names, owners_ref, first, capacity, experts, micro)
+        codes, gates = slot_codes(names, first, capacity, experts, micro)
         for m in range(micro):
-            picks = jnp.concatenate(
-                [
-                    jnp.where(
-                        codes[m][x : x + 1, :] == slot_of, gates[m][x : x + 1, :], 0.0
-                    ).astype(jnp.bfloat16)
-                    for x in range(experts)
-                ],
-                axis=0,
-            )
-            tokens = jnp.concatenate(
-                [tok_s[g, i, m * block : (m + 1) * block, :] for i in range(shards)], axis=0
-            )
-            q = jnp.dot(picks, tokens, preferred_element_type=jnp.float32).astype(jnp.bfloat16)
+            parts = []
+            for h in range(2):
+                picks = jnp.concatenate(
+                    [
+                        jnp.where(
+                            codes[m][h][x : x + 1, :] == slot_of[h],
+                            gates[m][h][x : x + 1, :],
+                            0.0,
+                        )
+                        for x in range(experts)
+                    ],
+                    axis=0,
+                ).astype(jnp.bfloat16)
+                tokens = jnp.concatenate(
+                    [
+                        tok_s[g, j, m * block : (m + 1) * block, :]
+                        for j in range(h * shards // 2, (h + 1) * shards // 2)
+                    ],
+                    axis=0,
+                )
+                rows = jnp.dot(picks, tokens, preferred_element_type=jnp.float32)
+                parts.append(rows.reshape(experts, -1, share))
+            q = join_windows(parts[0], parts[1], windows, padded, 1).astype(jnp.bfloat16)
             at = g * tall + m * padded
-            q_s[:, at : at + padded, :] = q.reshape(experts, padded, share)
+            q_s[:, at : at + padded, :] = q
     half = experts // 2
     for x in range(half):
         both = jnp.concatenate([u_refs[g][x] for g in range(group_count)], axis=0)
@@ -471,8 +551,6 @@
         return lax.all_to_all(array, "dp", split_axis=0, concat_axis=0, tiled=True)
 
     others = range(1, group_count)
-    u_all = [u] + [shift_groups(u, s) for s in others]
-
     names = jnp.concatenate(
         [chosen_expert_index.T.astype(jnp.bfloat16), routing_gate_weight.T], axis=0
     )
@@ -488,38 +566,46 @@
     for step in range(pairs - 1):
         near.append(lax.ppermute(near[-1], "expert", ring))
         far.append(swap_partners(near[step]))
-    early_columns = exchange_columns(near[:early] + far[:early])
-    early_columns, *u_all = lax.optimization_barrier((early_columns, *u_all))
-    early_columns = across_groups(early_columns)
-    late_columns = across_groups(exchange_columns(near[early:]))
+    early_columns = []
+    for k in range(early):
+        columns = exchange_columns([near[k], far[k]])
+        if early_columns:
+            columns, early_columns[-1] = lax.optimization_barrier((columns, early_columns[-1]))
+        early_columns.append(across_groups(columns))
+    u, early_columns[-1] = lax.optimization_barrier((u, early_columns[-1]))
+    u_all = [u] + [shift_groups(u, s) for s in others]
+    late_columns = exchange_columns(near[early:])
+    late_columns, u_all = lax.optimization_barrier((late_columns, u_all))
+    late_columns = across_groups(late_columns)
     far.append(swap_partners(near[-1]))
     pieces = near + far
 
     vmem = pl.BlockSpec(memory_space=pltpu.VMEM)
     smem = pl.BlockSpec(memory_space=pltpu.SMEM)
     anywhere = pl.BlockSpec(memory_space=pl.ANY)
-    hidden_grad, routed, part_a = pl.pallas_call(
+    part_a = jax.ShapeDtypeStruct((experts, rank, units // group_count), jnp.bfloat16)
+    hidden_grad, routed, *parts = pl.pallas_call(
         functools.partial(expert_kernel, capacity, group_count, sources),
         out_shape=(
             jax.ShapeDtypeStruct(hidden.shape, jnp.bfloat16),
             jax.ShapeDtypeStruct((sources, top, span), jnp.float32),
-            jax.ShapeDtypeStruct(
-                (group_count, experts, rank, units // group_count), jnp.bfloat16
-            ),
-        ),
+        )
+        + (part_a,) * group_count,
         in_specs=[smem] + [anywhere] * sources + [vmem, vmem, anywhere, vmem, anywhere],
-        out_specs=(vmem,) * 3,
+        out_specs=(vmem,) * 2 + (anywhere,) * group_count,
         scratch_shapes=[
             pltpu.VMEM((sources, span + extra, width), jnp.bfloat16),
             pltpu.VMEM((experts, units + rank, width), jnp.bfloat16),
             pltpu.VMEM((experts, micro * padded, width), jnp.bfloat16),
             pltpu.VMEM((experts, micro * padded, units + rank), jnp.float32),
-            pltpu.VMEM((micro, experts, sources * block), jnp.float32),
+            pltpu.VMEM((micro, 2, experts, sources // 2 * block), jnp.float32),
             pltpu.VMEM((experts, micro * padded, 1), jnp.float32),
-            pltpu.VMEM((micro, experts, sources * block), jnp.float32),
+            pltpu.VMEM((micro, 2, experts, sources // 2 * block), jnp.float32),
+            pltpu.VMEM((group_count, experts, rank, units // group_count), jnp.bfloat16),
             pltpu.SemaphoreType.DMA((sources,)),
             pltpu.SemaphoreType.DMA((experts,)),
             pltpu.SemaphoreType.DMA((experts,)),
+            pltpu.SemaphoreType.DMA((group_count,)),
         ],
         compiler_params=pltpu.CompilerParams(vmem_limit_bytes=58 * 1024 * 1024),
         cost_estimate=pl.CostEstimate(
@@ -530,15 +616,15 @@
         name="expert_rows",
     )(owners, *pieces, hidden, u, frozen_down_weight, amap, adapter_output_map)
 
-    late_columns, part_a, routed = lax.optimization_barrier((late_columns, part_a, routed))
+    late_columns, parts, routed = lax.optimization_barrier((late_columns, parts, routed))
     swapped = swap_partners(late_columns)
-    arrived = across_groups(part_a)
+    arrived = [shift_groups(parts[s], s) for s in others]
     home = lax.all_to_all(routed, "expert", split_axis=0, concat_axis=0, tiled=True)
 
     lora_b = pl.pallas_call(
         functools.partial(adapter_kernel, capacity, micro, span, top, group_count, sources),
         out_shape=jax.ShapeDtypeStruct((experts, rank, share), jnp.float32),
-        in_specs=[smem] + [anywhere] * 3 + [vmem] * group_count,
+        in_specs=[smem] + [anywhere] * (early + 2) + [vmem] * group_count,
         out_specs=vmem,
         scratch_shapes=[
             pltpu.VMEM((group_count, sources, span + extra, share), jnp.bfloat16),
@@ -552,11 +638,13 @@
             transcendentals=0,
         ),
         name="adapter_columns",
-    )(owners, early_columns, late_columns, swapped, *u_all)
+    )(owners, *early_columns, late_columns, swapped, *u_all)
 
     home, arrived, lora_b = lax.optimization_barrier((home, arrived, lora_b))
     router_grad = jnp.sum(home, axis=0).T
-    lora_a = jnp.sum(arrived.astype(jnp.float32), axis=0)
+    lora_a = parts[0].astype(jnp.float32)
+    for part in arrived:
+        lora_a = lora_a + part.astype(jnp.float32)
     return (hidden_grad, router_grad, lora_a, lora_b)
 
 

time: 145 us -> 129 us (0.89)
  waiting for transfers between devices: 54.2 us -> 41.5 us
  Pallas kernels: 40.2 us -> 37.6 us
  starting transfers between devices: 33.3 us -> 35.5 us
  local copies, waits for them, and re-layouts: 6.99 us -> 4.85 us
    all_to_all x3, waiting for transfers between devices: 29 us -> 18.5 us  [across_groups(): return lax.all_to_all(array, 'dp', split_axis=0, concat_axis=0, tiled=True)]
    ppermute x3 -> x6, waiting for transfers between devices: 0.01 us -> 7 us  [shift_groups(): lax.ppermute(array, 'dp', [(d, (d + by) % group_count) for d in range(gro...]
    ppermute x3, waiting for transfers between devices: 21.1 us -> 16 us  [local_by_tokens(): near.append(lax.ppermute(near[-1], 'expert', ring))]
    all_to_all x1, waiting for transfers between devices: 4.08 us -> 0.01 us  [local_by_tokens(): lax.all_to_all(routed, 'expert', split_axis=0, concat_axis=0, tiled=True)]
    ppermute x3 -> x6, starting transfers between devices: 5.56 us -> 9.27 us  [shift_groups(): lax.ppermute(array, 'dp', [(d, (d + by) % group_count) for d in range(gro...]
    another operation x6, local copies, waits for them, and re-layouts: 3.2 us -> 0.23 us  [exchange_columns(): jnp.stack([piece[:, g * share:(g + 1) * share] for piece in chosen])]
    pallas_call x1, Pallas kernels: 9.96 us -> 8.37 us  [local_by_tokens(): pl.pallas_call(functools.partial(adapter_kernel, capacity, micro, span, t...]
    unnamed x40 -> x32, local copies, waits for them, and re-layouts: 2.5 us -> 3.33 us
  transfers between devices with their start and end apart: 15 -> 18, of which waited for: 6 -> 8; matrix products, arithmetic and copies ran while one was open for 6% -> 5% of each run, Pallas kernels for 28% -> 29%
where the time goes in v5:
time: 129 us
  waiting for transfers between devices  41.5 us (32%)
  Pallas kernels  37.6 us (29%)
  starting transfers between devices  35.5 us (28%)
  other arithmetic  7.98 us (6%)
  local copies, waits for them, and re-layouts  4.85 us (4%)
    pallas_call x1, Pallas kernels, local_by_tokens(): pl.pallas_call(functools.partial(expert_kernel, capacity, group_count, so...  29.2 us
    all_to_all x3, waiting for transfers between devices, across_groups(): return lax.all_to_all(array, 'dp', split_axis=0, concat_axis=0, tiled=True)  18.5 us
    ppermute x3, waiting for transfers between devices, local_by_tokens(): near.append(lax.ppermute(near[-1], 'expert', ring))  16 us
    all_to_all x3, starting transfers between devices, across_groups(): return lax.all_to_all(array, 'dp', split_axis=0, concat_axis=0, tiled=True)  11.3 us
    ppermute x3, starting transfers between devices, local_by_tokens(): near.append(lax.ppermute(near[-1], 'expert', ring))  10.8 us
    ppermute x6, starting transfers between devices, shift_groups(): lax.ppermute(array, 'dp', [(d, (d + by) % group_count) for d in range(gro...  9.27 us
    pallas_call x1, Pallas kernels, local_by_tokens(): pl.pallas_call(functools.partial(adapter_kernel, capacity, micro, span, t...  8.37 us
    ppermute x6, waiting for transfers between devices, shift_groups(): lax.ppermute(array, 'dp', [(d, (d + by) % group_count) for d in range(gro...  7 us
  transfers between devices with their start and end apart: 18, of which 8 were waited for; matrix products, arithmetic and copies ran while one was open for 5% of the time, Pallas kernels for 29%

profile of v5, /device:TPU:0, one launch (start us, length us, event | category | flops | bytes accessed | tf_op | source)
XLA Modules:
  0.0 128.9 jit_solution(15891561678913581237)
XLA Ops:
  0.6 0.7 convert_bitcast_fusion
  1.3 0.7 pad_maximum_fusion.4
  2.1 1.2 fusion.3.refs_1_
  3.3 4.1 %collective-permute-start = (bf16[136,2048]{1,0:T(8,128)(2,1)S(1)}, bf16[136,2048]{1,0:T(8,128)(2,1)S(1)}, u32[]{:S(2)}, u32[]{:S(2)}) collective-permute-start(bf16[136,2048]{1,0:T(8,128)(2,1)S(1)} %fusion.3.refs_1_), channel_id=1, source_target_pairs={{0,4},{1,5},{2,0},{3,1},{4,6},{5,7},{6,2},{7,3},{8,12},{9,13},{10,... | collective-permute-start | bytes 1671176 | tf_op jit(solution)/shard_map/ppermute | solution.py:567
  8.0 11.3 %collective-permute-done.refs_2_ = bf16[136,2048]{1,0:T(8,128)(2,1)S(1)} collective-permute-done((bf16[136,2048]{1,0:T(8,128)(2,1)S(1)}, bf16[136,2048]{1,0:T(8,128)(2,1)S(1)}, u32[]{:S(2)}, u32[]{:S(2)}) %collective-permute-start) | collective-permute-done | bytes 557088 | tf_op jit(solution)/shard_map/ppermute | solution.py:567
  19.3 3.4 %collective-permute-start.1 = (bf16[136,2048]{1,0:T(8,128)(2,1)S(1)}, bf16[136,2048]{1,0:T(8,128)(2,1)S(1)}, u32[]{:S(2)}, u32[]{:S(2)}) collective-permute-start(bf16[136,2048]{1,0:T(8,128)(2,1)S(1)} %collective-permute-done.refs_2_), channel_id=1, source_target_pairs={{0,4},{1,5},{2,0},{3,1},{4,6},{5,7},{6,2},{7,3},{8,12},{9,13},{10,... | collective-permute-start | bytes 1671176 | tf_op jit(solution)/shard_map/ppermute | solution.py:567
  22.8 0.7 copy-done.2
  23.5 1.1 pad_maximum_fusion.1
  24.7 4.3 %all-to-all-start = ((bf16[4,2,136,512]{3,2,1,0:T(8,128)(2,1)}), bf16[4,2,136,512]{3,2,1,0:T(8,128)(2,1)}, u32[]{:S(2)}, u32[]{:S(2)}) async-start(bf16[4,2,136,512]{3,2,1,0:T(8,128)(2,1)} %pad_maximum_fusion.1), calls=%async_computation | async-start | bytes 2228224 | tf_op jit(solution)/shard_map/all_to_all | solution.py:551
  29.0 4.7 %collective-permute-done.1.refs_3_ = bf16[136,2048]{1,0:T(8,128)(2,1)S(1)} collective-permute-done((bf16[136,2048]{1,0:T(8,128)(2,1)S(1)}, bf16[136,2048]{1,0:T(8,128)(2,1)S(1)}, u32[]{:S(2)}, u32[]{:S(2)}) %collective-permute-start.1) | collective-permute-done | bytes 557088 | tf_op jit(solution)/shard_map/ppermute | solution.py:567
  33.7 3.4 %collective-permute-start.2 = (bf16[136,2048]{1,0:T(8,128)(2,1)S(1)}, bf16[136,2048]{1,0:T(8,128)(2,1)S(1)}, u32[]{:S(2)}, u32[]{:S(2)}) collective-permute-start(bf16[136,2048]{1,0:T(8,128)(2,1)S(1)} %collective-permute-done.1.refs_3_), channel_id=1, source_target_pairs={{0,4},{1,5},{2,0},{3,1},{4,6},{5,7},{6,2},{7,3},{8,12},{9,13},{10,... | collective-permute-start | bytes 1671176 | tf_op jit(solution)/shard_map/ppermute | solution.py:567
  37.2 0.7 copy-done.4
  37.9 1.1 pad_maximum_fusion
  39.1 5.2 %all-to-all-done.refs_1_ = bf16[4,2,136,512]{3,2,1,0:T(8,128)(2,1)} async-done(((bf16[4,2,136,512]{3,2,1,0:T(8,128)(2,1)}), bf16[4,2,136,512]{3,2,1,0:T(8,128)(2,1)}, u32[]{:S(2)}, u32[]{:S(2)}) %all-to-all-start) | async-done | bytes 1114144 | tf_op jit(solution)/shard_map/all_to_all | solution.py:551
  44.3 3.5 %all-to-all-start.1 = ((bf16[4,2,136,512]{3,2,1,0:T(8,128)(2,1)}), bf16[4,2,136,512]{3,2,1,0:T(8,128)(2,1)S(1)}, u32[]{:S(2)}, u32[]{:S(2)}) async-start(bf16[4,2,136,512]{3,2,1,0:T(8,128)(2,1)} %pad_maximum_fusion), calls=%async_computation.1 | async-start | bytes 2228224 | tf_op jit(solution)/shard_map/all_to_all | solution.py:551
  49.0 13.3 %all-to-all-done.1.refs_2_ = bf16[4,2,136,512]{3,2,1,0:T(8,128)(2,1)S(1)} async-done(((bf16[4,2,136,512]{3,2,1,0:T(8,128)(2,1)}), bf16[4,2,136,512]{3,2,1,0:T(8,128)(2,1)S(1)}, u32[]{:S(2)}, u32[]{:S(2)}) %all-to-all-start.1) | async-done | bytes 1114144 | tf_op jit(solution)/shard_map/all_to_all | solution.py:551
  62.3 1.4 %collective-permute-start.7 = (bf16[8,96,128]{2,1,0:T(8,128)(2,1)S(1)}, bf16[8,96,128]{2,1,0:T(8,128)(2,1)S(1)}, u32[]{:S(2)}, u32[]{:S(2)}) collective-permute-start(bf16[8,96,128]{2,1,0:T(8,128)(2,1)S(1)} %pad_maximum_fusion.3.refs_10_.refs_5_), channel_id=1, source_target_pairs={{0,8},{8,16},{16,24},{24,0},{1,9},{9,17},{17,25},{25,1},{2,10},{10... | collective-permute-start | bytes 589832 | tf_op jit(solution)/shard_map/ppermute | solution.py:536
  64.3 2.4 %collective-permute-start.9 = (bf16[8,96,128]{2,1,0:T(8,128)(2,1)S(1)}, bf16[8,96,128]{2,1,0:T(8,128)(2,1)}, u32[]{:S(2)}, u32[]{:S(2)}) collective-permute-start(bf16[8,96,128]{2,1,0:T(8,128)(2,1)S(1)} %pad_maximum_fusion.3.refs_10_.refs_5_), channel_id=1, source_target_pairs={{0,24},{8,0},{16,8},{24,16},{1,25},{9,1},{17,9},{25,17},{2,26},{10... | collective-permute-start | bytes 589832 | tf_op jit(solution)/shard_map/ppermute | solution.py:536
  66.7 1.1 pad_maximum_fusion.2
  67.9 3.2 %collective-permute-done.7.refs_6_ = bf16[8,96,128]{2,1,0:T(8,128)(2,1)S(1)} collective-permute-done((bf16[8,96,128]{2,1,0:T(8,128)(2,1)S(1)}, bf16[8,96,128]{2,1,0:T(8,128)(2,1)S(1)}, u32[]{:S(2)}, u32[]{:S(2)}) %collective-permute-start.7) | collective-permute-done | bytes 196640 | tf_op jit(solution)/shard_map/ppermute | solution.py:536
  71.0 2.2 %collective-permute-done.8.refs_7_ = bf16[8,96,128]{2,1,0:T(8,128)(2,1)S(1)} collective-permute-done((bf16[8,96,128]{2,1,0:T(8,128)(2,1)S(1)}, bf16[8,96,128]{2,1,0:T(8,128)(2,1)S(1)}, u32[]{:S(2)}, u32[]{:S(2)}) %collective-permute-start.8) | collective-permute-done | bytes 196640 | tf_op jit(solution)/shard_map/ppermute | solution.py:536
  73.9 3.5 %all-to-all-start.2 = ((bf16[4,2,136,512]{3,2,1,0:T(8,128)(2,1)}), bf16[4,2,136,512]{3,2,1,0:T(8,128)(2,1)S(1)}, u32[]{:S(2)}, u32[]{:S(2)}) async-start(bf16[4,2,136,512]{3,2,1,0:T(8,128)(2,1)} %pad_maximum_fusion.2), calls=%async_computation.2 | async-start | bytes 2228224 | tf_op jit(solution)/shard_map/all_to_all | solution.py:551
  77.4 1.2 dynamic-slice_bitcast_fusion.refs_0_
  78.7 29.2 %expert_rows.1 = (bf16[2,16,40,384]{3,2,1,0:T(8,128)(2,1)}, f32[8,8,128]{2,1,0:T(8,128)}, bf16[16,64,96]{2,1,0:T(8,128)(2,1)}, bf16[16,64,96]{2,1,0:T(8,128)(2,1...) custom-call(s32[8]{0:T(128)} %dynamic-slice_bitcast_fusion.refs_0_, bf16[136,2048]{1,0:T(8,128)(2,1)} %copy-done, ...), custom_call_target="tpu_custom_call" | custom-call | flops 6039797760 | bytes 33554432 | tf_op jit(solution)/shard_map/expert_rows/pallas_call | solution.py:587
  108.1 3.3 %all-to-all-start.3 = ((f32[8,8,128]{2,1,0:T(8,128)}), f32[8,8,128]{2,1,0:T(8,128)S(1)}, u32[]{:S(2)}, u32[]{:S(2)}) async-start(f32[8,8,128]{2,1,0:T(8,128)} %get-tuple-element.39), calls=%async_computation.3 | async-start | bytes 65536 | tf_op jit(solution)/shard_map/all_to_all | solution.py:622
  111.4 2.0 %collective-permute-start.10 = (bf16[16,64,96]{2,1,0:T(8,128)(2,1)}, bf16[16,64,96]{2,1,0:T(8,128)(2,1)S(1)}, u32[]{:S(2)}, u32[]{:S(2)}) collective-permute-start(bf16[16,64,96]{2,1,0:T(8,128)(2,1)} %get-tuple-element.40), channel_id=1, source_target_pairs={{0,8},{8,16},{16,24},{24,0},{1,9},{9,17},{17,25},{25,1},{2,10},{10... | collective-permute-start | bytes 589832 | tf_op jit(solution)/shard_map/ppermute | solution.py:536
  113.4 1.5 %collective-permute-start.11 = (bf16[16,64,96]{2,1,0:T(8,128)(2,1)}, bf16[16,64,96]{2,1,0:T(8,128)(2,1)S(1)}, u32[]{:S(2)}, u32[]{:S(2)}) collective-permute-start(bf16[16,64,96]{2,1,0:T(8,128)(2,1)} %get-tuple-element.41), channel_id=1, source_target_pairs={{0,16},{8,24},{16,0},{24,8},{1,17},{9,25},{17,1},{25,9},{2,18},{10... | collective-permute-start | bytes 589832 | tf_op jit(solution)/shard_map/ppermute | solution.py:536
  114.8 1.5 %collective-permute-start.12 = (bf16[16,64,96]{2,1,0:T(8,128)(2,1)}, bf16[16,64,96]{2,1,0:T(8,128)(2,1)S(1)}, u32[]{:S(2)}, u32[]{:S(2)}) collective-permute-start(bf16[16,64,96]{2,1,0:T(8,128)(2,1)} %get-tuple-element.42), channel_id=1, source_target_pairs={{0,24},{8,0},{16,8},{24,16},{1,25},{9,1},{17,9},{25,17},{2,26},{10... | collective-permute-start | bytes 589832 | tf_op jit(solution)/shard_map/ppermute | solution.py:536
  116.3 1.0 copy-done.12
  117.3 8.4 %adapter_columns.1 = f32[16,64,512]{2,1,0:T(8,128)} custom-call(s32[8]{0:T(128)} %dynamic-slice_bitcast_fusion.refs_0_, bf16[4,2,136,512]{3,2,1,0:T(8,128)(2,1)} %all-to-all-done.refs_1_, bf16[4,2,136,512]{3,2,1,0:T(8,128)(2,1)} %copy-done.6, bf16[4,2,136,512]{3,2,1,0:T(8,128)(2,1)} %copy-done.7, bf16[4,2,136,512]{3,2,1,0:T(8,128)(2,1)} %copy-done.12, ...), custom_call_target="tpu_custom_call" | custom-call | flops 3623878656 | bytes 6291456 | tf_op jit(solution)/shard_map/adapter_columns/pallas_call | solution.py:624
  125.7 1.3 %collective-permute-done.11 = bf16[16,64,96]{2,1,0:T(8,128)(2,1)S(1)} collective-permute-done((bf16[16,64,96]{2,1,0:T(8,128)(2,1)}, bf16[16,64,96]{2,1,0:T(8,128)(2,1)S(1)}, u32[]{:S(2)}, u32[]{:S(2)}) %collective-permute-start.11) | collective-permute-done | bytes 196640 | tf_op jit(solution)/shard_map/ppermute | solution.py:536
  127.9 1.0 convert_add_fusion
  (63 shorter events, 4.5 us)
Async XLA Ops:
  2.0 5.4 %copy-start.8 = (bf16[2,16,40,384]{3,2,1,0:T(8,128)(2,1)S(1)}, bf16[2,16,40,384]{3,2,1,0:T(8,128)(2,1)}, u32[]{:S(2)}) copy-start(bf16[2,16,40,384]{3,2,1,0:T(8,128)(2,1)} %refs_9_.1) | copy-start | bytes 2949124
  2.1 5.4 %copy-start.10 = (bf16[16,384,64]{1,2,0:T(8,128)(2,1)S(1)}, bf16[16,384,64]{1,2,0:T(8,128)(2,1)}, u32[]{:S(2)}) copy-start(bf16[16,384,64]{1,2,0:T(8,128)(2,1)} %param.13) | copy-start | bytes 2359300
  3.3 4.7 %copy-start = (bf16[136,2048]{1,0:T(8,128)(2,1)}, bf16[136,2048]{1,0:T(8,128)(2,1)S(1)}, u32[]{:S(2)}) copy-start(bf16[136,2048]{1,0:T(8,128)(2,1)S(1)} %fusion.3.refs_1_) | copy-start | bytes 1671172
  3.3 16.0 %collective-permute-start = (bf16[136,2048]{1,0:T(8,128)(2,1)S(1)}, bf16[136,2048]{1,0:T(8,128)(2,1)S(1)}, u32[]{:S(2)}, u32[]{:S(2)}) collective-permute-start(bf16[136,2048]{1,0:T(8,128)(2,1)S(1)} %fusion.3.refs_1_), channel_id=1, source_target_pairs={{0,4},{1,5},{2,0},{3,1},{4,6},{5,7},{6,2},{7,3},{8,12},{9,13},{10,... | collective-permute-start | bytes 1671176 | tf_op jit(solution)/shard_map/ppermute | solution.py:567
  7.4 15.3 %collective-permute-start.3 = (bf16[136,2048]{1,0:T(8,128)(2,1)S(1)}, bf16[136,2048]{1,0:T(8,128)(2,1)S(1)}, u32[]{:S(2)}, u32[]{:S(2)}) collective-permute-start(bf16[136,2048]{1,0:T(8,128)(2,1)S(1)} %fusion.3.refs_1_), channel_id=1, source_target_pairs={{0,1},{1,0},{2,3},{3,2},{4,5},{5,4},{6,7},{7,6},{8,9},{9,8},{10,11... | collective-permute-start | bytes 1671176 | tf_op jit(solution)/shard_map/ppermute | solution.py:541
  19.3 9.7 %copy-start.1 = (bf16[136,2048]{1,0:T(8,128)(2,1)}, bf16[136,2048]{1,0:T(8,128)(2,1)S(1)}, u32[]{:S(2)}) copy-start(bf16[136,2048]{1,0:T(8,128)(2,1)S(1)} %collective-permute-done.refs_2_) | copy-start | bytes 1671172
  19.3 14.4 %collective-permute-start.1 = (bf16[136,2048]{1,0:T(8,128)(2,1)S(1)}, bf16[136,2048]{1,0:T(8,128)(2,1)S(1)}, u32[]{:S(2)}, u32[]{:S(2)}) collective-permute-start(bf16[136,2048]{1,0:T(8,128)(2,1)S(1)} %collective-permute-done.refs_2_), channel_id=1, source_target_pairs={{0,4},{1,5},{2,0},{3,1},{4,6},{5,7},{6,2},{7,3},{8,12},{9,13},{10,... | collective-permute-start | bytes 1671176 | tf_op jit(solution)/shard_map/ppermute | solution.py:567
  22.7 14.4 %collective-permute-start.4 = (bf16[136,2048]{1,0:T(8,128)(2,1)S(1)}, bf16[136,2048]{1,0:T(8,128)(2,1)S(1)}, u32[]{:S(2)}, u32[]{:S(2)}) collective-permute-start(bf16[136,2048]{1,0:T(8,128)(2,1)S(1)} %collective-permute-done.refs_2_), channel_id=1, source_target_pairs={{0,1},{1,0},{2,3},{3,2},{4,5},{5,4},{6,7},{7,6},{8,9},{9,8},{10,11... | collective-permute-start | bytes 1671176 | tf_op jit(solution)/shard_map/ppermute | solution.py:541
  22.7 0.8 copy-start.2
  24.7 19.6 %all-to-all-start = ((bf16[4,2,136,512]{3,2,1,0:T(8,128)(2,1)}), bf16[4,2,136,512]{3,2,1,0:T(8,128)(2,1)}, u32[]{:S(2)}, u32[]{:S(2)}) async-start(bf16[4,2,136,512]{3,2,1,0:T(8,128)(2,1)} %pad_maximum_fusion.1), calls=%async_computation | async-start | bytes 2228224 | tf_op jit(solution)/shard_map/all_to_all | solution.py:551
  33.7 14.4 %copy-start.3 = (bf16[136,2048]{1,0:T(8,128)(2,1)}, bf16[136,2048]{1,0:T(8,128)(2,1)S(1)}, u32[]{:S(2)}) copy-start(bf16[136,2048]{1,0:T(8,128)(2,1)S(1)} %collective-permute-done.1.refs_3_) | copy-start | bytes 1671172
  33.7 14.5 %collective-permute-start.2 = (bf16[136,2048]{1,0:T(8,128)(2,1)S(1)}, bf16[136,2048]{1,0:T(8,128)(2,1)S(1)}, u32[]{:S(2)}, u32[]{:S(2)}) collective-permute-start(bf16[136,2048]{1,0:T(8,128)(2,1)S(1)} %collective-permute-done.1.refs_3_), channel_id=1, source_target_pairs={{0,4},{1,5},{2,0},{3,1},{4,6},{5,7},{6,2},{7,3},{8,12},{9,13},{10,... | collective-permute-start | bytes 1671176 | tf_op jit(solution)/shard_map/ppermute | solution.py:567
  37.0 0.8 copy-start.4
  44.3 18.0 %all-to-all-start.1 = ((bf16[4,2,136,512]{3,2,1,0:T(8,128)(2,1)}), bf16[4,2,136,512]{3,2,1,0:T(8,128)(2,1)S(1)}, u32[]{:S(2)}, u32[]{:S(2)}) async-start(bf16[4,2,136,512]{3,2,1,0:T(8,128)(2,1)} %pad_maximum_fusion), calls=%async_computation.1 | async-start | bytes 2228224 | tf_op jit(solution)/shard_map/all_to_all | solution.py:551
  48.0 16.3 %copy-start.9 = (bf16[8,96,128]{2,1,0:T(8,128)(2,1)}, bf16[8,96,128]{2,1,0:T(8,128)(2,1)S(1)}, u32[]{:S(2)}) copy-start(bf16[8,96,128]{2,1,0:T(8,128)(2,1)S(1)} %pad_maximum_fusion.3.refs_10_.refs_5_) | copy-start | bytes 589828
  48.0 30.6 %collective-permute-start.5 = (bf16[136,2048]{1,0:T(8,128)(2,1)S(1)}, bf16[136,2048]{1,0:T(8,128)(2,1)}, u32[]{:S(2)}, u32[]{:S(2)}) collective-permute-start(bf16[136,2048]{1,0:T(8,128)(2,1)S(1)} %collective-permute-done.1.refs_3_), channel_id=1, source_target_pairs={{0,1},{1,0},{2,3},{3,2},{4,5},{5,4},{6,7},{7,6},{8,9},{9,8},{10,11... | collective-permute-start | bytes 1671176 | tf_op jit(solution)/shard_map/ppermute | solution.py:541
  48.2 0.8 copy-start.5
  48.2 30.5 %collective-permute-start.6 = (bf16[136,2048]{1,0:T(8,128)(2,1)S(1)}, bf16[136,2048]{1,0:T(8,128)(2,1)}, u32[]{:S(2)}, u32[]{:S(2)}) collective-permute-start(bf16[136,2048]{1,0:T(8,128)(2,1)S(1)} %collective-permute-done.2.refs_4_), channel_id=1, source_target_pairs={{0,1},{1,0},{2,3},{3,2},{4,5},{5,4},{6,7},{7,6},{8,9},{9,8},{10,11... | collective-permute-start | bytes 1671176 | tf_op jit(solution)/shard_map/ppermute | solution.py:541
  62.3 5.6 %copy-start.6 = (bf16[4,2,136,512]{3,2,1,0:T(8,128)(2,1)}, bf16[4,2,136,512]{3,2,1,0:T(8,128)(2,1)S(1)}, u32[]{:S(2)}) copy-start(bf16[4,2,136,512]{3,2,1,0:T(8,128)(2,1)S(1)} %all-to-all-done.1.refs_2_) | copy-start | bytes 3342340
  62.3 8.7 %collective-permute-start.7 = (bf16[8,96,128]{2,1,0:T(8,128)(2,1)S(1)}, bf16[8,96,128]{2,1,0:T(8,128)(2,1)S(1)}, u32[]{:S(2)}, u32[]{:S(2)}) collective-permute-start(bf16[8,96,128]{2,1,0:T(8,128)(2,1)S(1)} %pad_maximum_fusion.3.refs_10_.refs_5_), channel_id=1, source_target_pairs={{0,8},{8,16},{16,24},{24,0},{1,9},{9,17},{17,25},{25,1},{2,10},{10... | collective-permute-start | bytes 589832 | tf_op jit(solution)/shard_map/ppermute | solution.py:536
  63.7 9.5 %collective-permute-start.8 = (bf16[8,96,128]{2,1,0:T(8,128)(2,1)S(1)}, bf16[8,96,128]{2,1,0:T(8,128)(2,1)S(1)}, u32[]{:S(2)}, u32[]{:S(2)}) collective-permute-start(bf16[8,96,128]{2,1,0:T(8,128)(2,1)S(1)} %pad_maximum_fusion.3.refs_10_.refs_5_), channel_id=1, source_target_pairs={{0,16},{8,24},{16,0},{24,8},{1,17},{9,25},{17,1},{25,9},{2,18},{10... | collective-permute-start | bytes 589832 | tf_op jit(solution)/shard_map/ppermute | solution.py:536
  64.3 9.7 %collective-permute-start.9 = (bf16[8,96,128]{2,1,0:T(8,128)(2,1)S(1)}, bf16[8,96,128]{2,1,0:T(8,128)(2,1)}, u32[]{:S(2)}, u32[]{:S(2)}) collective-permute-start(bf16[8,96,128]{2,1,0:T(8,128)(2,1)S(1)} %pad_maximum_fusion.3.refs_10_.refs_5_), channel_id=1, source_target_pairs={{0,24},{8,0},{16,8},{24,16},{1,25},{9,1},{17,9},{25,17},{2,26},{10... | collective-permute-start | bytes 589832 | tf_op jit(solution)/shard_map/ppermute | solution.py:536
  71.0 2.2 %copy-start.13 = (bf16[8,96,128]{2,1,0:T(8,128)(2,1)}, bf16[8,96,128]{2,1,0:T(8,128)(2,1)S(1)}, u32[]{:S(2)}) copy-start(bf16[8,96,128]{2,1,0:T(8,128)(2,1)S(1)} %collective-permute-done.7.refs_6_) | copy-start | bytes 589828
  73.9 34.0 %all-to-all-start.2 = ((bf16[4,2,136,512]{3,2,1,0:T(8,128)(2,1)}), bf16[4,2,136,512]{3,2,1,0:T(8,128)(2,1)S(1)}, u32[]{:S(2)}, u32[]{:S(2)}) async-start(bf16[4,2,136,512]{3,2,1,0:T(8,128)(2,1)} %pad_maximum_fusion.2), calls=%async_computation.2 | async-start | bytes 2228224 | tf_op jit(solution)/shard_map/all_to_all | solution.py:551
  107.9 8.4 %copy-start.7 = (bf16[4,2,136,512]{3,2,1,0:T(8,128)(2,1)}, bf16[4,2,136,512]{3,2,1,0:T(8,128)(2,1)S(1)}, u32[]{:S(2)}) copy-start(bf16[4,2,136,512]{3,2,1,0:T(8,128)(2,1)S(1)} %all-to-all-done.2.refs_3_) | copy-start | bytes 3342340
  107.9 8.4 %collective-permute-start.13 = (bf16[4,2,136,512]{3,2,1,0:T(8,128)(2,1)S(1)}, bf16[4,2,136,512]{3,2,1,0:T(8,128)(2,1)S(1)}, u32[]{:S(2)}, u32[]{:S(2)}) collective-permute-start(bf16[4,2,136,512]{3,2,1,0:T(8,128)(2,1)S(1)} %all-to-all-done.2.refs_3_), channel_id=1, source_target_pairs={{0,1},{1,0},{2,3},{3,2},{4,5},{5,4},{6,7},{7,6},{8,9},{9,8},{10,11... | collective-permute-start | bytes 3342344 | tf_op jit(solution)/shard_map/ppermute | solution.py:541
  108.1 17.6 %all-to-all-start.3 = ((f32[8,8,128]{2,1,0:T(8,128)}), f32[8,8,128]{2,1,0:T(8,128)S(1)}, u32[]{:S(2)}, u32[]{:S(2)}) async-start(f32[8,8,128]{2,1,0:T(8,128)} %get-tuple-element.39), calls=%async_computation.3 | async-start | bytes 65536 | tf_op jit(solution)/shard_map/all_to_all | solution.py:622
  111.4 16.5 %copy-start.11 = (bf16[16,64,96]{2,1,0:T(8,128)(2,1)S(1)}, bf16[16,64,96]{2,1,0:T(8,128)(2,1)}, u32[]{:S(2)}) copy-start(bf16[16,64,96]{2,1,0:T(8,128)(2,1)} %get-tuple-element.51) | copy-start | bytes 589828
  111.4 14.3 %collective-permute-start.10 = (bf16[16,64,96]{2,1,0:T(8,128)(2,1)}, bf16[16,64,96]{2,1,0:T(8,128)(2,1)S(1)}, u32[]{:S(2)}, u32[]{:S(2)}) collective-permute-start(bf16[16,64,96]{2,1,0:T(8,128)(2,1)} %get-tuple-element.40), channel_id=1, source_target_pairs={{0,8},{8,16},{16,24},{24,0},{1,9},{9,17},{17,25},{25,1},{2,10},{10... | collective-permute-start | bytes 589832 | tf_op jit(solution)/shard_map/ppermute | solution.py:536
  113.4 13.6 %collective-permute-start.11 = (bf16[16,64,96]{2,1,0:T(8,128)(2,1)}, bf16[16,64,96]{2,1,0:T(8,128)(2,1)S(1)}, u32[]{:S(2)}, u32[]{:S(2)}) collective-permute-start(bf16[16,64,96]{2,1,0:T(8,128)(2,1)} %get-tuple-element.41), channel_id=1, source_target_pairs={{0,16},{8,24},{16,0},{24,8},{1,17},{9,25},{17,1},{25,9},{2,18},{10... | collective-permute-start | bytes 589832 | tf_op jit(solution)/shard_map/ppermute | solution.py:536
  114.8 12.5 %collective-permute-start.12 = (bf16[16,64,96]{2,1,0:T(8,128)(2,1)}, bf16[16,64,96]{2,1,0:T(8,128)(2,1)S(1)}, u32[]{:S(2)}, u32[]{:S(2)}) collective-permute-start(bf16[16,64,96]{2,1,0:T(8,128)(2,1)} %get-tuple-element.42), channel_id=1, source_target_pairs={{0,24},{8,0},{16,8},{24,16},{1,25},{9,1},{17,9},{25,17},{2,26},{10... | collective-permute-start | bytes 589832 | tf_op jit(solution)/shard_map/ppermute | solution.py:536
  116.3 1.0 copy-start.12
  (1 other events, 0.7 us)

commit v6 on v5

--- a/solution.py
+++ b/solution.py
@@ -227,9 +227,10 @@
 contract_first = (((0,), (0,)), ((), ()))
 
 
-def expert_kernel(capacity, group_count, shards, *refs):
+def expert_kernel(capacity, group_count, shards, chunks, *refs):
     owners_ref = refs[0]
-    token_refs = refs[1 : 1 + shards]
+    token_refs = refs[1 : 1 + shards * chunks]
+    refs = refs[shards * (chunks - 1) :]
     hidden_ref, u_ref, weight_hbm, amap_ref, bmap_hbm = refs[1 + shards : 6 + shards]
     hg_ref, rk_ref = refs[6 + shards : 8 + shards]
     la_outs = refs[8 + shards : 8 + shards + group_count]
@@ -244,9 +245,15 @@
     padded = rows_s.shape[1] // micro
     first = (lax.axis_index("expert") * experts).astype(jnp.float32)
 
+    part = width // chunks
     token_copies = [
-        pltpu.make_async_copy(token_refs[i], dy_s.at[owners_ref[i]], dy_sem.at[i])
+        pltpu.make_async_copy(
+            token_refs[i * chunks + c],
+            dy_s.at[owners_ref[i], :, pl.ds(c * part, part)],
+            dy_sem.at[i, c],
+        )
         for i in range(shards)
+        for c in range(chunks)
     ]
     for copy in token_copies:
         copy.start()
@@ -412,12 +419,9 @@
 
 def adapter_kernel(capacity, micro, span, top, group_count, shards, *refs):
     pairs = shards // 2
-    early = pairs // 2
-    owners_ref = refs[0]
-    early_refs = refs[1 : 1 + early]
-    late_ref, swapped_ref = refs[1 + early : 3 + early]
-    u_refs = refs[3 + early : 3 + early + group_count]
-    lb_ref, tok_s, q_s, sem = refs[3 + early + group_count :]
+    owners_ref, near_ref, far_ref = refs[:3]
+    u_refs = refs[3 : 3 + group_count]
+    lb_ref, tok_s, q_s, sem = refs[3 + group_count :]
     experts, rank, share = lb_ref.shape
     tall = u_refs[0].shape[1]
     padded = tall // micro
@@ -428,11 +432,7 @@
     for g in range(group_count):
         home = lax.rem(group - g + group_count, group_count)
         for i in range(shards):
-            far, k = i // pairs, i % pairs
-            if k < early:
-                source = early_refs[k].at[home, far]
-            else:
-                source = (swapped_ref if far else late_ref).at[home, k - early]
+            source = (far_ref if i >= pairs else near_ref).at[home, i % pairs]
             copies.append(pltpu.make_async_copy(source, tok_s.at[g, owners_ref[i]], sem.at[g, i]))
     for copy in copies:
         copy.start()
@@ -540,12 +540,17 @@
     def swap_partners(array):
         return lax.ppermute(array, "expert", swap)
 
+    chunks = 2 if group_count % 2 == 0 else 1
+    part = width // chunks
+
     def exchange_columns(chosen):
-        parts = [
-            jnp.stack([piece[:, g * share : (g + 1) * share] for piece in chosen])
-            for g in range(group_count)
-        ]
-        return jnp.stack(parts)
+        def columns(pieces, g):
+            at = g * share % part
+            return pieces[g * share // part][:, at : at + share]
+
+        return jnp.stack(
+            [jnp.stack([columns(pieces, g) for pieces in chosen]) for g in range(group_count)]
+        )
 
     def across_groups(array):
         return lax.all_to_all(array, "dp", split_axis=0, concat_axis=0, tiled=True)
@@ -561,37 +566,32 @@
         [output_gradient, jnp.pad(names, ((0, extra - lines), (0, 0)))], axis=0
     )
 
-    early = pairs // 2
-    near, far = [sent], []
+    near, far = [[sent[:, c * part : (c + 1) * part] for c in range(chunks)]], []
     for step in range(pairs - 1):
-        near.append(lax.ppermute(near[-1], "expert", ring))
-        far.append(swap_partners(near[step]))
-    early_columns = []
-    for k in range(early):
-        columns = exchange_columns([near[k], far[k]])
-        if early_columns:
-            columns, early_columns[-1] = lax.optimization_barrier((columns, early_columns[-1]))
-        early_columns.append(across_groups(columns))
-    u, early_columns[-1] = lax.optimization_barrier((u, early_columns[-1]))
+        if step:
+            tied = [lax.optimization_barrier(pair) for pair in zip(near[step], far[-1])]
+            near[step], far[-1] = [a for a, _ in tied], [b for _, b in tied]
+        near.append([lax.ppermute(piece, "expert", ring) for piece in near[step]])
+        far.append([swap_partners(piece) for piece in near[step]])
     u_all = [u] + [shift_groups(u, s) for s in others]
-    late_columns = exchange_columns(near[early:])
-    late_columns, u_all = lax.optimization_barrier((late_columns, u_all))
-    late_columns = across_groups(late_columns)
-    far.append(swap_partners(near[-1]))
-    pieces = near + far
+    columns = exchange_columns(near)
+    columns, u_all, far[-1] = lax.optimization_barrier((columns, u_all, far[-1]))
+    columns = across_groups(columns)
+    far.append([swap_partners(piece) for piece in near[-1]])
+    pieces = [piece for shard in near + far for piece in shard]
 
     vmem = pl.BlockSpec(memory_space=pltpu.VMEM)
     smem = pl.BlockSpec(memory_space=pltpu.SMEM)
     anywhere = pl.BlockSpec(memory_space=pl.ANY)
     part_a = jax.ShapeDtypeStruct((experts, rank, units // group_count), jnp.bfloat16)
     hidden_grad, routed, *parts = pl.pallas_call(
-        functools.partial(expert_kernel, capacity, group_count, sources),
+        functools.partial(expert_kernel, capacity, group_count, sources, chunks),
         out_shape=(
             jax.ShapeDtypeStruct(hidden.shape, jnp.bfloat16),
             jax.ShapeDtypeStruct((sources, top, span), jnp.float32),
         )
         + (part_a,) * group_count,
-        in_specs=[smem] + [anywhere] * sources + [vmem, vmem, anywhere, vmem, anywhere],
+        in_specs=[smem] + [anywhere] * (sources * chunks) + [vmem, vmem, anywhere, vmem, anywhere],
         out_specs=(vmem,) * 2 + (anywhere,) * group_count,
         scratch_shapes=[
             pltpu.VMEM((sources, span + extra, width), jnp.bfloat16),
@@ -602,7 +602,7 @@
             pltpu.VMEM((experts, micro * padded, 1), jnp.float32),
             pltpu.VMEM((micro, 2, experts, sources // 2 * block), jnp.float32),
             pltpu.VMEM((group_count, experts, rank, units // group_count), jnp.bfloat16),
-            pltpu.SemaphoreType.DMA((sources,)),
+            pltpu.SemaphoreType.DMA((sources, chunks)),
             pltpu.SemaphoreType.DMA((experts,)),
             pltpu.SemaphoreType.DMA((experts,)),
             pltpu.SemaphoreType.DMA((group_count,)),
@@ -616,15 +616,15 @@
         name="expert_rows",
     )(owners, *pieces, hidden, u, frozen_down_weight, amap, adapter_output_map)
 
-    late_columns, parts, routed = lax.optimization_barrier((late_columns, parts, routed))
-    swapped = swap_partners(late_columns)
+    columns, parts, routed = lax.optimization_barrier((columns, parts, routed))
+    swapped = swap_partners(columns)
     arrived = [shift_groups(parts[s], s) for s in others]
     home = lax.all_to_all(routed, "expert", split_axis=0, concat_axis=0, tiled=True)
 
     lora_b = pl.pallas_call(
         functools.partial(adapter_kernel, capacity, micro, span, top, group_count, sources),
         out_shape=jax.ShapeDtypeStruct((experts, rank, share), jnp.float32),
-        in_specs=[smem] + [anywhere] * (early + 2) + [vmem] * group_count,
+        in_specs=[smem] + [anywhere] * 2 + [vmem] * group_count,
         out_specs=vmem,
         scratch_shapes=[
             pltpu.VMEM((group_count, sources, span + extra, share), jnp.bfloat16),
@@ -638,7 +638,7 @@
             transcendentals=0,
         ),
         name="adapter_columns",
-    )(owners, *early_columns, late_columns, swapped, *u_all)
+    )(owners, columns, swapped, *u_all)
 
     home, arrived, lora_b = lax.optimization_barrier((home, arrived, lora_b))
     router_grad = jnp.sum(home, axis=0).T
@@ -652,7 +652,7 @@
     sources, groups = lax.axis_size("expert"), lax.axis_size("dp")
     span, width = arrays[0].shape
     top, (micro, experts, slots, units) = arrays[1].shape[1], arrays[3].shape
-    even = sources % 4 == 0 and experts % 2 == 0 and width % (128 * groups) == 0 and units % groups == 0
+    even = sources % 2 == 0 and experts % 2 == 0 and width % (128 * groups) == 0 and units % groups == 0
     packs = 2 * top * span % (width // groups) == 0 and (width // groups) % span == 0
     exact = experts * sources <= 256
     if even and packs and exact and sources * span <= micro * experts * slots:

time: 129 us -> 110 us (0.85)
  waiting for transfers between devices: 41.5 us -> 20.3 us
  starting transfers between devices: 35.5 us -> 39.2 us
  other arithmetic: 7.98 us -> 6.21 us
    all_to_all x3 -> x1, waiting for transfers between devices: 18.5 us -> 0.01 us  [across_groups(): return lax.all_to_all(array, 'dp', split_axis=0, concat_axis=0, tiled=True)]
    ppermute x3 -> x6, starting transfers between devices: 10.8 us -> 18.7 us  [local_by_tokens(): near.append([lax.ppermute(piece, 'expert', ring) for piece in near[step]])]
    all_to_all x3 -> x1, starting transfers between devices: 11.3 us -> 3.72 us  [across_groups(): return lax.all_to_all(array, 'dp', split_axis=0, concat_axis=0, tiled=True)]
    ppermute x6, waiting for transfers between devices: 7 us -> 2.64 us  [shift_groups(): lax.ppermute(array, 'dp', [(d, (d + by) % group_count) for d in range(gro...]
    another operation x9 -> x3, other arithmetic: 3.71 us -> 1.94 us  [exchange_columns(): jnp.stack([jnp.stack([columns(pieces, g) for pieces in chosen]) for g in...]
    ppermute x3 -> x6, waiting for transfers between devices: 16 us -> 17.4 us  [local_by_tokens(): near.append([lax.ppermute(piece, 'expert', ring) for piece in near[step]])]
    ppermute x6, starting transfers between devices: 9.27 us -> 10.6 us  [shift_groups(): lax.ppermute(array, 'dp', [(d, (d + by) % group_count) for d in range(gro...]
    all_to_all x1, starting transfers between devices: 3.33 us -> 4.67 us  [local_by_tokens(): lax.all_to_all(routed, 'expert', split_axis=0, concat_axis=0, tiled=True)]
  transfers between devices with their start and end apart: 18 -> 23, of which waited for: 8 -> 9; matrix products, arithmetic and copies ran while one was open for 5% -> 4% of each run, Pallas kernels for 29% -> 34%
where the time goes in v6:
time: 110 us; the launch traced here: 109 us
  starting transfers between devices  39.2 us (36%)
  Pallas kernels  37.6 us (34%)
  waiting for transfers between devices  20.3 us (18%)
  other arithmetic  6.21 us (6%)
  local copies, waits for them, and re-layouts  4.31 us (4%)
    pallas_call x1, Pallas kernels, local_by_tokens(): pl.pallas_call(functools.partial(expert_kernel, capacity, group_count, so...  29.3 us
    ppermute x6, starting transfers between devices, local_by_tokens(): near.append([lax.ppermute(piece, 'expert', ring) for piece in near[step]])  18.7 us
    ppermute x6, waiting for transfers between devices, local_by_tokens(): near.append([lax.ppermute(piece, 'expert', ring) for piece in near[step]])  17.4 us
    ppermute x6, starting transfers between devices, shift_groups(): lax.ppermute(array, 'dp', [(d, (d + by) % group_count) for d in range(gro...  10.6 us
    pallas_call x1, Pallas kernels, local_by_tokens(): pl.pallas_call(functools.partial(adapter_kernel, capacity, micro, span, t...  8.38 us
    all_to_all x1, starting transfers between devices, local_by_tokens(): lax.all_to_all(routed, 'expert', split_axis=0, concat_axis=0, tiled=True)  4.67 us
    all_to_all x1, starting transfers between devices, across_groups(): return lax.all_to_all(array, 'dp', split_axis=0, concat_axis=0, tiled=True)  3.72 us
    unnamed x52, local copies, waits for them, and re-layouts  2.84 us
  transfers between devices with their start and end apart: 23, of which 9 were waited for; matrix products, arithmetic and copies ran while one was open for 4% of the time, Pallas kernels for 34%

profile of v6, /device:TPU:0, one launch (start us, length us, event | category | flops | bytes accessed | tf_op | source)
XLA Modules:
  0.0 109.2 jit_solution(17722972137019654100)
XLA Ops:
  0.7 0.8 convert_bitcast_fusion
  1.5 0.7 pad_maximum_fusion.2
  2.2 1.1 fusion.3
  3.9 3.6 %collective-permute-start.2 = (bf16[136,1024]{1,0:T(8,128)(2,1)S(1)}, bf16[136,1024]{1,0:T(8,128)(2,1)S(1)}, u32[]{:S(2)}, u32[]{:S(2)}) collective-permute-start(bf16[136,1024]{1,0:T(8,128)(2,1)S(1)} %get-tuple-element.72.refs_2_), channel_id=1, source_target_pairs={{0,4},{1,5},{2,0},{3,1},{4,6},{5,7},{6,2},{7,3},{8,12},{9,13},{10,... | collective-permute-start | bytes 835592 | tf_op jit(solution)/shard_map/ppermute | solution.py:574
  7.7 1.6 %collective-permute-start = (bf16[136,1024]{1,0:T(8,128)(2,1)S(1)}, bf16[136,1024]{1,0:T(8,128)(2,1)S(1)}, u32[]{:S(2)}, u32[]{:S(2)}) collective-permute-start(bf16[136,1024]{1,0:T(8,128)(2,1)S(1)} %get-tuple-element.73.refs_1_), channel_id=1, source_target_pairs={{0,4},{1,5},{2,0},{3,1},{4,6},{5,7},{6,2},{7,3},{8,12},{9,13},{10,... | collective-permute-start | bytes 835592 | tf_op jit(solution)/shard_map/ppermute | solution.py:574
  10.0 2.5 %collective-permute-start.12 = (bf16[8,96,128]{2,1,0:T(8,128)(2,1)S(1)}, bf16[8,96,128]{2,1,0:T(8,128)(2,1)S(1)}, u32[]{:S(2)}, u32[]{:S(2)}) collective-permute-start(bf16[8,96,128]{2,1,0:T(8,128)(2,1)S(1)} %pad_maximum_fusion.1.refs_18_.refs_3_), channel_id=1, source_target_pairs={{0,24},{8,0},{16,8},{24,16},{1,25},{9,1},{17,9},{25,17},{2,26},{10... | collective-permute-start | bytes 589832 | tf_op jit(solution)/shard_map/ppermute | solution.py:536
  12.6 1.9 %collective-permute-done.2.refs_4_ = bf16[136,1024]{1,0:T(8,128)(2,1)S(1)} collective-permute-done((bf16[136,1024]{1,0:T(8,128)(2,1)S(1)}, bf16[136,1024]{1,0:T(8,128)(2,1)S(1)}, u32[]{:S(2)}, u32[]{:S(2)}) %collective-permute-start.2) | collective-permute-done | bytes 278560 | tf_op jit(solution)/shard_map/ppermute | solution.py:574
  14.5 3.4 %collective-permute-start.6 = (bf16[136,1024]{1,0:T(8,128)(2,1)S(1)}, bf16[136,1024]{1,0:T(8,128)(2,1)S(1)}, u32[]{:S(2)}, u32[]{:S(2)}) collective-permute-start(bf16[136,1024]{1,0:T(8,128)(2,1)S(1)} %collective-permute-done.2.refs_4_), channel_id=1, source_target_pairs={{0,4},{1,5},{2,0},{3,1},{4,6},{5,7},{6,2},{7,3},{8,12},{9,13},{10,... | collective-permute-start | bytes 835592 | tf_op jit(solution)/shard_map/ppermute | solution.py:574
  17.9 2.5 %collective-permute-done.refs_3_ = bf16[136,1024]{1,0:T(8,128)(2,1)S(1)} collective-permute-done((bf16[136,1024]{1,0:T(8,128)(2,1)S(1)}, bf16[136,1024]{1,0:T(8,128)(2,1)S(1)}, u32[]{:S(2)}, u32[]{:S(2)}) %collective-permute-start) | collective-permute-done | bytes 278560 | tf_op jit(solution)/shard_map/ppermute | solution.py:574
  20.5 3.4 %collective-permute-start.4 = (bf16[136,1024]{1,0:T(8,128)(2,1)S(1)}, bf16[136,1024]{1,0:T(8,128)(2,1)S(1)}, u32[]{:S(2)}, u32[]{:S(2)}) collective-permute-start(bf16[136,1024]{1,0:T(8,128)(2,1)S(1)} %collective-permute-done.refs_3_), channel_id=1, source_target_pairs={{0,4},{1,5},{2,0},{3,1},{4,6},{5,7},{6,2},{7,3},{8,12},{9,13},{10,... | collective-permute-start | bytes 835592 | tf_op jit(solution)/shard_map/ppermute | solution.py:574
  23.9 1.6 %collective-permute-start.11 = (bf16[8,96,128]{2,1,0:T(8,128)(2,1)S(1)}, bf16[8,96,128]{2,1,0:T(8,128)(2,1)S(1)}, u32[]{:S(2)}, u32[]{:S(2)}) collective-permute-start(bf16[8,96,128]{2,1,0:T(8,128)(2,1)S(1)} %pad_maximum_fusion.1.refs_18_.refs_3_), channel_id=1, source_target_pairs={{0,16},{8,24},{16,0},{24,8},{1,17},{9,25},{17,1},{25,9},{2,18},{10... | collective-permute-start | bytes 589832 | tf_op jit(solution)/shard_map/ppermute | solution.py:536
  25.5 1.0 collective-permute-done.6.refs_6_
  26.4 3.4 %collective-permute-start.9 = (bf16[136,1024]{1,0:T(8,128)(2,1)S(1)}, bf16[136,1024]{1,0:T(8,128)(2,1)S(1)}, u32[]{:S(2)}, u32[]{:S(2)}) collective-permute-start(bf16[136,1024]{1,0:T(8,128)(2,1)S(1)} %collective-permute-done.6.refs_6_), channel_id=1, source_target_pairs={{0,4},{1,5},{2,0},{3,1},{4,6},{5,7},{6,2},{7,3},{8,12},{9,13},{10,... | collective-permute-start | bytes 835592 | tf_op jit(solution)/shard_map/ppermute | solution.py:574
  29.9 1.5 %collective-permute-start.10 = (bf16[8,96,128]{2,1,0:T(8,128)(2,1)S(1)}, bf16[8,96,128]{2,1,0:T(8,128)(2,1)S(1)}, u32[]{:S(2)}, u32[]{:S(2)}) collective-permute-start(bf16[8,96,128]{2,1,0:T(8,128)(2,1)S(1)} %pad_maximum_fusion.1.refs_18_.refs_3_), channel_id=1, source_target_pairs={{0,8},{8,16},{16,24},{24,0},{1,9},{9,17},{17,25},{25,1},{2,10},{10... | collective-permute-start | bytes 589832 | tf_op jit(solution)/shard_map/ppermute | solution.py:536
  31.4 1.0 collective-permute-done.4.refs_5_
  32.4 5.5 %collective-permute-done.9.refs_8_ = bf16[136,1024]{1,0:T(8,128)(2,1)S(1)} collective-permute-done((bf16[136,1024]{1,0:T(8,128)(2,1)S(1)}, bf16[136,1024]{1,0:T(8,128)(2,1)S(1)}, u32[]{:S(2)}, u32[]{:S(2)}) %collective-permute-start.9) | collective-permute-done | bytes 278560 | tf_op jit(solution)/shard_map/ppermute | solution.py:574
  37.9 3.4 %collective-permute-start.8 = (bf16[136,1024]{1,0:T(8,128)(2,1)S(1)}, bf16[136,1024]{1,0:T(8,128)(2,1)S(1)}, u32[]{:S(2)}, u32[]{:S(2)}) collective-permute-start(bf16[136,1024]{1,0:T(8,128)(2,1)S(1)} %collective-permute-done.4.refs_5_), channel_id=1, source_target_pairs={{0,4},{1,5},{2,0},{3,1},{4,6},{5,7},{6,2},{7,3},{8,12},{9,13},{10,... | collective-permute-start | bytes 835592 | tf_op jit(solution)/shard_map/ppermute | solution.py:574
  41.5 5.5 %collective-permute-done.8.refs_7_ = bf16[136,1024]{1,0:T(8,128)(2,1)S(1)} collective-permute-done((bf16[136,1024]{1,0:T(8,128)(2,1)S(1)}, bf16[136,1024]{1,0:T(8,128)(2,1)S(1)}, u32[]{:S(2)}, u32[]{:S(2)}) %collective-permute-start.8) | collective-permute-done | bytes 278560 | tf_op jit(solution)/shard_map/ppermute | solution.py:574
  47.8 1.6 %pad_maximum_fusion = bf16[4,4,136,512]{3,2,1,0:T(8,128)(2,1)} fusion(bf16[1,4,136,512]{3,2,1,0:T(8,128)(2,1)S(1)} %get-tuple-element.89, bf16[1,4,136,512]{3,2,1,0:T(8,128)(2,1)S(1)} %get-tuple-element.88, bf16[1,4,136,512]{3,2,1,0:T(8,128)(2,1)S(1)} %get-tuple-element.91, bf16[1,4,136,512]{3,2,1,0:T(8,128)(2,1)S(1)} %get-tuple-element.90), kind=kLoop, calls=%fused_computation | loop fusion | flops 3342336 | bytes 4456448 | tf_op jit(solution)/shard_map/stack | solution.py:551
  49.5 0.6 copy-done.22
  50.3 0.7 copy-done.18
  51.0 3.7 %all-to-all-start = ((bf16[4,4,136,512]{3,2,1,0:T(8,128)(2,1)}), bf16[4,4,136,512]{3,2,1,0:T(8,128)(2,1)S(1)}, u32[]{:S(2)}, u32[]{:S(2)}) async-start(bf16[4,4,136,512]{3,2,1,0:T(8,128)(2,1)} %pad_maximum_fusion), calls=%async_computation | async-start | bytes 4456448 | tf_op jit(solution)/shard_map/all_to_all | solution.py:556
  55.2 1.2 %dynamic-slice_bitcast_fusion.refs_0_ = s32[8]{0:T(128)} fusion(s32[8,8]{1,0:T(8,128)} %constant.14.clone, s32[]{:T(128)S(6)} %select_n.3), kind=kLoop, calls=%fused_computation.34 | loop fusion | bytes 68 | tf_op jit(solution)/shard_map/squeeze | solution.py:525
  57.4 29.3 %expert_rows.1 = (bf16[2,16,40,384]{3,2,1,0:T(8,128)(2,1)}, f32[8,8,128]{2,1,0:T(8,128)}, bf16[16,64,96]{2,1,0:T(8,128)(2,1)}, bf16[16,64,96]{2,1,0:T(8,128)(2,1...) custom-call(s32[8]{0:T(128)} %dynamic-slice_bitcast_fusion.refs_0_, bf16[136,1024]{1,0:T(8,128)(2,1)} %copy-done.2, ...), custom_call_target="tpu_custom_call" | custom-call | flops 6039797760 | bytes 33554432 | tf_op jit(solution)/shard_map/expert_rows/pallas_call | solution.py:587
  86.9 4.7 %all-to-all-start.1 = ((f32[8,8,128]{2,1,0:T(8,128)}), f32[8,8,128]{2,1,0:T(8,128)S(1)}, u32[]{:S(2)}, u32[]{:S(2)}) async-start(f32[8,8,128]{2,1,0:T(8,128)} %get-tuple-element.53), calls=%async_computation.1 | async-start | bytes 65536 | tf_op jit(solution)/shard_map/all_to_all | solution.py:622
  91.6 2.1 %collective-permute-start.17 = (bf16[16,64,96]{2,1,0:T(8,128)(2,1)}, bf16[16,64,96]{2,1,0:T(8,128)(2,1)S(1)}, u32[]{:S(2)}, u32[]{:S(2)}) collective-permute-start(bf16[16,64,96]{2,1,0:T(8,128)(2,1)} %get-tuple-element.54), channel_id=1, source_target_pairs={{0,8},{8,16},{16,24},{24,0},{1,9},{9,17},{17,25},{25,1},{2,10},{10... | collective-permute-start | bytes 589832 | tf_op jit(solution)/shard_map/ppermute | solution.py:536
  93.6 1.5 %collective-permute-start.18 = (bf16[16,64,96]{2,1,0:T(8,128)(2,1)}, bf16[16,64,96]{2,1,0:T(8,128)(2,1)S(1)}, u32[]{:S(2)}, u32[]{:S(2)}) collective-permute-start(bf16[16,64,96]{2,1,0:T(8,128)(2,1)} %get-tuple-element.55), channel_id=1, source_target_pairs={{0,16},{8,24},{16,0},{24,8},{1,17},{9,25},{17,1},{25,9},{2,18},{10... | collective-permute-start | bytes 589832 | tf_op jit(solution)/shard_map/ppermute | solution.py:536
  95.1 1.5 %collective-permute-start.19 = (bf16[16,64,96]{2,1,0:T(8,128)(2,1)}, bf16[16,64,96]{2,1,0:T(8,128)(2,1)S(1)}, u32[]{:S(2)}, u32[]{:S(2)}) collective-permute-start(bf16[16,64,96]{2,1,0:T(8,128)(2,1)} %get-tuple-element.56), channel_id=1, source_target_pairs={{0,24},{8,0},{16,8},{24,16},{1,25},{9,1},{17,9},{25,17},{2,26},{10... | collective-permute-start | bytes 589832 | tf_op jit(solution)/shard_map/ppermute | solution.py:536
  96.6 8.4 %adapter_columns.1 = f32[16,64,512]{2,1,0:T(8,128)} custom-call(s32[8]{0:T(128)} %dynamic-slice_bitcast_fusion.refs_0_, bf16[4,4,136,512]{3,2,1,0:T(8,128)(2,1)} %copy-done, bf16[4,4,136,512]{3,2,1,0:T(8,128)(2,1)} %collective-permute-done.20.refs_2_, bf16[8,96,128]{2,1,0:T(8,128)(2,1)} %copy-done.12, bf16[8,96,128]{2,1,0:T(8,128)(2,1)} %copy-done.24, ...), custom_call_target="tpu_custom_call" | custom-call | flops 3623878656 | bytes 6291456 | tf_op jit(solution)/shard_map/adapter_columns/pallas_call | solution.py:624
  105.0 2.3 %collective-permute-done.18 = bf16[16,64,96]{2,1,0:T(8,128)(2,1)S(1)} collective-permute-done((bf16[16,64,96]{2,1,0:T(8,128)(2,1)}, bf16[16,64,96]{2,1,0:T(8,128)(2,1)S(1)}, u32[]{:S(2)}, u32[]{:S(2)}) %collective-permute-start.18) | collective-permute-done | bytes 196640 | tf_op jit(solution)/shard_map/ppermute | solution.py:536
  107.6 0.6 reduce_sum.9
  108.2 1.0 convert_add_fusion
  (89 shorter events, 4.7 us)
Async XLA Ops:
  3.4 9.2 %collective-permute-start.3 = (bf16[136,1024]{1,0:T(8,128)(2,1)S(1)}, bf16[136,1024]{1,0:T(8,128)(2,1)S(1)}, u32[]{:S(2)}, u32[]{:S(2)}) collective-permute-start(bf16[136,1024]{1,0:T(8,128)(2,1)S(1)} %get-tuple-element.72.refs_2_), channel_id=1, source_target_pairs={{0,1},{1,0},{2,3},{3,2},{4,5},{5,4},{6,7},{7,6},{8,9},{9,8},{10,11... | collective-permute-start | bytes 835592 | tf_op jit(solution)/shard_map/ppermute | solution.py:541
  3.9 10.6 %collective-permute-start.2 = (bf16[136,1024]{1,0:T(8,128)(2,1)S(1)}, bf16[136,1024]{1,0:T(8,128)(2,1)S(1)}, u32[]{:S(2)}, u32[]{:S(2)}) collective-permute-start(bf16[136,1024]{1,0:T(8,128)(2,1)S(1)} %get-tuple-element.72.refs_2_), channel_id=1, source_target_pairs={{0,4},{1,5},{2,0},{3,1},{4,6},{5,7},{6,2},{7,3},{8,12},{9,13},{10,... | collective-permute-start | bytes 835592 | tf_op jit(solution)/shard_map/ppermute | solution.py:574
  7.5 10.4 %collective-permute-start.1 = (bf16[136,1024]{1,0:T(8,128)(2,1)S(1)}, bf16[136,1024]{1,0:T(8,128)(2,1)S(1)}, u32[]{:S(2)}, u32[]{:S(2)}) collective-permute-start(bf16[136,1024]{1,0:T(8,128)(2,1)S(1)} %get-tuple-element.73.refs_1_), channel_id=1, source_target_pairs={{0,1},{1,0},{2,3},{3,2},{4,5},{5,4},{6,7},{7,6},{8,9},{9,8},{10,11... | collective-permute-start | bytes 835592 | tf_op jit(solution)/shard_map/ppermute | solution.py:541
  7.7 12.8 %collective-permute-start = (bf16[136,1024]{1,0:T(8,128)(2,1)S(1)}, bf16[136,1024]{1,0:T(8,128)(2,1)S(1)}, u32[]{:S(2)}, u32[]{:S(2)}) collective-permute-start(bf16[136,1024]{1,0:T(8,128)(2,1)S(1)} %get-tuple-element.73.refs_1_), channel_id=1, source_target_pairs={{0,4},{1,5},{2,0},{3,1},{4,6},{5,7},{6,2},{7,3},{8,12},{9,13},{10,... | collective-permute-start | bytes 835592 | tf_op jit(solution)/shard_map/ppermute | solution.py:574
  10.0 31.5 %copy-start.12 = (bf16[8,96,128]{2,1,0:T(8,128)(2,1)}, bf16[8,96,128]{2,1,0:T(8,128)(2,1)S(1)}, u32[]{:S(2)}) copy-start(bf16[8,96,128]{2,1,0:T(8,128)(2,1)S(1)} %pad_maximum_fusion.1.refs_18_.refs_3_) | copy-start | bytes 589828
  10.0 39.4 %collective-permute-start.12 = (bf16[8,96,128]{2,1,0:T(8,128)(2,1)S(1)}, bf16[8,96,128]{2,1,0:T(8,128)(2,1)S(1)}, u32[]{:S(2)}, u32[]{:S(2)}) collective-permute-start(bf16[8,96,128]{2,1,0:T(8,128)(2,1)S(1)} %pad_maximum_fusion.1.refs_18_.refs_3_), channel_id=1, source_target_pairs={{0,24},{8,0},{16,8},{24,16},{1,25},{9,1},{17,9},{25,17},{2,26},{10... | collective-permute-start | bytes 589832 | tf_op jit(solution)/shard_map/ppermute | solution.py:536
  12.6 25.4 %copy-start.14 = (bf16[136,1024]{1,0:T(8,128)(2,1)}, bf16[136,1024]{1,0:T(8,128)(2,1)S(1)}, u32[]{:S(2)}) copy-start(bf16[136,1024]{1,0:T(8,128)(2,1)S(1)} %collective-permute-done.3.refs_10_) | copy-start | bytes 835588
  14.5 27.0 %copy-start.3 = (bf16[136,1024]{1,0:T(8,128)(2,1)}, bf16[136,1024]{1,0:T(8,128)(2,1)S(1)}, u32[]{:S(2)}) copy-start(bf16[136,1024]{1,0:T(8,128)(2,1)S(1)} %collective-permute-done.2.refs_4_) | copy-start | bytes 835588
  14.5 9.4 %collective-permute-start.7 = (bf16[136,1024]{1,0:T(8,128)(2,1)S(1)}, bf16[136,1024]{1,0:T(8,128)(2,1)S(1)}, u32[]{:S(2)}, u32[]{:S(2)}) collective-permute-start(bf16[136,1024]{1,0:T(8,128)(2,1)S(1)} %collective-permute-done.2.refs_4_), channel_id=1, source_target_pairs={{0,1},{1,0},{2,3},{3,2},{4,5},{5,4},{6,7},{7,6},{8,9},{9,8},{10,11... | collective-permute-start | bytes 835592 | tf_op jit(solution)/shard_map/ppermute | solution.py:541
  14.5 11.9 %collective-permute-start.6 = (bf16[136,1024]{1,0:T(8,128)(2,1)S(1)}, bf16[136,1024]{1,0:T(8,128)(2,1)S(1)}, u32[]{:S(2)}, u32[]{:S(2)}) collective-permute-start(bf16[136,1024]{1,0:T(8,128)(2,1)S(1)} %collective-permute-done.2.refs_4_), channel_id=1, source_target_pairs={{0,4},{1,5},{2,0},{3,1},{4,6},{5,7},{6,2},{7,3},{8,12},{9,13},{10,... | collective-permute-start | bytes 835592 | tf_op jit(solution)/shard_map/ppermute | solution.py:574
  17.9 23.6 %copy-start.15 = (bf16[136,1024]{1,0:T(8,128)(2,1)}, bf16[136,1024]{1,0:T(8,128)(2,1)S(1)}, u32[]{:S(2)}) copy-start(bf16[136,1024]{1,0:T(8,128)(2,1)S(1)} %collective-permute-done.1.refs_9_) | copy-start | bytes 835588
  20.5 21.1 %copy-start.4 = (bf16[136,1024]{1,0:T(8,128)(2,1)}, bf16[136,1024]{1,0:T(8,128)(2,1)S(1)}, u32[]{:S(2)}) copy-start(bf16[136,1024]{1,0:T(8,128)(2,1)S(1)} %collective-permute-done.refs_3_) | copy-start | bytes 835588
  20.5 9.4 %collective-permute-start.5 = (bf16[136,1024]{1,0:T(8,128)(2,1)S(1)}, bf16[136,1024]{1,0:T(8,128)(2,1)S(1)}, u32[]{:S(2)}, u32[]{:S(2)}) collective-permute-start(bf16[136,1024]{1,0:T(8,128)(2,1)S(1)} %collective-permute-done.refs_3_), channel_id=1, source_target_pairs={{0,1},{1,0},{2,3},{3,2},{4,5},{5,4},{6,7},{7,6},{8,9},{9,8},{10,11... | collective-permute-start | bytes 835592 | tf_op jit(solution)/shard_map/ppermute | solution.py:541
  20.5 11.9 %collective-permute-start.4 = (bf16[136,1024]{1,0:T(8,128)(2,1)S(1)}, bf16[136,1024]{1,0:T(8,128)(2,1)S(1)}, u32[]{:S(2)}, u32[]{:S(2)}) collective-permute-start(bf16[136,1024]{1,0:T(8,128)(2,1)S(1)} %collective-permute-done.refs_3_), channel_id=1, source_target_pairs={{0,4},{1,5},{2,0},{3,1},{4,6},{5,7},{6,2},{7,3},{8,12},{9,13},{10,... | collective-permute-start | bytes 835592 | tf_op jit(solution)/shard_map/ppermute | solution.py:574
  23.9 25.5 %collective-permute-start.11 = (bf16[8,96,128]{2,1,0:T(8,128)(2,1)S(1)}, bf16[8,96,128]{2,1,0:T(8,128)(2,1)S(1)}, u32[]{:S(2)}, u32[]{:S(2)}) collective-permute-start(bf16[8,96,128]{2,1,0:T(8,128)(2,1)S(1)} %pad_maximum_fusion.1.refs_18_.refs_3_), channel_id=1, source_target_pairs={{0,16},{8,24},{16,0},{24,8},{1,17},{9,25},{17,1},{25,9},{2,18},{10... | collective-permute-start | bytes 589832 | tf_op jit(solution)/shard_map/ppermute | solution.py:536
  26.4 20.6 %copy-start.5 = (bf16[136,1024]{1,0:T(8,128)(2,1)}, bf16[136,1024]{1,0:T(8,128)(2,1)S(1)}, u32[]{:S(2)}) copy-start(bf16[136,1024]{1,0:T(8,128)(2,1)S(1)} %collective-permute-done.6.refs_6_) | copy-start | bytes 835588
  26.4 11.5 %collective-permute-start.9 = (bf16[136,1024]{1,0:T(8,128)(2,1)S(1)}, bf16[136,1024]{1,0:T(8,128)(2,1)S(1)}, u32[]{:S(2)}, u32[]{:S(2)}) collective-permute-start(bf16[136,1024]{1,0:T(8,128)(2,1)S(1)} %collective-permute-done.6.refs_6_), channel_id=1, source_target_pairs={{0,4},{1,5},{2,0},{3,1},{4,6},{5,7},{6,2},{7,3},{8,12},{9,13},{10,... | collective-permute-start | bytes 835592 | tf_op jit(solution)/shard_map/ppermute | solution.py:574
  29.9 11.5 %copy-start.17 = (bf16[136,1024]{1,0:T(8,128)(2,1)}, bf16[136,1024]{1,0:T(8,128)(2,1)S(1)}, u32[]{:S(2)}) copy-start(bf16[136,1024]{1,0:T(8,128)(2,1)S(1)} %collective-permute-done.5.refs_11_) | copy-start | bytes 835588
  29.9 19.6 %collective-permute-start.10 = (bf16[8,96,128]{2,1,0:T(8,128)(2,1)S(1)}, bf16[8,96,128]{2,1,0:T(8,128)(2,1)S(1)}, u32[]{:S(2)}, u32[]{:S(2)}) collective-permute-start(bf16[8,96,128]{2,1,0:T(8,128)(2,1)S(1)} %pad_maximum_fusion.1.refs_18_.refs_3_), channel_id=1, source_target_pairs={{0,8},{8,16},{16,24},{24,0},{1,9},{9,17},{17,25},{25,1},{2,10},{10... | collective-permute-start | bytes 589832 | tf_op jit(solution)/shard_map/ppermute | solution.py:536
  32.4 14.8 %copy-start.6 = (bf16[136,1024]{1,0:T(8,128)(2,1)}, bf16[136,1024]{1,0:T(8,128)(2,1)S(1)}, u32[]{:S(2)}) copy-start(bf16[136,1024]{1,0:T(8,128)(2,1)S(1)} %collective-permute-done.4.refs_5_) | copy-start | bytes 835588
  32.4 17.1 %collective-permute-start.14 = (bf16[136,1024]{1,0:T(8,128)(2,1)S(1)}, bf16[136,1024]{1,0:T(8,128)(2,1)S(1)}, u32[]{:S(2)}, u32[]{:S(2)}) collective-permute-start(bf16[136,1024]{1,0:T(8,128)(2,1)S(1)} %collective-permute-done.6.refs_6_), channel_id=1, source_target_pairs={{0,1},{1,0},{2,3},{3,2},{4,5},{5,4},{6,7},{7,6},{8,9},{9,8},{10,11... | collective-permute-start | bytes 835592 | tf_op jit(solution)/shard_map/ppermute | solution.py:541
  37.9 9.1 %collective-permute-start.8 = (bf16[136,1024]{1,0:T(8,128)(2,1)S(1)}, bf16[136,1024]{1,0:T(8,128)(2,1)S(1)}, u32[]{:S(2)}, u32[]{:S(2)}) collective-permute-start(bf16[136,1024]{1,0:T(8,128)(2,1)S(1)} %collective-permute-done.4.refs_5_), channel_id=1, source_target_pairs={{0,4},{1,5},{2,0},{3,1},{4,6},{5,7},{6,2},{7,3},{8,12},{9,13},{10,... | collective-permute-start | bytes 835592 | tf_op jit(solution)/shard_map/ppermute | solution.py:574
  47.1 3.9 %collective-permute-start.13 = (bf16[136,1024]{1,0:T(8,128)(2,1)S(1)}, bf16[136,1024]{1,0:T(8,128)(2,1)}, u32[]{:S(2)}, u32[]{:S(2)}) collective-permute-start(bf16[136,1024]{1,0:T(8,128)(2,1)S(1)} %collective-permute-done.4.refs_5_), channel_id=1, source_target_pairs={{0,1},{1,0},{2,3},{3,2},{4,5},{5,4},{6,7},{7,6},{8,9},{9,8},{10,11... | collective-permute-start | bytes 835592 | tf_op jit(solution)/shard_map/ppermute | solution.py:541
  51.0 35.7 %all-to-all-start = ((bf16[4,4,136,512]{3,2,1,0:T(8,128)(2,1)}), bf16[4,4,136,512]{3,2,1,0:T(8,128)(2,1)S(1)}, u32[]{:S(2)}, u32[]{:S(2)}) async-start(bf16[4,4,136,512]{3,2,1,0:T(8,128)(2,1)} %pad_maximum_fusion), calls=%async_computation | async-start | bytes 4456448 | tf_op jit(solution)/shard_map/all_to_all | solution.py:556
  54.7 1.7 %collective-permute-start.16 = (bf16[136,1024]{1,0:T(8,128)(2,1)S(1)}, bf16[136,1024]{1,0:T(8,128)(2,1)S(1)}, u32[]{:S(2)}, u32[]{:S(2)}) collective-permute-start(bf16[136,1024]{1,0:T(8,128)(2,1)S(1)} %copy-done.8), channel_id=1, source_target_pairs={{0,1},{1,0},{2,3},{3,2},{4,5},{5,4},{6,7},{7,6},{8,9},{9,8},{10,11... | collective-permute-start | bytes 835592 | tf_op jit(solution)/shard_map/ppermute | solution.py:541
  54.7 1.9 %collective-permute-start.15 = (bf16[136,1024]{1,0:T(8,128)(2,1)S(1)}, bf16[136,1024]{1,0:T(8,128)(2,1)S(1)}, u32[]{:S(2)}, u32[]{:S(2)}) collective-permute-start(bf16[136,1024]{1,0:T(8,128)(2,1)S(1)} %copy-done.10), channel_id=1, source_target_pairs={{0,1},{1,0},{2,3},{3,2},{4,5},{5,4},{6,7},{7,6},{8,9},{9,8},{10,11... | collective-permute-start | bytes 835592 | tf_op jit(solution)/shard_map/ppermute | solution.py:541
  86.7 9.9 %collective-permute-start.20 = (bf16[4,4,136,512]{3,2,1,0:T(8,128)(2,1)S(1)}, bf16[4,4,136,512]{3,2,1,0:T(8,128)(2,1)}, u32[]{:S(2)}, u32[]{:S(2)}) collective-permute-start(bf16[4,4,136,512]{3,2,1,0:T(8,128)(2,1)S(1)} %all-to-all-done.refs_1_), channel_id=1, source_target_pairs={{0,1},{1,0},{2,3},{3,2},{4,5},{5,4},{6,7},{7,6},{8,9},{9,8},{10,11... | collective-permute-start | bytes 6684680 | tf_op jit(solution)/shard_map/ppermute | solution.py:541
  86.9 18.1 %all-to-all-start.1 = ((f32[8,8,128]{2,1,0:T(8,128)}), f32[8,8,128]{2,1,0:T(8,128)S(1)}, u32[]{:S(2)}, u32[]{:S(2)}) async-start(f32[8,8,128]{2,1,0:T(8,128)} %get-tuple-element.53), calls=%async_computation.1 | async-start | bytes 65536 | tf_op jit(solution)/shard_map/all_to_all | solution.py:622
  91.6 16.7 %copy-start.21 = (bf16[16,64,96]{2,1,0:T(8,128)(2,1)S(1)}, bf16[16,64,96]{2,1,0:T(8,128)(2,1)}, u32[]{:S(2)}) copy-start(bf16[16,64,96]{2,1,0:T(8,128)(2,1)} %get-tuple-element.63) | copy-start | bytes 589828
  91.6 13.4 %collective-permute-start.17 = (bf16[16,64,96]{2,1,0:T(8,128)(2,1)}, bf16[16,64,96]{2,1,0:T(8,128)(2,1)S(1)}, u32[]{:S(2)}, u32[]{:S(2)}) collective-permute-start(bf16[16,64,96]{2,1,0:T(8,128)(2,1)} %get-tuple-element.54), channel_id=1, source_target_pairs={{0,8},{8,16},{16,24},{24,0},{1,9},{9,17},{17,25},{25,1},{2,10},{10... | collective-permute-start | bytes 589832 | tf_op jit(solution)/shard_map/ppermute | solution.py:536
  93.6 13.6 %collective-permute-start.18 = (bf16[16,64,96]{2,1,0:T(8,128)(2,1)}, bf16[16,64,96]{2,1,0:T(8,128)(2,1)S(1)}, u32[]{:S(2)}, u32[]{:S(2)}) collective-permute-start(bf16[16,64,96]{2,1,0:T(8,128)(2,1)} %get-tuple-element.55), channel_id=1, source_target_pairs={{0,16},{8,24},{16,0},{24,8},{1,17},{9,25},{17,1},{25,9},{2,18},{10... | collective-permute-start | bytes 589832 | tf_op jit(solution)/shard_map/ppermute | solution.py:536
  95.1 12.5 %collective-permute-start.19 = (bf16[16,64,96]{2,1,0:T(8,128)(2,1)}, bf16[16,64,96]{2,1,0:T(8,128)(2,1)S(1)}, u32[]{:S(2)}, u32[]{:S(2)}) collective-permute-start(bf16[16,64,96]{2,1,0:T(8,128)(2,1)} %get-tuple-element.56), channel_id=1, source_target_pairs={{0,24},{8,0},{16,8},{24,16},{1,25},{9,1},{17,9},{25,17},{2,26},{10... | collective-permute-start | bytes 589832 | tf_op jit(solution)/shard_map/ppermute | solution.py:536
  (16 other events, 73.3 us)

commit v7 on v6

--- a/solution.py
+++ b/solution.py
@@ -227,14 +227,22 @@
 contract_first = (((0,), (0,)), ((), ()))
 
 
+def shard_owner(index, sources):
+    pairs = sources // 2
+    me = lax.axis_index("expert")
+    column, core = me // 2, lax.rem(me, 2)
+    place = jnp.where(lax.rem(column, 2) == 0, column // 2, pairs - 1 - column // 2)
+    place = lax.rem(place - index % pairs + pairs, pairs)
+    column = jnp.where(2 * place < pairs, 2 * place, 2 * (pairs - 1 - place) + 1)
+    return 2 * column + (core if index < pairs else 1 - core)
+
+
 def expert_kernel(capacity, group_count, shards, chunks, *refs):
-    owners_ref = refs[0]
-    token_refs = refs[1 : 1 + shards * chunks]
-    refs = refs[shards * (chunks - 1) :]
-    hidden_ref, u_ref, weight_hbm, amap_ref, bmap_hbm = refs[1 + shards : 6 + shards]
-    hg_ref, rk_ref = refs[6 + shards : 8 + shards]
-    la_outs = refs[8 + shards : 8 + shards + group_count]
-    scratch = refs[8 + shards + group_count :]
+    token_refs = refs[: shards * chunks]
+    refs = refs[shards * chunks :]
+    hidden_ref, u_ref, weight_hbm, amap_ref, bmap_hbm, hg_ref, rk_ref = refs[:7]
+    la_outs = refs[7 : 7 + group_count]
+    scratch = refs[7 + group_count :]
     dy_s, wb_s, rows_s, y_s, code_s, gate_s, back_s, la_s = scratch[:8]
     dy_sem, w_sem, b_sem, la_sem = scratch[8:]
     top, span = rk_ref.shape[1:]
@@ -246,10 +254,11 @@
     first = (lax.axis_index("expert") * experts).astype(jnp.float32)
 
     part = width // chunks
+    owners = [shard_owner(i, shards) for i in range(shards)]
     token_copies = [
         pltpu.make_async_copy(
             token_refs[i * chunks + c],
-            dy_s.at[owners_ref[i], :, pl.ds(c * part, part)],
+            dy_s.at[owners[i], :, pl.ds(c * part, part)],
             dy_sem.at[i, c],
         )
         for i in range(shards)
@@ -264,14 +273,27 @@
             pltpu.make_async_copy(bmap_hbm.at[x], wb_s.at[x, pl.ds(units, rank)], b_sem.at[x]),
         )
 
-    for x in range(experts):
-        for copy in weight_copies(x):
-            copy.start()
+    half = experts // 2
+    batch = 2 if half % 2 == 0 else 1
+    groups = half // batch
+
+    def members(step):
+        at = [step * batch + i for i in range(batch)]
+        picked = [(p, p, slice(0, rank)) for p in at]
+        return picked + [(p + half, p, slice(rank, 2 * rank)) for p in at]
+
+    def request_weights(step):
+        for x, _, _ in members(step):
+            for copy in weight_copies(x):
+                copy.start()
+
+    for step in range(min(2, groups)):
+        request_weights(step)
 
     for copy in token_copies:
         copy.wait()
     names = [
-        read_names(dy_s[i, span:, : width // group_count], span, top) for i in range(shards)
+        read_names(dy_s[i, span:, width - width // group_count :], span, top) for i in range(shards)
     ]
     codes, gates = slot_codes(names, first, capacity, experts, micro)
     windows = slot_windows(slots)
@@ -316,30 +338,30 @@
                 parts[0], parts[1], windows, padded, 1
             ).astype(jnp.bfloat16)
 
-    half = experts // 2
-
-    def main_products(x, carry):
-        for copy in weight_copies(2 * x) + weight_copies(2 * x + 1):
-            copy.wait()
-        for i in range(2):
-            y_s[2 * x + i] = lax.dot_general(
-                rows_s[2 * x + i],
-                wb_s[2 * x + i],
-                contract_last,
-                preferred_element_type=jnp.float32,
-            )
-        return carry
-
-    lax.fori_loop(0, half, main_products, 0)
+    def main_products(step):
+        xs = [x for x, _, _ in members(step)]
+        for x in xs:
+            for copy in weight_copies(x):
+                copy.wait()
+
+        @pl.when(step + 2 < groups)
+        def _():
+            request_weights(step + 2)
+
+        return [
+            lax.dot_general(rows_s[x], wb_s[x], contract_last, preferred_element_type=jnp.float32)
+            for x in xs
+        ]
+
+    def keep_products(step, products):
+        for (x, _, _), product in zip(members(step), products):
+            y_s[x] = product
 
     share = units // group_count
     filler = jnp.zeros((padded - slots, units), jnp.float32)
-    batch = 2 if half % 2 == 0 else 1
-
-    def small_steps(step, carry):
-        at = [step * batch + i for i in range(batch)]
-        picked = [(p, p, slice(0, rank)) for p in at]
-        picked += [(p + half, p, slice(rank, 2 * rank)) for p in at]
+
+    def small_steps(step):
+        picked = members(step)
         xs = [x for x, _, _ in picked]
         mains = [y_s[x, :, :units] for x in xs]
         vs = [y_s[x, :, units:].astype(jnp.bfloat16) for x in xs]
@@ -389,9 +411,16 @@
                 la_s[k, x] = (adapter_scale * la[:, k * share : (k + 1) * share]).astype(
                     la_s.dtype
                 )
+
+    def both_steps(step, carry):
+        products = main_products(step)
+        small_steps(step - 1)
+        keep_products(step, products)
         return carry
 
-    lax.fori_loop(0, half // batch, small_steps, 0)
+    keep_products(0, main_products(0))
+    lax.fori_loop(1, groups, both_steps, 0)
+    small_steps(groups - 1)
 
     group = lax.axis_index("dp")
     la_copies = [
@@ -419,22 +448,26 @@
 
 def adapter_kernel(capacity, micro, span, top, group_count, shards, *refs):
     pairs = shards // 2
-    owners_ref, near_ref, far_ref = refs[:3]
-    u_refs = refs[3 : 3 + group_count]
-    lb_ref, tok_s, q_s, sem = refs[3 + group_count :]
+    near_ref, far_ref = refs[:2]
+    u_hbm = refs[2 : 2 + group_count]
+    lb_ref, tok_s, q_s, u_refs, sem, u_sem = refs[2 + group_count :]
     experts, rank, share = lb_ref.shape
-    tall = u_refs[0].shape[1]
+    tall = u_refs.shape[2]
     padded = tall // micro
     block = span // micro
     first = (lax.axis_index("expert") * experts).astype(jnp.float32)
     group = lax.axis_index("dp")
+    owners = [shard_owner(i, shards) for i in range(shards)]
+    u_copies = [
+        pltpu.make_async_copy(u_hbm[g], u_refs.at[g], u_sem.at[g]) for g in range(group_count)
+    ]
     copies = []
     for g in range(group_count):
         home = lax.rem(group - g + group_count, group_count)
         for i in range(shards):
             source = (far_ref if i >= pairs else near_ref).at[home, i % pairs]
-            copies.append(pltpu.make_async_copy(source, tok_s.at[g, owners_ref[i]], sem.at[g, i]))
-    for copy in copies:
+            copies.append(pltpu.make_async_copy(source, tok_s.at[g, owners[i]], sem.at[g, i]))
+    for copy in copies + u_copies:
         copy.start()
     slots = capacity * shards
     windows = slot_windows(slots)
@@ -470,9 +503,11 @@
             q = join_windows(parts[0], parts[1], windows, padded, 1).astype(jnp.bfloat16)
             at = g * tall + m * padded
             q_s[:, at : at + padded, :] = q
+    for copy in u_copies:
+        copy.wait()
     half = experts // 2
     for x in range(half):
-        both = jnp.concatenate([u_refs[g][x] for g in range(group_count)], axis=0)
+        both = jnp.concatenate([u_refs[g, x] for g in range(group_count)], axis=0)
         lb_ref[x] = adapter_scale * lax.dot_general(
             both[:, :rank], q_s[x], contract_first, preferred_element_type=jnp.float32
         )
@@ -505,8 +540,8 @@
     padded = pad_rows(slots)
     share = width // group_count
     pairs = sources // 2
-    me = lax.axis_index("expert")
-    group = lax.axis_index("dp")
+    chunks = 2 if group_count % 2 == 0 else 1
+    part = width // chunks
 
     order = ring_order(pairs)
     place = {z: i for i, z in enumerate(order)}
@@ -514,15 +549,6 @@
         (2 * z + c, 2 * order[(place[z] + 1) % pairs] + c) for z in range(pairs) for c in range(2)
     ]
     swap = [(e, e ^ 1) for e in range(sources)]
-    owner_table = [
-        [
-            2 * order[(place[e // 2] - i) % pairs] + (e % 2 if near else 1 - e % 2)
-            for near in (True, False)
-            for i in range(pairs)
-        ]
-        for e in range(sources)
-    ]
-    owners = jnp.asarray(owner_table, jnp.int32)[me]
 
     amap = jnp.swapaxes(adapter_input_map, 1, 2)
     u = jnp.einsum("mesk,exk->emsx", hidden, amap, preferred_element_type=jnp.float32)
@@ -540,9 +566,6 @@
     def swap_partners(array):
         return lax.ppermute(array, "expert", swap)
 
-    chunks = 2 if group_count % 2 == 0 else 1
-    part = width // chunks
-
     def exchange_columns(chosen):
         def columns(pieces, g):
             at = g * share % part
@@ -567,21 +590,22 @@
     )
 
     near, far = [[sent[:, c * part : (c + 1) * part] for c in range(chunks)]], []
+    u_all = [shift_groups(u, s) for s in others]
     for step in range(pairs - 1):
         if step:
             tied = [lax.optimization_barrier(pair) for pair in zip(near[step], far[-1])]
             near[step], far[-1] = [a for a, _ in tied], [b for _, b in tied]
+        if step == pairs - 2:
+            near[step][0], u_all = lax.optimization_barrier((near[step][0], u_all))
         near.append([lax.ppermute(piece, "expert", ring) for piece in near[step]])
         far.append([swap_partners(piece) for piece in near[step]])
-    u_all = [u] + [shift_groups(u, s) for s in others]
     columns = exchange_columns(near)
-    columns, u_all, far[-1] = lax.optimization_barrier((columns, u_all, far[-1]))
+    columns, far[-1] = lax.optimization_barrier((columns, far[-1]))
     columns = across_groups(columns)
     far.append([swap_partners(piece) for piece in near[-1]])
     pieces = [piece for shard in near + far for piece in shard]
 
     vmem = pl.BlockSpec(memory_space=pltpu.VMEM)
-    smem = pl.BlockSpec(memory_space=pltpu.SMEM)
     anywhere = pl.BlockSpec(memory_space=pl.ANY)
     part_a = jax.ShapeDtypeStruct((experts, rank, units // group_count), jnp.bfloat16)
     hidden_grad, routed, *parts = pl.pallas_call(
@@ -591,7 +615,7 @@
             jax.ShapeDtypeStruct((sources, top, span), jnp.float32),
         )
         + (part_a,) * group_count,
-        in_specs=[smem] + [anywhere] * (sources * chunks) + [vmem, vmem, anywhere, vmem, anywhere],
+        in_specs=[anywhere] * (sources * chunks) + [vmem, vmem, anywhere, vmem, anywhere],
         out_specs=(vmem,) * 2 + (anywhere,) * group_count,
         scratch_shapes=[
             pltpu.VMEM((sources, span + extra, width), jnp.bfloat16),
@@ -614,7 +638,7 @@
             transcendentals=0,
         ),
         name="expert_rows",
-    )(owners, *pieces, hidden, u, frozen_down_weight, amap, adapter_output_map)
+    )(*pieces, hidden, u, frozen_down_weight, amap, adapter_output_map)
 
     columns, parts, routed = lax.optimization_barrier((columns, parts, routed))
     swapped = swap_partners(columns)
@@ -624,12 +648,14 @@
     lora_b = pl.pallas_call(
         functools.partial(adapter_kernel, capacity, micro, span, top, group_count, sources),
         out_shape=jax.ShapeDtypeStruct((experts, rank, share), jnp.float32),
-        in_specs=[smem] + [anywhere] * 2 + [vmem] * group_count,
+        in_specs=[anywhere] * (2 + group_count),
         out_specs=vmem,
         scratch_shapes=[
             pltpu.VMEM((group_count, sources, span + extra, share), jnp.bfloat16),
             pltpu.VMEM((experts, group_count * micro * padded, share), jnp.bfloat16),
+            pltpu.VMEM((group_count,) + u.shape, jnp.bfloat16),
             pltpu.SemaphoreType.DMA((group_count, sources)),
+            pltpu.SemaphoreType.DMA((group_count,)),
         ],
         compiler_params=pltpu.CompilerParams(vmem_limit_bytes=58 * 1024 * 1024),
         cost_estimate=pl.CostEstimate(
@@ -638,7 +664,7 @@
             transcendentals=0,
         ),
         name="adapter_columns",
-    )(owners, columns, swapped, *u_all)
+    )(columns, swapped, u, *u_all)
 
     home, arrived, lora_b = lax.optimization_barrier((home, arrived, lora_b))
     router_grad = jnp.sum(home, axis=0).T

time: 110 us -> 99.8 us (0.907)
  Pallas kernels: 37.6 us -> 30.9 us
  starting transfers between devices: 39.2 us -> 35.9 us
    pallas_call x1, Pallas kernels: 29.3 us -> 23.4 us  [local_by_tokens(): pl.pallas_call(functools.partial(expert_kernel, capacity, group_count, so...]
    ppermute x6, waiting for transfers between devices: 17.4 us -> 13.1 us  [local_by_tokens(): near.append([lax.ppermute(piece, 'expert', ring) for piece in near[step]])]
    ppermute x6, waiting for transfers between devices: 2.64 us -> 6.4 us  [shift_groups(): lax.ppermute(array, 'dp', [(d, (d + by) % group_count) for d in range(gro...]
    ppermute x6, starting transfers between devices: 18.7 us -> 16.9 us  [local_by_tokens(): near.append([lax.ppermute(piece, 'expert', ring) for piece in near[step]])]
    ppermute x9, waiting for transfers between devices: 0.26 us -> 1.46 us  [swap_partners(): return lax.ppermute(array, 'expert', swap)]
    squeeze x1 -> x0, local copies, waits for them, and re-layouts: 1.2 us -> none  [local_by_tokens(): owners = jnp.asarray(owner_table, jnp.int32)[me]]
  transfers between devices with their start and end apart: 23 -> 23, of which waited for: 9 -> 12; matrix products, arithmetic and copies ran while one was open for 4% -> 3% of each run, Pallas kernels for 34% -> 31%
where the time goes in v7:
time: 99.8 us; the launch traced here: 99.4 us
  starting transfers between devices  35.9 us (36%)
  Pallas kernels  30.9 us (31%)
  waiting for transfers between devices  21.2 us (21%)
  other arithmetic  6.2 us (6%)
  local copies, waits for them, and re-layouts  3.79 us (4%)
    pallas_call x1, Pallas kernels, local_by_tokens(): pl.pallas_call(functools.partial(expert_kernel, capacity, group_count, so...  23.4 us
    ppermute x6, starting transfers between devices, local_by_tokens(): near.append([lax.ppermute(piece, 'expert', ring) for piece in near[step]])  16.9 us
    ppermute x6, waiting for transfers between devices, local_by_tokens(): near.append([lax.ppermute(piece, 'expert', ring) for piece in near[step]])  13.1 us
    ppermute x6, starting transfers between devices, shift_groups(): lax.ppermute(array, 'dp', [(d, (d + by) % group_count) for d in range(gro...  10.5 us
    pallas_call x1, Pallas kernels, local_by_tokens(): pl.pallas_call(functools.partial(adapter_kernel, capacity, micro, span, t...  7.48 us
    ppermute x6, waiting for transfers between devices, shift_groups(): lax.ppermute(array, 'dp', [(d, (d + by) % group_count) for d in range(gro...  6.4 us
    all_to_all x1, starting transfers between devices, local_by_tokens(): lax.all_to_all(routed, 'expert', split_axis=0, concat_axis=0, tiled=True)  3.64 us
    all_to_all x1, starting transfers between devices, across_groups(): return lax.all_to_all(array, 'dp', split_axis=0, concat_axis=0, tiled=True)  3.62 us
  transfers between devices with their start and end apart: 23, of which 12 were waited for; matrix products, arithmetic and copies ran while one was open for 3% of the time, Pallas kernels for 31%

profile of v7, /device:TPU:0, one launch (start us, length us, event | category | flops | bytes accessed | tf_op | source)
XLA Modules:
  0.0 99.4 jit_solution(5328741768385487125)
XLA Ops:
  0.7 0.8 convert_bitcast_fusion
  1.5 0.7 pad_maximum_fusion.2
  2.2 1.1 %fusion.3 = bf16[136,2048]{1,0:T(8,128)(2,1)S(1)} fusion(bf16[4,2048]{1,0:T(4,128)(2,1)S(1)} %bitcast.58, bf16[128,2048]{1,0:T(8,128)(2,1)} %param.7), kind=kLoop, calls=%fused_computation.6 | loop fusion | flops 1671168 | bytes 1097728 | tf_op jit(solution)/shard_map/concatenate | solution.py:588
  3.9 3.6 %collective-permute-start.2 = (bf16[136,1024]{1,0:T(8,128)(2,1)S(1)}, bf16[136,1024]{1,0:T(8,128)(2,1)S(1)}, u32[]{:S(2)}, u32[]{:S(2)}) collective-permute-start(bf16[136,1024]{1,0:T(8,128)(2,1)S(1)} %get-tuple-element.72.refs_1_), channel_id=1, source_target_pairs={{0,4},{1,5},{2,0},{3,1},{4,6},{5,7},{6,2},{7,3},{8,12},{9,13},{10,... | collective-permute-start | bytes 835592 | tf_op jit(solution)/shard_map/ppermute | solution.py:600
  7.7 1.6 %collective-permute-start = (bf16[136,1024]{1,0:T(8,128)(2,1)S(1)}, bf16[136,1024]{1,0:T(8,128)(2,1)S(1)}, u32[]{:S(2)}, u32[]{:S(2)}) collective-permute-start(bf16[136,1024]{1,0:T(8,128)(2,1)S(1)} %get-tuple-element.73.refs_0_), channel_id=1, source_target_pairs={{0,4},{1,5},{2,0},{3,1},{4,6},{5,7},{6,2},{7,3},{8,12},{9,13},{10,... | collective-permute-start | bytes 835592 | tf_op jit(solution)/shard_map/ppermute | solution.py:600
  10.0 2.5 %collective-permute-start.8 = (bf16[8,96,128]{2,1,0:T(8,128)(2,1)S(1)}, bf16[8,96,128]{2,1,0:T(8,128)(2,1)S(1)}, u32[]{:S(2)}, u32[]{:S(2)}) collective-permute-start(bf16[8,96,128]{2,1,0:T(8,128)(2,1)S(1)} %pad_maximum_fusion.1.refs_17_.refs_2_), channel_id=1, source_target_pairs={{0,24},{8,0},{16,8},{24,16},{1,25},{9,1},{17,9},{25,17},{2,26},{10... | collective-permute-start | bytes 589832 | tf_op jit(solution)/shard_map/ppermute | solution.py:562
  12.6 1.9 %collective-permute-done.2.refs_3_ = bf16[136,1024]{1,0:T(8,128)(2,1)S(1)} collective-permute-done((bf16[136,1024]{1,0:T(8,128)(2,1)S(1)}, bf16[136,1024]{1,0:T(8,128)(2,1)S(1)}, u32[]{:S(2)}, u32[]{:S(2)}) %collective-permute-start.2) | collective-permute-done | bytes 278560 | tf_op jit(solution)/shard_map/ppermute | solution.py:600
  14.5 3.4 %collective-permute-start.9 = (bf16[136,1024]{1,0:T(8,128)(2,1)S(1)}, bf16[136,1024]{1,0:T(8,128)(2,1)S(1)}, u32[]{:S(2)}, u32[]{:S(2)}) collective-permute-start(bf16[136,1024]{1,0:T(8,128)(2,1)S(1)} %collective-permute-done.2.refs_3_), channel_id=1, source_target_pairs={{0,4},{1,5},{2,0},{3,1},{4,6},{5,7},{6,2},{7,3},{8,12},{9,13},{10,... | collective-permute-start | bytes 835592 | tf_op jit(solution)/shard_map/ppermute | solution.py:600
  17.9 2.6 %collective-permute-done.refs_2_ = bf16[136,1024]{1,0:T(8,128)(2,1)S(1)} collective-permute-done((bf16[136,1024]{1,0:T(8,128)(2,1)S(1)}, bf16[136,1024]{1,0:T(8,128)(2,1)S(1)}, u32[]{:S(2)}, u32[]{:S(2)}) %collective-permute-start) | collective-permute-done | bytes 278560 | tf_op jit(solution)/shard_map/ppermute | solution.py:600
  20.5 3.4 %collective-permute-start.4 = (bf16[136,1024]{1,0:T(8,128)(2,1)S(1)}, bf16[136,1024]{1,0:T(8,128)(2,1)S(1)}, u32[]{:S(2)}, u32[]{:S(2)}) collective-permute-start(bf16[136,1024]{1,0:T(8,128)(2,1)S(1)} %collective-permute-done.refs_2_), channel_id=1, source_target_pairs={{0,4},{1,5},{2,0},{3,1},{4,6},{5,7},{6,2},{7,3},{8,12},{9,13},{10,... | collective-permute-start | bytes 835592 | tf_op jit(solution)/shard_map/ppermute | solution.py:600
  24.0 1.6 %collective-permute-start.7 = (bf16[8,96,128]{2,1,0:T(8,128)(2,1)S(1)}, bf16[8,96,128]{2,1,0:T(8,128)(2,1)S(1)}, u32[]{:S(2)}, u32[]{:S(2)}) collective-permute-start(bf16[8,96,128]{2,1,0:T(8,128)(2,1)S(1)} %pad_maximum_fusion.1.refs_17_.refs_2_), channel_id=1, source_target_pairs={{0,16},{8,24},{16,0},{24,8},{1,17},{9,25},{17,1},{25,9},{2,18},{10... | collective-permute-start | bytes 589832 | tf_op jit(solution)/shard_map/ppermute | solution.py:562
  25.6 0.9 collective-permute-done.9.refs_5_
  26.4 1.5 %collective-permute-start.6 = (bf16[8,96,128]{2,1,0:T(8,128)(2,1)S(1)}, bf16[8,96,128]{2,1,0:T(8,128)(2,1)S(1)}, u32[]{:S(2)}, u32[]{:S(2)}) collective-permute-start(bf16[8,96,128]{2,1,0:T(8,128)(2,1)S(1)} %pad_maximum_fusion.1.refs_17_.refs_2_), channel_id=1, source_target_pairs={{0,8},{8,16},{16,24},{24,0},{1,9},{9,17},{17,25},{25,1},{2,10},{10... | collective-permute-start | bytes 589832 | tf_op jit(solution)/shard_map/ppermute | solution.py:562
  27.9 3.4 %collective-permute-start.12 = (bf16[136,1024]{1,0:T(8,128)(2,1)S(1)}, bf16[136,1024]{1,0:T(8,128)(2,1)S(1)}, u32[]{:S(2)}, u32[]{:S(2)}) collective-permute-start(bf16[136,1024]{1,0:T(8,128)(2,1)S(1)} %collective-permute-done.9.refs_5_), channel_id=1, source_target_pairs={{0,4},{1,5},{2,0},{3,1},{4,6},{5,7},{6,2},{7,3},{8,12},{9,13},{10,... | collective-permute-start | bytes 835592 | tf_op jit(solution)/shard_map/ppermute | solution.py:600
  31.4 1.0 %collective-permute-done.4.refs_4_ = bf16[136,1024]{1,0:T(8,128)(2,1)S(1)} collective-permute-done((bf16[136,1024]{1,0:T(8,128)(2,1)S(1)}, bf16[136,1024]{1,0:T(8,128)(2,1)S(1)}, u32[]{:S(2)}, u32[]{:S(2)}) %collective-permute-start.4) | collective-permute-done | bytes 278560 | tf_op jit(solution)/shard_map/ppermute | solution.py:600
  32.4 2.9 %collective-permute-done.7.refs_4_ = bf16[8,96,128]{2,1,0:T(8,128)(2,1)S(1)} collective-permute-done((bf16[8,96,128]{2,1,0:T(8,128)(2,1)S(1)}, bf16[8,96,128]{2,1,0:T(8,128)(2,1)S(1)}, u32[]{:S(2)}, u32[]{:S(2)}) %collective-permute-start.7) | collective-permute-done | bytes 196640 | tf_op jit(solution)/shard_map/ppermute | solution.py:562
  35.3 0.8 copy-done.24
  36.1 1.4 %collective-permute-start.11 = (bf16[136,1024]{1,0:T(8,128)(2,1)S(1)}, bf16[136,1024]{1,0:T(8,128)(2,1)S(1)}, u32[]{:S(2)}, u32[]{:S(2)}) collective-permute-start(bf16[136,1024]{1,0:T(8,128)(2,1)S(1)} %collective-permute-done.4.refs_4_), channel_id=1, source_target_pairs={{0,4},{1,5},{2,0},{3,1},{4,6},{5,7},{6,2},{7,3},{8,12},{9,13},{10,... | collective-permute-start | bytes 835592 | tf_op jit(solution)/shard_map/ppermute | solution.py:600
  37.9 0.7 copy-done.7
  38.8 6.3 %collective-permute-done.11.refs_6_ = bf16[136,1024]{1,0:T(8,128)(2,1)S(1)} collective-permute-done((bf16[136,1024]{1,0:T(8,128)(2,1)S(1)}, bf16[136,1024]{1,0:T(8,128)(2,1)S(1)}, u32[]{:S(2)}, u32[]{:S(2)}) %collective-permute-start.11) | collective-permute-done | bytes 278560 | tf_op jit(solution)/shard_map/ppermute | solution.py:600
  45.9 1.6 %pad_maximum_fusion = bf16[4,4,136,512]{3,2,1,0:T(8,128)(2,1)} fusion(bf16[1,4,136,512]{3,2,1,0:T(8,128)(2,1)S(1)} %get-tuple-element.89, bf16[1,4,136,512]{3,2,1,0:T(8,128)(2,1)S(1)} %get-tuple-element.88, bf16[1,4,136,512]{3,2,1,0:T(8,128)(2,1)S(1)} %get-tuple-element.91, bf16[1,4,136,512]{3,2,1,0:T(8,128)(2,1)S(1)} %get-tuple-element.90), kind=kLoop, calls=%fused_computation | loop fusion | flops 3342336 | bytes 4456448 | tf_op jit(solution)/shard_map/stack | solution.py:574
  47.5 0.7 copy-done.18
  48.2 3.6 %all-to-all-start = ((bf16[4,4,136,512]{3,2,1,0:T(8,128)(2,1)}), bf16[4,4,136,512]{3,2,1,0:T(8,128)(2,1)S(1)}, u32[]{:S(2)}, u32[]{:S(2)}) async-start(bf16[4,4,136,512]{3,2,1,0:T(8,128)(2,1)} %pad_maximum_fusion), calls=%async_computation | async-start | bytes 4456448 | tf_op jit(solution)/shard_map/all_to_all | solution.py:579
  52.5 1.0 %collective-permute-done.16.refs_15_ = bf16[136,1024]{1,0:T(8,128)(2,1)S(1)} collective-permute-done((bf16[136,1024]{1,0:T(8,128)(2,1)S(1)}, bf16[136,1024]{1,0:T(8,128)(2,1)S(1)}, u32[]{:S(2)}, u32[]{:S(2)}) %collective-permute-start.16) | collective-permute-done | bytes 278560 | tf_op jit(solution)/shard_map/ppermute | solution.py:567
  54.6 23.4 %expert_rows.1 = (bf16[2,16,40,384]{3,2,1,0:T(8,128)(2,1)}, f32[8,8,128]{2,1,0:T(8,128)}, bf16[16,64,96]{2,1,0:T(8,128)(2,1)}, bf16[16,64,96]{2,1,0:T(8,128)(2,1...) custom-call(bf16[136,1024]{1,0:T(8,128)(2,1)} %copy-done.2, bf16[136,1024]{1,0:T(8,128)(2,1)} %copy-done.1, ...), custom_call_target="tpu_custom_call" | custom-call | flops 6039797760 | bytes 33554432 | tf_op jit(solution)/shard_map/expert_rows/pallas_call | solution.py:611
  78.2 3.6 %all-to-all-start.1 = ((f32[8,8,128]{2,1,0:T(8,128)}), f32[8,8,128]{2,1,0:T(8,128)S(1)}, u32[]{:S(2)}, u32[]{:S(2)}) async-start(f32[8,8,128]{2,1,0:T(8,128)} %get-tuple-element.54), calls=%async_computation.1 | async-start | bytes 65536 | tf_op jit(solution)/shard_map/all_to_all | solution.py:646
  81.9 2.0 %collective-permute-start.17 = (bf16[16,64,96]{2,1,0:T(8,128)(2,1)}, bf16[16,64,96]{2,1,0:T(8,128)(2,1)S(1)}, u32[]{:S(2)}, u32[]{:S(2)}) collective-permute-start(bf16[16,64,96]{2,1,0:T(8,128)(2,1)} %get-tuple-element.55), channel_id=1, source_target_pairs={{0,8},{8,16},{16,24},{24,0},{1,9},{9,17},{17,25},{25,1},{2,10},{10... | collective-permute-start | bytes 589832 | tf_op jit(solution)/shard_map/ppermute | solution.py:562
  83.8 1.5 %collective-permute-start.18 = (bf16[16,64,96]{2,1,0:T(8,128)(2,1)}, bf16[16,64,96]{2,1,0:T(8,128)(2,1)S(1)}, u32[]{:S(2)}, u32[]{:S(2)}) collective-permute-start(bf16[16,64,96]{2,1,0:T(8,128)(2,1)} %get-tuple-element.56), channel_id=1, source_target_pairs={{0,16},{8,24},{16,0},{24,8},{1,17},{9,25},{17,1},{25,9},{2,18},{10... | collective-permute-start | bytes 589832 | tf_op jit(solution)/shard_map/ppermute | solution.py:562
  85.3 1.5 %collective-permute-start.19 = (bf16[16,64,96]{2,1,0:T(8,128)(2,1)}, bf16[16,64,96]{2,1,0:T(8,128)(2,1)S(1)}, u32[]{:S(2)}, u32[]{:S(2)}) collective-permute-start(bf16[16,64,96]{2,1,0:T(8,128)(2,1)} %get-tuple-element.57), channel_id=1, source_target_pairs={{0,24},{8,0},{16,8},{24,16},{1,25},{9,1},{17,9},{25,17},{2,26},{10... | collective-permute-start | bytes 589832 | tf_op jit(solution)/shard_map/ppermute | solution.py:562
  86.8 7.5 %adapter_columns.1 = f32[16,64,512]{2,1,0:T(8,128)} custom-call(bf16[4,4,136,512]{3,2,1,0:T(8,128)(2,1)} %copy-done, bf16[4,4,136,512]{3,2,1,0:T(8,128)(2,1)} %collective-permute-done.20.refs_1_, bf16[8,96,128]{2,1,0:T(8,128)(2,1)} %copy-done.12, bf16[8,96,128]{2,1,0:T(8,128)(2,1)} %copy-done.24, bf16[8,96,128]{2,1,0:T(8,128)(2,1)} %copy-done.23, ...), custom_call_target="tpu_custom_call" | custom-call | flops 3623878656 | bytes 6291456 | tf_op jit(solution)/shard_map/adapter_columns/pallas_call | solution.py:648
  94.3 3.2 %collective-permute-done.18 = bf16[16,64,96]{2,1,0:T(8,128)(2,1)S(1)} collective-permute-done((bf16[16,64,96]{2,1,0:T(8,128)(2,1)}, bf16[16,64,96]{2,1,0:T(8,128)(2,1)S(1)}, u32[]{:S(2)}, u32[]{:S(2)}) %collective-permute-start.18) | collective-permute-done | bytes 196640 | tf_op jit(solution)/shard_map/ppermute | solution.py:562
  98.4 1.0 convert_add_fusion
  (88 shorter events, 5.7 us)
Async XLA Ops:
  3.4 9.2 %collective-permute-start.3 = (bf16[136,1024]{1,0:T(8,128)(2,1)S(1)}, bf16[136,1024]{1,0:T(8,128)(2,1)S(1)}, u32[]{:S(2)}, u32[]{:S(2)}) collective-permute-start(bf16[136,1024]{1,0:T(8,128)(2,1)S(1)} %get-tuple-element.72.refs_1_), channel_id=1, source_target_pairs={{0,1},{1,0},{2,3},{3,2},{4,5},{5,4},{6,7},{7,6},{8,9},{9,8},{10,11... | collective-permute-start | bytes 835592 | tf_op jit(solution)/shard_map/ppermute | solution.py:567
  3.9 10.6 %collective-permute-start.2 = (bf16[136,1024]{1,0:T(8,128)(2,1)S(1)}, bf16[136,1024]{1,0:T(8,128)(2,1)S(1)}, u32[]{:S(2)}, u32[]{:S(2)}) collective-permute-start(bf16[136,1024]{1,0:T(8,128)(2,1)S(1)} %get-tuple-element.72.refs_1_), channel_id=1, source_target_pairs={{0,4},{1,5},{2,0},{3,1},{4,6},{5,7},{6,2},{7,3},{8,12},{9,13},{10,... | collective-permute-start | bytes 835592 | tf_op jit(solution)/shard_map/ppermute | solution.py:600
  7.5 10.4 %collective-permute-start.1 = (bf16[136,1024]{1,0:T(8,128)(2,1)S(1)}, bf16[136,1024]{1,0:T(8,128)(2,1)S(1)}, u32[]{:S(2)}, u32[]{:S(2)}) collective-permute-start(bf16[136,1024]{1,0:T(8,128)(2,1)S(1)} %get-tuple-element.73.refs_0_), channel_id=1, source_target_pairs={{0,1},{1,0},{2,3},{3,2},{4,5},{5,4},{6,7},{7,6},{8,9},{9,8},{10,11... | collective-permute-start | bytes 835592 | tf_op jit(solution)/shard_map/ppermute | solution.py:567
  7.7 12.8 %collective-permute-start = (bf16[136,1024]{1,0:T(8,128)(2,1)S(1)}, bf16[136,1024]{1,0:T(8,128)(2,1)S(1)}, u32[]{:S(2)}, u32[]{:S(2)}) collective-permute-start(bf16[136,1024]{1,0:T(8,128)(2,1)S(1)} %get-tuple-element.73.refs_0_), channel_id=1, source_target_pairs={{0,4},{1,5},{2,0},{3,1},{4,6},{5,7},{6,2},{7,3},{8,12},{9,13},{10,... | collective-permute-start | bytes 835592 | tf_op jit(solution)/shard_map/ppermute | solution.py:600
  10.0 28.8 %copy-start.12 = (bf16[8,96,128]{2,1,0:T(8,128)(2,1)}, bf16[8,96,128]{2,1,0:T(8,128)(2,1)S(1)}, u32[]{:S(2)}) copy-start(bf16[8,96,128]{2,1,0:T(8,128)(2,1)S(1)} %pad_maximum_fusion.1.refs_17_.refs_2_) | copy-start | bytes 589828
  10.0 22.4 %collective-permute-start.8 = (bf16[8,96,128]{2,1,0:T(8,128)(2,1)S(1)}, bf16[8,96,128]{2,1,0:T(8,128)(2,1)S(1)}, u32[]{:S(2)}, u32[]{:S(2)}) collective-permute-start(bf16[8,96,128]{2,1,0:T(8,128)(2,1)S(1)} %pad_maximum_fusion.1.refs_17_.refs_2_), channel_id=1, source_target_pairs={{0,24},{8,0},{16,8},{24,16},{1,25},{9,1},{17,9},{25,17},{2,26},{10... | collective-permute-start | bytes 589832 | tf_op jit(solution)/shard_map/ppermute | solution.py:562
  12.6 25.0 %copy-start.14 = (bf16[136,1024]{1,0:T(8,128)(2,1)}, bf16[136,1024]{1,0:T(8,128)(2,1)S(1)}, u32[]{:S(2)}) copy-start(bf16[136,1024]{1,0:T(8,128)(2,1)S(1)} %collective-permute-done.3.refs_9_) | copy-start | bytes 835588
  14.5 24.3 %copy-start.3 = (bf16[136,1024]{1,0:T(8,128)(2,1)}, bf16[136,1024]{1,0:T(8,128)(2,1)S(1)}, u32[]{:S(2)}) copy-start(bf16[136,1024]{1,0:T(8,128)(2,1)S(1)} %collective-permute-done.2.refs_3_) | copy-start | bytes 835588
  14.5 9.5 %collective-permute-start.10 = (bf16[136,1024]{1,0:T(8,128)(2,1)S(1)}, bf16[136,1024]{1,0:T(8,128)(2,1)S(1)}, u32[]{:S(2)}, u32[]{:S(2)}) collective-permute-start(bf16[136,1024]{1,0:T(8,128)(2,1)S(1)} %collective-permute-done.2.refs_3_), channel_id=1, source_target_pairs={{0,1},{1,0},{2,3},{3,2},{4,5},{5,4},{6,7},{7,6},{8,9},{9,8},{10,11... | collective-permute-start | bytes 835592 | tf_op jit(solution)/shard_map/ppermute | solution.py:567
  14.5 11.9 %collective-permute-start.9 = (bf16[136,1024]{1,0:T(8,128)(2,1)S(1)}, bf16[136,1024]{1,0:T(8,128)(2,1)S(1)}, u32[]{:S(2)}, u32[]{:S(2)}) collective-permute-start(bf16[136,1024]{1,0:T(8,128)(2,1)S(1)} %collective-permute-done.2.refs_3_), channel_id=1, source_target_pairs={{0,4},{1,5},{2,0},{3,1},{4,6},{5,7},{6,2},{7,3},{8,12},{9,13},{10,... | collective-permute-start | bytes 835592 | tf_op jit(solution)/shard_map/ppermute | solution.py:600
  17.9 20.9 %copy-start.15 = (bf16[136,1024]{1,0:T(8,128)(2,1)}, bf16[136,1024]{1,0:T(8,128)(2,1)S(1)}, u32[]{:S(2)}) copy-start(bf16[136,1024]{1,0:T(8,128)(2,1)S(1)} %collective-permute-done.1.refs_8_) | copy-start | bytes 835588
  20.5 18.4 %copy-start.4 = (bf16[136,1024]{1,0:T(8,128)(2,1)}, bf16[136,1024]{1,0:T(8,128)(2,1)S(1)}, u32[]{:S(2)}) copy-start(bf16[136,1024]{1,0:T(8,128)(2,1)S(1)} %collective-permute-done.refs_2_) | copy-start | bytes 835588
  20.5 7.5 %collective-permute-start.5 = (bf16[136,1024]{1,0:T(8,128)(2,1)S(1)}, bf16[136,1024]{1,0:T(8,128)(2,1)S(1)}, u32[]{:S(2)}, u32[]{:S(2)}) collective-permute-start(bf16[136,1024]{1,0:T(8,128)(2,1)S(1)} %collective-permute-done.refs_2_), channel_id=1, source_target_pairs={{0,1},{1,0},{2,3},{3,2},{4,5},{5,4},{6,7},{7,6},{8,9},{9,8},{10,11... | collective-permute-start | bytes 835592 | tf_op jit(solution)/shard_map/ppermute | solution.py:567
  20.5 11.9 %collective-permute-start.4 = (bf16[136,1024]{1,0:T(8,128)(2,1)S(1)}, bf16[136,1024]{1,0:T(8,128)(2,1)S(1)}, u32[]{:S(2)}, u32[]{:S(2)}) collective-permute-start(bf16[136,1024]{1,0:T(8,128)(2,1)S(1)} %collective-permute-done.refs_2_), channel_id=1, source_target_pairs={{0,4},{1,5},{2,0},{3,1},{4,6},{5,7},{6,2},{7,3},{8,12},{9,13},{10,... | collective-permute-start | bytes 835592 | tf_op jit(solution)/shard_map/ppermute | solution.py:600
  24.0 11.3 %collective-permute-start.7 = (bf16[8,96,128]{2,1,0:T(8,128)(2,1)S(1)}, bf16[8,96,128]{2,1,0:T(8,128)(2,1)S(1)}, u32[]{:S(2)}, u32[]{:S(2)}) collective-permute-start(bf16[8,96,128]{2,1,0:T(8,128)(2,1)S(1)} %pad_maximum_fusion.1.refs_17_.refs_2_), channel_id=1, source_target_pairs={{0,16},{8,24},{16,0},{24,8},{1,17},{9,25},{17,1},{25,9},{2,18},{10... | collective-permute-start | bytes 589832 | tf_op jit(solution)/shard_map/ppermute | solution.py:562
  26.4 18.7 %copy-start.5 = (bf16[136,1024]{1,0:T(8,128)(2,1)}, bf16[136,1024]{1,0:T(8,128)(2,1)S(1)}, u32[]{:S(2)}) copy-start(bf16[136,1024]{1,0:T(8,128)(2,1)S(1)} %collective-permute-done.9.refs_5_) | copy-start | bytes 835588
  26.4 8.9 %collective-permute-start.6 = (bf16[8,96,128]{2,1,0:T(8,128)(2,1)S(1)}, bf16[8,96,128]{2,1,0:T(8,128)(2,1)S(1)}, u32[]{:S(2)}, u32[]{:S(2)}) collective-permute-start(bf16[8,96,128]{2,1,0:T(8,128)(2,1)S(1)} %pad_maximum_fusion.1.refs_17_.refs_2_), channel_id=1, source_target_pairs={{0,8},{8,16},{16,24},{24,0},{1,9},{9,17},{17,25},{25,1},{2,10},{10... | collective-permute-start | bytes 589832 | tf_op jit(solution)/shard_map/ppermute | solution.py:562
  27.9 10.0 %collective-permute-start.12 = (bf16[136,1024]{1,0:T(8,128)(2,1)S(1)}, bf16[136,1024]{1,0:T(8,128)(2,1)S(1)}, u32[]{:S(2)}, u32[]{:S(2)}) collective-permute-start(bf16[136,1024]{1,0:T(8,128)(2,1)S(1)} %collective-permute-done.9.refs_5_), channel_id=1, source_target_pairs={{0,4},{1,5},{2,0},{3,1},{4,6},{5,7},{6,2},{7,3},{8,12},{9,13},{10,... | collective-permute-start | bytes 835592 | tf_op jit(solution)/shard_map/ppermute | solution.py:600
  32.4 12.9 %copy-start.6 = (bf16[136,1024]{1,0:T(8,128)(2,1)}, bf16[136,1024]{1,0:T(8,128)(2,1)S(1)}, u32[]{:S(2)}) copy-start(bf16[136,1024]{1,0:T(8,128)(2,1)S(1)} %collective-permute-done.4.refs_4_) | copy-start | bytes 835588
  32.4 15.1 %collective-permute-start.14 = (bf16[136,1024]{1,0:T(8,128)(2,1)S(1)}, bf16[136,1024]{1,0:T(8,128)(2,1)S(1)}, u32[]{:S(2)}, u32[]{:S(2)}) collective-permute-start(bf16[136,1024]{1,0:T(8,128)(2,1)S(1)} %collective-permute-done.9.refs_5_), channel_id=1, source_target_pairs={{0,1},{1,0},{2,3},{3,2},{4,5},{5,4},{6,7},{7,6},{8,9},{9,8},{10,11... | collective-permute-start | bytes 835592 | tf_op jit(solution)/shard_map/ppermute | solution.py:567
  32.4 12.9 %copy-start.22 = (bf16[8,96,128]{2,1,0:T(8,128)(2,1)}, bf16[8,96,128]{2,1,0:T(8,128)(2,1)S(1)}, u32[]{:S(2)}) copy-start(bf16[8,96,128]{2,1,0:T(8,128)(2,1)S(1)} %collective-permute-done.8.refs_5_) | copy-start | bytes 589828
  36.1 12.2 %collective-permute-start.13 = (bf16[136,1024]{1,0:T(8,128)(2,1)S(1)}, bf16[136,1024]{1,0:T(8,128)(2,1)}, u32[]{:S(2)}, u32[]{:S(2)}) collective-permute-start(bf16[136,1024]{1,0:T(8,128)(2,1)S(1)} %collective-permute-done.4.refs_4_), channel_id=1, source_target_pairs={{0,1},{1,0},{2,3},{3,2},{4,5},{5,4},{6,7},{7,6},{8,9},{9,8},{10,11... | collective-permute-start | bytes 835592 | tf_op jit(solution)/shard_map/ppermute | solution.py:567
  36.1 9.1 %collective-permute-start.11 = (bf16[136,1024]{1,0:T(8,128)(2,1)S(1)}, bf16[136,1024]{1,0:T(8,128)(2,1)S(1)}, u32[]{:S(2)}, u32[]{:S(2)}) collective-permute-start(bf16[136,1024]{1,0:T(8,128)(2,1)S(1)} %collective-permute-done.4.refs_4_), channel_id=1, source_target_pairs={{0,4},{1,5},{2,0},{3,1},{4,6},{5,7},{6,2},{7,3},{8,12},{9,13},{10,... | collective-permute-start | bytes 835592 | tf_op jit(solution)/shard_map/ppermute | solution.py:600
  48.2 30.0 %all-to-all-start = ((bf16[4,4,136,512]{3,2,1,0:T(8,128)(2,1)}), bf16[4,4,136,512]{3,2,1,0:T(8,128)(2,1)S(1)}, u32[]{:S(2)}, u32[]{:S(2)}) async-start(bf16[4,4,136,512]{3,2,1,0:T(8,128)(2,1)} %pad_maximum_fusion), calls=%async_computation | async-start | bytes 4456448 | tf_op jit(solution)/shard_map/all_to_all | solution.py:579
  51.9 1.6 %collective-permute-start.16 = (bf16[136,1024]{1,0:T(8,128)(2,1)S(1)}, bf16[136,1024]{1,0:T(8,128)(2,1)S(1)}, u32[]{:S(2)}, u32[]{:S(2)}) collective-permute-start(bf16[136,1024]{1,0:T(8,128)(2,1)S(1)} %copy-done.8), channel_id=1, source_target_pairs={{0,1},{1,0},{2,3},{3,2},{4,5},{5,4},{6,7},{7,6},{8,9},{9,8},{10,11... | collective-permute-start | bytes 835592 | tf_op jit(solution)/shard_map/ppermute | solution.py:567
  52.0 1.9 %collective-permute-start.15 = (bf16[136,1024]{1,0:T(8,128)(2,1)S(1)}, bf16[136,1024]{1,0:T(8,128)(2,1)S(1)}, u32[]{:S(2)}, u32[]{:S(2)}) collective-permute-start(bf16[136,1024]{1,0:T(8,128)(2,1)S(1)} %copy-done.10), channel_id=1, source_target_pairs={{0,1},{1,0},{2,3},{3,2},{4,5},{5,4},{6,7},{7,6},{8,9},{9,8},{10,11... | collective-permute-start | bytes 835592 | tf_op jit(solution)/shard_map/ppermute | solution.py:567
  78.2 8.5 %collective-permute-start.20 = (bf16[4,4,136,512]{3,2,1,0:T(8,128)(2,1)S(1)}, bf16[4,4,136,512]{3,2,1,0:T(8,128)(2,1)}, u32[]{:S(2)}, u32[]{:S(2)}) collective-permute-start(bf16[4,4,136,512]{3,2,1,0:T(8,128)(2,1)S(1)} %all-to-all-done.refs_0_), channel_id=1, source_target_pairs={{0,1},{1,0},{2,3},{3,2},{4,5},{5,4},{6,7},{7,6},{8,9},{9,8},{10,11... | collective-permute-start | bytes 6684680 | tf_op jit(solution)/shard_map/ppermute | solution.py:567
  78.2 16.0 %all-to-all-start.1 = ((f32[8,8,128]{2,1,0:T(8,128)}), f32[8,8,128]{2,1,0:T(8,128)S(1)}, u32[]{:S(2)}, u32[]{:S(2)}) async-start(f32[8,8,128]{2,1,0:T(8,128)} %get-tuple-element.54), calls=%async_computation.1 | async-start | bytes 65536 | tf_op jit(solution)/shard_map/all_to_all | solution.py:646
  81.9 16.5 %copy-start.21 = (bf16[16,64,96]{2,1,0:T(8,128)(2,1)S(1)}, bf16[16,64,96]{2,1,0:T(8,128)(2,1)}, u32[]{:S(2)}) copy-start(bf16[16,64,96]{2,1,0:T(8,128)(2,1)} %get-tuple-element.63) | copy-start | bytes 589828
  81.9 12.4 %collective-permute-start.17 = (bf16[16,64,96]{2,1,0:T(8,128)(2,1)}, bf16[16,64,96]{2,1,0:T(8,128)(2,1)S(1)}, u32[]{:S(2)}, u32[]{:S(2)}) collective-permute-start(bf16[16,64,96]{2,1,0:T(8,128)(2,1)} %get-tuple-element.55), channel_id=1, source_target_pairs={{0,8},{8,16},{16,24},{24,0},{1,9},{9,17},{17,25},{25,1},{2,10},{10... | collective-permute-start | bytes 589832 | tf_op jit(solution)/shard_map/ppermute | solution.py:562
  83.8 13.6 %collective-permute-start.18 = (bf16[16,64,96]{2,1,0:T(8,128)(2,1)}, bf16[16,64,96]{2,1,0:T(8,128)(2,1)S(1)}, u32[]{:S(2)}, u32[]{:S(2)}) collective-permute-start(bf16[16,64,96]{2,1,0:T(8,128)(2,1)} %get-tuple-element.56), channel_id=1, source_target_pairs={{0,16},{8,24},{16,0},{24,8},{1,17},{9,25},{17,1},{25,9},{2,18},{10... | collective-permute-start | bytes 589832 | tf_op jit(solution)/shard_map/ppermute | solution.py:562
  85.3 12.5 %collective-permute-start.19 = (bf16[16,64,96]{2,1,0:T(8,128)(2,1)}, bf16[16,64,96]{2,1,0:T(8,128)(2,1)S(1)}, u32[]{:S(2)}, u32[]{:S(2)}) collective-permute-start(bf16[16,64,96]{2,1,0:T(8,128)(2,1)} %get-tuple-element.57), channel_id=1, source_target_pairs={{0,24},{8,0},{16,8},{24,16},{1,25},{9,1},{17,9},{25,17},{2,26},{10... | collective-permute-start | bytes 589832 | tf_op jit(solution)/shard_map/ppermute | solution.py:562
  (16 other events, 70.3 us)

commit v8 on v7

--- a/solution.py
+++ b/solution.py
@@ -569,7 +569,9 @@
     def exchange_columns(chosen):
         def columns(pieces, g):
             at = g * share % part
-            return pieces[g * share // part][:, at : at + share]
+            own = pieces[g * share // part][:, at : at + share]
+            line = lax.broadcasted_iota(jnp.int32, own.shape, 0)
+            return jnp.where(line < span, own, pieces[-1][:, :share])
 
         return jnp.stack(
             [jnp.stack([columns(pieces, g) for pieces in chosen]) for g in range(group_count)]
@@ -579,30 +581,50 @@
         return lax.all_to_all(array, "dp", split_axis=0, concat_axis=0, tiled=True)
 
     others = range(1, group_count)
+    lines = 2 * top * span // share
+    extra = -(-lines // 8) * 8
+    part_rows, chosen_expert_index = lax.optimization_barrier(
+        (
+            jnp.pad(output_gradient[:, :part], ((0, extra), (0, 0))),
+            chosen_expert_index,
+        )
+    )
     names = jnp.concatenate(
         [chosen_expert_index.T.astype(jnp.bfloat16), routing_gate_weight.T], axis=0
     )
-    lines = 2 * top * span // share
-    names = jnp.tile(names.reshape(lines, share), (1, group_count))
-    extra = -(-lines // 8) * 8
-    sent = jnp.concatenate(
-        [output_gradient, jnp.pad(names, ((0, extra - lines), (0, 0)))], axis=0
-    )
-
-    near, far = [[sent[:, c * part : (c + 1) * part] for c in range(chunks)]], []
+    names = jnp.tile(names.reshape(lines, share), (1, group_count // chunks))
+    below = jnp.pad(names, ((0, extra - lines), (0, 0)))
+    last = jnp.concatenate([output_gradient[:, width - part :], below], axis=0)
+    sent = [part_rows, last] if chunks == 2 else [last]
+
+    near, far = [sent], []
     u_all = [shift_groups(u, s) for s in others]
+    halves = [(step, c) for step in range(1, pairs - 1) for c in range(chunks)][1:]
+    moments = [halves[min(k, len(halves) - 1)] for k in range(len(u_all)) if halves]
     for step in range(pairs - 1):
+        here = near[step]
+        if step > 1:
+            tied = [
+                lax.optimization_barrier((here[c], [shard[c] for shard in far]))
+                for c in range(chunks)
+            ]
+            here = [a for a, _ in tied]
+            far = [[b[k] for _, b in tied] for k in range(len(far))]
+        for k, (at, c) in enumerate(moments):
+            if at == step:
+                here[c], u_all[k] = lax.optimization_barrier((here[c], u_all[k]))
+        near[step] = here
+        near.append([lax.ppermute(piece, "expert", ring) for piece in here])
         if step:
-            tied = [lax.optimization_barrier(pair) for pair in zip(near[step], far[-1])]
-            near[step], far[-1] = [a for a, _ in tied], [b for _, b in tied]
-        if step == pairs - 2:
-            near[step][0], u_all = lax.optimization_barrier((near[step][0], u_all))
-        near.append([lax.ppermute(piece, "expert", ring) for piece in near[step]])
-        far.append([swap_partners(piece) for piece in near[step]])
+            far.append([swap_partners(piece) for piece in here])
+        else:
+            tied = [lax.optimization_barrier(pair) for pair in zip(here, near[1])]
+            near[1] = [b for _, b in tied]
+            far.append([swap_partners(a) for a, _ in tied])
+    far.append([swap_partners(piece) for piece in near[-1]])
     columns = exchange_columns(near)
-    columns, far[-1] = lax.optimization_barrier((columns, far[-1]))
+    columns, far[-2:] = lax.optimization_barrier((columns, far[-2:]))
     columns = across_groups(columns)
-    far.append([swap_partners(piece) for piece in near[-1]])
     pieces = [piece for shard in near + far for piece in shard]
 
     vmem = pl.BlockSpec(memory_space=pltpu.VMEM)
@@ -631,7 +653,7 @@
             pltpu.SemaphoreType.DMA((experts,)),
             pltpu.SemaphoreType.DMA((group_count,)),
         ],
-        compiler_params=pltpu.CompilerParams(vmem_limit_bytes=58 * 1024 * 1024),
+        compiler_params=pltpu.CompilerParams(vmem_limit_bytes=52 * 1024 * 1024),
         cost_estimate=pl.CostEstimate(
             flops=2 * experts * micro * padded * width * (units + rank + sources * block),
             bytes_accessed=2 * experts * width * (units + rank) + 2 * sources * span * width,

time: 99.8 us -> 103 us (1.032)
  waiting for transfers between devices: 21.2 us -> 26.8 us
  starting transfers between devices: 35.9 us -> 33.5 us
  matrix products: 0.5 us -> 1.91 us
  Pallas kernels: 30.9 us -> 29.8 us
    all_to_all x1, waiting for transfers between devices: 0.22 us -> 5.35 us  [across_groups(): return lax.all_to_all(array, 'dp', split_axis=0, concat_axis=0, tiled=True)]
    ppermute x6, starting transfers between devices: 16.9 us -> 14.6 us  [local_by_tokens(): near.append([lax.ppermute(piece, 'expert', ring) for piece in here])]
    ppermute x6, starting transfers between devices: 10.5 us -> 8.24 us  [shift_groups(): lax.ppermute(array, 'dp', [(d, (d + by) % group_count) for d in range(gro...]
    ppermute x9, waiting for transfers between devices: 1.46 us -> 0.02 us  [swap_partners(): return lax.ppermute(array, 'expert', swap)]
    dot_general x1, matrix products: 0.5 us -> 1.91 us  [local_by_tokens(): jnp.einsum('mesk,exk->emsx', hidden, amap, preferred_element_type=jnp.flo...]
    pallas_call x1, Pallas kernels: 23.4 us -> 22.2 us  [local_by_tokens(): pl.pallas_call(functools.partial(expert_kernel, capacity, group_count, so...]
    concatenate x1, other arithmetic: 1.09 us -> 0.02 us  [local_by_tokens(): last = jnp.concatenate([output_gradient[:, width - part:], below], axis=0)]
    unnamed x52 -> x38, local copies, waits for them, and re-layouts: 3.52 us -> 3.29 us
  transfers between devices with their start and end apart: 23 -> 23, of which waited for: 12 -> 8; matrix products, arithmetic and copies ran while one was open for 3% -> 4% of each run, Pallas kernels for 31% -> 29%
where the time goes in v8:
time: 103 us
  starting transfers between devices  33.5 us (33%)
  Pallas kernels  29.8 us (29%)
  waiting for transfers between devices  26.8 us (26%)
  other arithmetic  5.33 us (5%)
  local copies, waits for them, and re-layouts  4.45 us (4%)
  matrix products  1.91 us (2%)
    pallas_call x1, Pallas kernels, local_by_tokens(): pl.pallas_call(functools.partial(expert_kernel, capacity, group_count, so...  22.2 us
    ppermute x6, starting transfers between devices, local_by_tokens(): near.append([lax.ppermute(piece, 'expert', ring) for piece in here])  14.6 us
    ppermute x6, waiting for transfers between devices, local_by_tokens(): near.append([lax.ppermute(piece, 'expert', ring) for piece in here])  14 us
    ppermute x6, starting transfers between devices, shift_groups(): lax.ppermute(array, 'dp', [(d, (d + by) % group_count) for d in range(gro...  8.24 us
    pallas_call x1, Pallas kernels, local_by_tokens(): pl.pallas_call(functools.partial(adapter_kernel, capacity, micro, span, t...  7.52 us
    ppermute x6, waiting for transfers between devices, shift_groups(): lax.ppermute(array, 'dp', [(d, (d + by) % group_count) for d in range(gro...  7.41 us
    all_to_all x1, waiting for transfers between devices, across_groups(): return lax.all_to_all(array, 'dp', split_axis=0, concat_axis=0, tiled=True)  5.35 us
    all_to_all x1, starting transfers between devices, local_by_tokens(): lax.all_to_all(routed, 'expert', split_axis=0, concat_axis=0, tiled=True)  4.66 us
  transfers between devices with their start and end apart: 23, of which 8 were waited for; matrix products, arithmetic and copies ran while one was open for 4% of the time, Pallas kernels for 29%

profile of v8, /device:TPU:0, one launch (start us, length us, event | category | flops | bytes accessed | tf_op | source)
XLA Modules:
  0.0 102.7 jit_solution(7844421350407647557)
XLA Ops:
  0.6 1.1 %fusion.8 = (bf16[128,1024]{1,0:T(8,128)(2,1)S(1)}, bf16[128,1024]{1,0:T(8,128)(2,1)S(1)}) fusion(bf16[128,2048]{1,0:T(8,128)(2,1)} %param.7), kind=kLoop, calls=%fused_computation.39 | loop fusion | bytes 1048576 | tf_op jit(solution)/shard_map/slice | solution.py:597
  1.7 0.7 convert_bitcast_fusion
  2.4 0.7 pad_maximum_fusion.2
  3.2 4.1 %collective-permute-start.1 = (bf16[136,1024]{1,0:T(8,128)(2,1)S(1)}, bf16[136,1024]{1,0:T(8,128)(2,1)S(1)}, u32[]{:S(2)}, u32[]{:S(2)}) collective-permute-start(bf16[136,1024]{1,0:T(8,128)(2,1)S(1)} %fusion.3.refs_1_), channel_id=1, source_target_pairs={{0,4},{1,5},{2,0},{3,1},{4,6},{5,7},{6,2},{7,3},{8,12},{9,13},{10,... | collective-permute-start | bytes 835592 | tf_op jit(solution)/shard_map/ppermute | solution.py:617
  7.3 1.9 %convolution_convert_fusion = bf16[16,2,40,64]{3,2,1,0:T(8,128)(2,1)S(1)} fusion(bf16[2,16,40,384]{3,2,1,0:T(8,128)(2,1)} %refs_16_.1, bf16[16,384,64]{1,2,0:T(8,128)(2,1)} %param.12), kind=kOutput, calls=%fused_computation.1 | convolution fusion | flops 62996480 | bytes 1933312 | tf_op jit(solution)/shard_map/mesk,exk->emsx/dot_general | solution.py:554
  9.4 1.5 %collective-permute-start.2 = (bf16[8,96,128]{2,1,0:T(8,128)(2,1)S(1)}, bf16[8,96,128]{2,1,0:T(8,128)(2,1)S(1)}, u32[]{:S(2)}, u32[]{:S(2)}) collective-permute-start(bf16[8,96,128]{2,1,0:T(8,128)(2,1)S(1)} %pad_maximum_fusion.1.refs_17_.refs_2_), channel_id=1, source_target_pairs={{0,8},{8,16},{16,24},{24,0},{1,9},{9,17},{17,25},{25,1},{2,10},{10... | collective-permute-start | bytes 589832 | tf_op jit(solution)/shard_map/ppermute | solution.py:562
  10.9 1.6 %collective-permute-start = (bf16[136,1024]{1,0:T(8,128)(2,1)S(1)}, bf16[136,1024]{1,0:T(8,128)(2,1)S(1)}, u32[]{:S(2)}, u32[]{:S(2)}) collective-permute-start(bf16[136,1024]{1,0:T(8,128)(2,1)S(1)} %pad.12.refs_0_), channel_id=1, source_target_pairs={{0,4},{1,5},{2,0},{3,1},{4,6},{5,7},{6,2},{7,3},{8,12},{9,13},{10,... | collective-permute-start | bytes 835592 | tf_op jit(solution)/shard_map/ppermute | solution.py:617
  12.5 1.8 %collective-permute-done.1.refs_3_ = bf16[136,1024]{1,0:T(8,128)(2,1)S(1)} collective-permute-done((bf16[136,1024]{1,0:T(8,128)(2,1)S(1)}, bf16[136,1024]{1,0:T(8,128)(2,1)S(1)}, u32[]{:S(2)}, u32[]{:S(2)}) %collective-permute-start.1) | collective-permute-done | bytes 278560 | tf_op jit(solution)/shard_map/ppermute | solution.py:617
  14.3 2.4 %collective-permute-done.2.refs_3_ = bf16[8,96,128]{2,1,0:T(8,128)(2,1)S(1)} collective-permute-done((bf16[8,96,128]{2,1,0:T(8,128)(2,1)S(1)}, bf16[8,96,128]{2,1,0:T(8,128)(2,1)S(1)}, u32[]{:S(2)}, u32[]{:S(2)}) %collective-permute-start.2) | collective-permute-done | bytes 196640 | tf_op jit(solution)/shard_map/ppermute | solution.py:562
  16.7 0.7 copy-done.15
  17.4 1.6 %collective-permute-start.7 = (bf16[136,1024]{1,0:T(8,128)(2,1)S(1)}, bf16[136,1024]{1,0:T(8,128)(2,1)S(1)}, u32[]{:S(2)}, u32[]{:S(2)}) collective-permute-start(bf16[136,1024]{1,0:T(8,128)(2,1)S(1)} %collective-permute-done.1.refs_3_), channel_id=1, source_target_pairs={{0,4},{1,5},{2,0},{3,1},{4,6},{5,7},{6,2},{7,3},{8,12},{9,13},{10,... | collective-permute-start | bytes 835592 | tf_op jit(solution)/shard_map/ppermute | solution.py:617
  19.5 0.8 collective-permute-done.refs_2_
  20.3 3.4 %collective-permute-start.3 = (bf16[136,1024]{1,0:T(8,128)(2,1)S(1)}, bf16[136,1024]{1,0:T(8,128)(2,1)S(1)}, u32[]{:S(2)}, u32[]{:S(2)}) collective-permute-start(bf16[136,1024]{1,0:T(8,128)(2,1)S(1)} %collective-permute-done.refs_2_), channel_id=1, source_target_pairs={{0,4},{1,5},{2,0},{3,1},{4,6},{5,7},{6,2},{7,3},{8,12},{9,13},{10,... | collective-permute-start | bytes 835592 | tf_op jit(solution)/shard_map/ppermute | solution.py:617
  23.7 3.3 %collective-permute-done.7.refs_5_ = bf16[136,1024]{1,0:T(8,128)(2,1)S(1)} collective-permute-done((bf16[136,1024]{1,0:T(8,128)(2,1)S(1)}, bf16[136,1024]{1,0:T(8,128)(2,1)S(1)}, u32[]{:S(2)}, u32[]{:S(2)}) %collective-permute-start.7) | collective-permute-done | bytes 278560 | tf_op jit(solution)/shard_map/ppermute | solution.py:617
  27.0 1.8 %collective-permute-start.10 = (bf16[8,96,128]{2,1,0:T(8,128)(2,1)S(1)}, bf16[8,96,128]{2,1,0:T(8,128)(2,1)S(1)}, u32[]{:S(2)}, u32[]{:S(2)}) collective-permute-start(bf16[8,96,128]{2,1,0:T(8,128)(2,1)S(1)} %pad_maximum_fusion.1.refs_17_.refs_2_), channel_id=1, source_target_pairs={{0,24},{8,0},{16,8},{24,16},{1,25},{9,1},{17,9},{25,17},{2,26},{10... | collective-permute-start | bytes 589832 | tf_op jit(solution)/shard_map/ppermute | solution.py:562
  29.3 5.0 %collective-permute-done.10.refs_5_ = bf16[8,96,128]{2,1,0:T(8,128)(2,1)S(1)} collective-permute-done((bf16[8,96,128]{2,1,0:T(8,128)(2,1)S(1)}, bf16[8,96,128]{2,1,0:T(8,128)(2,1)S(1)}, u32[]{:S(2)}, u32[]{:S(2)}) %collective-permute-start.10) | collective-permute-done | bytes 196640 | tf_op jit(solution)/shard_map/ppermute | solution.py:562
  34.3 2.7 %collective-permute-start.12 = (bf16[136,1024]{1,0:T(8,128)(2,1)S(1)}, bf16[136,1024]{1,0:T(8,128)(2,1)S(1)}, u32[]{:S(2)}, u32[]{:S(2)}) collective-permute-start(bf16[136,1024]{1,0:T(8,128)(2,1)S(1)} %collective-permute-done.7.refs_5_), channel_id=1, source_target_pairs={{0,4},{1,5},{2,0},{3,1},{4,6},{5,7},{6,2},{7,3},{8,12},{9,13},{10,... | collective-permute-start | bytes 835592 | tf_op jit(solution)/shard_map/ppermute | solution.py:617
  37.0 0.8 copy-done.10
  37.9 0.7 copy-done.17
  38.5 1.3 %collective-permute-start.11 = (bf16[136,1024]{1,0:T(8,128)(2,1)S(1)}, bf16[136,1024]{1,0:T(8,128)(2,1)S(1)}, u32[]{:S(2)}, u32[]{:S(2)}) collective-permute-start(bf16[136,1024]{1,0:T(8,128)(2,1)S(1)} %collective-permute-done.3.refs_4_), channel_id=1, source_target_pairs={{0,4},{1,5},{2,0},{3,1},{4,6},{5,7},{6,2},{7,3},{8,12},{9,13},{10,... | collective-permute-start | bytes 835592 | tf_op jit(solution)/shard_map/ppermute | solution.py:617
  40.6 3.5 %collective-permute-done.12.refs_7_ = bf16[136,1024]{1,0:T(8,128)(2,1)S(1)} collective-permute-done((bf16[136,1024]{1,0:T(8,128)(2,1)S(1)}, bf16[136,1024]{1,0:T(8,128)(2,1)S(1)}, u32[]{:S(2)}, u32[]{:S(2)}) %collective-permute-start.12) | collective-permute-done | bytes 278560 | tf_op jit(solution)/shard_map/ppermute | solution.py:617
  44.1 4.6 %collective-permute-done.11.refs_6_ = bf16[136,1024]{1,0:T(8,128)(2,1)S(1)} collective-permute-done((bf16[136,1024]{1,0:T(8,128)(2,1)S(1)}, bf16[136,1024]{1,0:T(8,128)(2,1)S(1)}, u32[]{:S(2)}, u32[]{:S(2)}) %collective-permute-start.11) | collective-permute-done | bytes 278560 | tf_op jit(solution)/shard_map/ppermute | solution.py:617
  49.8 1.7 %pad_maximum_fusion = bf16[4,4,136,512]{3,2,1,0:T(8,128)(2,1)} fusion(bf16[1,4,136,512]{3,2,1,0:T(8,128)(2,1)S(1)} %get-tuple-element.115, bf16[1,4,136,512]{3,2,1,0:T(8,128)(2,1)S(1)} %get-tuple-element.114, bf16[1,4,136,512]{3,2,1,0:T(8,128)(2,1)S(1)} %get-tuple-element.113, bf16[1,4,136,512]{3,2,1,0:T(8,128)(2,1)S(1)} %get-tuple-element.112), kind=kLoop, calls=%fused_computation | loop fusion | flops 3342336 | bytes 4456448 | tf_op jit(solution)/shard_map/stack | solution.py:576
  51.5 0.7 copy-done.11
  52.2 4.6 %all-to-all-start = ((bf16[4,4,136,512]{3,2,1,0:T(8,128)(2,1)}), bf16[4,4,136,512]{3,2,1,0:T(8,128)(2,1)}, u32[]{:S(2)}, u32[]{:S(2)}) async-start(bf16[4,4,136,512]{3,2,1,0:T(8,128)(2,1)} %pad_maximum_fusion), calls=%async_computation | async-start | bytes 4456448 | tf_op jit(solution)/shard_map/all_to_all | solution.py:581
  56.9 22.2 %expert_rows.1 = (bf16[2,16,40,384]{3,2,1,0:T(8,128)(2,1)}, f32[8,8,128]{2,1,0:T(8,128)}, bf16[16,64,96]{2,1,0:T(8,128)(2,1)S(1)}, bf16[16,64,96]{2,1,0:T(8,128)...) custom-call(bf16[136,1024]{1,0:T(8,128)(2,1)S(1)} %pad.12.refs_0_, ...), custom_call_target="tpu_custom_call" | custom-call | flops 6039797760 | bytes 33554432 | tf_op jit(solution)/shard_map/expert_rows/pallas_call | solution.py:633
  79.2 5.3 %all-to-all-done.refs_0_ = bf16[4,4,136,512]{3,2,1,0:T(8,128)(2,1)} async-done(((bf16[4,4,136,512]{3,2,1,0:T(8,128)(2,1)}), bf16[4,4,136,512]{3,2,1,0:T(8,128)(2,1)}, u32[]{:S(2)}, u32[]{:S(2)}) %all-to-all-start) | async-done | bytes 2228256 | tf_op jit(solution)/shard_map/all_to_all | solution.py:581
  84.5 1.5 %collective-permute-start.17 = (bf16[16,64,96]{2,1,0:T(8,128)(2,1)S(1)}, bf16[16,64,96]{2,1,0:T(8,128)(2,1)S(1)}, u32[]{:S(2)}, u32[]{:S(2)}) collective-permute-start(bf16[16,64,96]{2,1,0:T(8,128)(2,1)S(1)} %get-tuple-element.71), channel_id=1, source_target_pairs={{0,8},{8,16},{16,24},{24,0},{1,9},{9,17},{17,25},{25,1},{2,10},{10... | collective-permute-start | bytes 589832 | tf_op jit(solution)/shard_map/ppermute | solution.py:562
  86.5 2.4 %collective-permute-start.19 = (bf16[16,64,96]{2,1,0:T(8,128)(2,1)S(1)}, bf16[16,64,96]{2,1,0:T(8,128)(2,1)S(1)}, u32[]{:S(2)}, u32[]{:S(2)}) collective-permute-start(bf16[16,64,96]{2,1,0:T(8,128)(2,1)S(1)} %get-tuple-element.73), channel_id=1, source_target_pairs={{0,24},{8,0},{16,8},{24,16},{1,25},{9,1},{17,9},{25,17},{2,26},{10... | collective-permute-start | bytes 589832 | tf_op jit(solution)/shard_map/ppermute | solution.py:562
  88.9 4.7 %all-to-all-start.1 = ((f32[8,8,128]{2,1,0:T(8,128)}), f32[8,8,128]{2,1,0:T(8,128)S(1)}, u32[]{:S(2)}, u32[]{:S(2)}) async-start(f32[8,8,128]{2,1,0:T(8,128)} %get-tuple-element.70), calls=%async_computation.1 | async-start | bytes 65536 | tf_op jit(solution)/shard_map/all_to_all | solution.py:668
  93.6 7.5 %adapter_columns.1 = f32[16,64,512]{2,1,0:T(8,128)} custom-call(bf16[4,4,136,512]{3,2,1,0:T(8,128)(2,1)} %all-to-all-done.refs_0_, bf16[4,4,136,512]{3,2,1,0:T(8,128)(2,1)} %collective-permute-done.20.refs_1_, bf16[8,96,128]{2,1,0:T(8,128)(2,1)} %copy-done, bf16[8,96,128]{2,1,0:T(8,128)(2,1)} %copy-done.15, bf16[8,96,128]{2,1,0:T(8,128)(2,1)} %copy-done.17, ...), custom_call_target="tpu_custom_call" | custom-call | flops 3623878656 | bytes 6291456 | tf_op jit(solution)/shard_map/adapter_columns/pallas_call | solution.py:670
  101.8 1.0 convert_add_fusion
  (71 shorter events, 4.3 us)
Async XLA Ops:
  3.2 11.2 %collective-permute-start.1 = (bf16[136,1024]{1,0:T(8,128)(2,1)S(1)}, bf16[136,1024]{1,0:T(8,128)(2,1)S(1)}, u32[]{:S(2)}, u32[]{:S(2)}) collective-permute-start(bf16[136,1024]{1,0:T(8,128)(2,1)S(1)} %fusion.3.refs_1_), channel_id=1, source_target_pairs={{0,4},{1,5},{2,0},{3,1},{4,6},{5,7},{6,2},{7,3},{8,12},{9,13},{10,... | collective-permute-start | bytes 835592 | tf_op jit(solution)/shard_map/ppermute | solution.py:617
  9.4 47.5 %copy-start = (bf16[8,96,128]{2,1,0:T(8,128)(2,1)}, bf16[8,96,128]{2,1,0:T(8,128)(2,1)S(1)}, u32[]{:S(2)}) copy-start(bf16[8,96,128]{2,1,0:T(8,128)(2,1)S(1)} %pad_maximum_fusion.1.refs_17_.refs_2_) | copy-start | bytes 589828
  9.4 7.3 %collective-permute-start.2 = (bf16[8,96,128]{2,1,0:T(8,128)(2,1)S(1)}, bf16[8,96,128]{2,1,0:T(8,128)(2,1)S(1)}, u32[]{:S(2)}, u32[]{:S(2)}) collective-permute-start(bf16[8,96,128]{2,1,0:T(8,128)(2,1)S(1)} %pad_maximum_fusion.1.refs_17_.refs_2_), channel_id=1, source_target_pairs={{0,8},{8,16},{16,24},{24,0},{1,9},{9,17},{17,25},{25,1},{2,10},{10... | collective-permute-start | bytes 589832 | tf_op jit(solution)/shard_map/ppermute | solution.py:562
  10.9 9.3 %collective-permute-start = (bf16[136,1024]{1,0:T(8,128)(2,1)S(1)}, bf16[136,1024]{1,0:T(8,128)(2,1)S(1)}, u32[]{:S(2)}, u32[]{:S(2)}) collective-permute-start(bf16[136,1024]{1,0:T(8,128)(2,1)S(1)} %pad.12.refs_0_), channel_id=1, source_target_pairs={{0,4},{1,5},{2,0},{3,1},{4,6},{5,7},{6,2},{7,3},{8,12},{9,13},{10,... | collective-permute-start | bytes 835592 | tf_op jit(solution)/shard_map/ppermute | solution.py:617
  14.3 34.5 %copy-start.1 = (bf16[136,1024]{1,0:T(8,128)(2,1)}, bf16[136,1024]{1,0:T(8,128)(2,1)S(1)}, u32[]{:S(2)}) copy-start(bf16[136,1024]{1,0:T(8,128)(2,1)S(1)} %collective-permute-done.1.refs_3_) | copy-start | bytes 835588
  17.4 9.6 %collective-permute-start.7 = (bf16[136,1024]{1,0:T(8,128)(2,1)S(1)}, bf16[136,1024]{1,0:T(8,128)(2,1)S(1)}, u32[]{:S(2)}, u32[]{:S(2)}) collective-permute-start(bf16[136,1024]{1,0:T(8,128)(2,1)S(1)} %collective-permute-done.1.refs_3_), channel_id=1, source_target_pairs={{0,4},{1,5},{2,0},{3,1},{4,6},{5,7},{6,2},{7,3},{8,12},{9,13},{10,... | collective-permute-start | bytes 835592 | tf_op jit(solution)/shard_map/ppermute | solution.py:617
  19.0 8.0 %collective-permute-start.9 = (bf16[136,1024]{1,0:T(8,128)(2,1)S(1)}, bf16[136,1024]{1,0:T(8,128)(2,1)S(1)}, u32[]{:S(2)}, u32[]{:S(2)}) collective-permute-start(bf16[136,1024]{1,0:T(8,128)(2,1)S(1)} %collective-permute-done.1.refs_3_), channel_id=1, source_target_pairs={{0,1},{1,0},{2,3},{3,2},{4,5},{5,4},{6,7},{7,6},{8,9},{9,8},{10,11... | collective-permute-start | bytes 835592 | tf_op jit(solution)/shard_map/ppermute | solution.py:567
  19.0 9.8 %collective-permute-start.8 = (bf16[136,1024]{1,0:T(8,128)(2,1)S(1)}, bf16[136,1024]{1,0:T(8,128)(2,1)S(1)}, u32[]{:S(2)}, u32[]{:S(2)}) collective-permute-start(bf16[136,1024]{1,0:T(8,128)(2,1)S(1)} %fusion.3.refs_1_), channel_id=1, source_target_pairs={{0,1},{1,0},{2,3},{3,2},{4,5},{5,4},{6,7},{7,6},{8,9},{9,8},{10,11... | collective-permute-start | bytes 835592 | tf_op jit(solution)/shard_map/ppermute | solution.py:567
  20.3 28.6 %copy-start.2 = (bf16[136,1024]{1,0:T(8,128)(2,1)}, bf16[136,1024]{1,0:T(8,128)(2,1)S(1)}, u32[]{:S(2)}) copy-start(bf16[136,1024]{1,0:T(8,128)(2,1)S(1)} %collective-permute-done.refs_2_) | copy-start | bytes 835588
  20.3 16.7 %collective-permute-start.3 = (bf16[136,1024]{1,0:T(8,128)(2,1)S(1)}, bf16[136,1024]{1,0:T(8,128)(2,1)S(1)}, u32[]{:S(2)}, u32[]{:S(2)}) collective-permute-start(bf16[136,1024]{1,0:T(8,128)(2,1)S(1)} %collective-permute-done.refs_2_), channel_id=1, source_target_pairs={{0,4},{1,5},{2,0},{3,1},{4,6},{5,7},{6,2},{7,3},{8,12},{9,13},{10,... | collective-permute-start | bytes 835592 | tf_op jit(solution)/shard_map/ppermute | solution.py:617
  23.7 13.3 %collective-permute-start.5 = (bf16[136,1024]{1,0:T(8,128)(2,1)S(1)}, bf16[136,1024]{1,0:T(8,128)(2,1)S(1)}, u32[]{:S(2)}, u32[]{:S(2)}) collective-permute-start(bf16[136,1024]{1,0:T(8,128)(2,1)S(1)} %collective-permute-done.refs_2_), channel_id=1, source_target_pairs={{0,1},{1,0},{2,3},{3,2},{4,5},{5,4},{6,7},{7,6},{8,9},{9,8},{10,11... | collective-permute-start | bytes 835592 | tf_op jit(solution)/shard_map/ppermute | solution.py:567
  27.0 21.9 %copy-start.3 = (bf16[136,1024]{1,0:T(8,128)(2,1)}, bf16[136,1024]{1,0:T(8,128)(2,1)S(1)}, u32[]{:S(2)}) copy-start(bf16[136,1024]{1,0:T(8,128)(2,1)S(1)} %collective-permute-done.7.refs_5_) | copy-start | bytes 835588
  27.0 10.0 %collective-permute-start.4 = (bf16[136,1024]{1,0:T(8,128)(2,1)S(1)}, bf16[136,1024]{1,0:T(8,128)(2,1)S(1)}, u32[]{:S(2)}, u32[]{:S(2)}) collective-permute-start(bf16[136,1024]{1,0:T(8,128)(2,1)S(1)} %pad.12.refs_0_), channel_id=1, source_target_pairs={{0,1},{1,0},{2,3},{3,2},{4,5},{5,4},{6,7},{7,6},{8,9},{9,8},{10,11... | collective-permute-start | bytes 835592 | tf_op jit(solution)/shard_map/ppermute | solution.py:567
  27.0 12.8 %copy-start.7 = (bf16[136,1024]{1,0:T(8,128)(2,1)}, bf16[136,1024]{1,0:T(8,128)(2,1)S(1)}, u32[]{:S(2)}) copy-start(bf16[136,1024]{1,0:T(8,128)(2,1)S(1)} %collective-permute-done.9.refs_11_) | copy-start | bytes 835588
  27.0 7.3 %collective-permute-start.10 = (bf16[8,96,128]{2,1,0:T(8,128)(2,1)S(1)}, bf16[8,96,128]{2,1,0:T(8,128)(2,1)S(1)}, u32[]{:S(2)}, u32[]{:S(2)}) collective-permute-start(bf16[8,96,128]{2,1,0:T(8,128)(2,1)S(1)} %pad_maximum_fusion.1.refs_17_.refs_2_), channel_id=1, source_target_pairs={{0,24},{8,0},{16,8},{24,16},{1,25},{9,1},{17,9},{25,17},{2,26},{10... | collective-permute-start | bytes 589832 | tf_op jit(solution)/shard_map/ppermute | solution.py:562
  28.8 11.1 %copy-start.8 = (bf16[136,1024]{1,0:T(8,128)(2,1)}, bf16[136,1024]{1,0:T(8,128)(2,1)S(1)}, u32[]{:S(2)}) copy-start(bf16[136,1024]{1,0:T(8,128)(2,1)S(1)} %collective-permute-done.8.refs_9_) | copy-start | bytes 835588
  28.8 8.2 %collective-permute-start.6 = (bf16[8,96,128]{2,1,0:T(8,128)(2,1)S(1)}, bf16[8,96,128]{2,1,0:T(8,128)(2,1)S(1)}, u32[]{:S(2)}, u32[]{:S(2)}) collective-permute-start(bf16[8,96,128]{2,1,0:T(8,128)(2,1)S(1)} %pad_maximum_fusion.1.refs_17_.refs_2_), channel_id=1, source_target_pairs={{0,16},{8,24},{16,0},{24,8},{1,17},{9,25},{17,1},{25,9},{2,18},{10... | collective-permute-start | bytes 589832 | tf_op jit(solution)/shard_map/ppermute | solution.py:562
  34.3 9.8 %collective-permute-start.12 = (bf16[136,1024]{1,0:T(8,128)(2,1)S(1)}, bf16[136,1024]{1,0:T(8,128)(2,1)S(1)}, u32[]{:S(2)}, u32[]{:S(2)}) collective-permute-start(bf16[136,1024]{1,0:T(8,128)(2,1)S(1)} %collective-permute-done.7.refs_5_), channel_id=1, source_target_pairs={{0,4},{1,5},{2,0},{3,1},{4,6},{5,7},{6,2},{7,3},{8,12},{9,13},{10,... | collective-permute-start | bytes 835592 | tf_op jit(solution)/shard_map/ppermute | solution.py:617
  37.0 11.9 %copy-start.4 = (bf16[136,1024]{1,0:T(8,128)(2,1)}, bf16[136,1024]{1,0:T(8,128)(2,1)S(1)}, u32[]{:S(2)}) copy-start(bf16[136,1024]{1,0:T(8,128)(2,1)S(1)} %collective-permute-done.3.refs_4_) | copy-start | bytes 835588
  38.5 10.2 %collective-permute-start.11 = (bf16[136,1024]{1,0:T(8,128)(2,1)S(1)}, bf16[136,1024]{1,0:T(8,128)(2,1)S(1)}, u32[]{:S(2)}, u32[]{:S(2)}) collective-permute-start(bf16[136,1024]{1,0:T(8,128)(2,1)S(1)} %collective-permute-done.3.refs_4_), channel_id=1, source_target_pairs={{0,4},{1,5},{2,0},{3,1},{4,6},{5,7},{6,2},{7,3},{8,12},{9,13},{10,... | collective-permute-start | bytes 835592 | tf_op jit(solution)/shard_map/ppermute | solution.py:617
  40.0 11.5 %collective-permute-start.14 = (bf16[136,1024]{1,0:T(8,128)(2,1)S(1)}, bf16[136,1024]{1,0:T(8,128)(2,1)S(1)}, u32[]{:S(2)}, u32[]{:S(2)}) collective-permute-start(bf16[136,1024]{1,0:T(8,128)(2,1)S(1)} %collective-permute-done.7.refs_5_), channel_id=1, source_target_pairs={{0,1},{1,0},{2,3},{3,2},{4,5},{5,4},{6,7},{7,6},{8,9},{9,8},{10,11... | collective-permute-start | bytes 835592 | tf_op jit(solution)/shard_map/ppermute | solution.py:567
  40.1 11.4 %collective-permute-start.13 = (bf16[136,1024]{1,0:T(8,128)(2,1)S(1)}, bf16[136,1024]{1,0:T(8,128)(2,1)S(1)}, u32[]{:S(2)}, u32[]{:S(2)}) collective-permute-start(bf16[136,1024]{1,0:T(8,128)(2,1)S(1)} %collective-permute-done.3.refs_4_), channel_id=1, source_target_pairs={{0,1},{1,0},{2,3},{3,2},{4,5},{5,4},{6,7},{7,6},{8,9},{9,8},{10,11... | collective-permute-start | bytes 835592 | tf_op jit(solution)/shard_map/ppermute | solution.py:567
  44.1 5.0 %copy-start.5 = (bf16[136,1024]{1,0:T(8,128)(2,1)}, bf16[136,1024]{1,0:T(8,128)(2,1)S(1)}, u32[]{:S(2)}) copy-start(bf16[136,1024]{1,0:T(8,128)(2,1)S(1)} %collective-permute-done.12.refs_7_) | copy-start | bytes 835588
  49.0 2.4 %collective-permute-start.16 = (bf16[136,1024]{1,0:T(8,128)(2,1)S(1)}, bf16[136,1024]{1,0:T(8,128)(2,1)S(1)}, u32[]{:S(2)}, u32[]{:S(2)}) collective-permute-start(bf16[136,1024]{1,0:T(8,128)(2,1)S(1)} %collective-permute-done.12.refs_7_), channel_id=1, source_target_pairs={{0,1},{1,0},{2,3},{3,2},{4,5},{5,4},{6,7},{7,6},{8,9},{9,8},{10,11... | collective-permute-start | bytes 835592 | tf_op jit(solution)/shard_map/ppermute | solution.py:567
  49.4 2.9 %collective-permute-start.15 = (bf16[136,1024]{1,0:T(8,128)(2,1)S(1)}, bf16[136,1024]{1,0:T(8,128)(2,1)S(1)}, u32[]{:S(2)}, u32[]{:S(2)}) collective-permute-start(bf16[136,1024]{1,0:T(8,128)(2,1)S(1)} %collective-permute-done.11.refs_6_), channel_id=1, source_target_pairs={{0,1},{1,0},{2,3},{3,2},{4,5},{5,4},{6,7},{7,6},{8,9},{9,8},{10,11... | collective-permute-start | bytes 835592 | tf_op jit(solution)/shard_map/ppermute | solution.py:567
  52.2 4.7 %copy-start.13 = (bf16[136,1024]{1,0:T(8,128)(2,1)}, bf16[136,1024]{1,0:T(8,128)(2,1)S(1)}, u32[]{:S(2)}) copy-start(bf16[136,1024]{1,0:T(8,128)(2,1)S(1)} %collective-permute-done.16.refs_15_) | copy-start | bytes 835588
  52.2 32.3 %all-to-all-start = ((bf16[4,4,136,512]{3,2,1,0:T(8,128)(2,1)}), bf16[4,4,136,512]{3,2,1,0:T(8,128)(2,1)}, u32[]{:S(2)}, u32[]{:S(2)}) async-start(bf16[4,4,136,512]{3,2,1,0:T(8,128)(2,1)} %pad_maximum_fusion), calls=%async_computation | async-start | bytes 4456448 | tf_op jit(solution)/shard_map/all_to_all | solution.py:581
  84.5 9.1 %collective-permute-start.20 = (bf16[4,4,136,512]{3,2,1,0:T(8,128)(2,1)}, bf16[4,4,136,512]{3,2,1,0:T(8,128)(2,1)}, u32[]{:S(2)}, u32[]{:S(2)}) collective-permute-start(bf16[4,4,136,512]{3,2,1,0:T(8,128)(2,1)} %all-to-all-done.refs_0_), channel_id=1, source_target_pairs={{0,1},{1,0},{2,3},{3,2},{4,5},{5,4},{6,7},{7,6},{8,9},{9,8},{10,11... | collective-permute-start | bytes 6684680 | tf_op jit(solution)/shard_map/ppermute | solution.py:567
  84.5 16.6 %collective-permute-start.17 = (bf16[16,64,96]{2,1,0:T(8,128)(2,1)S(1)}, bf16[16,64,96]{2,1,0:T(8,128)(2,1)S(1)}, u32[]{:S(2)}, u32[]{:S(2)}) collective-permute-start(bf16[16,64,96]{2,1,0:T(8,128)(2,1)S(1)} %get-tuple-element.71), channel_id=1, source_target_pairs={{0,8},{8,16},{16,24},{24,0},{1,9},{9,17},{17,25},{25,1},{2,10},{10... | collective-permute-start | bytes 589832 | tf_op jit(solution)/shard_map/ppermute | solution.py:562
  86.0 15.2 %collective-permute-start.18 = (bf16[16,64,96]{2,1,0:T(8,128)(2,1)S(1)}, bf16[16,64,96]{2,1,0:T(8,128)(2,1)S(1)}, u32[]{:S(2)}, u32[]{:S(2)}) collective-permute-start(bf16[16,64,96]{2,1,0:T(8,128)(2,1)S(1)} %get-tuple-element.72), channel_id=1, source_target_pairs={{0,16},{8,24},{16,0},{24,8},{1,17},{9,25},{17,1},{25,9},{2,18},{10... | collective-permute-start | bytes 589832 | tf_op jit(solution)/shard_map/ppermute | solution.py:562
  86.5 14.6 %collective-permute-start.19 = (bf16[16,64,96]{2,1,0:T(8,128)(2,1)S(1)}, bf16[16,64,96]{2,1,0:T(8,128)(2,1)S(1)}, u32[]{:S(2)}, u32[]{:S(2)}) collective-permute-start(bf16[16,64,96]{2,1,0:T(8,128)(2,1)S(1)} %get-tuple-element.73), channel_id=1, source_target_pairs={{0,24},{8,0},{16,8},{24,16},{1,25},{9,1},{17,9},{25,17},{2,26},{10... | collective-permute-start | bytes 589832 | tf_op jit(solution)/shard_map/ppermute | solution.py:562
  88.9 12.2 %all-to-all-start.1 = ((f32[8,8,128]{2,1,0:T(8,128)}), f32[8,8,128]{2,1,0:T(8,128)S(1)}, u32[]{:S(2)}, u32[]{:S(2)}) async-start(f32[8,8,128]{2,1,0:T(8,128)} %get-tuple-element.70), calls=%async_computation.1 | async-start | bytes 65536 | tf_op jit(solution)/shard_map/all_to_all | solution.py:668
  (9 other events, 14.6 us)

commit v9 on v7

--- a/solution.py
+++ b/solution.py
@@ -448,25 +448,29 @@
 
 def adapter_kernel(capacity, micro, span, top, group_count, shards, *refs):
     pairs = shards // 2
-    near_ref, far_ref = refs[:2]
-    u_hbm = refs[2 : 2 + group_count]
-    lb_ref, tok_s, q_s, u_refs, sem, u_sem = refs[2 + group_count :]
+    early_ref, early_far_ref, near_ref, far_ref = refs[:4]
+    lb_ref, tok_s, q_s, u_refs, sem, u_sem = refs[4:]
     experts, rank, share = lb_ref.shape
-    tall = u_refs.shape[2]
+    blocks, tall = u_refs.shape[1:3]
     padded = tall // micro
     block = span // micro
     first = (lax.axis_index("expert") * experts).astype(jnp.float32)
     group = lax.axis_index("dp")
     owners = [shard_owner(i, shards) for i in range(shards)]
-    u_copies = [
-        pltpu.make_async_copy(u_hbm[g], u_refs.at[g], u_sem.at[g]) for g in range(group_count)
-    ]
-    copies = []
+    copies, u_copies = [], []
     for g in range(group_count):
         home = lax.rem(group - g + group_count, group_count)
         for i in range(shards):
-            source = (far_ref if i >= pairs else near_ref).at[home, i % pairs]
+            if i % pairs:
+                source = (far_ref if i >= pairs else near_ref).at[home, i % pairs - 1]
+            elif i:
+                source = early_far_ref.at[home]
+            else:
+                source = early_ref.at[home, pl.ds(blocks * tall, tok_s.shape[2])]
             copies.append(pltpu.make_async_copy(source, tok_s.at[g, owners[i]], sem.at[g, i]))
+        for k in range(blocks):
+            source = early_ref.at[home, pl.ds(k * tall, tall)]
+            u_copies.append(pltpu.make_async_copy(source, u_refs.at[g, k], u_sem.at[g, k]))
     for copy in copies + u_copies:
         copy.start()
     slots = capacity * shards
@@ -507,7 +511,10 @@
         copy.wait()
     half = experts // 2
     for x in range(half):
-        both = jnp.concatenate([u_refs[g, x] for g in range(group_count)], axis=0)
+        lane = x // blocks * 2 * rank
+        both = jnp.concatenate(
+            [u_refs[g, x % blocks, :, lane : lane + 2 * rank] for g in range(group_count)], axis=0
+        )
         lb_ref[x] = adapter_scale * lax.dot_general(
             both[:, :rank], q_s[x], contract_first, preferred_element_type=jnp.float32
         )
@@ -590,19 +597,34 @@
     )
 
     near, far = [[sent[:, c * part : (c + 1) * part] for c in range(chunks)]], []
-    u_all = [shift_groups(u, s) for s in others]
+    blocks = experts // 2 * 2 * rank // share
+    packed = jnp.concatenate(
+        [u[k * blocks : (k + 1) * blocks] for k in range(experts // 2 // blocks)], axis=-1
+    ).reshape(blocks * micro * padded, share)
+    early = jnp.stack(
+        [
+            jnp.concatenate([packed, sent[:, g * share : (g + 1) * share]], axis=0)
+            for g in range(group_count)
+        ]
+    )
+    early = across_groups(early)
+    early_far = swap_partners(early[:, blocks * micro * padded :])
     for step in range(pairs - 1):
-        if step:
-            tied = [lax.optimization_barrier(pair) for pair in zip(near[step], far[-1])]
-            near[step], far[-1] = [a for a, _ in tied], [b for _, b in tied]
-        if step == pairs - 2:
-            near[step][0], u_all = lax.optimization_barrier((near[step][0], u_all))
+        if step > 1:
+            tied = [
+                lax.optimization_barrier((near[step][c], [shard[c] for shard in far]))
+                for c in range(chunks)
+            ]
+            near[step] = [a for a, _ in tied]
+            far = [[b[k] for _, b in tied] for k in range(len(far))]
         near.append([lax.ppermute(piece, "expert", ring) for piece in near[step]])
         far.append([swap_partners(piece) for piece in near[step]])
-    columns = exchange_columns(near)
-    columns, far[-1] = lax.optimization_barrier((columns, far[-1]))
+    far.append([swap_partners(piece) for piece in near[-1]])
+    columns = exchange_columns(near[1:])
+    columns, early, early_far, far[-2:] = lax.optimization_barrier(
+        (columns, early, early_far, far[-2:])
+    )
     columns = across_groups(columns)
-    far.append([swap_partners(piece) for piece in near[-1]])
     pieces = [piece for shard in near + far for piece in shard]
 
     vmem = pl.BlockSpec(memory_space=pltpu.VMEM)
@@ -631,7 +653,7 @@
             pltpu.SemaphoreType.DMA((experts,)),
             pltpu.SemaphoreType.DMA((group_count,)),
         ],
-        compiler_params=pltpu.CompilerParams(vmem_limit_bytes=58 * 1024 * 1024),
+        compiler_params=pltpu.CompilerParams(vmem_limit_bytes=52 * 1024 * 1024),
         cost_estimate=pl.CostEstimate(
             flops=2 * experts * micro * padded * width * (units + rank + sources * block),
             bytes_accessed=2 * experts * width * (units + rank) + 2 * sources * span * width,
@@ -648,14 +670,14 @@
     lora_b = pl.pallas_call(
         functools.partial(adapter_kernel, capacity, micro, span, top, group_count, sources),
         out_shape=jax.ShapeDtypeStruct((experts, rank, share), jnp.float32),
-        in_specs=[anywhere] * (2 + group_count),
+        in_specs=[anywhere] * 4,
         out_specs=vmem,
         scratch_shapes=[
             pltpu.VMEM((group_count, sources, span + extra, share), jnp.bfloat16),
             pltpu.VMEM((experts, group_count * micro * padded, share), jnp.bfloat16),
-            pltpu.VMEM((group_count,) + u.shape, jnp.bfloat16),
+            pltpu.VMEM((group_count, blocks, micro * padded, share), jnp.bfloat16),
             pltpu.SemaphoreType.DMA((group_count, sources)),
-            pltpu.SemaphoreType.DMA((group_count,)),
+            pltpu.SemaphoreType.DMA((group_count, blocks)),
         ],
         compiler_params=pltpu.CompilerParams(vmem_limit_bytes=58 * 1024 * 1024),
         cost_estimate=pl.CostEstimate(
@@ -664,7 +686,7 @@
             transcendentals=0,
         ),
         name="adapter_columns",
-    )(columns, swapped, u, *u_all)
+    )(early, early_far, columns, swapped)
 
     home, arrived, lora_b = lax.optimization_barrier((home, arrived, lora_b))
     router_grad = jnp.sum(home, axis=0).T
@@ -678,8 +700,10 @@
     sources, groups = lax.axis_size("expert"), lax.axis_size("dp")
     span, width = arrays[0].shape
     top, (micro, experts, slots, units) = arrays[1].shape[1], arrays[3].shape
-    even = sources % 2 == 0 and experts % 2 == 0 and width % (128 * groups) == 0 and units % groups == 0
-    packs = 2 * top * span % (width // groups) == 0 and (width // groups) % span == 0
+    even = sources % 4 == 0 and experts % 2 == 0 and width % (128 * groups) == 0 and units % groups == 0
+    rank = arrays[5].shape[2]
+    packs = width // groups % (2 * rank) == 0 and experts * rank % (width // groups) == 0
+    packs = packs and 2 * top * span % (width // groups) == 0 and (width // groups) % span == 0
     exact = experts * sources <= 256
     if even and packs and exact and sources * span <= micro * experts * slots:
         return local_by_tokens(*arrays)

time: 99.8 us -> 98 us (0.982)
  waiting for transfers between devices: 21.2 us -> 12.2 us
  local copies, waits for them, and re-layouts: 3.79 us -> 7.53 us
  other arithmetic: 6.2 us -> 9.74 us
  Pallas kernels: 30.9 us -> 29.8 us
    ppermute x6 -> x3, starting transfers between devices: 10.5 us -> 4.69 us  [shift_groups(): lax.ppermute(array, 'dp', [(d, (d + by) % group_count) for d in range(gro...]
    another operation x7 -> x6, local copies, waits for them, and re-layouts: 0.15 us -> 5.85 us  [exchange_columns(): jnp.stack([columns(pieces, g) for pieces in chosen])]
    ppermute x6, waiting for transfers between devices: 13.1 us -> 8.77 us  [local_by_tokens(): near.append([lax.ppermute(piece, 'expert', ring) for piece in near[step]])]
    all_to_all x1 -> x2, starting transfers between devices: 3.62 us -> 7.44 us  [across_groups(): return lax.all_to_all(array, 'dp', split_axis=0, concat_axis=0, tiled=True)]
    ppermute x6 -> x3, waiting for transfers between devices: 6.4 us -> 3.44 us  [shift_groups(): lax.ppermute(array, 'dp', [(d, (d + by) % group_count) for d in range(gro...]
    unnamed x52 -> x34, local copies, waits for them, and re-layouts: 3.52 us -> 1.49 us
    ppermute x9 -> x10, waiting for transfers between devices: 1.46 us -> 0.03 us  [swap_partners(): return lax.ppermute(array, 'expert', swap)]
    ppermute x6, starting transfers between devices: 16.9 us -> 18.3 us  [local_by_tokens(): near.append([lax.ppermute(piece, 'expert', ring) for piece in near[step]])]
  transfers between devices with their start and end apart: 23 -> 22, of which waited for: 12 -> 7; matrix products, arithmetic and copies ran while one was open for 3% -> 12% of each run, Pallas kernels for 31% -> 31%
where the time goes in v9:
time: 98 us; the launch traced here: 97.3 us
  starting transfers between devices  36.6 us (37%)
  Pallas kernels  29.8 us (30%)
  waiting for transfers between devices  12.2 us (12%)
  other arithmetic  9.74 us (10%)
  local copies, waits for them, and re-layouts  7.53 us (8%)
    pallas_call x1, Pallas kernels, local_by_tokens(): pl.pallas_call(functools.partial(expert_kernel, capacity, group_count, so...  22.3 us
    ppermute x6, starting transfers between devices, local_by_tokens(): near.append([lax.ppermute(piece, 'expert', ring) for piece in near[step]])  18.3 us
    ppermute x6, waiting for transfers between devices, local_by_tokens(): near.append([lax.ppermute(piece, 'expert', ring) for piece in near[step]])  8.77 us
    pallas_call x1, Pallas kernels, local_by_tokens(): pl.pallas_call(functools.partial(adapter_kernel, capacity, micro, span, t...  7.52 us
    all_to_all x2, starting transfers between devices, across_groups(): return lax.all_to_all(array, 'dp', split_axis=0, concat_axis=0, tiled=True)  7.44 us
    another operation x6, local copies, waits for them, and re-layouts, exchange_columns(): jnp.stack([columns(pieces, g) for pieces in chosen])  5.85 us
    all_to_all x1, starting transfers between devices, local_by_tokens(): lax.all_to_all(routed, 'expert', split_axis=0, concat_axis=0, tiled=True)  4.77 us
    ppermute x3, starting transfers between devices, shift_groups(): lax.ppermute(array, 'dp', [(d, (d + by) % group_count) for d in range(gro...  4.69 us
  transfers between devices with their start and end apart: 22, of which 7 were waited for; matrix products, arithmetic and copies ran while one was open for 12% of the time, Pallas kernels for 31%

profile of v9, /device:TPU:0, one launch (start us, length us, event | category | flops | bytes accessed | tf_op | source)
XLA Modules:
  0.0 97.3 jit_solution(14985504144750712930)
XLA Ops:
  0.6 0.7 convert_bitcast_fusion
  2.0 1.1 %fusion.3 = bf16[136,2048]{1,0:T(8,128)(2,1)S(1)} fusion(bf16[4,2048]{1,0:T(4,128)(2,1)S(1)} %bitcast.62, bf16[128,2048]{1,0:T(8,128)(2,1)} %param.7), kind=kLoop, calls=%fused_computation.7 | loop fusion | flops 1671168 | bytes 1097728 | tf_op jit(solution)/shard_map/concatenate | solution.py:595
  3.7 3.6 %collective-permute-start.1 = (bf16[136,1024]{1,0:T(8,128)(2,1)S(1)}, bf16[136,1024]{1,0:T(8,128)(2,1)S(1)}, u32[]{:S(2)}, u32[]{:S(2)}) collective-permute-start(bf16[136,1024]{1,0:T(8,128)(2,1)S(1)} %get-tuple-element.68.refs_1_), channel_id=1, source_target_pairs={{0,4},{1,5},{2,0},{3,1},{4,6},{5,7},{6,2},{7,3},{8,12},{9,13},{10,... | collective-permute-start | bytes 835592 | tf_op jit(solution)/shard_map/ppermute | solution.py:620
  7.5 1.6 %collective-permute-start = (bf16[136,1024]{1,0:T(8,128)(2,1)S(1)}, bf16[136,1024]{1,0:T(8,128)(2,1)S(1)}, u32[]{:S(2)}, u32[]{:S(2)}) collective-permute-start(bf16[136,1024]{1,0:T(8,128)(2,1)S(1)} %get-tuple-element.69.refs_0_), channel_id=1, source_target_pairs={{0,4},{1,5},{2,0},{3,1},{4,6},{5,7},{6,2},{7,3},{8,12},{9,13},{10,... | collective-permute-start | bytes 835592 | tf_op jit(solution)/shard_map/ppermute | solution.py:620
  10.0 1.2 %pad_maximum_fusion.1 = bf16[4,328,512]{2,1,0:T(8,128)(2,1)} fusion(bf16[1,328,512]{2,1,0:T(8,128)(2,1)S(1)} %get-tuple-element.91, bf16[1,328,512]{2,1,0:T(8,128)(2,1)S(1)} %get-tuple-element.90, bf16[1,328,512]{2,1,0:T(8,128)(2,1)S(1)} %get-tuple-element.89, bf16[1,328,512]{2,1,0:T(8,128)(2,1)S(1)} %get-tuple-element.88), kind=kLoop, calls=%fused_computation.1 | loop fusion | flops 2015232 | bytes 2686976 | tf_op jit(solution)/shard_map/stack | solution.py:604
  11.3 3.7 %all-to-all-start = ((bf16[4,328,512]{2,1,0:T(8,128)(2,1)}), bf16[4,328,512]{2,1,0:T(8,128)(2,1)S(1)}, u32[]{:S(2)}, u32[]{:S(2)}) async-start(bf16[4,328,512]{2,1,0:T(8,128)(2,1)} %pad_maximum_fusion.1), calls=%async_computation | async-start | bytes 2686976 | tf_op jit(solution)/shard_map/all_to_all | solution.py:586
  15.1 2.7 %collective-permute-start.5 = (bf16[136,1024]{1,0:T(8,128)(2,1)S(1)}, bf16[136,1024]{1,0:T(8,128)(2,1)}, u32[]{:S(2)}, u32[]{:S(2)}) collective-permute-start(bf16[136,1024]{1,0:T(8,128)(2,1)S(1)} %collective-permute-done.1.refs_3_), channel_id=1, source_target_pairs={{0,4},{1,5},{2,0},{3,1},{4,6},{5,7},{6,2},{7,3},{8,12},{9,13},{10,... | collective-permute-start | bytes 835592 | tf_op jit(solution)/shard_map/ppermute | solution.py:620
  17.8 2.6 %collective-permute-done.refs_2_ = bf16[136,1024]{1,0:T(8,128)(2,1)S(1)} collective-permute-done((bf16[136,1024]{1,0:T(8,128)(2,1)S(1)}, bf16[136,1024]{1,0:T(8,128)(2,1)S(1)}, u32[]{:S(2)}, u32[]{:S(2)}) %collective-permute-start) | collective-permute-done | bytes 278560 | tf_op jit(solution)/shard_map/ppermute | solution.py:620
  20.3 3.4 %collective-permute-start.2 = (bf16[136,1024]{1,0:T(8,128)(2,1)S(1)}, bf16[136,1024]{1,0:T(8,128)(2,1)}, u32[]{:S(2)}, u32[]{:S(2)}) collective-permute-start(bf16[136,1024]{1,0:T(8,128)(2,1)S(1)} %collective-permute-done.refs_2_), channel_id=1, source_target_pairs={{0,4},{1,5},{2,0},{3,1},{4,6},{5,7},{6,2},{7,3},{8,12},{9,13},{10,... | collective-permute-start | bytes 835592 | tf_op jit(solution)/shard_map/ppermute | solution.py:620
  24.5 1.8 %collective-permute-done.5.refs_5_ = bf16[136,1024]{1,0:T(8,128)(2,1)} collective-permute-done((bf16[136,1024]{1,0:T(8,128)(2,1)S(1)}, bf16[136,1024]{1,0:T(8,128)(2,1)}, u32[]{:S(2)}, u32[]{:S(2)}) %collective-permute-start.5) | collective-permute-done | bytes 278560 | tf_op jit(solution)/shard_map/ppermute | solution.py:620
  26.3 3.5 %collective-permute-start.9 = (bf16[136,1024]{1,0:T(8,128)(2,1)}, bf16[136,1024]{1,0:T(8,128)(2,1)S(1)}, u32[]{:S(2)}, u32[]{:S(2)}) collective-permute-start(bf16[136,1024]{1,0:T(8,128)(2,1)} %collective-permute-done.5.refs_5_), channel_id=1, source_target_pairs={{0,4},{1,5},{2,0},{3,1},{4,6},{5,7},{6,2},{7,3},{8,12},{9,13},{10,... | collective-permute-start | bytes 835592 | tf_op jit(solution)/shard_map/ppermute | solution.py:620
  29.8 1.7 %slice_bitcast_fusion.9 = (bf16[1,136,512]{2,1,0:T(8,128)(2,1)}, bf16[1,136,512]{2,1,0:T(8,128)(2,1)}) fusion(bf16[136,1024]{1,0:T(8,128)(2,1)} %collective-permute-done.5.refs_5_), kind=kLoop, calls=%fused_computation.33 | loop fusion | bytes 557056 | tf_op jit(solution)/shard_map/stack | solution.py:582
  31.5 0.8 collective-permute-done.2.refs_4_
  32.3 3.5 %collective-permute-start.8 = (bf16[136,1024]{1,0:T(8,128)(2,1)}, bf16[136,1024]{1,0:T(8,128)(2,1)}, u32[]{:S(2)}, u32[]{:S(2)}) collective-permute-start(bf16[136,1024]{1,0:T(8,128)(2,1)} %collective-permute-done.2.refs_4_), channel_id=1, source_target_pairs={{0,4},{1,5},{2,0},{3,1},{4,6},{5,7},{6,2},{7,3},{8,12},{9,13},{10,... | collective-permute-start | bytes 835592 | tf_op jit(solution)/shard_map/ppermute | solution.py:620
  35.8 1.7 %slice_bitcast_fusion.11 = (bf16[1,136,512]{2,1,0:T(8,128)(2,1)}, bf16[1,136,512]{2,1,0:T(8,128)(2,1)}) fusion(bf16[136,1024]{1,0:T(8,128)(2,1)} %collective-permute-done.2.refs_4_), kind=kLoop, calls=%fused_computation.35 | loop fusion | bytes 557056 | tf_op jit(solution)/shard_map/stack | solution.py:582
  37.5 0.9 collective-permute-done.9.refs_7_
  38.3 0.8 slice_bitcast_fusion.2
  39.3 1.7 %maximum_bitcast_fusion.2 = (bf16[1,3,136,512]{3,2,1,0:T(8,128)(2,1)S(1)}, bf16[1,3,136,512]{3,2,1,0:T(8,128)(2,1)S(1)}) fusion(bf16[1,136,512]{2,1,0:T(8,128)(2,1)} %get-tuple-element.86, bf16[1,136,512]{2,1,0:T(8,128)(2,1)} %get-tuple-element.84, bf16[1,136,512]{2,1,0:T(8,128)(2,1)S(1)} %get-tuple-element.82, bf16[1,136,512]{2,1,0:T(8,128)(2,1)} %get-tuple-element.87, ...), kind=kLoop, calls=%fused_computation.15 | loop fusion | flops 835584 | bytes 1671168 | tf_op jit(solution)/shard_map/stack | solution.py:581
  41.1 2.7 %collective-permute-done.8.refs_6_ = bf16[136,1024]{1,0:T(8,128)(2,1)} collective-permute-done((bf16[136,1024]{1,0:T(8,128)(2,1)}, bf16[136,1024]{1,0:T(8,128)(2,1)}, u32[]{:S(2)}, u32[]{:S(2)}) %collective-permute-start.8) | collective-permute-done | bytes 278560 | tf_op jit(solution)/shard_map/ppermute | solution.py:620
  43.9 1.0 %slice_bitcast_fusion.6 = (bf16[1,136,512]{2,1,0:T(8,128)(2,1)S(1)}, bf16[1,136,512]{2,1,0:T(8,128)(2,1)S(1)}) fusion(bf16[136,1024]{1,0:T(8,128)(2,1)} %collective-permute-done.8.refs_6_), kind=kLoop, calls=%fused_computation.30 | loop fusion | bytes 557056 | tf_op jit(solution)/shard_map/stack | solution.py:582
  45.0 1.4 %pad_maximum_fusion = bf16[4,3,136,512]{3,2,1,0:T(8,128)(2,1)} fusion(bf16[1,3,136,512]{3,2,1,0:T(8,128)(2,1)S(1)} %get-tuple-element.93, bf16[1,3,136,512]{3,2,1,0:T(8,128)(2,1)S(1)} %get-tuple-element.92, bf16[1,3,136,512]{3,2,1,0:T(8,128)(2,1)S(1)} %get-tuple-element.95, bf16[1,3,136,512]{3,2,1,0:T(8,128)(2,1)S(1)} %get-tuple-element.94), kind=kLoop, calls=%fused_computation | loop fusion | flops 2506752 | bytes 3342336 | tf_op jit(solution)/shard_map/stack | solution.py:581
  46.4 0.7 copy-done.14
  47.1 0.7 copy-done.15
  47.8 3.7 %all-to-all-start.1 = ((bf16[4,3,136,512]{3,2,1,0:T(8,128)(2,1)}), bf16[4,3,136,512]{3,2,1,0:T(8,128)(2,1)S(1)}, u32[]{:S(2)}, u32[]{:S(2)}) async-start(bf16[4,3,136,512]{3,2,1,0:T(8,128)(2,1)} %pad_maximum_fusion), calls=%async_computation.1 | async-start | bytes 3342336 | tf_op jit(solution)/shard_map/all_to_all | solution.py:586
  51.7 22.3 %expert_rows.1 = (bf16[2,16,40,384]{3,2,1,0:T(8,128)(2,1)}, f32[8,8,128]{2,1,0:T(8,128)}, bf16[16,64,96]{2,1,0:T(8,128)(2,1)S(1)}, bf16[16,64,96]{2,1,0:T(8,128)...) custom-call(bf16[136,1024]{1,0:T(8,128)(2,1)S(1)} %get-tuple-element.69.refs_0_, ...), custom_call_target="tpu_custom_call" | custom-call | flops 6039797760 | bytes 33554432 | tf_op jit(solution)/shard_map/expert_rows/pallas_call | solution.py:633
  74.4 4.8 %all-to-all-start.2 = ((f32[8,8,128]{2,1,0:T(8,128)}), f32[8,8,128]{2,1,0:T(8,128)S(1)}, u32[]{:S(2)}, u32[]{:S(2)}) async-start(f32[8,8,128]{2,1,0:T(8,128)} %get-tuple-element.51), calls=%async_computation.2 | async-start | bytes 65536 | tf_op jit(solution)/shard_map/all_to_all | solution.py:668
  79.2 1.8 %collective-permute-start.15 = (bf16[16,64,96]{2,1,0:T(8,128)(2,1)S(1)}, bf16[16,64,96]{2,1,0:T(8,128)(2,1)S(1)}, u32[]{:S(2)}, u32[]{:S(2)}) collective-permute-start(bf16[16,64,96]{2,1,0:T(8,128)(2,1)S(1)} %get-tuple-element.52), channel_id=1, source_target_pairs={{0,8},{8,16},{16,24},{24,0},{1,9},{9,17},{17,25},{25,1},{2,10},{10... | collective-permute-start | bytes 589832 | tf_op jit(solution)/shard_map/ppermute | solution.py:569
  80.9 1.5 %collective-permute-start.16 = (bf16[16,64,96]{2,1,0:T(8,128)(2,1)S(1)}, bf16[16,64,96]{2,1,0:T(8,128)(2,1)S(1)}, u32[]{:S(2)}, u32[]{:S(2)}) collective-permute-start(bf16[16,64,96]{2,1,0:T(8,128)(2,1)S(1)} %get-tuple-element.53), channel_id=1, source_target_pairs={{0,16},{8,24},{16,0},{24,8},{1,17},{9,25},{17,1},{25,9},{2,18},{10... | collective-permute-start | bytes 589832 | tf_op jit(solution)/shard_map/ppermute | solution.py:569
  82.4 1.5 %collective-permute-start.17 = (bf16[16,64,96]{2,1,0:T(8,128)(2,1)S(1)}, bf16[16,64,96]{2,1,0:T(8,128)(2,1)}, u32[]{:S(2)}, u32[]{:S(2)}) collective-permute-start(bf16[16,64,96]{2,1,0:T(8,128)(2,1)S(1)} %get-tuple-element.54), channel_id=1, source_target_pairs={{0,24},{8,0},{16,8},{24,16},{1,25},{9,1},{17,9},{25,17},{2,26},{10... | collective-permute-start | bytes 589832 | tf_op jit(solution)/shard_map/ppermute | solution.py:569
  83.9 7.5 %adapter_columns.1 = f32[16,64,512]{2,1,0:T(8,128)} custom-call(bf16[4,328,512]{2,1,0:T(8,128)(2,1)} %copy-done, bf16[4,136,512]{2,1,0:T(8,128)(2,1)} %collective-permute-done.10.refs_1_, bf16[4,3,136,512]{3,2,1,0:T(8,128)(2,1)} %copy-done.1, bf16[4,3,136,512]{3,2,1,0:T(8,128)(2,1)} %collective-permute-done.18.refs_3_), custom_call_target="tpu_custom_call" | custom-call | flops 3623878656 | bytes 6291456 | tf_op jit(solution)/shard_map/adapter_columns/pallas_call | solution.py:670
  91.4 3.0 %collective-permute-done.16 = bf16[16,64,96]{2,1,0:T(8,128)(2,1)S(1)} collective-permute-done((bf16[16,64,96]{2,1,0:T(8,128)(2,1)S(1)}, bf16[16,64,96]{2,1,0:T(8,128)(2,1)S(1)}, u32[]{:S(2)}, u32[]{:S(2)}) %collective-permute-start.16) | collective-permute-done | bytes 196640 | tf_op jit(solution)/shard_map/ppermute | solution.py:569
  95.4 1.9 %convert_add_fusion = f32[16,64,96]{2,1,0:T(8,128)} fusion(bf16[16,64,96]{2,1,0:T(8,128)(2,1)} %collective-permute-done.17, bf16[16,64,96]{2,1,0:T(8,128)(2,1)S(1)} %collective-permute-done.16, bf16[16,64,96]{2,1,0:T(8,128)(2,1)S(1)} %collective-permute-done.15, bf16[16,64,96]{2,1,0:T(8,128)(2,1)S(1)} %get-tuple-element.59), kind=kLoop, calls=%fused_computation.8 | loop fusion | flops 688128 | bytes 1179648 | tf_op jit(solution)/shard_map/add | solution.py:695
  (73 shorter events, 5.1 us)
Async XLA Ops:
  3.1 6.0 %copy-start.6 = (bf16[2,16,40,384]{3,2,1,0:T(8,128)(2,1)S(1)}, bf16[2,16,40,384]{3,2,1,0:T(8,128)(2,1)}, u32[]{:S(2)}) copy-start(bf16[2,16,40,384]{3,2,1,0:T(8,128)(2,1)} %refs_16_.1) | copy-start | bytes 2949124
  3.2 6.0 %copy-start.7 = (bf16[16,384,64]{1,2,0:T(8,128)(2,1)S(1)}, bf16[16,384,64]{1,2,0:T(8,128)(2,1)}, u32[]{:S(2)}) copy-start(bf16[16,384,64]{1,2,0:T(8,128)(2,1)} %param.12) | copy-start | bytes 2359300
  3.2 17.1 %collective-permute-start.6 = (bf16[136,1024]{1,0:T(8,128)(2,1)S(1)}, bf16[136,1024]{1,0:T(8,128)(2,1)S(1)}, u32[]{:S(2)}, u32[]{:S(2)}) collective-permute-start(bf16[136,1024]{1,0:T(8,128)(2,1)S(1)} %get-tuple-element.68.refs_1_), channel_id=1, source_target_pairs={{0,1},{1,0},{2,3},{3,2},{4,5},{5,4},{6,7},{7,6},{8,9},{9,8},{10,11... | collective-permute-start | bytes 835592 | tf_op jit(solution)/shard_map/ppermute | solution.py:574
  3.7 11.3 %collective-permute-start.1 = (bf16[136,1024]{1,0:T(8,128)(2,1)S(1)}, bf16[136,1024]{1,0:T(8,128)(2,1)S(1)}, u32[]{:S(2)}, u32[]{:S(2)}) collective-permute-start(bf16[136,1024]{1,0:T(8,128)(2,1)S(1)} %get-tuple-element.68.refs_1_), channel_id=1, source_target_pairs={{0,4},{1,5},{2,0},{3,1},{4,6},{5,7},{6,2},{7,3},{8,12},{9,13},{10,... | collective-permute-start | bytes 835592 | tf_op jit(solution)/shard_map/ppermute | solution.py:620
  7.4 24.1 %collective-permute-start.3 = (bf16[136,1024]{1,0:T(8,128)(2,1)S(1)}, bf16[136,1024]{1,0:T(8,128)(2,1)}, u32[]{:S(2)}, u32[]{:S(2)}) collective-permute-start(bf16[136,1024]{1,0:T(8,128)(2,1)S(1)} %get-tuple-element.69.refs_0_), channel_id=1, source_target_pairs={{0,1},{1,0},{2,3},{3,2},{4,5},{5,4},{6,7},{7,6},{8,9},{9,8},{10,11... | collective-permute-start | bytes 835592 | tf_op jit(solution)/shard_map/ppermute | solution.py:574
  7.5 12.8 %collective-permute-start = (bf16[136,1024]{1,0:T(8,128)(2,1)S(1)}, bf16[136,1024]{1,0:T(8,128)(2,1)S(1)}, u32[]{:S(2)}, u32[]{:S(2)}) collective-permute-start(bf16[136,1024]{1,0:T(8,128)(2,1)S(1)} %get-tuple-element.69.refs_0_), channel_id=1, source_target_pairs={{0,4},{1,5},{2,0},{3,1},{4,6},{5,7},{6,2},{7,3},{8,12},{9,13},{10,... | collective-permute-start | bytes 835592 | tf_op jit(solution)/shard_map/ppermute | solution.py:620
  11.3 27.8 %all-to-all-start = ((bf16[4,328,512]{2,1,0:T(8,128)(2,1)}), bf16[4,328,512]{2,1,0:T(8,128)(2,1)S(1)}, u32[]{:S(2)}, u32[]{:S(2)}) async-start(bf16[4,328,512]{2,1,0:T(8,128)(2,1)} %pad_maximum_fusion.1), calls=%async_computation | async-start | bytes 2686976 | tf_op jit(solution)/shard_map/all_to_all | solution.py:586
  15.0 24.1 %copy-start.2 = (bf16[136,1024]{1,0:T(8,128)(2,1)}, bf16[136,1024]{1,0:T(8,128)(2,1)S(1)}, u32[]{:S(2)}) copy-start(bf16[136,1024]{1,0:T(8,128)(2,1)S(1)} %collective-permute-done.1.refs_3_) | copy-start | bytes 835588
  15.0 9.4 %collective-permute-start.7 = (bf16[136,1024]{1,0:T(8,128)(2,1)S(1)}, bf16[136,1024]{1,0:T(8,128)(2,1)S(1)}, u32[]{:S(2)}, u32[]{:S(2)}) collective-permute-start(bf16[136,1024]{1,0:T(8,128)(2,1)S(1)} %collective-permute-done.1.refs_3_), channel_id=1, source_target_pairs={{0,1},{1,0},{2,3},{3,2},{4,5},{5,4},{6,7},{7,6},{8,9},{9,8},{10,11... | collective-permute-start | bytes 835592 | tf_op jit(solution)/shard_map/ppermute | solution.py:574
  15.1 11.2 %collective-permute-start.5 = (bf16[136,1024]{1,0:T(8,128)(2,1)S(1)}, bf16[136,1024]{1,0:T(8,128)(2,1)}, u32[]{:S(2)}, u32[]{:S(2)}) collective-permute-start(bf16[136,1024]{1,0:T(8,128)(2,1)S(1)} %collective-permute-done.1.refs_3_), channel_id=1, source_target_pairs={{0,4},{1,5},{2,0},{3,1},{4,6},{5,7},{6,2},{7,3},{8,12},{9,13},{10,... | collective-permute-start | bytes 835592 | tf_op jit(solution)/shard_map/ppermute | solution.py:620
  20.3 18.8 %copy-start.3 = (bf16[136,1024]{1,0:T(8,128)(2,1)}, bf16[136,1024]{1,0:T(8,128)(2,1)S(1)}, u32[]{:S(2)}) copy-start(bf16[136,1024]{1,0:T(8,128)(2,1)S(1)} %collective-permute-done.refs_2_) | copy-start | bytes 835588
  20.3 11.2 %collective-permute-start.4 = (bf16[136,1024]{1,0:T(8,128)(2,1)S(1)}, bf16[136,1024]{1,0:T(8,128)(2,1)S(1)}, u32[]{:S(2)}, u32[]{:S(2)}) collective-permute-start(bf16[136,1024]{1,0:T(8,128)(2,1)S(1)} %collective-permute-done.refs_2_), channel_id=1, source_target_pairs={{0,1},{1,0},{2,3},{3,2},{4,5},{5,4},{6,7},{7,6},{8,9},{9,8},{10,11... | collective-permute-start | bytes 835592 | tf_op jit(solution)/shard_map/ppermute | solution.py:574
  20.3 11.9 %collective-permute-start.2 = (bf16[136,1024]{1,0:T(8,128)(2,1)S(1)}, bf16[136,1024]{1,0:T(8,128)(2,1)}, u32[]{:S(2)}, u32[]{:S(2)}) collective-permute-start(bf16[136,1024]{1,0:T(8,128)(2,1)S(1)} %collective-permute-done.refs_2_), channel_id=1, source_target_pairs={{0,4},{1,5},{2,0},{3,1},{4,6},{5,7},{6,2},{7,3},{8,12},{9,13},{10,... | collective-permute-start | bytes 835592 | tf_op jit(solution)/shard_map/ppermute | solution.py:620
  24.5 13.9 %copy-start.12 = (bf16[136,1024]{1,0:T(8,128)(2,1)}, bf16[136,1024]{1,0:T(8,128)(2,1)S(1)}, u32[]{:S(2)}) copy-start(bf16[136,1024]{1,0:T(8,128)(2,1)S(1)} %collective-permute-done.7.refs_11_) | copy-start | bytes 835588
  26.3 12.0 %collective-permute-start.9 = (bf16[136,1024]{1,0:T(8,128)(2,1)}, bf16[136,1024]{1,0:T(8,128)(2,1)S(1)}, u32[]{:S(2)}, u32[]{:S(2)}) collective-permute-start(bf16[136,1024]{1,0:T(8,128)(2,1)} %collective-permute-done.5.refs_5_), channel_id=1, source_target_pairs={{0,4},{1,5},{2,0},{3,1},{4,6},{5,7},{6,2},{7,3},{8,12},{9,13},{10,... | collective-permute-start | bytes 835592 | tf_op jit(solution)/shard_map/ppermute | solution.py:620
  31.5 14.9 %collective-permute-start.12 = (bf16[136,1024]{1,0:T(8,128)(2,1)}, bf16[136,1024]{1,0:T(8,128)(2,1)}, u32[]{:S(2)}, u32[]{:S(2)}) collective-permute-start(bf16[136,1024]{1,0:T(8,128)(2,1)} %collective-permute-done.5.refs_5_), channel_id=1, source_target_pairs={{0,1},{1,0},{2,3},{3,2},{4,5},{5,4},{6,7},{7,6},{8,9},{9,8},{10,11... | collective-permute-start | bytes 835592 | tf_op jit(solution)/shard_map/ppermute | solution.py:574
  31.5 6.8 %copy-start.13 = (bf16[136,1024]{1,0:T(8,128)(2,1)}, bf16[136,1024]{1,0:T(8,128)(2,1)S(1)}, u32[]{:S(2)}) copy-start(bf16[136,1024]{1,0:T(8,128)(2,1)S(1)} %collective-permute-done.4.refs_10_) | copy-start | bytes 835588
  32.3 14.1 %collective-permute-start.11 = (bf16[136,1024]{1,0:T(8,128)(2,1)}, bf16[136,1024]{1,0:T(8,128)(2,1)}, u32[]{:S(2)}, u32[]{:S(2)}) collective-permute-start(bf16[136,1024]{1,0:T(8,128)(2,1)} %collective-permute-done.2.refs_4_), channel_id=1, source_target_pairs={{0,1},{1,0},{2,3},{3,2},{4,5},{5,4},{6,7},{7,6},{8,9},{9,8},{10,11... | collective-permute-start | bytes 835592 | tf_op jit(solution)/shard_map/ppermute | solution.py:574
  32.3 11.6 %collective-permute-start.8 = (bf16[136,1024]{1,0:T(8,128)(2,1)}, bf16[136,1024]{1,0:T(8,128)(2,1)}, u32[]{:S(2)}, u32[]{:S(2)}) collective-permute-start(bf16[136,1024]{1,0:T(8,128)(2,1)} %collective-permute-done.2.refs_4_), channel_id=1, source_target_pairs={{0,4},{1,5},{2,0},{3,1},{4,6},{5,7},{6,2},{7,3},{8,12},{9,13},{10,... | collective-permute-start | bytes 835592 | tf_op jit(solution)/shard_map/ppermute | solution.py:620
  39.2 5.7 %copy-start.8 = (bf16[1,136,512]{2,1,0:T(8,128)(2,1)S(1)}, bf16[1,136,512]{2,1,0:T(8,128)(2,1)}, u32[]{:S(2)}) copy-start(bf16[1,136,512]{2,1,0:T(8,128)(2,1)} %get-tuple-element.77) | copy-start | bytes 417796
  39.2 5.7 %copy-start.9 = (bf16[1,136,512]{2,1,0:T(8,128)(2,1)S(1)}, bf16[1,136,512]{2,1,0:T(8,128)(2,1)}, u32[]{:S(2)}) copy-start(bf16[1,136,512]{2,1,0:T(8,128)(2,1)} %get-tuple-element.78) | copy-start | bytes 417796
  39.2 5.7 %copy-start.10 = (bf16[1,136,512]{2,1,0:T(8,128)(2,1)S(1)}, bf16[1,136,512]{2,1,0:T(8,128)(2,1)}, u32[]{:S(2)}) copy-start(bf16[1,136,512]{2,1,0:T(8,128)(2,1)} %get-tuple-element.79) | copy-start | bytes 417796
  39.2 8.6 %collective-permute-start.10 = (bf16[4,136,512]{2,1,0:T(8,128)(2,1)S(1)}, bf16[4,136,512]{2,1,0:T(8,128)(2,1)}, u32[]{:S(2)}, u32[]{:S(2)}) collective-permute-start(bf16[4,136,512]{2,1,0:T(8,128)(2,1)S(1)} %slice.124), channel_id=1, source_target_pairs={{0,1},{1,0},{2,3},{3,2},{4,5},{5,4},{6,7},{7,6},{8,9},{9,8},{10,11... | collective-permute-start | bytes 1671176 | tf_op jit(solution)/shard_map/ppermute | solution.py:574
  41.0 5.4 %collective-permute-start.14 = (bf16[136,1024]{1,0:T(8,128)(2,1)S(1)}, bf16[136,1024]{1,0:T(8,128)(2,1)S(1)}, u32[]{:S(2)}, u32[]{:S(2)}) collective-permute-start(bf16[136,1024]{1,0:T(8,128)(2,1)S(1)} %copy-done.5), channel_id=1, source_target_pairs={{0,1},{1,0},{2,3},{3,2},{4,5},{5,4},{6,7},{7,6},{8,9},{9,8},{10,11... | collective-permute-start | bytes 835592 | tf_op jit(solution)/shard_map/ppermute | solution.py:574
  43.9 3.2 %collective-permute-start.13 = (bf16[136,1024]{1,0:T(8,128)(2,1)}, bf16[136,1024]{1,0:T(8,128)(2,1)S(1)}, u32[]{:S(2)}, u32[]{:S(2)}) collective-permute-start(bf16[136,1024]{1,0:T(8,128)(2,1)} %collective-permute-done.8.refs_6_), channel_id=1, source_target_pairs={{0,1},{1,0},{2,3},{3,2},{4,5},{5,4},{6,7},{7,6},{8,9},{9,8},{10,11... | collective-permute-start | bytes 835592 | tf_op jit(solution)/shard_map/ppermute | solution.py:574
  47.8 26.1 %all-to-all-start.1 = ((bf16[4,3,136,512]{3,2,1,0:T(8,128)(2,1)}), bf16[4,3,136,512]{3,2,1,0:T(8,128)(2,1)S(1)}, u32[]{:S(2)}, u32[]{:S(2)}) async-start(bf16[4,3,136,512]{3,2,1,0:T(8,128)(2,1)} %pad_maximum_fusion), calls=%async_computation.1 | async-start | bytes 3342336 | tf_op jit(solution)/shard_map/all_to_all | solution.py:586
  73.9 9.9 %copy-start.1 = (bf16[4,3,136,512]{3,2,1,0:T(8,128)(2,1)}, bf16[4,3,136,512]{3,2,1,0:T(8,128)(2,1)S(1)}, u32[]{:S(2)}) copy-start(bf16[4,3,136,512]{3,2,1,0:T(8,128)(2,1)S(1)} %all-to-all-done.1.refs_2_) | copy-start | bytes 5013508
  74.0 9.9 %collective-permute-start.18 = (bf16[4,3,136,512]{3,2,1,0:T(8,128)(2,1)S(1)}, bf16[4,3,136,512]{3,2,1,0:T(8,128)(2,1)}, u32[]{:S(2)}, u32[]{:S(2)}) collective-permute-start(bf16[4,3,136,512]{3,2,1,0:T(8,128)(2,1)S(1)} %all-to-all-done.1.refs_2_), channel_id=1, source_target_pairs={{0,1},{1,0},{2,3},{3,2},{4,5},{5,4},{6,7},{7,6},{8,9},{9,8},{10,11... | collective-permute-start | bytes 5013512 | tf_op jit(solution)/shard_map/ppermute | solution.py:574
  74.4 17.0 %all-to-all-start.2 = ((f32[8,8,128]{2,1,0:T(8,128)}), f32[8,8,128]{2,1,0:T(8,128)S(1)}, u32[]{:S(2)}, u32[]{:S(2)}) async-start(f32[8,8,128]{2,1,0:T(8,128)} %get-tuple-element.51), calls=%async_computation.2 | async-start | bytes 65536 | tf_op jit(solution)/shard_map/all_to_all | solution.py:668
  79.2 12.2 %collective-permute-start.15 = (bf16[16,64,96]{2,1,0:T(8,128)(2,1)S(1)}, bf16[16,64,96]{2,1,0:T(8,128)(2,1)S(1)}, u32[]{:S(2)}, u32[]{:S(2)}) collective-permute-start(bf16[16,64,96]{2,1,0:T(8,128)(2,1)S(1)} %get-tuple-element.52), channel_id=1, source_target_pairs={{0,8},{8,16},{16,24},{24,0},{1,9},{9,17},{17,25},{25,1},{2,10},{10... | collective-permute-start | bytes 589832 | tf_op jit(solution)/shard_map/ppermute | solution.py:569
  80.9 13.5 %collective-permute-start.16 = (bf16[16,64,96]{2,1,0:T(8,128)(2,1)S(1)}, bf16[16,64,96]{2,1,0:T(8,128)(2,1)S(1)}, u32[]{:S(2)}, u32[]{:S(2)}) collective-permute-start(bf16[16,64,96]{2,1,0:T(8,128)(2,1)S(1)} %get-tuple-element.53), channel_id=1, source_target_pairs={{0,16},{8,24},{16,0},{24,8},{1,17},{9,25},{17,1},{25,9},{2,18},{10... | collective-permute-start | bytes 589832 | tf_op jit(solution)/shard_map/ppermute | solution.py:569
  82.4 12.5 %collective-permute-start.17 = (bf16[16,64,96]{2,1,0:T(8,128)(2,1)S(1)}, bf16[16,64,96]{2,1,0:T(8,128)(2,1)}, u32[]{:S(2)}, u32[]{:S(2)}) collective-permute-start(bf16[16,64,96]{2,1,0:T(8,128)(2,1)S(1)} %get-tuple-element.54), channel_id=1, source_target_pairs={{0,24},{8,0},{16,8},{24,16},{1,25},{9,1},{17,9},{25,17},{2,26},{10... | collective-permute-start | bytes 589832 | tf_op jit(solution)/shard_map/ppermute | solution.py:569
  (6 other events, 10.0 us)

commit v10 on v9

--- a/solution.py
+++ b/solution.py
@@ -237,6 +237,23 @@
     return 2 * column + (core if index < pairs else 1 - core)
 
 
+def payload_kernel(share, dy_ref, index_ref, gate_ref, *outs):
+    top, span = index_ref.shape
+    part = outs[0].shape[1]
+    per = share // span
+    names, gates = index_ref[...].astype(jnp.float32), gate_ref[...].astype(jnp.float32)
+    lines = [names[k : k + 1] for k in range(top)] + [gates[k : k + 1] for k in range(top)]
+    rows = [jnp.concatenate(lines[k : k + per], axis=1) for k in range(0, 2 * top, per)]
+    spare = outs[0].shape[0] - span - len(rows)
+    if spare:
+        rows.append(jnp.zeros((spare, share), jnp.float32))
+    below = jnp.concatenate(rows, axis=0).astype(jnp.bfloat16)
+    for c, out in enumerate(outs):
+        out[:span] = dy_ref[:, c * part : (c + 1) * part]
+        for at in range(0, part, share):
+            out[span:, at : at + share] = below
+
+
 def expert_kernel(capacity, group_count, shards, chunks, *refs):
     token_refs = refs[: shards * chunks]
     refs = refs[shards * chunks :]
@@ -267,10 +284,10 @@
     for copy in token_copies:
         copy.start()
 
-    def weight_copies(x):
+    def weight_copies(x, slot):
         return (
-            pltpu.make_async_copy(weight_hbm.at[x], wb_s.at[x, pl.ds(0, units)], w_sem.at[x]),
-            pltpu.make_async_copy(bmap_hbm.at[x], wb_s.at[x, pl.ds(units, rank)], b_sem.at[x]),
+            pltpu.make_async_copy(weight_hbm.at[x], wb_s.at[slot, pl.ds(0, units)], w_sem.at[x]),
+            pltpu.make_async_copy(bmap_hbm.at[x], wb_s.at[slot, pl.ds(units, rank)], b_sem.at[x]),
         )
 
     half = experts // 2
@@ -282,9 +299,12 @@
         picked = [(p, p, slice(0, rank)) for p in at]
         return picked + [(p + half, p, slice(rank, 2 * rank)) for p in at]
 
+    def slot_at(step, i):
+        return lax.rem(step, wb_s.shape[0] // (2 * batch)) * 2 * batch + i
+
     def request_weights(step):
-        for x, _, _ in members(step):
-            for copy in weight_copies(x):
+        for i, (x, _, _) in enumerate(members(step)):
+            for copy in weight_copies(x, slot_at(step, i)):
                 copy.start()
 
     for step in range(min(2, groups)):
@@ -340,8 +360,8 @@
 
     def main_products(step):
         xs = [x for x, _, _ in members(step)]
-        for x in xs:
-            for copy in weight_copies(x):
+        for i, x in enumerate(xs):
+            for copy in weight_copies(x, slot_at(step, i)):
                 copy.wait()
 
         @pl.when(step + 2 < groups)
@@ -349,8 +369,13 @@
             request_weights(step + 2)
 
         return [
-            lax.dot_general(rows_s[x], wb_s[x], contract_last, preferred_element_type=jnp.float32)
-            for x in xs
+            lax.dot_general(
+                rows_s[x],
+                wb_s[slot_at(step, i)],
+                contract_last,
+                preferred_element_type=jnp.float32,
+            )
+            for i, x in enumerate(xs)
         ]
 
     def keep_products(step, products):
@@ -449,8 +474,11 @@
 def adapter_kernel(capacity, micro, span, top, group_count, shards, *refs):
     pairs = shards // 2
     early_ref, early_far_ref, near_ref, far_ref = refs[:4]
-    lb_ref, tok_s, q_s, u_refs, sem, u_sem = refs[4:]
+    lb_hbm, tok_s, q_s, u_refs, lb_ref, sem, u_sem, lb_sem = refs[4:]
     experts, rank, share = lb_ref.shape
+    lb_copies = [
+        pltpu.make_async_copy(lb_ref.at[x], lb_hbm.at[x], lb_sem.at[x]) for x in range(experts)
+    ]
     blocks, tall = u_refs.shape[1:3]
     padded = tall // micro
     block = span // micro
@@ -521,6 +549,10 @@
         lb_ref[x + half] = adapter_scale * lax.dot_general(
             both[:, rank:], q_s[x + half], contract_first, preferred_element_type=jnp.float32
         )
+        lb_copies[x].start()
+        lb_copies[x + half].start()
+    for copy in lb_copies:
+        copy.wait()
 
 
 def ring_order(count):
@@ -586,24 +618,28 @@
         return lax.all_to_all(array, "dp", split_axis=0, concat_axis=0, tiled=True)
 
     others = range(1, group_count)
-    names = jnp.concatenate(
-        [chosen_expert_index.T.astype(jnp.bfloat16), routing_gate_weight.T], axis=0
-    )
     lines = 2 * top * span // share
-    names = jnp.tile(names.reshape(lines, share), (1, group_count))
     extra = -(-lines // 8) * 8
-    sent = jnp.concatenate(
-        [output_gradient, jnp.pad(names, ((0, extra - lines), (0, 0)))], axis=0
-    )
-
-    near, far = [[sent[:, c * part : (c + 1) * part] for c in range(chunks)]], []
+    vmem = pl.BlockSpec(memory_space=pltpu.VMEM)
+    sent = pl.pallas_call(
+        functools.partial(payload_kernel, share),
+        out_shape=[jax.ShapeDtypeStruct((span + extra, part), jnp.bfloat16)] * chunks,
+        in_specs=[vmem] * 3,
+        out_specs=[vmem] * chunks,
+        compiler_params=pltpu.CompilerParams(vmem_limit_bytes=58 * 1024 * 1024),
+        name="ring_payload",
+    )(output_gradient, chosen_expert_index.T, routing_gate_weight.T)
+
+    near, far = [list(sent)], []
     blocks = experts // 2 * 2 * rank // share
     packed = jnp.concatenate(
         [u[k * blocks : (k + 1) * blocks] for k in range(experts // 2 // blocks)], axis=-1
     ).reshape(blocks * micro * padded, share)
     early = jnp.stack(
         [
-            jnp.concatenate([packed, sent[:, g * share : (g + 1) * share]], axis=0)
+            jnp.concatenate(
+                [packed, sent[g * share // part][:, g * share % part :][:, :share]], axis=0
+            )
             for g in range(group_count)
         ]
     )
@@ -627,8 +663,8 @@
     columns = across_groups(columns)
     pieces = [piece for shard in near + far for piece in shard]
 
-    vmem = pl.BlockSpec(memory_space=pltpu.VMEM)
     anywhere = pl.BlockSpec(memory_space=pl.ANY)
+    kept = 3 * (4 if experts % 4 == 0 else 2)
     part_a = jax.ShapeDtypeStruct((experts, rank, units // group_count), jnp.bfloat16)
     hidden_grad, routed, *parts = pl.pallas_call(
         functools.partial(expert_kernel, capacity, group_count, sources, chunks),
@@ -641,7 +677,7 @@
         out_specs=(vmem,) * 2 + (anywhere,) * group_count,
         scratch_shapes=[
             pltpu.VMEM((sources, span + extra, width), jnp.bfloat16),
-            pltpu.VMEM((experts, units + rank, width), jnp.bfloat16),
+            pltpu.VMEM((min(experts, kept), units + rank, width), jnp.bfloat16),
             pltpu.VMEM((experts, micro * padded, width), jnp.bfloat16),
             pltpu.VMEM((experts, micro * padded, units + rank), jnp.float32),
             pltpu.VMEM((micro, 2, experts, sources // 2 * block), jnp.float32),
@@ -653,7 +689,7 @@
             pltpu.SemaphoreType.DMA((experts,)),
             pltpu.SemaphoreType.DMA((group_count,)),
         ],
-        compiler_params=pltpu.CompilerParams(vmem_limit_bytes=52 * 1024 * 1024),
+        compiler_params=pltpu.CompilerParams(vmem_limit_bytes=45 * 1024 * 1024),
         cost_estimate=pl.CostEstimate(
             flops=2 * experts * micro * padded * width * (units + rank + sources * block),
             bytes_accessed=2 * experts * width * (units + rank) + 2 * sources * span * width,
@@ -665,19 +701,22 @@
     columns, parts, routed = lax.optimization_barrier((columns, parts, routed))
     swapped = swap_partners(columns)
     arrived = [shift_groups(parts[s], s) for s in others]
+    swapped, routed = lax.optimization_barrier((swapped, routed))
     home = lax.all_to_all(routed, "expert", split_axis=0, concat_axis=0, tiled=True)
 
     lora_b = pl.pallas_call(
         functools.partial(adapter_kernel, capacity, micro, span, top, group_count, sources),
         out_shape=jax.ShapeDtypeStruct((experts, rank, share), jnp.float32),
         in_specs=[anywhere] * 4,
-        out_specs=vmem,
+        out_specs=anywhere,
         scratch_shapes=[
             pltpu.VMEM((group_count, sources, span + extra, share), jnp.bfloat16),
             pltpu.VMEM((experts, group_count * micro * padded, share), jnp.bfloat16),
             pltpu.VMEM((group_count, blocks, micro * padded, share), jnp.bfloat16),
+            pltpu.VMEM((experts, rank, share), jnp.float32),
             pltpu.SemaphoreType.DMA((group_count, sources)),
             pltpu.SemaphoreType.DMA((group_count, blocks)),
+            pltpu.SemaphoreType.DMA((experts,)),
         ],
         compiler_params=pltpu.CompilerParams(vmem_limit_bytes=58 * 1024 * 1024),
         cost_estimate=pl.CostEstimate(

time: 98 us -> 95.9 us (0.979)
  local copies, waits for them, and re-layouts: 7.53 us -> 16.9 us
  Pallas kernels: 29.8 us -> 24.9 us
  starting transfers between devices: 36.6 us -> 32 us
  other arithmetic: 9.74 us -> 6.99 us
  matrix products: 0.5 us -> 1.92 us
    unnamed x34 -> x50, local copies, waits for them, and re-layouts: 1.49 us -> 10.9 us
    pallas_call x1, Pallas kernels: 22.3 us -> 15.9 us  [local_by_tokens(): pl.pallas_call(functools.partial(expert_kernel, capacity, group_count, so...]
    ppermute x6, starting transfers between devices: 18.3 us -> 13 us  [local_by_tokens(): near.append([lax.ppermute(piece, 'expert', ring) for piece in near[step]])]
    ppermute x3, waiting for transfers between devices: 3.44 us -> 0.01 us  [shift_groups(): lax.ppermute(array, 'dp', [(d, (d + by) % group_count) for d in range(gro...]
    ppermute x6, waiting for transfers between devices: 8.77 us -> 11.6 us  [local_by_tokens(): near.append([lax.ppermute(piece, 'expert', ring) for piece in near[step]])]
    another operation x6, local copies, waits for them, and re-layouts: 5.85 us -> 3.61 us  [exchange_columns(): jnp.stack([columns(pieces, g) for pieces in chosen])]
    pallas_call x0 -> x1, Pallas kernels: none -> 1.89 us  [local_by_tokens(): pl.pallas_call(functools.partial(payload_kernel, share), out_shape=[jax.S...]
    concatenate x2 -> x0, other arithmetic: 1.78 us -> none  [the longest x1 1.09 us: local_by_tokens(): jnp.concatenate([output_gradient, jnp.pad(names, ((0, extra - lines), (0,...]
  transfers between devices with their start and end apart: 22 -> 22, of which waited for: 7 -> 5; matrix products, arithmetic and copies ran while one was open for 12% -> 14% of each run, Pallas kernels for 31% -> 24%
where the time goes in v10:
time: 95.9 us; the launch traced here: 95.2 us
  starting transfers between devices  32 us (33%)
  Pallas kernels  24.9 us (26%)
  local copies, waits for them, and re-layouts  16.9 us (18%)
  waiting for transfers between devices  11.6 us (12%)
  other arithmetic  6.99 us (7%)
  matrix products  1.92 us (2%)
  between operations  1 us (1%)
    pallas_call x1, Pallas kernels, local_by_tokens(): pl.pallas_call(functools.partial(expert_kernel, capacity, group_count, so...  15.9 us
    ppermute x6, starting transfers between devices, local_by_tokens(): near.append([lax.ppermute(piece, 'expert', ring) for piece in near[step]])  13 us
    ppermute x6, waiting for transfers between devices, local_by_tokens(): near.append([lax.ppermute(piece, 'expert', ring) for piece in near[step]])  11.6 us
    unnamed x50, local copies, waits for them, and re-layouts  10.9 us
    all_to_all x2, starting transfers between devices, across_groups(): return lax.all_to_all(array, 'dp', split_axis=0, concat_axis=0, tiled=True)  8.66 us
    pallas_call x1, Pallas kernels, local_by_tokens(): pl.pallas_call(functools.partial(adapter_kernel, capacity, micro, span, t...  7.11 us
    ppermute x3, starting transfers between devices, shift_groups(): lax.ppermute(array, 'dp', [(d, (d + by) % group_count) for d in range(gro...  4.86 us
    another operation x6, local copies, waits for them, and re-layouts, exchange_columns(): jnp.stack([columns(pieces, g) for pieces in chosen])  3.61 us
  transfers between devices with their start and end apart: 22, of which 5 were waited for; matrix products, arithmetic and copies ran while one was open for 14% of the time, Pallas kernels for 24%

profile of v10, /device:TPU:0, one launch (start us, length us, event | category | flops | bytes accessed | tf_op | source)
XLA Modules:
  0.0 95.2 jit_solution(8900988935456122096)
XLA Ops:
  0.6 1.9 %ring_payload.1 = (bf16[136,1024]{1,0:T(8,128)(2,1)}, bf16[136,1024]{1,0:T(8,128)(2,1)}) custom-call(bf16[128,2048]{1,0:T(8,128)(2,1)} %dy_ref.1, s32[8,128]{1,0:T(8,128)} %bitcast.58, bf16[8,128]{1,0:T(8,128)(2,1)} %bitcast.60), custom_call_target="tpu_custom_call" | custom-call | tf_op jit(solution)/shard_map/ring_payload/pallas_call | solution.py:624
  3.0 3.6 %collective-permute-start = (bf16[136,1024]{1,0:T(8,128)(2,1)}, bf16[136,1024]{1,0:T(8,128)(2,1)S(1)}, u32[]{:S(2)}, u32[]{:S(2)}) collective-permute-start(bf16[136,1024]{1,0:T(8,128)(2,1)} %get-tuple-element.38.refs_0_), channel_id=1, source_target_pairs={{0,4},{1,5},{2,0},{3,1},{4,6},{5,7},{6,2},{7,3},{8,12},{9,13},{10,... | collective-permute-start | bytes 835592 | tf_op jit(solution)/shard_map/ppermute | solution.py:656
  6.8 1.6 %collective-permute-start.1 = (bf16[136,1024]{1,0:T(8,128)(2,1)}, bf16[136,1024]{1,0:T(8,128)(2,1)S(1)}, u32[]{:S(2)}, u32[]{:S(2)}) collective-permute-start(bf16[136,1024]{1,0:T(8,128)(2,1)} %get-tuple-element.39.refs_1_), channel_id=1, source_target_pairs={{0,4},{1,5},{2,0},{3,1},{4,6},{5,7},{6,2},{7,3},{8,12},{9,13},{10,... | collective-permute-start | bytes 835592 | tf_op jit(solution)/shard_map/ppermute | solution.py:656
  8.4 1.1 %fusion.10 = (bf16[136,512]{1,0:T(8,128)(2,1)S(1)}, bf16[136,512]{1,0:T(8,128)(2,1)S(1)}, bf16[136,512]{1,0:T(8,128)(2,1)S(1)}, bf16[136,512]{1,0:T(8,128)(2,1)S(1)}) fusion(bf16[136,1024]{1,0:T(8,128)(2,1)} %get-tuple-element.38.refs_0_, bf16[136,1024]{1,0:T(8,128)(2,1)} %get-tuple-element.39.refs_1_), kind=kLoop, calls=%fused_computation.46 | loop fusion | bytes 1114112 | tf_op jit(solution)/shard_map/slice | solution.py:641
  9.5 1.9 %convolution_convert_fusion = bf16[16,2,40,64]{3,2,1,0:T(8,128)(2,1)S(1)} fusion(bf16[2,16,40,384]{3,2,1,0:T(8,128)(2,1)} %refs_16_.1, bf16[16,384,64]{1,2,0:T(8,128)(2,1)} %param.12), kind=kOutput, calls=%fused_computation.2 | convolution fusion | flops 62996480 | bytes 1933312 | tf_op jit(solution)/shard_map/mesk,exk->emsx/dot_general | solution.py:593
  11.8 1.2 %pad_maximum_fusion.1 = bf16[4,328,512]{2,1,0:T(8,128)(2,1)} fusion(bf16[1,328,512]{2,1,0:T(8,128)(2,1)S(1)} %get-tuple-element.97, bf16[1,328,512]{2,1,0:T(8,128)(2,1)S(1)} %get-tuple-element.96, bf16[1,328,512]{2,1,0:T(8,128)(2,1)S(1)} %get-tuple-element.95, bf16[1,328,512]{2,1,0:T(8,128)(2,1)S(1)} %get-tuple-element.94), kind=kLoop, calls=%fused_computation.1 | loop fusion | flops 2015232 | bytes 2686976 | tf_op jit(solution)/shard_map/stack | solution.py:638
  13.0 4.3 %all-to-all-start = ((bf16[4,328,512]{2,1,0:T(8,128)(2,1)}), bf16[4,328,512]{2,1,0:T(8,128)(2,1)}, u32[]{:S(2)}, u32[]{:S(2)}) async-start(bf16[4,328,512]{2,1,0:T(8,128)(2,1)} %pad_maximum_fusion.1), calls=%async_computation | async-start | bytes 2686976 | tf_op jit(solution)/shard_map/all_to_all | solution.py:618
  18.6 1.2 %collective-permute-done.1.refs_3_ = bf16[136,1024]{1,0:T(8,128)(2,1)S(1)} collective-permute-done((bf16[136,1024]{1,0:T(8,128)(2,1)}, bf16[136,1024]{1,0:T(8,128)(2,1)S(1)}, u32[]{:S(2)}, u32[]{:S(2)}) %collective-permute-start.1) | collective-permute-done | bytes 278560 | tf_op jit(solution)/shard_map/ppermute | solution.py:656
  19.8 3.3 %collective-permute-start.5 = (bf16[136,1024]{1,0:T(8,128)(2,1)S(1)}, bf16[136,1024]{1,0:T(8,128)(2,1)S(1)}, u32[]{:S(2)}, u32[]{:S(2)}) collective-permute-start(bf16[136,1024]{1,0:T(8,128)(2,1)S(1)} %collective-permute-done.1.refs_3_), channel_id=1, source_target_pairs={{0,4},{1,5},{2,0},{3,1},{4,6},{5,7},{6,2},{7,3},{8,12},{9,13},{10,... | collective-permute-start | bytes 835592 | tf_op jit(solution)/shard_map/ppermute | solution.py:656
  23.8 3.2 %collective-permute-done.2.refs_4_ = bf16[136,1024]{1,0:T(8,128)(2,1)S(1)} collective-permute-done((bf16[136,1024]{1,0:T(8,128)(2,1)S(1)}, bf16[136,1024]{1,0:T(8,128)(2,1)S(1)}, u32[]{:S(2)}, u32[]{:S(2)}) %collective-permute-start.2) | collective-permute-done | bytes 278560 | tf_op jit(solution)/shard_map/ppermute | solution.py:656
  27.0 2.1 %collective-permute-start.8 = (bf16[136,1024]{1,0:T(8,128)(2,1)S(1)}, bf16[136,1024]{1,0:T(8,128)(2,1)S(1)}, u32[]{:S(2)}, u32[]{:S(2)}) collective-permute-start(bf16[136,1024]{1,0:T(8,128)(2,1)S(1)} %collective-permute-done.2.refs_4_), channel_id=1, source_target_pairs={{0,4},{1,5},{2,0},{3,1},{4,6},{5,7},{6,2},{7,3},{8,12},{9,13},{10,... | collective-permute-start | bytes 835592 | tf_op jit(solution)/shard_map/ppermute | solution.py:656
  30.6 2.4 %collective-permute-done.5.refs_5_ = bf16[136,1024]{1,0:T(8,128)(2,1)S(1)} collective-permute-done((bf16[136,1024]{1,0:T(8,128)(2,1)S(1)}, bf16[136,1024]{1,0:T(8,128)(2,1)S(1)}, u32[]{:S(2)}, u32[]{:S(2)}) %collective-permute-start.5) | collective-permute-done | bytes 278560 | tf_op jit(solution)/shard_map/ppermute | solution.py:656
  32.9 2.1 %collective-permute-start.9 = (bf16[136,1024]{1,0:T(8,128)(2,1)S(1)}, bf16[136,1024]{1,0:T(8,128)(2,1)S(1)}, u32[]{:S(2)}, u32[]{:S(2)}) collective-permute-start(bf16[136,1024]{1,0:T(8,128)(2,1)S(1)} %collective-permute-done.5.refs_5_), channel_id=1, source_target_pairs={{0,4},{1,5},{2,0},{3,1},{4,6},{5,7},{6,2},{7,3},{8,12},{9,13},{10,... | collective-permute-start | bytes 835592 | tf_op jit(solution)/shard_map/ppermute | solution.py:656
  35.8 3.1 %collective-permute-done.8.refs_6_ = bf16[136,1024]{1,0:T(8,128)(2,1)S(1)} collective-permute-done((bf16[136,1024]{1,0:T(8,128)(2,1)S(1)}, bf16[136,1024]{1,0:T(8,128)(2,1)S(1)}, u32[]{:S(2)}, u32[]{:S(2)}) %collective-permute-start.8) | collective-permute-done | bytes 278560 | tf_op jit(solution)/shard_map/ppermute | solution.py:656
  39.6 1.1 %slice.110 = bf16[4,136,512]{2,1,0:T(8,128)(2,1)S(1)} slice(bf16[4,328,512]{2,1,0:T(8,128)(2,1)} %all-to-all-done.refs_0_), slice={[0:4], [192:328], [0:512]} | slice | bytes 1114112 | tf_op jit(solution)/shard_map/slice | solution.py:647
  40.9 1.3 %maximum_bitcast_fusion = (bf16[1,3,136,512]{3,2,1,0:T(8,128)(2,1)S(1)}, bf16[1,3,136,512]{3,2,1,0:T(8,128)(2,1)S(1)}) fusion(bf16[1,136,512]{2,1,0:T(8,128)(2,1)} %get-tuple-element.86, bf16[1,136,512]{2,1,0:T(8,128)(2,1)} %get-tuple-element.84, bf16[1,136,512]{2,1,0:T(8,128)(2,1)} %get-tuple-element.82, bf16[1,136,512]{2,1,0:T(8,128)(2,1)} %get-tuple-element.87, ...), kind=kLoop, calls=%fused_computation.10 | loop fusion | flops 835584 | bytes 1671168 | tf_op jit(solution)/shard_map/stack | solution.py:613
  42.8 1.6 %collective-permute-done.9.refs_7_ = bf16[136,1024]{1,0:T(8,128)(2,1)S(1)} collective-permute-done((bf16[136,1024]{1,0:T(8,128)(2,1)S(1)}, bf16[136,1024]{1,0:T(8,128)(2,1)S(1)}, u32[]{:S(2)}, u32[]{:S(2)}) %collective-permute-start.9) | collective-permute-done | bytes 278560 | tf_op jit(solution)/shard_map/ppermute | solution.py:656
  44.6 1.4 %pad_maximum_fusion = bf16[4,3,136,512]{3,2,1,0:T(8,128)(2,1)} fusion(bf16[1,3,136,512]{3,2,1,0:T(8,128)(2,1)S(1)} %get-tuple-element.101, bf16[1,3,136,512]{3,2,1,0:T(8,128)(2,1)S(1)} %get-tuple-element.100, bf16[1,3,136,512]{3,2,1,0:T(8,128)(2,1)S(1)} %get-tuple-element.103, bf16[1,3,136,512]{3,2,1,0:T(8,128)(2,1)S(1)} %get-tuple-element.102), kind=kLoop, calls=%fused_computation | loop fusion | flops 2506752 | bytes 3342336 | tf_op jit(solution)/shard_map/stack | solution.py:613
  47.4 4.4 %all-to-all-start.1 = ((bf16[4,3,136,512]{3,2,1,0:T(8,128)(2,1)}), bf16[4,3,136,512]{3,2,1,0:T(8,128)(2,1)}, u32[]{:S(2)}, u32[]{:S(2)}) async-start(bf16[4,3,136,512]{3,2,1,0:T(8,128)(2,1)} %pad_maximum_fusion), calls=%async_computation.1 | async-start | bytes 3342336 | tf_op jit(solution)/shard_map/all_to_all | solution.py:618
  51.8 1.1 %pad_maximum_fusion.7.refs_17_ = bf16[8,96,128]{2,1,0:T(8,128)(2,1)S(1)} fusion(bf16[8,96,64]{2,1,0:T(8,128)(2,1)} %bitcast.54, bf16[8,96,64]{2,1,0:T(8,128)(2,1)} %bitcast.56), kind=kLoop, calls=%fused_computation.37 | loop fusion | flops 393216 | bytes 393216 | tf_op jit(solution)/shard_map/concatenate | solution.py:598
  53.0 1.1 %copy-done.3 = bf16[16,384,64]{1,2,0:T(8,128)(2,1)S(1)} copy-done((bf16[16,384,64]{1,2,0:T(8,128)(2,1)S(1)}, bf16[16,384,64]{1,2,0:T(8,128)(2,1)}, u32[]{:S(2)}) %copy-start.3) | copy-done | bytes 786456
  54.1 1.0 %copy-done.5 = bf16[136,1024]{1,0:T(8,128)(2,1)S(1)} copy-done((bf16[136,1024]{1,0:T(8,128)(2,1)S(1)}, bf16[136,1024]{1,0:T(8,128)(2,1)}, u32[]{:S(2)}) %copy-start.5) | copy-done | bytes 278552
  55.1 1.0 %copy-done.7 = bf16[136,1024]{1,0:T(8,128)(2,1)S(1)} copy-done((bf16[136,1024]{1,0:T(8,128)(2,1)S(1)}, bf16[136,1024]{1,0:T(8,128)(2,1)}, u32[]{:S(2)}) %copy-start.7) | copy-done | bytes 278552
  56.0 1.0 %copy-done.9 = bf16[136,1024]{1,0:T(8,128)(2,1)S(1)} copy-done((bf16[136,1024]{1,0:T(8,128)(2,1)S(1)}, bf16[136,1024]{1,0:T(8,128)(2,1)}, u32[]{:S(2)}) %copy-start.9) | copy-done | bytes 278552
  57.0 1.0 %copy-done.11 = bf16[136,1024]{1,0:T(8,128)(2,1)S(1)} copy-done((bf16[136,1024]{1,0:T(8,128)(2,1)S(1)}, bf16[136,1024]{1,0:T(8,128)(2,1)}, u32[]{:S(2)}) %copy-start.11) | copy-done | bytes 278552
  57.9 1.0 %copy-done.13 = bf16[136,1024]{1,0:T(8,128)(2,1)S(1)} copy-done((bf16[136,1024]{1,0:T(8,128)(2,1)S(1)}, bf16[136,1024]{1,0:T(8,128)(2,1)}, u32[]{:S(2)}) %copy-start.13) | copy-done | bytes 278552
  58.9 15.9 %expert_rows.1 = (bf16[2,16,40,384]{3,2,1,0:T(8,128)(2,1)}, f32[8,8,128]{2,1,0:T(8,128)}, bf16[16,64,96]{2,1,0:T(8,128)(2,1)S(1)}, bf16[16,64,96]{2,1,0:T(8,128)...) custom-call(bf16[136,1024]{1,0:T(8,128)(2,1)S(1)} %copy-done, ...), custom_call_target="tpu_custom_call" | custom-call | flops 6039797760 | bytes 33554432 | tf_op jit(solution)/shard_map/expert_rows/pallas_call | solution.py:669
  78.1 2.0 %collective-permute-start.16 = (bf16[16,64,96]{2,1,0:T(8,128)(2,1)}, bf16[16,64,96]{2,1,0:T(8,128)(2,1)S(1)}, u32[]{:S(2)}, u32[]{:S(2)}) collective-permute-start(bf16[16,64,96]{2,1,0:T(8,128)(2,1)} %copy-done.18), channel_id=1, source_target_pairs={{0,8},{8,16},{16,24},{24,0},{1,9},{9,17},{17,25},{25,1},{2,10},{10... | collective-permute-start | bytes 589832 | tf_op jit(solution)/shard_map/ppermute | solution.py:601
  80.0 1.5 %collective-permute-start.17 = (bf16[16,64,96]{2,1,0:T(8,128)(2,1)}, bf16[16,64,96]{2,1,0:T(8,128)(2,1)S(1)}, u32[]{:S(2)}, u32[]{:S(2)}) collective-permute-start(bf16[16,64,96]{2,1,0:T(8,128)(2,1)} %copy-done.17), channel_id=1, source_target_pairs={{0,16},{8,24},{16,0},{24,8},{1,17},{9,25},{17,1},{25,9},{2,18},{10... | collective-permute-start | bytes 589832 | tf_op jit(solution)/shard_map/ppermute | solution.py:601
  81.5 1.5 %collective-permute-start.18 = (bf16[16,64,96]{2,1,0:T(8,128)(2,1)}, bf16[16,64,96]{2,1,0:T(8,128)(2,1)S(1)}, u32[]{:S(2)}, u32[]{:S(2)}) collective-permute-start(bf16[16,64,96]{2,1,0:T(8,128)(2,1)} %copy-done.16), channel_id=1, source_target_pairs={{0,24},{8,0},{16,8},{24,16},{1,25},{9,1},{17,9},{25,17},{2,26},{10... | collective-permute-start | bytes 589832 | tf_op jit(solution)/shard_map/ppermute | solution.py:601
  83.0 3.5 %all-to-all-start.2 = ((f32[8,8,128]{2,1,0:T(8,128)}), f32[8,8,128]{2,1,0:T(8,128)S(1)}, u32[]{:S(2)}, u32[]{:S(2)}) async-start(f32[8,8,128]{2,1,0:T(8,128)} %get-tuple-element.59), calls=%async_computation.2 | async-start | bytes 65536 | tf_op jit(solution)/shard_map/all_to_all | solution.py:705
  86.5 7.1 %adapter_columns.1 = f32[16,64,512]{2,1,0:T(8,128)} custom-call(bf16[4,328,512]{2,1,0:T(8,128)(2,1)} %all-to-all-done.refs_0_, bf16[4,136,512]{2,1,0:T(8,128)(2,1)} %collective-permute-done.10.refs_1_, bf16[4,3,136,512]{3,2,1,0:T(8,128)(2,1)} %all-to-all-done.1.refs_2_, bf16[4,3,136,512]{3,2,1,0:T(8,128)(2,1)} %copy-done.24), custom_call_target="tpu_custom_call" | custom-call | flops 3623878656 | bytes 6291456 | tf_op jit(solution)/shard_map/adapter_columns/pallas_call | solution.py:707
  (85 shorter events, 12.9 us)
Async XLA Ops:
  2.5 17.3 %collective-permute-start.3 = (bf16[136,1024]{1,0:T(8,128)(2,1)}, bf16[136,1024]{1,0:T(8,128)(2,1)S(1)}, u32[]{:S(2)}, u32[]{:S(2)}) collective-permute-start(bf16[136,1024]{1,0:T(8,128)(2,1)} %get-tuple-element.38.refs_0_), channel_id=1, source_target_pairs={{0,1},{1,0},{2,3},{3,2},{4,5},{5,4},{6,7},{7,6},{8,9},{9,8},{10,11... | collective-permute-start | bytes 835592 | tf_op jit(solution)/shard_map/ppermute | solution.py:606
  3.0 14.4 %collective-permute-start = (bf16[136,1024]{1,0:T(8,128)(2,1)}, bf16[136,1024]{1,0:T(8,128)(2,1)S(1)}, u32[]{:S(2)}, u32[]{:S(2)}) collective-permute-start(bf16[136,1024]{1,0:T(8,128)(2,1)} %get-tuple-element.38.refs_0_), channel_id=1, source_target_pairs={{0,4},{1,5},{2,0},{3,1},{4,6},{5,7},{6,2},{7,3},{8,12},{9,13},{10,... | collective-permute-start | bytes 835592 | tf_op jit(solution)/shard_map/ppermute | solution.py:656
  6.6 23.2 %collective-permute-start.6 = (bf16[136,1024]{1,0:T(8,128)(2,1)}, bf16[136,1024]{1,0:T(8,128)(2,1)S(1)}, u32[]{:S(2)}, u32[]{:S(2)}) collective-permute-start(bf16[136,1024]{1,0:T(8,128)(2,1)} %get-tuple-element.39.refs_1_), channel_id=1, source_target_pairs={{0,1},{1,0},{2,3},{3,2},{4,5},{5,4},{6,7},{7,6},{8,9},{9,8},{10,11... | collective-permute-start | bytes 835592 | tf_op jit(solution)/shard_map/ppermute | solution.py:606
  6.8 13.0 %collective-permute-start.1 = (bf16[136,1024]{1,0:T(8,128)(2,1)}, bf16[136,1024]{1,0:T(8,128)(2,1)S(1)}, u32[]{:S(2)}, u32[]{:S(2)}) collective-permute-start(bf16[136,1024]{1,0:T(8,128)(2,1)} %get-tuple-element.39.refs_1_), channel_id=1, source_target_pairs={{0,4},{1,5},{2,0},{3,1},{4,6},{5,7},{6,2},{7,3},{8,12},{9,13},{10,... | collective-permute-start | bytes 835592 | tf_op jit(solution)/shard_map/ppermute | solution.py:656
  11.5 5.8 %copy-start.19 = (bf16[8,2,48,64]{3,2,1,0:T(8,128)(2,1)}, bf16[8,2,48,64]{3,2,1,0:T(8,128)(2,1)S(1)}, u32[]{:S(2)}) copy-start(bf16[8,2,48,64]{3,2,1,0:T(8,128)(2,1)S(1)} %get-tuple-element.76) | copy-start | bytes 294916
  11.5 5.8 %copy-start.20 = (bf16[8,2,48,64]{3,2,1,0:T(8,128)(2,1)}, bf16[8,2,48,64]{3,2,1,0:T(8,128)(2,1)S(1)}, u32[]{:S(2)}) copy-start(bf16[8,2,48,64]{3,2,1,0:T(8,128)(2,1)S(1)} %get-tuple-element.77) | copy-start | bytes 294916
  13.0 26.6 %all-to-all-start = ((bf16[4,328,512]{2,1,0:T(8,128)(2,1)}), bf16[4,328,512]{2,1,0:T(8,128)(2,1)}, u32[]{:S(2)}, u32[]{:S(2)}) async-start(bf16[4,328,512]{2,1,0:T(8,128)(2,1)} %pad_maximum_fusion.1), calls=%async_computation | async-start | bytes 2686976 | tf_op jit(solution)/shard_map/all_to_all | solution.py:618
  17.4 6.4 %collective-permute-start.4 = (bf16[136,1024]{1,0:T(8,128)(2,1)S(1)}, bf16[136,1024]{1,0:T(8,128)(2,1)S(1)}, u32[]{:S(2)}, u32[]{:S(2)}) collective-permute-start(bf16[136,1024]{1,0:T(8,128)(2,1)S(1)} %collective-permute-done.refs_2_), channel_id=1, source_target_pairs={{0,1},{1,0},{2,3},{3,2},{4,5},{5,4},{6,7},{7,6},{8,9},{9,8},{10,11... | collective-permute-start | bytes 835592 | tf_op jit(solution)/shard_map/ppermute | solution.py:606
  17.4 9.5 %collective-permute-start.2 = (bf16[136,1024]{1,0:T(8,128)(2,1)S(1)}, bf16[136,1024]{1,0:T(8,128)(2,1)S(1)}, u32[]{:S(2)}, u32[]{:S(2)}) collective-permute-start(bf16[136,1024]{1,0:T(8,128)(2,1)S(1)} %collective-permute-done.refs_2_), channel_id=1, source_target_pairs={{0,4},{1,5},{2,0},{3,1},{4,6},{5,7},{6,2},{7,3},{8,12},{9,13},{10,... | collective-permute-start | bytes 835592 | tf_op jit(solution)/shard_map/ppermute | solution.py:656
  19.8 10.0 %collective-permute-start.7 = (bf16[136,1024]{1,0:T(8,128)(2,1)S(1)}, bf16[136,1024]{1,0:T(8,128)(2,1)S(1)}, u32[]{:S(2)}, u32[]{:S(2)}) collective-permute-start(bf16[136,1024]{1,0:T(8,128)(2,1)S(1)} %collective-permute-done.1.refs_3_), channel_id=1, source_target_pairs={{0,1},{1,0},{2,3},{3,2},{4,5},{5,4},{6,7},{7,6},{8,9},{9,8},{10,11... | collective-permute-start | bytes 835592 | tf_op jit(solution)/shard_map/ppermute | solution.py:606
  19.8 13.1 %collective-permute-start.5 = (bf16[136,1024]{1,0:T(8,128)(2,1)S(1)}, bf16[136,1024]{1,0:T(8,128)(2,1)S(1)}, u32[]{:S(2)}, u32[]{:S(2)}) collective-permute-start(bf16[136,1024]{1,0:T(8,128)(2,1)S(1)} %collective-permute-done.1.refs_3_), channel_id=1, source_target_pairs={{0,4},{1,5},{2,0},{3,1},{4,6},{5,7},{6,2},{7,3},{8,12},{9,13},{10,... | collective-permute-start | bytes 835592 | tf_op jit(solution)/shard_map/ppermute | solution.py:656
  23.8 18.4 %copy-start.6 = (bf16[136,1024]{1,0:T(8,128)(2,1)}, bf16[136,1024]{1,0:T(8,128)(2,1)S(1)}, u32[]{:S(2)}) copy-start(bf16[136,1024]{1,0:T(8,128)(2,1)S(1)} %collective-permute-done.4.refs_10_) | copy-start | bytes 835588
  27.0 11.9 %collective-permute-start.8 = (bf16[136,1024]{1,0:T(8,128)(2,1)S(1)}, bf16[136,1024]{1,0:T(8,128)(2,1)S(1)}, u32[]{:S(2)}, u32[]{:S(2)}) collective-permute-start(bf16[136,1024]{1,0:T(8,128)(2,1)S(1)} %collective-permute-done.2.refs_4_), channel_id=1, source_target_pairs={{0,4},{1,5},{2,0},{3,1},{4,6},{5,7},{6,2},{7,3},{8,12},{9,13},{10,... | collective-permute-start | bytes 835592 | tf_op jit(solution)/shard_map/ppermute | solution.py:656
  29.8 16.2 %collective-permute-start.11 = (bf16[136,1024]{1,0:T(8,128)(2,1)S(1)}, bf16[136,1024]{1,0:T(8,128)(2,1)}, u32[]{:S(2)}, u32[]{:S(2)}) collective-permute-start(bf16[136,1024]{1,0:T(8,128)(2,1)S(1)} %collective-permute-done.2.refs_4_), channel_id=1, source_target_pairs={{0,1},{1,0},{2,3},{3,2},{4,5},{5,4},{6,7},{7,6},{8,9},{9,8},{10,11... | collective-permute-start | bytes 835592 | tf_op jit(solution)/shard_map/ppermute | solution.py:606
  29.8 12.4 %copy-start.4 = (bf16[136,1024]{1,0:T(8,128)(2,1)}, bf16[136,1024]{1,0:T(8,128)(2,1)S(1)}, u32[]{:S(2)}) copy-start(bf16[136,1024]{1,0:T(8,128)(2,1)S(1)} %collective-permute-done.6.refs_9_) | copy-start | bytes 835588
  32.9 13.0 %collective-permute-start.12 = (bf16[136,1024]{1,0:T(8,128)(2,1)S(1)}, bf16[136,1024]{1,0:T(8,128)(2,1)}, u32[]{:S(2)}, u32[]{:S(2)}) collective-permute-start(bf16[136,1024]{1,0:T(8,128)(2,1)S(1)} %collective-permute-done.5.refs_5_), channel_id=1, source_target_pairs={{0,1},{1,0},{2,3},{3,2},{4,5},{5,4},{6,7},{7,6},{8,9},{9,8},{10,11... | collective-permute-start | bytes 835592 | tf_op jit(solution)/shard_map/ppermute | solution.py:606
  32.9 11.5 %collective-permute-start.9 = (bf16[136,1024]{1,0:T(8,128)(2,1)S(1)}, bf16[136,1024]{1,0:T(8,128)(2,1)S(1)}, u32[]{:S(2)}, u32[]{:S(2)}) collective-permute-start(bf16[136,1024]{1,0:T(8,128)(2,1)S(1)} %collective-permute-done.5.refs_5_), channel_id=1, source_target_pairs={{0,4},{1,5},{2,0},{3,1},{4,6},{5,7},{6,2},{7,3},{8,12},{9,13},{10,... | collective-permute-start | bytes 835592 | tf_op jit(solution)/shard_map/ppermute | solution.py:656
  39.6 4.8 %copy-start.22 = (bf16[1,136,512]{2,1,0:T(8,128)(2,1)S(1)}, bf16[1,136,512]{2,1,0:T(8,128)(2,1)}, u32[]{:S(2)}) copy-start(bf16[1,136,512]{2,1,0:T(8,128)(2,1)} %get-tuple-element.90) | copy-start | bytes 417796
  39.6 4.8 %copy-start.23 = (bf16[1,136,512]{2,1,0:T(8,128)(2,1)S(1)}, bf16[1,136,512]{2,1,0:T(8,128)(2,1)}, u32[]{:S(2)}) copy-start(bf16[1,136,512]{2,1,0:T(8,128)(2,1)} %get-tuple-element.91) | copy-start | bytes 417796
  40.8 6.6 %collective-permute-start.10 = (bf16[4,136,512]{2,1,0:T(8,128)(2,1)S(1)}, bf16[4,136,512]{2,1,0:T(8,128)(2,1)}, u32[]{:S(2)}, u32[]{:S(2)}) collective-permute-start(bf16[4,136,512]{2,1,0:T(8,128)(2,1)S(1)} %slice.110), channel_id=1, source_target_pairs={{0,1},{1,0},{2,3},{3,2},{4,5},{5,4},{6,7},{7,6},{8,9},{9,8},{10,11... | collective-permute-start | bytes 1671176 | tf_op jit(solution)/shard_map/ppermute | solution.py:606
  42.2 3.8 %collective-permute-start.13 = (bf16[136,1024]{1,0:T(8,128)(2,1)S(1)}, bf16[136,1024]{1,0:T(8,128)(2,1)S(1)}, u32[]{:S(2)}, u32[]{:S(2)}) collective-permute-start(bf16[136,1024]{1,0:T(8,128)(2,1)S(1)} %collective-permute-done.8.refs_6_), channel_id=1, source_target_pairs={{0,1},{1,0},{2,3},{3,2},{4,5},{5,4},{6,7},{7,6},{8,9},{9,8},{10,11... | collective-permute-start | bytes 835592 | tf_op jit(solution)/shard_map/ppermute | solution.py:606
  44.4 2.3 %collective-permute-start.14 = (bf16[136,1024]{1,0:T(8,128)(2,1)S(1)}, bf16[136,1024]{1,0:T(8,128)(2,1)S(1)}, u32[]{:S(2)}, u32[]{:S(2)}) collective-permute-start(bf16[136,1024]{1,0:T(8,128)(2,1)S(1)} %collective-permute-done.9.refs_7_), channel_id=1, source_target_pairs={{0,1},{1,0},{2,3},{3,2},{4,5},{5,4},{6,7},{7,6},{8,9},{9,8},{10,11... | collective-permute-start | bytes 835592 | tf_op jit(solution)/shard_map/ppermute | solution.py:606
  46.0 7.0 %copy-start = (bf16[136,1024]{1,0:T(8,128)(2,1)S(1)}, bf16[136,1024]{1,0:T(8,128)(2,1)}, u32[]{:S(2)}) copy-start(bf16[136,1024]{1,0:T(8,128)(2,1)} %get-tuple-element.38.refs_0_) | copy-start | bytes 835588
  46.0 7.0 %copy-start.1 = (bf16[136,1024]{1,0:T(8,128)(2,1)S(1)}, bf16[136,1024]{1,0:T(8,128)(2,1)}, u32[]{:S(2)}) copy-start(bf16[136,1024]{1,0:T(8,128)(2,1)} %get-tuple-element.39.refs_1_) | copy-start | bytes 835588
  46.0 7.0 %copy-start.2 = (bf16[2,16,40,384]{3,2,1,0:T(8,128)(2,1)S(1)}, bf16[2,16,40,384]{3,2,1,0:T(8,128)(2,1)}, u32[]{:S(2)}) copy-start(bf16[2,16,40,384]{3,2,1,0:T(8,128)(2,1)} %refs_16_.1) | copy-start | bytes 2949124
  47.4 30.2 %all-to-all-start.1 = ((bf16[4,3,136,512]{3,2,1,0:T(8,128)(2,1)}), bf16[4,3,136,512]{3,2,1,0:T(8,128)(2,1)}, u32[]{:S(2)}, u32[]{:S(2)}) async-start(bf16[4,3,136,512]{3,2,1,0:T(8,128)(2,1)} %pad_maximum_fusion), calls=%async_computation.1 | async-start | bytes 3342336 | tf_op jit(solution)/shard_map/all_to_all | solution.py:618
  77.6 5.4 %collective-permute-start.15 = (bf16[4,3,136,512]{3,2,1,0:T(8,128)(2,1)}, bf16[4,3,136,512]{3,2,1,0:T(8,128)(2,1)S(1)}, u32[]{:S(2)}, u32[]{:S(2)}) collective-permute-start(bf16[4,3,136,512]{3,2,1,0:T(8,128)(2,1)} %all-to-all-done.1.refs_2_), channel_id=1, source_target_pairs={{0,1},{1,0},{2,3},{3,2},{4,5},{5,4},{6,7},{7,6},{8,9},{9,8},{10,11... | collective-permute-start | bytes 5013512 | tf_op jit(solution)/shard_map/ppermute | solution.py:606
  78.1 15.5 %collective-permute-start.16 = (bf16[16,64,96]{2,1,0:T(8,128)(2,1)}, bf16[16,64,96]{2,1,0:T(8,128)(2,1)S(1)}, u32[]{:S(2)}, u32[]{:S(2)}) collective-permute-start(bf16[16,64,96]{2,1,0:T(8,128)(2,1)} %copy-done.18), channel_id=1, source_target_pairs={{0,8},{8,16},{16,24},{24,0},{1,9},{9,17},{17,25},{25,1},{2,10},{10... | collective-permute-start | bytes 589832 | tf_op jit(solution)/shard_map/ppermute | solution.py:601
  80.0 13.6 %collective-permute-start.17 = (bf16[16,64,96]{2,1,0:T(8,128)(2,1)}, bf16[16,64,96]{2,1,0:T(8,128)(2,1)S(1)}, u32[]{:S(2)}, u32[]{:S(2)}) collective-permute-start(bf16[16,64,96]{2,1,0:T(8,128)(2,1)} %copy-done.17), channel_id=1, source_target_pairs={{0,16},{8,24},{16,0},{24,8},{1,17},{9,25},{17,1},{25,9},{2,18},{10... | collective-permute-start | bytes 589832 | tf_op jit(solution)/shard_map/ppermute | solution.py:601
  81.5 12.1 %collective-permute-start.18 = (bf16[16,64,96]{2,1,0:T(8,128)(2,1)}, bf16[16,64,96]{2,1,0:T(8,128)(2,1)S(1)}, u32[]{:S(2)}, u32[]{:S(2)}) collective-permute-start(bf16[16,64,96]{2,1,0:T(8,128)(2,1)} %copy-done.16), channel_id=1, source_target_pairs={{0,24},{8,0},{16,8},{24,16},{1,25},{9,1},{17,9},{25,17},{2,26},{10... | collective-permute-start | bytes 589832 | tf_op jit(solution)/shard_map/ppermute | solution.py:601
  83.0 10.7 %all-to-all-start.2 = ((f32[8,8,128]{2,1,0:T(8,128)}), f32[8,8,128]{2,1,0:T(8,128)S(1)}, u32[]{:S(2)}, u32[]{:S(2)}) async-start(f32[8,8,128]{2,1,0:T(8,128)} %get-tuple-element.59), calls=%async_computation.2 | async-start | bytes 65536 | tf_op jit(solution)/shard_map/all_to_all | solution.py:705
  86.5 7.8 %copy-start.15 = (bf16[16,64,96]{2,1,0:T(8,128)(2,1)S(1)}, bf16[16,64,96]{2,1,0:T(8,128)(2,1)}, u32[]{:S(2)}) copy-start(bf16[16,64,96]{2,1,0:T(8,128)(2,1)} %copy-done.14) | copy-start | bytes 589828
  (15 other events, 19.2 us)

commit v11 on v10

--- a/solution.py
+++ b/solution.py
@@ -257,11 +257,11 @@
 def expert_kernel(capacity, group_count, shards, chunks, *refs):
     token_refs = refs[: shards * chunks]
     refs = refs[shards * chunks :]
-    hidden_ref, u_ref, weight_hbm, amap_ref, bmap_hbm, hg_ref, rk_ref = refs[:7]
+    hidden_hbm, u_hbm, weight_hbm, amap_hbm, bmap_hbm, hg_ref, rk_ref = refs[:7]
     la_outs = refs[7 : 7 + group_count]
     scratch = refs[7 + group_count :]
     dy_s, wb_s, rows_s, y_s, code_s, gate_s, back_s, la_s = scratch[:8]
-    dy_sem, w_sem, b_sem, la_sem = scratch[8:]
+    hidden_ref, u_ref, amap_ref, dy_sem, w_sem, b_sem, la_sem, in_sem = scratch[8:]
     top, span = rk_ref.shape[1:]
     micro, experts, slots, units = hidden_ref.shape
     rank = amap_ref.shape[1]
@@ -307,8 +307,17 @@
             for copy in weight_copies(x, slot_at(step, i)):
                 copy.start()
 
-    for step in range(min(2, groups)):
-        request_weights(step)
+    request_weights(0)
+    late_copies = [
+        pltpu.make_async_copy(source, target, in_sem.at[k])
+        for k, (source, target) in enumerate(
+            [(hidden_hbm, hidden_ref), (u_hbm, u_ref), (amap_hbm, amap_ref)]
+        )
+    ]
+    for copy in late_copies:
+        copy.start()
+    if groups > 1:
+        request_weights(1)
 
     for copy in token_copies:
         copy.wait()
@@ -444,6 +453,8 @@
         return carry
 
     keep_products(0, main_products(0))
+    for copy in late_copies:
+        copy.wait()
     lax.fori_loop(1, groups, both_steps, 0)
     small_steps(groups - 1)
 
@@ -673,7 +684,7 @@
             jax.ShapeDtypeStruct((sources, top, span), jnp.float32),
         )
         + (part_a,) * group_count,
-        in_specs=[anywhere] * (sources * chunks) + [vmem, vmem, anywhere, vmem, anywhere],
+        in_specs=[anywhere] * (sources * chunks) + [anywhere] * 5,
         out_specs=(vmem,) * 2 + (anywhere,) * group_count,
         scratch_shapes=[
             pltpu.VMEM((sources, span + extra, width), jnp.bfloat16),
@@ -684,12 +695,16 @@
             pltpu.VMEM((experts, micro * padded, 1), jnp.float32),
             pltpu.VMEM((micro, 2, experts, sources // 2 * block), jnp.float32),
             pltpu.VMEM((group_count, experts, rank, units // group_count), jnp.bfloat16),
+            pltpu.VMEM(hidden.shape, jnp.bfloat16),
+            pltpu.VMEM(u.shape, jnp.bfloat16),
+            pltpu.VMEM(amap.shape, jnp.bfloat16),
             pltpu.SemaphoreType.DMA((sources, chunks)),
             pltpu.SemaphoreType.DMA((experts,)),
             pltpu.SemaphoreType.DMA((experts,)),
             pltpu.SemaphoreType.DMA((group_count,)),
+            pltpu.SemaphoreType.DMA((3,)),
         ],
-        compiler_params=pltpu.CompilerParams(vmem_limit_bytes=45 * 1024 * 1024),
+        compiler_params=pltpu.CompilerParams(vmem_limit_bytes=58 * 1024 * 1024),
         cost_estimate=pl.CostEstimate(
             flops=2 * experts * micro * padded * width * (units + rank + sources * block),
             bytes_accessed=2 * experts * width * (units + rank) + 2 * sources * span * width,

time: 95.9 us -> 92 us (0.959)
  local copies, waits for them, and re-layouts: 16.9 us -> 7.05 us
  Pallas kernels: 24.9 us -> 31.1 us
    unnamed x50 -> x34, local copies, waits for them, and re-layouts: 10.9 us -> 2.15 us
    pallas_call x1, Pallas kernels: 15.9 us -> 22.1 us  [local_by_tokens(): pl.pallas_call(functools.partial(expert_kernel, capacity, group_count, so...]
    ppermute x6, starting transfers between devices: 13 us -> 14.4 us  [local_by_tokens(): near.append([lax.ppermute(piece, 'expert', ring) for piece in near[step]])]
    slice x1, local copies, waits for them, and re-layouts: 1.15 us -> 0.04 us  [local_by_tokens(): early_far = swap_partners(early[:, blocks * micro * padded:])]
  transfers between devices with their start and end apart: 22 -> 22, of which waited for: 5 -> 6; matrix products, arithmetic and copies ran while one was open for 14% -> 14% of each run, Pallas kernels for 24% -> 32%
where the time goes in v11:
time: 92 us; the launch traced here: 91.5 us
  starting transfers between devices  32 us (35%)
  Pallas kernels  31.1 us (34%)
  waiting for transfers between devices  11.4 us (12%)
  other arithmetic  7.15 us (8%)
  local copies, waits for them, and re-layouts  7.05 us (8%)
  matrix products  1.91 us (2%)
  between operations  0.94 us (1%)
    pallas_call x1, Pallas kernels, local_by_tokens(): pl.pallas_call(functools.partial(expert_kernel, capacity, group_count, so...  22.1 us
    ppermute x6, starting transfers between devices, local_by_tokens(): near.append([lax.ppermute(piece, 'expert', ring) for piece in near[step]])  14.4 us
    ppermute x6, waiting for transfers between devices, local_by_tokens(): near.append([lax.ppermute(piece, 'expert', ring) for piece in near[step]])  11.2 us
    all_to_all x2, starting transfers between devices, across_groups(): return lax.all_to_all(array, 'dp', split_axis=0, concat_axis=0, tiled=True)  7.85 us
    pallas_call x1, Pallas kernels, local_by_tokens(): pl.pallas_call(functools.partial(adapter_kernel, capacity, micro, span, t...  7.08 us
    ppermute x3, starting transfers between devices, shift_groups(): lax.ppermute(array, 'dp', [(d, (d + by) % group_count) for d in range(gro...  4.79 us
    all_to_all x1, starting transfers between devices, local_by_tokens(): lax.all_to_all(routed, 'expert', split_axis=0, concat_axis=0, tiled=True)  3.78 us
    another operation x6, local copies, waits for them, and re-layouts, exchange_columns(): jnp.stack([columns(pieces, g) for pieces in chosen])  3.66 us
  transfers between devices with their start and end apart: 22, of which 6 were waited for; matrix products, arithmetic and copies ran while one was open for 14% of the time, Pallas kernels for 32%

profile of v11, /device:TPU:0, one launch (start us, length us, event | category | flops | bytes accessed | tf_op | source)
XLA Modules:
  0.0 91.5 jit_solution(4052395653530230630)
XLA Ops:
  0.6 1.9 %ring_payload.1 = (bf16[136,1024]{1,0:T(8,128)(2,1)}, bf16[136,1024]{1,0:T(8,128)(2,1)}) custom-call(bf16[128,2048]{1,0:T(8,128)(2,1)} %dy_ref.1, s32[8,128]{1,0:T(8,128)} %bitcast.58, bf16[8,128]{1,0:T(8,128)(2,1)} %bitcast.60), custom_call_target="tpu_custom_call" | custom-call | tf_op jit(solution)/shard_map/ring_payload/pallas_call | solution.py:635
  3.0 3.6 %collective-permute-start = (bf16[136,1024]{1,0:T(8,128)(2,1)}, bf16[136,1024]{1,0:T(8,128)(2,1)S(1)}, u32[]{:S(2)}, u32[]{:S(2)}) collective-permute-start(bf16[136,1024]{1,0:T(8,128)(2,1)} %get-tuple-element.38.refs_0_), channel_id=1, source_target_pairs={{0,4},{1,5},{2,0},{3,1},{4,6},{5,7},{6,2},{7,3},{8,12},{9,13},{10,... | collective-permute-start | bytes 835592 | tf_op jit(solution)/shard_map/ppermute | solution.py:667
  6.8 1.6 %collective-permute-start.1 = (bf16[136,1024]{1,0:T(8,128)(2,1)}, bf16[136,1024]{1,0:T(8,128)(2,1)S(1)}, u32[]{:S(2)}, u32[]{:S(2)}) collective-permute-start(bf16[136,1024]{1,0:T(8,128)(2,1)} %get-tuple-element.39.refs_1_), channel_id=1, source_target_pairs={{0,4},{1,5},{2,0},{3,1},{4,6},{5,7},{6,2},{7,3},{8,12},{9,13},{10,... | collective-permute-start | bytes 835592 | tf_op jit(solution)/shard_map/ppermute | solution.py:667
  8.4 1.1 %fusion.10 = (bf16[136,512]{1,0:T(8,128)(2,1)S(1)}, bf16[136,512]{1,0:T(8,128)(2,1)S(1)}, bf16[136,512]{1,0:T(8,128)(2,1)S(1)}, bf16[136,512]{1,0:T(8,128)(2,1)S(1)}) fusion(bf16[136,1024]{1,0:T(8,128)(2,1)} %get-tuple-element.38.refs_0_, bf16[136,1024]{1,0:T(8,128)(2,1)} %get-tuple-element.39.refs_1_), kind=kLoop, calls=%fused_computation.46 | loop fusion | bytes 1114112 | tf_op jit(solution)/shard_map/slice | solution.py:652
  9.5 1.9 %convolution_convert_fusion = bf16[16,2,40,64]{3,2,1,0:T(8,128)(2,1)S(1)} fusion(bf16[2,16,40,384]{3,2,1,0:T(8,128)(2,1)} %refs_16_.1, bf16[16,384,64]{1,2,0:T(8,128)(2,1)} %param.12), kind=kOutput, calls=%fused_computation.2 | convolution fusion | flops 62996480 | bytes 1933312 | tf_op jit(solution)/shard_map/mesk,exk->emsx/dot_general | solution.py:604
  11.8 1.2 %pad_maximum_fusion.1 = bf16[4,328,512]{2,1,0:T(8,128)(2,1)} fusion(bf16[1,328,512]{2,1,0:T(8,128)(2,1)S(1)} %get-tuple-element.97, bf16[1,328,512]{2,1,0:T(8,128)(2,1)S(1)} %get-tuple-element.96, bf16[1,328,512]{2,1,0:T(8,128)(2,1)S(1)} %get-tuple-element.95, bf16[1,328,512]{2,1,0:T(8,128)(2,1)S(1)} %get-tuple-element.94), kind=kLoop, calls=%fused_computation.1 | loop fusion | flops 2015232 | bytes 2686976 | tf_op jit(solution)/shard_map/stack | solution.py:649
  13.0 3.7 %all-to-all-start = ((bf16[4,328,512]{2,1,0:T(8,128)(2,1)}), bf16[4,328,512]{2,1,0:T(8,128)(2,1)S(1)}, u32[]{:S(2)}, u32[]{:S(2)}) async-start(bf16[4,328,512]{2,1,0:T(8,128)(2,1)} %pad_maximum_fusion.1), calls=%async_computation | async-start | bytes 2686976 | tf_op jit(solution)/shard_map/all_to_all | solution.py:629
  17.2 0.7 slice_bitcast_fusion.7
  17.9 1.9 %collective-permute-done.1.refs_3_ = bf16[136,1024]{1,0:T(8,128)(2,1)S(1)} collective-permute-done((bf16[136,1024]{1,0:T(8,128)(2,1)}, bf16[136,1024]{1,0:T(8,128)(2,1)S(1)}, u32[]{:S(2)}, u32[]{:S(2)}) %collective-permute-start.1) | collective-permute-done | bytes 278560 | tf_op jit(solution)/shard_map/ppermute | solution.py:667
  19.8 3.3 %collective-permute-start.5 = (bf16[136,1024]{1,0:T(8,128)(2,1)S(1)}, bf16[136,1024]{1,0:T(8,128)(2,1)S(1)}, u32[]{:S(2)}, u32[]{:S(2)}) collective-permute-start(bf16[136,1024]{1,0:T(8,128)(2,1)S(1)} %collective-permute-done.1.refs_3_), channel_id=1, source_target_pairs={{0,4},{1,5},{2,0},{3,1},{4,6},{5,7},{6,2},{7,3},{8,12},{9,13},{10,... | collective-permute-start | bytes 835592 | tf_op jit(solution)/shard_map/ppermute | solution.py:667
  23.8 0.7 copy-done.12
  24.5 1.8 %collective-permute-done.2.refs_4_ = bf16[136,1024]{1,0:T(8,128)(2,1)S(1)} collective-permute-done((bf16[136,1024]{1,0:T(8,128)(2,1)S(1)}, bf16[136,1024]{1,0:T(8,128)(2,1)S(1)}, u32[]{:S(2)}, u32[]{:S(2)}) %collective-permute-start.2) | collective-permute-done | bytes 278560 | tf_op jit(solution)/shard_map/ppermute | solution.py:667
  26.3 2.7 %collective-permute-start.8 = (bf16[136,1024]{1,0:T(8,128)(2,1)S(1)}, bf16[136,1024]{1,0:T(8,128)(2,1)S(1)}, u32[]{:S(2)}, u32[]{:S(2)}) collective-permute-start(bf16[136,1024]{1,0:T(8,128)(2,1)S(1)} %collective-permute-done.2.refs_4_), channel_id=1, source_target_pairs={{0,4},{1,5},{2,0},{3,1},{4,6},{5,7},{6,2},{7,3},{8,12},{9,13},{10,... | collective-permute-start | bytes 835592 | tf_op jit(solution)/shard_map/ppermute | solution.py:667
  29.1 0.7 slice_bitcast_fusion.11
  29.8 2.5 %collective-permute-done.5.refs_5_ = bf16[136,1024]{1,0:T(8,128)(2,1)S(1)} collective-permute-done((bf16[136,1024]{1,0:T(8,128)(2,1)S(1)}, bf16[136,1024]{1,0:T(8,128)(2,1)S(1)}, u32[]{:S(2)}, u32[]{:S(2)}) %collective-permute-start.5) | collective-permute-done | bytes 278560 | tf_op jit(solution)/shard_map/ppermute | solution.py:667
  32.3 2.8 %collective-permute-start.9 = (bf16[136,1024]{1,0:T(8,128)(2,1)S(1)}, bf16[136,1024]{1,0:T(8,128)(2,1)S(1)}, u32[]{:S(2)}, u32[]{:S(2)}) collective-permute-start(bf16[136,1024]{1,0:T(8,128)(2,1)S(1)} %collective-permute-done.5.refs_5_), channel_id=1, source_target_pairs={{0,4},{1,5},{2,0},{3,1},{4,6},{5,7},{6,2},{7,3},{8,12},{9,13},{10,... | collective-permute-start | bytes 835592 | tf_op jit(solution)/shard_map/ppermute | solution.py:667
  35.1 0.7 slice_bitcast_fusion.9
  35.8 2.5 %collective-permute-done.8.refs_6_ = bf16[136,1024]{1,0:T(8,128)(2,1)S(1)} collective-permute-done((bf16[136,1024]{1,0:T(8,128)(2,1)S(1)}, bf16[136,1024]{1,0:T(8,128)(2,1)S(1)}, u32[]{:S(2)}, u32[]{:S(2)}) %collective-permute-start.8) | collective-permute-done | bytes 278560 | tf_op jit(solution)/shard_map/ppermute | solution.py:667
  38.3 0.8 slice_bitcast_fusion.6
  39.2 1.8 %maximum_bitcast_fusion = (bf16[1,3,136,512]{3,2,1,0:T(8,128)(2,1)S(1)}, bf16[1,3,136,512]{3,2,1,0:T(8,128)(2,1)S(1)}) fusion(bf16[1,136,512]{2,1,0:T(8,128)(2,1)} %get-tuple-element.86, bf16[1,136,512]{2,1,0:T(8,128)(2,1)} %get-tuple-element.84, bf16[1,136,512]{2,1,0:T(8,128)(2,1)} %get-tuple-element.82, bf16[1,136,512]{2,1,0:T(8,128)(2,1)} %get-tuple-element.87, ...), kind=kLoop, calls=%fused_computation.10 | loop fusion | flops 835584 | bytes 1671168 | tf_op jit(solution)/shard_map/stack | solution.py:624
  41.2 2.6 %collective-permute-done.9.refs_7_ = bf16[136,1024]{1,0:T(8,128)(2,1)S(1)} collective-permute-done((bf16[136,1024]{1,0:T(8,128)(2,1)S(1)}, bf16[136,1024]{1,0:T(8,128)(2,1)S(1)}, u32[]{:S(2)}, u32[]{:S(2)}) %collective-permute-start.9) | collective-permute-done | bytes 278560 | tf_op jit(solution)/shard_map/ppermute | solution.py:667
  43.9 1.4 %pad_maximum_fusion = bf16[4,3,136,512]{3,2,1,0:T(8,128)(2,1)} fusion(bf16[1,3,136,512]{3,2,1,0:T(8,128)(2,1)S(1)} %get-tuple-element.101, bf16[1,3,136,512]{3,2,1,0:T(8,128)(2,1)S(1)} %get-tuple-element.100, bf16[1,3,136,512]{3,2,1,0:T(8,128)(2,1)S(1)} %get-tuple-element.103, bf16[1,3,136,512]{3,2,1,0:T(8,128)(2,1)S(1)} %get-tuple-element.102), kind=kLoop, calls=%fused_computation | loop fusion | flops 2506752 | bytes 3342336 | tf_op jit(solution)/shard_map/stack | solution.py:624
  46.1 0.7 copy-done.15
  46.8 4.1 %all-to-all-start.1 = ((bf16[4,3,136,512]{3,2,1,0:T(8,128)(2,1)}), bf16[4,3,136,512]{3,2,1,0:T(8,128)(2,1)S(1)}, u32[]{:S(2)}, u32[]{:S(2)}) async-start(bf16[4,3,136,512]{3,2,1,0:T(8,128)(2,1)} %pad_maximum_fusion), calls=%async_computation.1 | async-start | bytes 3342336 | tf_op jit(solution)/shard_map/all_to_all | solution.py:629
  50.9 0.8 pad_maximum_fusion.7.refs_17_
  51.7 22.1 %expert_rows.1 = (bf16[2,16,40,384]{3,2,1,0:T(8,128)(2,1)}, f32[8,8,128]{2,1,0:T(8,128)}, bf16[16,64,96]{2,1,0:T(8,128)(2,1)}, bf16[16,64,96]{2,1,0:T(8,128)(2,1...) custom-call(bf16[136,1024]{1,0:T(8,128)(2,1)} %get-tuple-element.38.refs_0_, ...), custom_call_target="tpu_custom_call" | custom-call | flops 6039797760 | bytes 33554432 | tf_op jit(solution)/shard_map/expert_rows/pallas_call | solution.py:680
  74.1 1.9 %collective-permute-start.16 = (bf16[16,64,96]{2,1,0:T(8,128)(2,1)}, bf16[16,64,96]{2,1,0:T(8,128)(2,1)S(1)}, u32[]{:S(2)}, u32[]{:S(2)}) collective-permute-start(bf16[16,64,96]{2,1,0:T(8,128)(2,1)} %get-tuple-element.60), channel_id=1, source_target_pairs={{0,8},{8,16},{16,24},{24,0},{1,9},{9,17},{17,25},{25,1},{2,10},{10... | collective-permute-start | bytes 589832 | tf_op jit(solution)/shard_map/ppermute | solution.py:612
  76.0 1.5 %collective-permute-start.17 = (bf16[16,64,96]{2,1,0:T(8,128)(2,1)}, bf16[16,64,96]{2,1,0:T(8,128)(2,1)S(1)}, u32[]{:S(2)}, u32[]{:S(2)}) collective-permute-start(bf16[16,64,96]{2,1,0:T(8,128)(2,1)} %get-tuple-element.61), channel_id=1, source_target_pairs={{0,16},{8,24},{16,0},{24,8},{1,17},{9,25},{17,1},{25,9},{2,18},{10... | collective-permute-start | bytes 589832 | tf_op jit(solution)/shard_map/ppermute | solution.py:612
  77.5 1.5 %collective-permute-start.18 = (bf16[16,64,96]{2,1,0:T(8,128)(2,1)}, bf16[16,64,96]{2,1,0:T(8,128)(2,1)S(1)}, u32[]{:S(2)}, u32[]{:S(2)}) collective-permute-start(bf16[16,64,96]{2,1,0:T(8,128)(2,1)} %get-tuple-element.62), channel_id=1, source_target_pairs={{0,24},{8,0},{16,8},{24,16},{1,25},{9,1},{17,9},{25,17},{2,26},{10... | collective-permute-start | bytes 589832 | tf_op jit(solution)/shard_map/ppermute | solution.py:612
  78.9 3.8 %all-to-all-start.2 = ((f32[8,8,128]{2,1,0:T(8,128)}), f32[8,8,128]{2,1,0:T(8,128)S(1)}, u32[]{:S(2)}, u32[]{:S(2)}) async-start(f32[8,8,128]{2,1,0:T(8,128)} %get-tuple-element.59), calls=%async_computation.2 | async-start | bytes 65536 | tf_op jit(solution)/shard_map/all_to_all | solution.py:720
  82.7 7.1 %adapter_columns.1 = f32[16,64,512]{2,1,0:T(8,128)} custom-call(bf16[4,328,512]{2,1,0:T(8,128)(2,1)} %copy-done, bf16[4,136,512]{2,1,0:T(8,128)(2,1)} %collective-permute-done.10.refs_1_, bf16[4,3,136,512]{3,2,1,0:T(8,128)(2,1)} %copy-done.1, bf16[4,3,136,512]{3,2,1,0:T(8,128)(2,1)} %collective-permute-done.15.refs_3_), custom_call_target="tpu_custom_call" | custom-call | flops 3623878656 | bytes 6291456 | tf_op jit(solution)/shard_map/adapter_columns/pallas_call | solution.py:722
  90.6 1.0 %convert_add_fusion = f32[16,64,96]{2,1,0:T(8,128)} fusion(bf16[16,64,96]{2,1,0:T(8,128)(2,1)S(1)} %collective-permute-done.18, bf16[16,64,96]{2,1,0:T(8,128)(2,1)S(1)} %collective-permute-done.17, bf16[16,64,96]{2,1,0:T(8,128)(2,1)S(1)} %collective-permute-done.16, bf16[16,64,96]{2,1,0:T(8,128)(2,1)S(1)} %copy-done.16), kind=kLoop, calls=%fused_computation.5 | loop fusion | flops 688128 | bytes 1179648 | tf_op jit(solution)/shard_map/add | solution.py:749
  (69 shorter events, 4.3 us)
Async XLA Ops:
  2.5 17.3 %collective-permute-start.3 = (bf16[136,1024]{1,0:T(8,128)(2,1)}, bf16[136,1024]{1,0:T(8,128)(2,1)}, u32[]{:S(2)}, u32[]{:S(2)}) collective-permute-start(bf16[136,1024]{1,0:T(8,128)(2,1)} %get-tuple-element.38.refs_0_), channel_id=1, source_target_pairs={{0,1},{1,0},{2,3},{3,2},{4,5},{5,4},{6,7},{7,6},{8,9},{9,8},{10,11... | collective-permute-start | bytes 835592 | tf_op jit(solution)/shard_map/ppermute | solution.py:617
  3.0 13.8 %collective-permute-start = (bf16[136,1024]{1,0:T(8,128)(2,1)}, bf16[136,1024]{1,0:T(8,128)(2,1)S(1)}, u32[]{:S(2)}, u32[]{:S(2)}) collective-permute-start(bf16[136,1024]{1,0:T(8,128)(2,1)} %get-tuple-element.38.refs_0_), channel_id=1, source_target_pairs={{0,4},{1,5},{2,0},{3,1},{4,6},{5,7},{6,2},{7,3},{8,12},{9,13},{10,... | collective-permute-start | bytes 835592 | tf_op jit(solution)/shard_map/ppermute | solution.py:667
  6.6 23.2 %collective-permute-start.6 = (bf16[136,1024]{1,0:T(8,128)(2,1)}, bf16[136,1024]{1,0:T(8,128)(2,1)S(1)}, u32[]{:S(2)}, u32[]{:S(2)}) collective-permute-start(bf16[136,1024]{1,0:T(8,128)(2,1)} %get-tuple-element.39.refs_1_), channel_id=1, source_target_pairs={{0,1},{1,0},{2,3},{3,2},{4,5},{5,4},{6,7},{7,6},{8,9},{9,8},{10,11... | collective-permute-start | bytes 835592 | tf_op jit(solution)/shard_map/ppermute | solution.py:617
  6.8 13.0 %collective-permute-start.1 = (bf16[136,1024]{1,0:T(8,128)(2,1)}, bf16[136,1024]{1,0:T(8,128)(2,1)S(1)}, u32[]{:S(2)}, u32[]{:S(2)}) collective-permute-start(bf16[136,1024]{1,0:T(8,128)(2,1)} %get-tuple-element.39.refs_1_), channel_id=1, source_target_pairs={{0,4},{1,5},{2,0},{3,1},{4,6},{5,7},{6,2},{7,3},{8,12},{9,13},{10,... | collective-permute-start | bytes 835592 | tf_op jit(solution)/shard_map/ppermute | solution.py:667
  13.0 26.0 %all-to-all-start = ((bf16[4,328,512]{2,1,0:T(8,128)(2,1)}), bf16[4,328,512]{2,1,0:T(8,128)(2,1)S(1)}, u32[]{:S(2)}, u32[]{:S(2)}) async-start(bf16[4,328,512]{2,1,0:T(8,128)(2,1)} %pad_maximum_fusion.1), calls=%async_computation | async-start | bytes 2686976 | tf_op jit(solution)/shard_map/all_to_all | solution.py:629
  16.7 22.4 %copy-start.2 = (bf16[136,1024]{1,0:T(8,128)(2,1)}, bf16[136,1024]{1,0:T(8,128)(2,1)S(1)}, u32[]{:S(2)}) copy-start(bf16[136,1024]{1,0:T(8,128)(2,1)S(1)} %collective-permute-done.refs_2_) | copy-start | bytes 835588
  16.7 7.1 %collective-permute-start.4 = (bf16[136,1024]{1,0:T(8,128)(2,1)S(1)}, bf16[136,1024]{1,0:T(8,128)(2,1)S(1)}, u32[]{:S(2)}, u32[]{:S(2)}) collective-permute-start(bf16[136,1024]{1,0:T(8,128)(2,1)S(1)} %collective-permute-done.refs_2_), channel_id=1, source_target_pairs={{0,1},{1,0},{2,3},{3,2},{4,5},{5,4},{6,7},{7,6},{8,9},{9,8},{10,11... | collective-permute-start | bytes 835592 | tf_op jit(solution)/shard_map/ppermute | solution.py:617
  16.8 9.5 %collective-permute-start.2 = (bf16[136,1024]{1,0:T(8,128)(2,1)S(1)}, bf16[136,1024]{1,0:T(8,128)(2,1)S(1)}, u32[]{:S(2)}, u32[]{:S(2)}) collective-permute-start(bf16[136,1024]{1,0:T(8,128)(2,1)S(1)} %collective-permute-done.refs_2_), channel_id=1, source_target_pairs={{0,4},{1,5},{2,0},{3,1},{4,6},{5,7},{6,2},{7,3},{8,12},{9,13},{10,... | collective-permute-start | bytes 835592 | tf_op jit(solution)/shard_map/ppermute | solution.py:667
  19.8 19.3 %copy-start.3 = (bf16[136,1024]{1,0:T(8,128)(2,1)}, bf16[136,1024]{1,0:T(8,128)(2,1)S(1)}, u32[]{:S(2)}) copy-start(bf16[136,1024]{1,0:T(8,128)(2,1)S(1)} %collective-permute-done.1.refs_3_) | copy-start | bytes 835588
  19.8 10.0 %collective-permute-start.7 = (bf16[136,1024]{1,0:T(8,128)(2,1)S(1)}, bf16[136,1024]{1,0:T(8,128)(2,1)S(1)}, u32[]{:S(2)}, u32[]{:S(2)}) collective-permute-start(bf16[136,1024]{1,0:T(8,128)(2,1)S(1)} %collective-permute-done.1.refs_3_), channel_id=1, source_target_pairs={{0,1},{1,0},{2,3},{3,2},{4,5},{5,4},{6,7},{7,6},{8,9},{9,8},{10,11... | collective-permute-start | bytes 835592 | tf_op jit(solution)/shard_map/ppermute | solution.py:617
  19.8 12.5 %collective-permute-start.5 = (bf16[136,1024]{1,0:T(8,128)(2,1)S(1)}, bf16[136,1024]{1,0:T(8,128)(2,1)S(1)}, u32[]{:S(2)}, u32[]{:S(2)}) collective-permute-start(bf16[136,1024]{1,0:T(8,128)(2,1)S(1)} %collective-permute-done.1.refs_3_), channel_id=1, source_target_pairs={{0,4},{1,5},{2,0},{3,1},{4,6},{5,7},{6,2},{7,3},{8,12},{9,13},{10,... | collective-permute-start | bytes 835592 | tf_op jit(solution)/shard_map/ppermute | solution.py:667
  26.3 14.7 %copy-start.4 = (bf16[136,1024]{1,0:T(8,128)(2,1)}, bf16[136,1024]{1,0:T(8,128)(2,1)S(1)}, u32[]{:S(2)}) copy-start(bf16[136,1024]{1,0:T(8,128)(2,1)S(1)} %collective-permute-done.2.refs_4_) | copy-start | bytes 835588
  26.3 11.9 %collective-permute-start.8 = (bf16[136,1024]{1,0:T(8,128)(2,1)S(1)}, bf16[136,1024]{1,0:T(8,128)(2,1)S(1)}, u32[]{:S(2)}, u32[]{:S(2)}) collective-permute-start(bf16[136,1024]{1,0:T(8,128)(2,1)S(1)} %collective-permute-done.2.refs_4_), channel_id=1, source_target_pairs={{0,4},{1,5},{2,0},{3,1},{4,6},{5,7},{6,2},{7,3},{8,12},{9,13},{10,... | collective-permute-start | bytes 835592 | tf_op jit(solution)/shard_map/ppermute | solution.py:667
  29.8 15.5 %collective-permute-start.11 = (bf16[136,1024]{1,0:T(8,128)(2,1)S(1)}, bf16[136,1024]{1,0:T(8,128)(2,1)}, u32[]{:S(2)}, u32[]{:S(2)}) collective-permute-start(bf16[136,1024]{1,0:T(8,128)(2,1)S(1)} %collective-permute-done.2.refs_4_), channel_id=1, source_target_pairs={{0,1},{1,0},{2,3},{3,2},{4,5},{5,4},{6,7},{7,6},{8,9},{9,8},{10,11... | collective-permute-start | bytes 835592 | tf_op jit(solution)/shard_map/ppermute | solution.py:617
  29.8 8.4 %copy-start.13 = (bf16[136,1024]{1,0:T(8,128)(2,1)}, bf16[136,1024]{1,0:T(8,128)(2,1)S(1)}, u32[]{:S(2)}) copy-start(bf16[136,1024]{1,0:T(8,128)(2,1)S(1)} %collective-permute-done.7.refs_11_) | copy-start | bytes 835588
  32.3 8.8 %copy-start.5 = (bf16[136,1024]{1,0:T(8,128)(2,1)}, bf16[136,1024]{1,0:T(8,128)(2,1)S(1)}, u32[]{:S(2)}) copy-start(bf16[136,1024]{1,0:T(8,128)(2,1)S(1)} %collective-permute-done.5.refs_5_) | copy-start | bytes 835588
  32.3 13.0 %collective-permute-start.12 = (bf16[136,1024]{1,0:T(8,128)(2,1)S(1)}, bf16[136,1024]{1,0:T(8,128)(2,1)}, u32[]{:S(2)}, u32[]{:S(2)}) collective-permute-start(bf16[136,1024]{1,0:T(8,128)(2,1)S(1)} %collective-permute-done.5.refs_5_), channel_id=1, source_target_pairs={{0,1},{1,0},{2,3},{3,2},{4,5},{5,4},{6,7},{7,6},{8,9},{9,8},{10,11... | collective-permute-start | bytes 835592 | tf_op jit(solution)/shard_map/ppermute | solution.py:617
  32.3 11.5 %collective-permute-start.9 = (bf16[136,1024]{1,0:T(8,128)(2,1)S(1)}, bf16[136,1024]{1,0:T(8,128)(2,1)S(1)}, u32[]{:S(2)}, u32[]{:S(2)}) collective-permute-start(bf16[136,1024]{1,0:T(8,128)(2,1)S(1)} %collective-permute-done.5.refs_5_), channel_id=1, source_target_pairs={{0,4},{1,5},{2,0},{3,1},{4,6},{5,7},{6,2},{7,3},{8,12},{9,13},{10,... | collective-permute-start | bytes 835592 | tf_op jit(solution)/shard_map/ppermute | solution.py:667
  39.1 4.8 %copy-start.8 = (bf16[1,136,512]{2,1,0:T(8,128)(2,1)S(1)}, bf16[1,136,512]{2,1,0:T(8,128)(2,1)}, u32[]{:S(2)}) copy-start(bf16[1,136,512]{2,1,0:T(8,128)(2,1)} %get-tuple-element.89) | copy-start | bytes 417796
  39.1 4.8 %copy-start.9 = (bf16[1,136,512]{2,1,0:T(8,128)(2,1)S(1)}, bf16[1,136,512]{2,1,0:T(8,128)(2,1)}, u32[]{:S(2)}) copy-start(bf16[1,136,512]{2,1,0:T(8,128)(2,1)} %get-tuple-element.90) | copy-start | bytes 417796
  39.1 4.8 %copy-start.10 = (bf16[1,136,512]{2,1,0:T(8,128)(2,1)S(1)}, bf16[1,136,512]{2,1,0:T(8,128)(2,1)}, u32[]{:S(2)}) copy-start(bf16[1,136,512]{2,1,0:T(8,128)(2,1)} %get-tuple-element.91) | copy-start | bytes 417796
  39.1 7.6 %collective-permute-start.10 = (bf16[4,136,512]{2,1,0:T(8,128)(2,1)S(1)}, bf16[4,136,512]{2,1,0:T(8,128)(2,1)}, u32[]{:S(2)}, u32[]{:S(2)}) collective-permute-start(bf16[4,136,512]{2,1,0:T(8,128)(2,1)S(1)} %slice.110), channel_id=1, source_target_pairs={{0,1},{1,0},{2,3},{3,2},{4,5},{5,4},{6,7},{7,6},{8,9},{9,8},{10,11... | collective-permute-start | bytes 1671176 | tf_op jit(solution)/shard_map/ppermute | solution.py:617
  41.1 4.3 %collective-permute-start.13 = (bf16[136,1024]{1,0:T(8,128)(2,1)S(1)}, bf16[136,1024]{1,0:T(8,128)(2,1)S(1)}, u32[]{:S(2)}, u32[]{:S(2)}) collective-permute-start(bf16[136,1024]{1,0:T(8,128)(2,1)S(1)} %collective-permute-done.8.refs_6_), channel_id=1, source_target_pairs={{0,1},{1,0},{2,3},{3,2},{4,5},{5,4},{6,7},{7,6},{8,9},{9,8},{10,11... | collective-permute-start | bytes 835592 | tf_op jit(solution)/shard_map/ppermute | solution.py:617
  43.8 1.6 %collective-permute-start.14 = (bf16[136,1024]{1,0:T(8,128)(2,1)S(1)}, bf16[136,1024]{1,0:T(8,128)(2,1)S(1)}, u32[]{:S(2)}, u32[]{:S(2)}) collective-permute-start(bf16[136,1024]{1,0:T(8,128)(2,1)S(1)} %collective-permute-done.9.refs_7_), channel_id=1, source_target_pairs={{0,1},{1,0},{2,3},{3,2},{4,5},{5,4},{6,7},{7,6},{8,9},{9,8},{10,11... | collective-permute-start | bytes 835592 | tf_op jit(solution)/shard_map/ppermute | solution.py:617
  46.8 27.0 %all-to-all-start.1 = ((bf16[4,3,136,512]{3,2,1,0:T(8,128)(2,1)}), bf16[4,3,136,512]{3,2,1,0:T(8,128)(2,1)S(1)}, u32[]{:S(2)}, u32[]{:S(2)}) async-start(bf16[4,3,136,512]{3,2,1,0:T(8,128)(2,1)} %pad_maximum_fusion), calls=%async_computation.1 | async-start | bytes 3342336 | tf_op jit(solution)/shard_map/all_to_all | solution.py:629
  73.8 8.9 %copy-start.1 = (bf16[4,3,136,512]{3,2,1,0:T(8,128)(2,1)}, bf16[4,3,136,512]{3,2,1,0:T(8,128)(2,1)S(1)}, u32[]{:S(2)}) copy-start(bf16[4,3,136,512]{3,2,1,0:T(8,128)(2,1)S(1)} %all-to-all-done.1.refs_2_) | copy-start | bytes 5013508
  73.8 5.1 %collective-permute-start.15 = (bf16[4,3,136,512]{3,2,1,0:T(8,128)(2,1)S(1)}, bf16[4,3,136,512]{3,2,1,0:T(8,128)(2,1)}, u32[]{:S(2)}, u32[]{:S(2)}) collective-permute-start(bf16[4,3,136,512]{3,2,1,0:T(8,128)(2,1)S(1)} %all-to-all-done.1.refs_2_), channel_id=1, source_target_pairs={{0,1},{1,0},{2,3},{3,2},{4,5},{5,4},{6,7},{7,6},{8,9},{9,8},{10,11... | collective-permute-start | bytes 5013512 | tf_op jit(solution)/shard_map/ppermute | solution.py:617
  74.1 15.7 %collective-permute-start.16 = (bf16[16,64,96]{2,1,0:T(8,128)(2,1)}, bf16[16,64,96]{2,1,0:T(8,128)(2,1)S(1)}, u32[]{:S(2)}, u32[]{:S(2)}) collective-permute-start(bf16[16,64,96]{2,1,0:T(8,128)(2,1)} %get-tuple-element.60), channel_id=1, source_target_pairs={{0,8},{8,16},{16,24},{24,0},{1,9},{9,17},{17,25},{25,1},{2,10},{10... | collective-permute-start | bytes 589832 | tf_op jit(solution)/shard_map/ppermute | solution.py:612
  76.0 13.8 %collective-permute-start.17 = (bf16[16,64,96]{2,1,0:T(8,128)(2,1)}, bf16[16,64,96]{2,1,0:T(8,128)(2,1)S(1)}, u32[]{:S(2)}, u32[]{:S(2)}) collective-permute-start(bf16[16,64,96]{2,1,0:T(8,128)(2,1)} %get-tuple-element.61), channel_id=1, source_target_pairs={{0,16},{8,24},{16,0},{24,8},{1,17},{9,25},{17,1},{25,9},{2,18},{10... | collective-permute-start | bytes 589832 | tf_op jit(solution)/shard_map/ppermute | solution.py:612
  77.5 12.5 %collective-permute-start.18 = (bf16[16,64,96]{2,1,0:T(8,128)(2,1)}, bf16[16,64,96]{2,1,0:T(8,128)(2,1)S(1)}, u32[]{:S(2)}, u32[]{:S(2)}) collective-permute-start(bf16[16,64,96]{2,1,0:T(8,128)(2,1)} %get-tuple-element.62), channel_id=1, source_target_pairs={{0,24},{8,0},{16,8},{24,16},{1,25},{9,1},{17,9},{25,17},{2,26},{10... | collective-permute-start | bytes 589832 | tf_op jit(solution)/shard_map/ppermute | solution.py:612
  78.9 11.0 %all-to-all-start.2 = ((f32[8,8,128]{2,1,0:T(8,128)}), f32[8,8,128]{2,1,0:T(8,128)S(1)}, u32[]{:S(2)}, u32[]{:S(2)}) async-start(f32[8,8,128]{2,1,0:T(8,128)} %get-tuple-element.59), calls=%async_computation.2 | async-start | bytes 65536 | tf_op jit(solution)/shard_map/all_to_all | solution.py:720
  82.7 7.9 %copy-start.16 = (bf16[16,64,96]{2,1,0:T(8,128)(2,1)S(1)}, bf16[16,64,96]{2,1,0:T(8,128)(2,1)}, u32[]{:S(2)}) copy-start(bf16[16,64,96]{2,1,0:T(8,128)(2,1)} %get-tuple-element.67) | copy-start | bytes 589828
  (7 other events, 13.7 us)

commit v12 on v11

--- a/solution.py
+++ b/solution.py
@@ -307,24 +307,24 @@
             for copy in weight_copies(x, slot_at(step, i)):
                 copy.start()
 
-    request_weights(0)
     late_copies = [
         pltpu.make_async_copy(source, target, in_sem.at[k])
         for k, (source, target) in enumerate(
             [(hidden_hbm, hidden_ref), (u_hbm, u_ref), (amap_hbm, amap_ref)]
         )
     ]
+
+    for copy in token_copies:
+        copy.wait()
+    request_weights(0)
     for copy in late_copies:
         copy.start()
-    if groups > 1:
-        request_weights(1)
-
-    for copy in token_copies:
-        copy.wait()
     names = [
         read_names(dy_s[i, span:, width - width // group_count :], span, top) for i in range(shards)
     ]
     codes, gates = slot_codes(names, first, capacity, experts, micro)
+    if groups > 1:
+        request_weights(1)
     windows = slot_windows(slots)
     lanes_of = shards // 2 * block
     slot_of = [slot_iota(window, lanes_of) for window in windows]
@@ -510,14 +510,16 @@
         for k in range(blocks):
             source = early_ref.at[home, pl.ds(k * tall, tall)]
             u_copies.append(pltpu.make_async_copy(source, u_refs.at[g, k], u_sem.at[g, k]))
-    for copy in copies + u_copies:
+    for copy in copies[:shards]:
         copy.start()
     slots = capacity * shards
     windows = slot_windows(slots)
     slot_of = [slot_iota(window, shards // 2 * block) for window in windows]
     for g in range(group_count):
-        for i in range(shards):
-            copies[g * shards + i].wait()
+        for copy in copies[g * shards : (g + 1) * shards]:
+            copy.wait()
+        for copy in copies[(g + 1) * shards : (g + 2) * shards] + (u_copies if g == 0 else []):
+            copy.start()
         names = [read_names(tok_s[g, i, span:, :], span, top) for i in range(shards)]
         codes, gates = slot_codes(names, first, capacity, experts, micro)
         for m in range(micro):
@@ -606,7 +608,7 @@
     u = jnp.pad(u, ((0, 0), (0, 0), (0, padded - slots), (0, 0))).reshape(
         2, experts // 2, micro * padded, rank
     )
-    u = jnp.concatenate([u[0], u[1]], axis=-1)
+    u = lax.optimization_barrier(jnp.concatenate([u[0], u[1]], axis=-1))
 
     def shift_groups(array, by):
         return lax.ppermute(

time: 92 us -> 91 us (0.989)
  waiting for transfers between devices: 11.4 us -> 14.2 us
  Pallas kernels: 31.1 us -> 29.3 us
    pallas_call x1, Pallas kernels: 22.1 us -> 18.8 us  [local_by_tokens(): pl.pallas_call(functools.partial(expert_kernel, capacity, group_count, so...]
    all_to_all x2, waiting for transfers between devices: 0.01 us -> 2.14 us  [across_groups(): return lax.all_to_all(array, 'dp', split_axis=0, concat_axis=0, tiled=True)]
    pallas_call x1, Pallas kernels: 7.08 us -> 8.58 us  [local_by_tokens(): pl.pallas_call(functools.partial(adapter_kernel, capacity, micro, span, t...]
  transfers between devices with their start and end apart: 22 -> 22, of which waited for: 6 -> 6; matrix products, arithmetic and copies ran while one was open for 14% -> 12% of each run, Pallas kernels for 32% -> 30%
where the time goes in v12:
time: 91 us; the launch traced here: 90.4 us
  starting transfers between devices  31.4 us (35%)
  Pallas kernels  29.3 us (32%)
  waiting for transfers between devices  14.2 us (16%)
  local copies, waits for them, and re-layouts  6.35 us (7%)
  other arithmetic  6.25 us (7%)
  matrix products  1.91 us (2%)
  between operations  0.95 us (1%)
    pallas_call x1, Pallas kernels, local_by_tokens(): pl.pallas_call(functools.partial(expert_kernel, capacity, group_count, so...  18.8 us
    ppermute x6, starting transfers between devices, local_by_tokens(): near.append([lax.ppermute(piece, 'expert', ring) for piece in near[step]])  14.3 us
    ppermute x6, waiting for transfers between devices, local_by_tokens(): near.append([lax.ppermute(piece, 'expert', ring) for piece in near[step]])  12.1 us
    pallas_call x1, Pallas kernels, local_by_tokens(): pl.pallas_call(functools.partial(adapter_kernel, capacity, micro, span, t...  8.58 us
    all_to_all x2, starting transfers between devices, across_groups(): return lax.all_to_all(array, 'dp', split_axis=0, concat_axis=0, tiled=True)  7.85 us
    ppermute x3, starting transfers between devices, shift_groups(): lax.ppermute(array, 'dp', [(d, (d + by) % group_count) for d in range(gro...  4.39 us
    all_to_all x1, starting transfers between devices, local_by_tokens(): lax.all_to_all(routed, 'expert', split_axis=0, concat_axis=0, tiled=True)  3.85 us
    another operation x3, other arithmetic, exchange_columns(): jnp.stack([jnp.stack([columns(pieces, g) for pieces in chosen]) for g in...  3.21 us
  transfers between devices with their start and end apart: 22, of which 6 were waited for; matrix products, arithmetic and copies ran while one was open for 12% of the time, Pallas kernels for 30%

profile of v12, /device:TPU:0, one launch (start us, length us, event | category | flops | bytes accessed | tf_op | source)
XLA Modules:
  0.0 90.4 jit_solution(3507614973316449040)
XLA Ops:
  0.6 1.9 %ring_payload.1 = (bf16[136,1024]{1,0:T(8,128)(2,1)}, bf16[136,1024]{1,0:T(8,128)(2,1)}) custom-call(bf16[128,2048]{1,0:T(8,128)(2,1)} %dy_ref.1, s32[8,128]{1,0:T(8,128)} %bitcast.56, bf16[8,128]{1,0:T(8,128)(2,1)} %bitcast.58), custom_call_target="tpu_custom_call" | custom-call | tf_op jit(solution)/shard_map/ring_payload/pallas_call | solution.py:637
  3.0 3.6 %collective-permute-start = (bf16[136,1024]{1,0:T(8,128)(2,1)}, bf16[136,1024]{1,0:T(8,128)(2,1)S(1)}, u32[]{:S(2)}, u32[]{:S(2)}) collective-permute-start(bf16[136,1024]{1,0:T(8,128)(2,1)} %get-tuple-element.38.refs_0_), channel_id=1, source_target_pairs={{0,4},{1,5},{2,0},{3,1},{4,6},{5,7},{6,2},{7,3},{8,12},{9,13},{10,... | collective-permute-start | bytes 835592 | tf_op jit(solution)/shard_map/ppermute | solution.py:669
  6.8 1.6 %collective-permute-start.1 = (bf16[136,1024]{1,0:T(8,128)(2,1)}, bf16[136,1024]{1,0:T(8,128)(2,1)S(1)}, u32[]{:S(2)}, u32[]{:S(2)}) collective-permute-start(bf16[136,1024]{1,0:T(8,128)(2,1)} %get-tuple-element.39.refs_1_), channel_id=1, source_target_pairs={{0,4},{1,5},{2,0},{3,1},{4,6},{5,7},{6,2},{7,3},{8,12},{9,13},{10,... | collective-permute-start | bytes 835592 | tf_op jit(solution)/shard_map/ppermute | solution.py:669
  8.4 1.1 %fusion.6 = (bf16[136,512]{1,0:T(8,128)(2,1)S(1)}, bf16[136,512]{1,0:T(8,128)(2,1)S(1)}, bf16[136,512]{1,0:T(8,128)(2,1)S(1)}, bf16[136,512]{1,0:T(8,128)(2,1)S(1)}) fusion(bf16[136,1024]{1,0:T(8,128)(2,1)} %get-tuple-element.38.refs_0_, bf16[136,1024]{1,0:T(8,128)(2,1)} %get-tuple-element.39.refs_1_), kind=kLoop, calls=%fused_computation.34 | loop fusion | bytes 1114112 | tf_op jit(solution)/shard_map/slice | solution.py:654
  9.5 1.9 %convolution_convert_fusion = bf16[16,2,40,64]{3,2,1,0:T(8,128)(2,1)S(1)} fusion(bf16[2,16,40,384]{3,2,1,0:T(8,128)(2,1)} %refs_16_.1, bf16[16,384,64]{1,2,0:T(8,128)(2,1)} %param.12), kind=kOutput, calls=%fused_computation.2 | convolution fusion | flops 62996480 | bytes 1933312 | tf_op jit(solution)/shard_map/mesk,exk->emsx/dot_general | solution.py:606
  11.8 1.2 %pad_maximum_fusion.1 = bf16[4,328,512]{2,1,0:T(8,128)(2,1)} fusion(bf16[1,328,512]{2,1,0:T(8,128)(2,1)S(1)} %get-tuple-element.93, bf16[1,328,512]{2,1,0:T(8,128)(2,1)S(1)} %get-tuple-element.92, bf16[1,328,512]{2,1,0:T(8,128)(2,1)S(1)} %get-tuple-element.91, bf16[1,328,512]{2,1,0:T(8,128)(2,1)S(1)} %get-tuple-element.90), kind=kLoop, calls=%fused_computation.1 | loop fusion | flops 2015232 | bytes 2686976 | tf_op jit(solution)/shard_map/stack | solution.py:651
  13.1 3.7 %all-to-all-start = ((bf16[4,328,512]{2,1,0:T(8,128)(2,1)}), bf16[4,328,512]{2,1,0:T(8,128)(2,1)S(1)}, u32[]{:S(2)}, u32[]{:S(2)}) async-start(bf16[4,328,512]{2,1,0:T(8,128)(2,1)} %pad_maximum_fusion.1), calls=%async_computation | async-start | bytes 2686976 | tf_op jit(solution)/shard_map/all_to_all | solution.py:631
  17.2 0.7 slice_bitcast_fusion.7
  17.9 1.9 %collective-permute-done.1.refs_3_ = bf16[136,1024]{1,0:T(8,128)(2,1)S(1)} collective-permute-done((bf16[136,1024]{1,0:T(8,128)(2,1)}, bf16[136,1024]{1,0:T(8,128)(2,1)S(1)}, u32[]{:S(2)}, u32[]{:S(2)}) %collective-permute-start.1) | collective-permute-done | bytes 278560 | tf_op jit(solution)/shard_map/ppermute | solution.py:669
  19.8 3.3 %collective-permute-start.5 = (bf16[136,1024]{1,0:T(8,128)(2,1)S(1)}, bf16[136,1024]{1,0:T(8,128)(2,1)S(1)}, u32[]{:S(2)}, u32[]{:S(2)}) collective-permute-start(bf16[136,1024]{1,0:T(8,128)(2,1)S(1)} %collective-permute-done.1.refs_3_), channel_id=1, source_target_pairs={{0,4},{1,5},{2,0},{3,1},{4,6},{5,7},{6,2},{7,3},{8,12},{9,13},{10,... | collective-permute-start | bytes 835592 | tf_op jit(solution)/shard_map/ppermute | solution.py:669
  23.2 0.7 copy-done.12
  23.9 2.5 %collective-permute-done.2.refs_4_ = bf16[136,1024]{1,0:T(8,128)(2,1)S(1)} collective-permute-done((bf16[136,1024]{1,0:T(8,128)(2,1)S(1)}, bf16[136,1024]{1,0:T(8,128)(2,1)S(1)}, u32[]{:S(2)}, u32[]{:S(2)}) %collective-permute-start.2) | collective-permute-done | bytes 278560 | tf_op jit(solution)/shard_map/ppermute | solution.py:669
  26.4 2.7 %collective-permute-start.8 = (bf16[136,1024]{1,0:T(8,128)(2,1)S(1)}, bf16[136,1024]{1,0:T(8,128)(2,1)S(1)}, u32[]{:S(2)}, u32[]{:S(2)}) collective-permute-start(bf16[136,1024]{1,0:T(8,128)(2,1)S(1)} %collective-permute-done.2.refs_4_), channel_id=1, source_target_pairs={{0,4},{1,5},{2,0},{3,1},{4,6},{5,7},{6,2},{7,3},{8,12},{9,13},{10,... | collective-permute-start | bytes 835592 | tf_op jit(solution)/shard_map/ppermute | solution.py:669
  29.1 0.7 slice_bitcast_fusion.11
  29.8 2.5 %collective-permute-done.5.refs_5_ = bf16[136,1024]{1,0:T(8,128)(2,1)S(1)} collective-permute-done((bf16[136,1024]{1,0:T(8,128)(2,1)S(1)}, bf16[136,1024]{1,0:T(8,128)(2,1)S(1)}, u32[]{:S(2)}, u32[]{:S(2)}) %collective-permute-start.5) | collective-permute-done | bytes 278560 | tf_op jit(solution)/shard_map/ppermute | solution.py:669
  32.3 2.8 %collective-permute-start.9 = (bf16[136,1024]{1,0:T(8,128)(2,1)S(1)}, bf16[136,1024]{1,0:T(8,128)(2,1)S(1)}, u32[]{:S(2)}, u32[]{:S(2)}) collective-permute-start(bf16[136,1024]{1,0:T(8,128)(2,1)S(1)} %collective-permute-done.5.refs_5_), channel_id=1, source_target_pairs={{0,4},{1,5},{2,0},{3,1},{4,6},{5,7},{6,2},{7,3},{8,12},{9,13},{10,... | collective-permute-start | bytes 835592 | tf_op jit(solution)/shard_map/ppermute | solution.py:669
  35.1 0.7 slice_bitcast_fusion.9
  35.8 2.5 %collective-permute-done.8.refs_6_ = bf16[136,1024]{1,0:T(8,128)(2,1)S(1)} collective-permute-done((bf16[136,1024]{1,0:T(8,128)(2,1)S(1)}, bf16[136,1024]{1,0:T(8,128)(2,1)S(1)}, u32[]{:S(2)}, u32[]{:S(2)}) %collective-permute-start.8) | collective-permute-done | bytes 278560 | tf_op jit(solution)/shard_map/ppermute | solution.py:669
  38.3 0.8 slice_bitcast_fusion.6
  39.2 1.7 %maximum_bitcast_fusion = (bf16[1,3,136,512]{3,2,1,0:T(8,128)(2,1)S(1)}, bf16[1,3,136,512]{3,2,1,0:T(8,128)(2,1)S(1)}) fusion(bf16[1,136,512]{2,1,0:T(8,128)(2,1)} %get-tuple-element.82, bf16[1,136,512]{2,1,0:T(8,128)(2,1)} %get-tuple-element.80, bf16[1,136,512]{2,1,0:T(8,128)(2,1)S(1)} %get-tuple-element.78, bf16[1,136,512]{2,1,0:T(8,128)(2,1)} %get-tuple-element.83, ...), kind=kLoop, calls=%fused_computation.10 | loop fusion | flops 835584 | bytes 1671168 | tf_op jit(solution)/shard_map/stack | solution.py:626
  41.1 2.7 %collective-permute-done.9.refs_7_ = bf16[136,1024]{1,0:T(8,128)(2,1)S(1)} collective-permute-done((bf16[136,1024]{1,0:T(8,128)(2,1)S(1)}, bf16[136,1024]{1,0:T(8,128)(2,1)S(1)}, u32[]{:S(2)}, u32[]{:S(2)}) %collective-permute-start.9) | collective-permute-done | bytes 278560 | tf_op jit(solution)/shard_map/ppermute | solution.py:669
  44.0 1.4 %pad_maximum_fusion = bf16[4,3,136,512]{3,2,1,0:T(8,128)(2,1)} fusion(bf16[1,3,136,512]{3,2,1,0:T(8,128)(2,1)S(1)} %get-tuple-element.101, bf16[1,3,136,512]{3,2,1,0:T(8,128)(2,1)S(1)} %get-tuple-element.100, bf16[1,3,136,512]{3,2,1,0:T(8,128)(2,1)S(1)} %get-tuple-element.103, bf16[1,3,136,512]{3,2,1,0:T(8,128)(2,1)S(1)} %get-tuple-element.102), kind=kLoop, calls=%fused_computation | loop fusion | flops 2506752 | bytes 3342336 | tf_op jit(solution)/shard_map/stack | solution.py:626
  45.4 0.7 copy-done.14
  46.1 0.7 copy-done.15
  46.8 4.1 %all-to-all-start.1 = ((bf16[4,3,136,512]{3,2,1,0:T(8,128)(2,1)}), bf16[4,3,136,512]{3,2,1,0:T(8,128)(2,1)S(1)}, u32[]{:S(2)}, u32[]{:S(2)}) async-start(bf16[4,3,136,512]{3,2,1,0:T(8,128)(2,1)} %pad_maximum_fusion), calls=%async_computation.1 | async-start | bytes 3342336 | tf_op jit(solution)/shard_map/all_to_all | solution.py:631
  50.9 18.8 %expert_rows.1 = (bf16[2,16,40,384]{3,2,1,0:T(8,128)(2,1)}, f32[8,8,128]{2,1,0:T(8,128)}, bf16[16,64,96]{2,1,0:T(8,128)(2,1)}, bf16[16,64,96]{2,1,0:T(8,128)(2,1...) custom-call(bf16[136,1024]{1,0:T(8,128)(2,1)} %get-tuple-element.38.refs_0_, ...), custom_call_target="tpu_custom_call" | custom-call | flops 6039797760 | bytes 33554432 | tf_op jit(solution)/shard_map/expert_rows/pallas_call | solution.py:682
  69.8 2.1 %all-to-all-done.1.refs_2_ = bf16[4,3,136,512]{3,2,1,0:T(8,128)(2,1)S(1)} async-done(((bf16[4,3,136,512]{3,2,1,0:T(8,128)(2,1)}), bf16[4,3,136,512]{3,2,1,0:T(8,128)(2,1)S(1)}, u32[]{:S(2)}, u32[]{:S(2)}) %all-to-all-start.1) | async-done | bytes 1671200 | tf_op jit(solution)/shard_map/all_to_all | solution.py:631
  71.9 1.4 %collective-permute-start.16 = (bf16[16,64,96]{2,1,0:T(8,128)(2,1)}, bf16[16,64,96]{2,1,0:T(8,128)(2,1)S(1)}, u32[]{:S(2)}, u32[]{:S(2)}) collective-permute-start(bf16[16,64,96]{2,1,0:T(8,128)(2,1)} %get-tuple-element.60), channel_id=1, source_target_pairs={{0,8},{8,16},{16,24},{24,0},{1,9},{9,17},{17,25},{25,1},{2,10},{10... | collective-permute-start | bytes 589832 | tf_op jit(solution)/shard_map/ppermute | solution.py:614
  73.9 2.4 %collective-permute-start.18 = (bf16[16,64,96]{2,1,0:T(8,128)(2,1)}, bf16[16,64,96]{2,1,0:T(8,128)(2,1)S(1)}, u32[]{:S(2)}, u32[]{:S(2)}) collective-permute-start(bf16[16,64,96]{2,1,0:T(8,128)(2,1)} %get-tuple-element.62), channel_id=1, source_target_pairs={{0,24},{8,0},{16,8},{24,16},{1,25},{9,1},{17,9},{25,17},{2,26},{10... | collective-permute-start | bytes 589832 | tf_op jit(solution)/shard_map/ppermute | solution.py:614
  76.3 3.9 %all-to-all-start.2 = ((f32[8,8,128]{2,1,0:T(8,128)}), f32[8,8,128]{2,1,0:T(8,128)S(1)}, u32[]{:S(2)}, u32[]{:S(2)}) async-start(f32[8,8,128]{2,1,0:T(8,128)} %get-tuple-element.59), calls=%async_computation.2 | async-start | bytes 65536 | tf_op jit(solution)/shard_map/all_to_all | solution.py:722
  80.2 8.6 %adapter_columns.1 = f32[16,64,512]{2,1,0:T(8,128)} custom-call(bf16[4,328,512]{2,1,0:T(8,128)(2,1)} %copy-done, bf16[4,136,512]{2,1,0:T(8,128)(2,1)} %collective-permute-done.10.refs_1_, bf16[4,3,136,512]{3,2,1,0:T(8,128)(2,1)} %copy-done.2, bf16[4,3,136,512]{3,2,1,0:T(8,128)(2,1)} %collective-permute-done.15.refs_3_), custom_call_target="tpu_custom_call" | custom-call | flops 3623878656 | bytes 6291456 | tf_op jit(solution)/shard_map/adapter_columns/pallas_call | solution.py:724
  89.4 1.0 %convert_add_fusion = f32[16,64,96]{2,1,0:T(8,128)} fusion(bf16[16,64,96]{2,1,0:T(8,128)(2,1)S(1)} %collective-permute-done.18, bf16[16,64,96]{2,1,0:T(8,128)(2,1)S(1)} %collective-permute-done.17, bf16[16,64,96]{2,1,0:T(8,128)(2,1)S(1)} %collective-permute-done.16, bf16[16,64,96]{2,1,0:T(8,128)(2,1)S(1)} %copy-done.16), kind=kLoop, calls=%fused_computation.5 | loop fusion | flops 688128 | bytes 1179648 | tf_op jit(solution)/shard_map/add | solution.py:751
  (69 shorter events, 3.1 us)
Async XLA Ops:
  2.5 17.3 %collective-permute-start.3 = (bf16[136,1024]{1,0:T(8,128)(2,1)}, bf16[136,1024]{1,0:T(8,128)(2,1)}, u32[]{:S(2)}, u32[]{:S(2)}) collective-permute-start(bf16[136,1024]{1,0:T(8,128)(2,1)} %get-tuple-element.38.refs_0_), channel_id=1, source_target_pairs={{0,1},{1,0},{2,3},{3,2},{4,5},{5,4},{6,7},{7,6},{8,9},{9,8},{10,11... | collective-permute-start | bytes 835592 | tf_op jit(solution)/shard_map/ppermute | solution.py:619
  3.0 13.8 %collective-permute-start = (bf16[136,1024]{1,0:T(8,128)(2,1)}, bf16[136,1024]{1,0:T(8,128)(2,1)S(1)}, u32[]{:S(2)}, u32[]{:S(2)}) collective-permute-start(bf16[136,1024]{1,0:T(8,128)(2,1)} %get-tuple-element.38.refs_0_), channel_id=1, source_target_pairs={{0,4},{1,5},{2,0},{3,1},{4,6},{5,7},{6,2},{7,3},{8,12},{9,13},{10,... | collective-permute-start | bytes 835592 | tf_op jit(solution)/shard_map/ppermute | solution.py:669
  6.6 23.3 %collective-permute-start.6 = (bf16[136,1024]{1,0:T(8,128)(2,1)}, bf16[136,1024]{1,0:T(8,128)(2,1)S(1)}, u32[]{:S(2)}, u32[]{:S(2)}) collective-permute-start(bf16[136,1024]{1,0:T(8,128)(2,1)} %get-tuple-element.39.refs_1_), channel_id=1, source_target_pairs={{0,1},{1,0},{2,3},{3,2},{4,5},{5,4},{6,7},{7,6},{8,9},{9,8},{10,11... | collective-permute-start | bytes 835592 | tf_op jit(solution)/shard_map/ppermute | solution.py:619
  6.8 13.0 %collective-permute-start.1 = (bf16[136,1024]{1,0:T(8,128)(2,1)}, bf16[136,1024]{1,0:T(8,128)(2,1)S(1)}, u32[]{:S(2)}, u32[]{:S(2)}) collective-permute-start(bf16[136,1024]{1,0:T(8,128)(2,1)} %get-tuple-element.39.refs_1_), channel_id=1, source_target_pairs={{0,4},{1,5},{2,0},{3,1},{4,6},{5,7},{6,2},{7,3},{8,12},{9,13},{10,... | collective-permute-start | bytes 835592 | tf_op jit(solution)/shard_map/ppermute | solution.py:669
  13.1 26.0 %all-to-all-start = ((bf16[4,328,512]{2,1,0:T(8,128)(2,1)}), bf16[4,328,512]{2,1,0:T(8,128)(2,1)S(1)}, u32[]{:S(2)}, u32[]{:S(2)}) async-start(bf16[4,328,512]{2,1,0:T(8,128)(2,1)} %pad_maximum_fusion.1), calls=%async_computation | async-start | bytes 2686976 | tf_op jit(solution)/shard_map/all_to_all | solution.py:631
  16.8 22.4 %copy-start.3 = (bf16[136,1024]{1,0:T(8,128)(2,1)}, bf16[136,1024]{1,0:T(8,128)(2,1)S(1)}, u32[]{:S(2)}) copy-start(bf16[136,1024]{1,0:T(8,128)(2,1)S(1)} %collective-permute-done.refs_2_) | copy-start | bytes 835588
  16.8 6.4 %collective-permute-start.4 = (bf16[136,1024]{1,0:T(8,128)(2,1)S(1)}, bf16[136,1024]{1,0:T(8,128)(2,1)S(1)}, u32[]{:S(2)}, u32[]{:S(2)}) collective-permute-start(bf16[136,1024]{1,0:T(8,128)(2,1)S(1)} %collective-permute-done.refs_2_), channel_id=1, source_target_pairs={{0,1},{1,0},{2,3},{3,2},{4,5},{5,4},{6,7},{7,6},{8,9},{9,8},{10,11... | collective-permute-start | bytes 835592 | tf_op jit(solution)/shard_map/ppermute | solution.py:619
  16.8 9.5 %collective-permute-start.2 = (bf16[136,1024]{1,0:T(8,128)(2,1)S(1)}, bf16[136,1024]{1,0:T(8,128)(2,1)S(1)}, u32[]{:S(2)}, u32[]{:S(2)}) collective-permute-start(bf16[136,1024]{1,0:T(8,128)(2,1)S(1)} %collective-permute-done.refs_2_), channel_id=1, source_target_pairs={{0,4},{1,5},{2,0},{3,1},{4,6},{5,7},{6,2},{7,3},{8,12},{9,13},{10,... | collective-permute-start | bytes 835592 | tf_op jit(solution)/shard_map/ppermute | solution.py:669
  19.8 19.3 %copy-start.4 = (bf16[136,1024]{1,0:T(8,128)(2,1)}, bf16[136,1024]{1,0:T(8,128)(2,1)S(1)}, u32[]{:S(2)}) copy-start(bf16[136,1024]{1,0:T(8,128)(2,1)S(1)} %collective-permute-done.1.refs_3_) | copy-start | bytes 835588
  19.8 10.0 %collective-permute-start.7 = (bf16[136,1024]{1,0:T(8,128)(2,1)S(1)}, bf16[136,1024]{1,0:T(8,128)(2,1)S(1)}, u32[]{:S(2)}, u32[]{:S(2)}) collective-permute-start(bf16[136,1024]{1,0:T(8,128)(2,1)S(1)} %collective-permute-done.1.refs_3_), channel_id=1, source_target_pairs={{0,1},{1,0},{2,3},{3,2},{4,5},{5,4},{6,7},{7,6},{8,9},{9,8},{10,11... | collective-permute-start | bytes 835592 | tf_op jit(solution)/shard_map/ppermute | solution.py:619
  19.8 12.5 %collective-permute-start.5 = (bf16[136,1024]{1,0:T(8,128)(2,1)S(1)}, bf16[136,1024]{1,0:T(8,128)(2,1)S(1)}, u32[]{:S(2)}, u32[]{:S(2)}) collective-permute-start(bf16[136,1024]{1,0:T(8,128)(2,1)S(1)} %collective-permute-done.1.refs_3_), channel_id=1, source_target_pairs={{0,4},{1,5},{2,0},{3,1},{4,6},{5,7},{6,2},{7,3},{8,12},{9,13},{10,... | collective-permute-start | bytes 835592 | tf_op jit(solution)/shard_map/ppermute | solution.py:669
  26.4 14.6 %copy-start.5 = (bf16[136,1024]{1,0:T(8,128)(2,1)}, bf16[136,1024]{1,0:T(8,128)(2,1)S(1)}, u32[]{:S(2)}) copy-start(bf16[136,1024]{1,0:T(8,128)(2,1)S(1)} %collective-permute-done.2.refs_4_) | copy-start | bytes 835588
  26.4 11.9 %collective-permute-start.8 = (bf16[136,1024]{1,0:T(8,128)(2,1)S(1)}, bf16[136,1024]{1,0:T(8,128)(2,1)S(1)}, u32[]{:S(2)}, u32[]{:S(2)}) collective-permute-start(bf16[136,1024]{1,0:T(8,128)(2,1)S(1)} %collective-permute-done.2.refs_4_), channel_id=1, source_target_pairs={{0,4},{1,5},{2,0},{3,1},{4,6},{5,7},{6,2},{7,3},{8,12},{9,13},{10,... | collective-permute-start | bytes 835592 | tf_op jit(solution)/shard_map/ppermute | solution.py:669
  29.8 15.6 %collective-permute-start.11 = (bf16[136,1024]{1,0:T(8,128)(2,1)S(1)}, bf16[136,1024]{1,0:T(8,128)(2,1)}, u32[]{:S(2)}, u32[]{:S(2)}) collective-permute-start(bf16[136,1024]{1,0:T(8,128)(2,1)S(1)} %collective-permute-done.2.refs_4_), channel_id=1, source_target_pairs={{0,1},{1,0},{2,3},{3,2},{4,5},{5,4},{6,7},{7,6},{8,9},{9,8},{10,11... | collective-permute-start | bytes 835592 | tf_op jit(solution)/shard_map/ppermute | solution.py:619
  29.8 8.5 %copy-start.13 = (bf16[136,1024]{1,0:T(8,128)(2,1)}, bf16[136,1024]{1,0:T(8,128)(2,1)S(1)}, u32[]{:S(2)}) copy-start(bf16[136,1024]{1,0:T(8,128)(2,1)S(1)} %collective-permute-done.7.refs_11_) | copy-start | bytes 835588
  32.3 8.7 %copy-start.6 = (bf16[136,1024]{1,0:T(8,128)(2,1)}, bf16[136,1024]{1,0:T(8,128)(2,1)S(1)}, u32[]{:S(2)}) copy-start(bf16[136,1024]{1,0:T(8,128)(2,1)S(1)} %collective-permute-done.5.refs_5_) | copy-start | bytes 835588
  32.3 13.0 %collective-permute-start.12 = (bf16[136,1024]{1,0:T(8,128)(2,1)S(1)}, bf16[136,1024]{1,0:T(8,128)(2,1)}, u32[]{:S(2)}, u32[]{:S(2)}) collective-permute-start(bf16[136,1024]{1,0:T(8,128)(2,1)S(1)} %collective-permute-done.5.refs_5_), channel_id=1, source_target_pairs={{0,1},{1,0},{2,3},{3,2},{4,5},{5,4},{6,7},{7,6},{8,9},{9,8},{10,11... | collective-permute-start | bytes 835592 | tf_op jit(solution)/shard_map/ppermute | solution.py:619
  32.3 11.5 %collective-permute-start.9 = (bf16[136,1024]{1,0:T(8,128)(2,1)S(1)}, bf16[136,1024]{1,0:T(8,128)(2,1)S(1)}, u32[]{:S(2)}, u32[]{:S(2)}) collective-permute-start(bf16[136,1024]{1,0:T(8,128)(2,1)S(1)} %collective-permute-done.5.refs_5_), channel_id=1, source_target_pairs={{0,4},{1,5},{2,0},{3,1},{4,6},{5,7},{6,2},{7,3},{8,12},{9,13},{10,... | collective-permute-start | bytes 835592 | tf_op jit(solution)/shard_map/ppermute | solution.py:669
  39.1 4.8 %copy-start = (bf16[4,328,512]{2,1,0:T(8,128)(2,1)}, bf16[4,328,512]{2,1,0:T(8,128)(2,1)S(1)}, u32[]{:S(2)}) copy-start(bf16[4,328,512]{2,1,0:T(8,128)(2,1)S(1)} %all-to-all-done.refs_0_) | copy-start | bytes 4030468
  39.1 4.8 %copy-start.9 = (bf16[1,136,512]{2,1,0:T(8,128)(2,1)S(1)}, bf16[1,136,512]{2,1,0:T(8,128)(2,1)}, u32[]{:S(2)}) copy-start(bf16[1,136,512]{2,1,0:T(8,128)(2,1)} %get-tuple-element.86) | copy-start | bytes 417796
  39.1 4.8 %copy-start.10 = (bf16[1,136,512]{2,1,0:T(8,128)(2,1)S(1)}, bf16[1,136,512]{2,1,0:T(8,128)(2,1)}, u32[]{:S(2)}) copy-start(bf16[1,136,512]{2,1,0:T(8,128)(2,1)} %get-tuple-element.87) | copy-start | bytes 417796
  39.2 7.6 %collective-permute-start.10 = (bf16[4,136,512]{2,1,0:T(8,128)(2,1)S(1)}, bf16[4,136,512]{2,1,0:T(8,128)(2,1)}, u32[]{:S(2)}, u32[]{:S(2)}) collective-permute-start(bf16[4,136,512]{2,1,0:T(8,128)(2,1)S(1)} %slice.106), channel_id=1, source_target_pairs={{0,1},{1,0},{2,3},{3,2},{4,5},{5,4},{6,7},{7,6},{8,9},{9,8},{10,11... | collective-permute-start | bytes 1671176 | tf_op jit(solution)/shard_map/ppermute | solution.py:619
  41.0 4.4 %collective-permute-start.13 = (bf16[136,1024]{1,0:T(8,128)(2,1)S(1)}, bf16[136,1024]{1,0:T(8,128)(2,1)S(1)}, u32[]{:S(2)}, u32[]{:S(2)}) collective-permute-start(bf16[136,1024]{1,0:T(8,128)(2,1)S(1)} %collective-permute-done.8.refs_6_), channel_id=1, source_target_pairs={{0,1},{1,0},{2,3},{3,2},{4,5},{5,4},{6,7},{7,6},{8,9},{9,8},{10,11... | collective-permute-start | bytes 835592 | tf_op jit(solution)/shard_map/ppermute | solution.py:619
  43.8 1.6 %collective-permute-start.14 = (bf16[136,1024]{1,0:T(8,128)(2,1)S(1)}, bf16[136,1024]{1,0:T(8,128)(2,1)S(1)}, u32[]{:S(2)}, u32[]{:S(2)}) collective-permute-start(bf16[136,1024]{1,0:T(8,128)(2,1)S(1)} %collective-permute-done.9.refs_7_), channel_id=1, source_target_pairs={{0,1},{1,0},{2,3},{3,2},{4,5},{5,4},{6,7},{7,6},{8,9},{9,8},{10,11... | collective-permute-start | bytes 835592 | tf_op jit(solution)/shard_map/ppermute | solution.py:619
  46.8 25.1 %all-to-all-start.1 = ((bf16[4,3,136,512]{3,2,1,0:T(8,128)(2,1)}), bf16[4,3,136,512]{3,2,1,0:T(8,128)(2,1)S(1)}, u32[]{:S(2)}, u32[]{:S(2)}) async-start(bf16[4,3,136,512]{3,2,1,0:T(8,128)(2,1)} %pad_maximum_fusion), calls=%async_computation.1 | async-start | bytes 3342336 | tf_op jit(solution)/shard_map/all_to_all | solution.py:631
  71.9 8.3 %copy-start.2 = (bf16[4,3,136,512]{3,2,1,0:T(8,128)(2,1)}, bf16[4,3,136,512]{3,2,1,0:T(8,128)(2,1)S(1)}, u32[]{:S(2)}) copy-start(bf16[4,3,136,512]{3,2,1,0:T(8,128)(2,1)S(1)} %all-to-all-done.1.refs_2_) | copy-start | bytes 5013508
  71.9 4.4 %collective-permute-start.15 = (bf16[4,3,136,512]{3,2,1,0:T(8,128)(2,1)S(1)}, bf16[4,3,136,512]{3,2,1,0:T(8,128)(2,1)}, u32[]{:S(2)}, u32[]{:S(2)}) collective-permute-start(bf16[4,3,136,512]{3,2,1,0:T(8,128)(2,1)S(1)} %all-to-all-done.1.refs_2_), channel_id=1, source_target_pairs={{0,1},{1,0},{2,3},{3,2},{4,5},{5,4},{6,7},{7,6},{8,9},{9,8},{10,11... | collective-permute-start | bytes 5013512 | tf_op jit(solution)/shard_map/ppermute | solution.py:619
  71.9 16.9 %collective-permute-start.16 = (bf16[16,64,96]{2,1,0:T(8,128)(2,1)}, bf16[16,64,96]{2,1,0:T(8,128)(2,1)S(1)}, u32[]{:S(2)}, u32[]{:S(2)}) collective-permute-start(bf16[16,64,96]{2,1,0:T(8,128)(2,1)} %get-tuple-element.60), channel_id=1, source_target_pairs={{0,8},{8,16},{16,24},{24,0},{1,9},{9,17},{17,25},{25,1},{2,10},{10... | collective-permute-start | bytes 589832 | tf_op jit(solution)/shard_map/ppermute | solution.py:614
  73.3 15.4 %collective-permute-start.17 = (bf16[16,64,96]{2,1,0:T(8,128)(2,1)}, bf16[16,64,96]{2,1,0:T(8,128)(2,1)S(1)}, u32[]{:S(2)}, u32[]{:S(2)}) collective-permute-start(bf16[16,64,96]{2,1,0:T(8,128)(2,1)} %get-tuple-element.61), channel_id=1, source_target_pairs={{0,16},{8,24},{16,0},{24,8},{1,17},{9,25},{17,1},{25,9},{2,18},{10... | collective-permute-start | bytes 589832 | tf_op jit(solution)/shard_map/ppermute | solution.py:614
  73.9 14.9 %collective-permute-start.18 = (bf16[16,64,96]{2,1,0:T(8,128)(2,1)}, bf16[16,64,96]{2,1,0:T(8,128)(2,1)S(1)}, u32[]{:S(2)}, u32[]{:S(2)}) collective-permute-start(bf16[16,64,96]{2,1,0:T(8,128)(2,1)} %get-tuple-element.62), channel_id=1, source_target_pairs={{0,24},{8,0},{16,8},{24,16},{1,25},{9,1},{17,9},{25,17},{2,26},{10... | collective-permute-start | bytes 589832 | tf_op jit(solution)/shard_map/ppermute | solution.py:614
  76.3 12.5 %all-to-all-start.2 = ((f32[8,8,128]{2,1,0:T(8,128)}), f32[8,8,128]{2,1,0:T(8,128)S(1)}, u32[]{:S(2)}, u32[]{:S(2)}) async-start(f32[8,8,128]{2,1,0:T(8,128)} %get-tuple-element.59), calls=%async_computation.2 | async-start | bytes 65536 | tf_op jit(solution)/shard_map/all_to_all | solution.py:722
  80.2 9.2 %copy-start.16 = (bf16[16,64,96]{2,1,0:T(8,128)(2,1)S(1)}, bf16[16,64,96]{2,1,0:T(8,128)(2,1)}, u32[]{:S(2)}) copy-start(bf16[16,64,96]{2,1,0:T(8,128)(2,1)} %get-tuple-element.67) | copy-start | bytes 589828
  (7 other events, 10.3 us)

commit v13 on v12

--- a/solution.py
+++ b/solution.py
@@ -510,7 +510,7 @@
         for k in range(blocks):
             source = early_ref.at[home, pl.ds(k * tall, tall)]
             u_copies.append(pltpu.make_async_copy(source, u_refs.at[g, k], u_sem.at[g, k]))
-    for copy in copies[:shards]:
+    for copy in copies + u_copies:
         copy.start()
     slots = capacity * shards
     windows = slot_windows(slots)
@@ -518,8 +518,6 @@
     for g in range(group_count):
         for copy in copies[g * shards : (g + 1) * shards]:
             copy.wait()
-        for copy in copies[(g + 1) * shards : (g + 2) * shards] + (u_copies if g == 0 else []):
-            copy.start()
         names = [read_names(tok_s[g, i, span:, :], span, top) for i in range(shards)]
         codes, gates = slot_codes(names, first, capacity, experts, micro)
         for m in range(micro):

time: 91 us -> 89.4 us (0.982)
  Pallas kernels: 29.3 us -> 27.8 us
    pallas_call x1, Pallas kernels: 8.58 us -> 7.09 us  [local_by_tokens(): pl.pallas_call(functools.partial(adapter_kernel, capacity, micro, span, t...]
  transfers between devices with their start and end apart: 22 -> 22, of which waited for: 6 -> 7; matrix products, arithmetic and copies ran while one was open for 12% -> 12% of each run, Pallas kernels for 30% -> 29%
where the time goes in v13:
time: 89.4 us; the launch traced here: 89 us
  starting transfers between devices  31.4 us (35%)
  Pallas kernels  27.8 us (31%)
  waiting for transfers between devices  14.4 us (16%)
  local copies, waits for them, and re-layouts  6.35 us (7%)
  other arithmetic  6.25 us (7%)
  matrix products  1.91 us (2%)
  between operations  0.93 us (1%)
    pallas_call x1, Pallas kernels, local_by_tokens(): pl.pallas_call(functools.partial(expert_kernel, capacity, group_count, so...  18.8 us
    ppermute x6, starting transfers between devices, local_by_tokens(): near.append([lax.ppermute(piece, 'expert', ring) for piece in near[step]])  14.3 us
    ppermute x6, waiting for transfers between devices, local_by_tokens(): near.append([lax.ppermute(piece, 'expert', ring) for piece in near[step]])  12.1 us
    all_to_all x2, starting transfers between devices, across_groups(): return lax.all_to_all(array, 'dp', split_axis=0, concat_axis=0, tiled=True)  7.85 us
    pallas_call x1, Pallas kernels, local_by_tokens(): pl.pallas_call(functools.partial(adapter_kernel, capacity, micro, span, t...  7.09 us
    ppermute x3, starting transfers between devices, shift_groups(): lax.ppermute(array, 'dp', [(d, (d + by) % group_count) for d in range(gro...  4.39 us
    all_to_all x1, starting transfers between devices, local_by_tokens(): lax.all_to_all(routed, 'expert', split_axis=0, concat_axis=0, tiled=True)  3.85 us
    another operation x3, other arithmetic, exchange_columns(): jnp.stack([jnp.stack([columns(pieces, g) for pieces in chosen]) for g in...  3.21 us
  transfers between devices with their start and end apart: 22, of which 7 were waited for; matrix products, arithmetic and copies ran while one was open for 12% of the time, Pallas kernels for 29%

profile of v13, /device:TPU:0, one launch (start us, length us, event | category | flops | bytes accessed | tf_op | source)
XLA Modules:
  0.0 89.0 jit_solution(7396849265345782792)
XLA Ops:
  0.6 1.9 %ring_payload.1 = (bf16[136,1024]{1,0:T(8,128)(2,1)}, bf16[136,1024]{1,0:T(8,128)(2,1)}) custom-call(bf16[128,2048]{1,0:T(8,128)(2,1)} %dy_ref.1, s32[8,128]{1,0:T(8,128)} %bitcast.56, bf16[8,128]{1,0:T(8,128)(2,1)} %bitcast.58), custom_call_target="tpu_custom_call" | custom-call | tf_op jit(solution)/shard_map/ring_payload/pallas_call | solution.py:635
  3.0 3.6 %collective-permute-start = (bf16[136,1024]{1,0:T(8,128)(2,1)}, bf16[136,1024]{1,0:T(8,128)(2,1)S(1)}, u32[]{:S(2)}, u32[]{:S(2)}) collective-permute-start(bf16[136,1024]{1,0:T(8,128)(2,1)} %get-tuple-element.38.refs_0_), channel_id=1, source_target_pairs={{0,4},{1,5},{2,0},{3,1},{4,6},{5,7},{6,2},{7,3},{8,12},{9,13},{10,... | collective-permute-start | bytes 835592 | tf_op jit(solution)/shard_map/ppermute | solution.py:667
  6.8 1.6 %collective-permute-start.1 = (bf16[136,1024]{1,0:T(8,128)(2,1)}, bf16[136,1024]{1,0:T(8,128)(2,1)S(1)}, u32[]{:S(2)}, u32[]{:S(2)}) collective-permute-start(bf16[136,1024]{1,0:T(8,128)(2,1)} %get-tuple-element.39.refs_1_), channel_id=1, source_target_pairs={{0,4},{1,5},{2,0},{3,1},{4,6},{5,7},{6,2},{7,3},{8,12},{9,13},{10,... | collective-permute-start | bytes 835592 | tf_op jit(solution)/shard_map/ppermute | solution.py:667
  8.4 1.1 %fusion.6 = (bf16[136,512]{1,0:T(8,128)(2,1)S(1)}, bf16[136,512]{1,0:T(8,128)(2,1)S(1)}, bf16[136,512]{1,0:T(8,128)(2,1)S(1)}, bf16[136,512]{1,0:T(8,128)(2,1)S(1)}) fusion(bf16[136,1024]{1,0:T(8,128)(2,1)} %get-tuple-element.38.refs_0_, bf16[136,1024]{1,0:T(8,128)(2,1)} %get-tuple-element.39.refs_1_), kind=kLoop, calls=%fused_computation.34 | loop fusion | bytes 1114112 | tf_op jit(solution)/shard_map/slice | solution.py:652
  9.5 1.9 %convolution_convert_fusion = bf16[16,2,40,64]{3,2,1,0:T(8,128)(2,1)S(1)} fusion(bf16[2,16,40,384]{3,2,1,0:T(8,128)(2,1)} %refs_16_.1, bf16[16,384,64]{1,2,0:T(8,128)(2,1)} %param.12), kind=kOutput, calls=%fused_computation.2 | convolution fusion | flops 62996480 | bytes 1933312 | tf_op jit(solution)/shard_map/mesk,exk->emsx/dot_general | solution.py:604
  11.8 1.2 %pad_maximum_fusion.1 = bf16[4,328,512]{2,1,0:T(8,128)(2,1)} fusion(bf16[1,328,512]{2,1,0:T(8,128)(2,1)S(1)} %get-tuple-element.93, bf16[1,328,512]{2,1,0:T(8,128)(2,1)S(1)} %get-tuple-element.92, bf16[1,328,512]{2,1,0:T(8,128)(2,1)S(1)} %get-tuple-element.91, bf16[1,328,512]{2,1,0:T(8,128)(2,1)S(1)} %get-tuple-element.90), kind=kLoop, calls=%fused_computation.1 | loop fusion | flops 2015232 | bytes 2686976 | tf_op jit(solution)/shard_map/stack | solution.py:649
  13.1 3.7 %all-to-all-start = ((bf16[4,328,512]{2,1,0:T(8,128)(2,1)}), bf16[4,328,512]{2,1,0:T(8,128)(2,1)S(1)}, u32[]{:S(2)}, u32[]{:S(2)}) async-start(bf16[4,328,512]{2,1,0:T(8,128)(2,1)} %pad_maximum_fusion.1), calls=%async_computation | async-start | bytes 2686976 | tf_op jit(solution)/shard_map/all_to_all | solution.py:629
  17.2 0.7 slice_bitcast_fusion.7
  17.9 1.9 %collective-permute-done.1.refs_3_ = bf16[136,1024]{1,0:T(8,128)(2,1)S(1)} collective-permute-done((bf16[136,1024]{1,0:T(8,128)(2,1)}, bf16[136,1024]{1,0:T(8,128)(2,1)S(1)}, u32[]{:S(2)}, u32[]{:S(2)}) %collective-permute-start.1) | collective-permute-done | bytes 278560 | tf_op jit(solution)/shard_map/ppermute | solution.py:667
  19.8 3.3 %collective-permute-start.5 = (bf16[136,1024]{1,0:T(8,128)(2,1)S(1)}, bf16[136,1024]{1,0:T(8,128)(2,1)S(1)}, u32[]{:S(2)}, u32[]{:S(2)}) collective-permute-start(bf16[136,1024]{1,0:T(8,128)(2,1)S(1)} %collective-permute-done.1.refs_3_), channel_id=1, source_target_pairs={{0,4},{1,5},{2,0},{3,1},{4,6},{5,7},{6,2},{7,3},{8,12},{9,13},{10,... | collective-permute-start | bytes 835592 | tf_op jit(solution)/shard_map/ppermute | solution.py:667
  23.2 0.7 copy-done.12
  23.9 2.5 %collective-permute-done.2.refs_4_ = bf16[136,1024]{1,0:T(8,128)(2,1)S(1)} collective-permute-done((bf16[136,1024]{1,0:T(8,128)(2,1)S(1)}, bf16[136,1024]{1,0:T(8,128)(2,1)S(1)}, u32[]{:S(2)}, u32[]{:S(2)}) %collective-permute-start.2) | collective-permute-done | bytes 278560 | tf_op jit(solution)/shard_map/ppermute | solution.py:667
  26.4 2.7 %collective-permute-start.8 = (bf16[136,1024]{1,0:T(8,128)(2,1)S(1)}, bf16[136,1024]{1,0:T(8,128)(2,1)S(1)}, u32[]{:S(2)}, u32[]{:S(2)}) collective-permute-start(bf16[136,1024]{1,0:T(8,128)(2,1)S(1)} %collective-permute-done.2.refs_4_), channel_id=1, source_target_pairs={{0,4},{1,5},{2,0},{3,1},{4,6},{5,7},{6,2},{7,3},{8,12},{9,13},{10,... | collective-permute-start | bytes 835592 | tf_op jit(solution)/shard_map/ppermute | solution.py:667
  29.1 0.7 slice_bitcast_fusion.11
  29.8 2.5 %collective-permute-done.5.refs_5_ = bf16[136,1024]{1,0:T(8,128)(2,1)S(1)} collective-permute-done((bf16[136,1024]{1,0:T(8,128)(2,1)S(1)}, bf16[136,1024]{1,0:T(8,128)(2,1)S(1)}, u32[]{:S(2)}, u32[]{:S(2)}) %collective-permute-start.5) | collective-permute-done | bytes 278560 | tf_op jit(solution)/shard_map/ppermute | solution.py:667
  32.3 2.8 %collective-permute-start.9 = (bf16[136,1024]{1,0:T(8,128)(2,1)S(1)}, bf16[136,1024]{1,0:T(8,128)(2,1)S(1)}, u32[]{:S(2)}, u32[]{:S(2)}) collective-permute-start(bf16[136,1024]{1,0:T(8,128)(2,1)S(1)} %collective-permute-done.5.refs_5_), channel_id=1, source_target_pairs={{0,4},{1,5},{2,0},{3,1},{4,6},{5,7},{6,2},{7,3},{8,12},{9,13},{10,... | collective-permute-start | bytes 835592 | tf_op jit(solution)/shard_map/ppermute | solution.py:667
  35.1 0.7 slice_bitcast_fusion.9
  35.8 2.5 %collective-permute-done.8.refs_6_ = bf16[136,1024]{1,0:T(8,128)(2,1)S(1)} collective-permute-done((bf16[136,1024]{1,0:T(8,128)(2,1)S(1)}, bf16[136,1024]{1,0:T(8,128)(2,1)S(1)}, u32[]{:S(2)}, u32[]{:S(2)}) %collective-permute-start.8) | collective-permute-done | bytes 278560 | tf_op jit(solution)/shard_map/ppermute | solution.py:667
  38.3 0.8 slice_bitcast_fusion.6
  39.2 1.7 %maximum_bitcast_fusion = (bf16[1,3,136,512]{3,2,1,0:T(8,128)(2,1)S(1)}, bf16[1,3,136,512]{3,2,1,0:T(8,128)(2,1)S(1)}) fusion(bf16[1,136,512]{2,1,0:T(8,128)(2,1)} %get-tuple-element.82, bf16[1,136,512]{2,1,0:T(8,128)(2,1)} %get-tuple-element.80, bf16[1,136,512]{2,1,0:T(8,128)(2,1)S(1)} %get-tuple-element.78, bf16[1,136,512]{2,1,0:T(8,128)(2,1)} %get-tuple-element.83, ...), kind=kLoop, calls=%fused_computation.10 | loop fusion | flops 835584 | bytes 1671168 | tf_op jit(solution)/shard_map/stack | solution.py:624
  41.1 2.7 %collective-permute-done.9.refs_7_ = bf16[136,1024]{1,0:T(8,128)(2,1)S(1)} collective-permute-done((bf16[136,1024]{1,0:T(8,128)(2,1)S(1)}, bf16[136,1024]{1,0:T(8,128)(2,1)S(1)}, u32[]{:S(2)}, u32[]{:S(2)}) %collective-permute-start.9) | collective-permute-done | bytes 278560 | tf_op jit(solution)/shard_map/ppermute | solution.py:667
  44.0 1.4 %pad_maximum_fusion = bf16[4,3,136,512]{3,2,1,0:T(8,128)(2,1)} fusion(bf16[1,3,136,512]{3,2,1,0:T(8,128)(2,1)S(1)} %get-tuple-element.101, bf16[1,3,136,512]{3,2,1,0:T(8,128)(2,1)S(1)} %get-tuple-element.100, bf16[1,3,136,512]{3,2,1,0:T(8,128)(2,1)S(1)} %get-tuple-element.103, bf16[1,3,136,512]{3,2,1,0:T(8,128)(2,1)S(1)} %get-tuple-element.102), kind=kLoop, calls=%fused_computation | loop fusion | flops 2506752 | bytes 3342336 | tf_op jit(solution)/shard_map/stack | solution.py:624
  45.4 0.7 copy-done.14
  46.1 0.7 copy-done.15
  46.8 4.1 %all-to-all-start.1 = ((bf16[4,3,136,512]{3,2,1,0:T(8,128)(2,1)}), bf16[4,3,136,512]{3,2,1,0:T(8,128)(2,1)S(1)}, u32[]{:S(2)}, u32[]{:S(2)}) async-start(bf16[4,3,136,512]{3,2,1,0:T(8,128)(2,1)} %pad_maximum_fusion), calls=%async_computation.1 | async-start | bytes 3342336 | tf_op jit(solution)/shard_map/all_to_all | solution.py:629
  50.9 18.8 %expert_rows.1 = (bf16[2,16,40,384]{3,2,1,0:T(8,128)(2,1)}, f32[8,8,128]{2,1,0:T(8,128)}, bf16[16,64,96]{2,1,0:T(8,128)(2,1)}, bf16[16,64,96]{2,1,0:T(8,128)(2,1...) custom-call(bf16[136,1024]{1,0:T(8,128)(2,1)} %get-tuple-element.38.refs_0_, ...), custom_call_target="tpu_custom_call" | custom-call | flops 6039797760 | bytes 33554432 | tf_op jit(solution)/shard_map/expert_rows/pallas_call | solution.py:680
  69.8 2.1 %all-to-all-done.1.refs_2_ = bf16[4,3,136,512]{3,2,1,0:T(8,128)(2,1)S(1)} async-done(((bf16[4,3,136,512]{3,2,1,0:T(8,128)(2,1)}), bf16[4,3,136,512]{3,2,1,0:T(8,128)(2,1)S(1)}, u32[]{:S(2)}, u32[]{:S(2)}) %all-to-all-start.1) | async-done | bytes 1671200 | tf_op jit(solution)/shard_map/all_to_all | solution.py:629
  71.9 1.4 %collective-permute-start.16 = (bf16[16,64,96]{2,1,0:T(8,128)(2,1)}, bf16[16,64,96]{2,1,0:T(8,128)(2,1)S(1)}, u32[]{:S(2)}, u32[]{:S(2)}) collective-permute-start(bf16[16,64,96]{2,1,0:T(8,128)(2,1)} %get-tuple-element.60), channel_id=1, source_target_pairs={{0,8},{8,16},{16,24},{24,0},{1,9},{9,17},{17,25},{25,1},{2,10},{10... | collective-permute-start | bytes 589832 | tf_op jit(solution)/shard_map/ppermute | solution.py:612
  73.9 2.4 %collective-permute-start.18 = (bf16[16,64,96]{2,1,0:T(8,128)(2,1)}, bf16[16,64,96]{2,1,0:T(8,128)(2,1)S(1)}, u32[]{:S(2)}, u32[]{:S(2)}) collective-permute-start(bf16[16,64,96]{2,1,0:T(8,128)(2,1)} %get-tuple-element.62), channel_id=1, source_target_pairs={{0,24},{8,0},{16,8},{24,16},{1,25},{9,1},{17,9},{25,17},{2,26},{10... | collective-permute-start | bytes 589832 | tf_op jit(solution)/shard_map/ppermute | solution.py:612
  76.3 3.9 %all-to-all-start.2 = ((f32[8,8,128]{2,1,0:T(8,128)}), f32[8,8,128]{2,1,0:T(8,128)S(1)}, u32[]{:S(2)}, u32[]{:S(2)}) async-start(f32[8,8,128]{2,1,0:T(8,128)} %get-tuple-element.59), calls=%async_computation.2 | async-start | bytes 65536 | tf_op jit(solution)/shard_map/all_to_all | solution.py:720
  80.2 7.1 %adapter_columns.1 = f32[16,64,512]{2,1,0:T(8,128)} custom-call(bf16[4,328,512]{2,1,0:T(8,128)(2,1)} %copy-done, bf16[4,136,512]{2,1,0:T(8,128)(2,1)} %collective-permute-done.10.refs_1_, bf16[4,3,136,512]{3,2,1,0:T(8,128)(2,1)} %copy-done.2, bf16[4,3,136,512]{3,2,1,0:T(8,128)(2,1)} %collective-permute-done.15.refs_3_), custom_call_target="tpu_custom_call" | custom-call | flops 3623878656 | bytes 6291456 | tf_op jit(solution)/shard_map/adapter_columns/pallas_call | solution.py:722
  88.0 1.0 %convert_add_fusion = f32[16,64,96]{2,1,0:T(8,128)} fusion(bf16[16,64,96]{2,1,0:T(8,128)(2,1)S(1)} %collective-permute-done.18, bf16[16,64,96]{2,1,0:T(8,128)(2,1)S(1)} %collective-permute-done.17, bf16[16,64,96]{2,1,0:T(8,128)(2,1)S(1)} %collective-permute-done.16, bf16[16,64,96]{2,1,0:T(8,128)(2,1)S(1)} %copy-done.16), kind=kLoop, calls=%fused_computation.5 | loop fusion | flops 688128 | bytes 1179648 | tf_op jit(solution)/shard_map/add | solution.py:749
  (69 shorter events, 3.2 us)
Async XLA Ops:
  2.5 17.3 %collective-permute-start.3 = (bf16[136,1024]{1,0:T(8,128)(2,1)}, bf16[136,1024]{1,0:T(8,128)(2,1)}, u32[]{:S(2)}, u32[]{:S(2)}) collective-permute-start(bf16[136,1024]{1,0:T(8,128)(2,1)} %get-tuple-element.38.refs_0_), channel_id=1, source_target_pairs={{0,1},{1,0},{2,3},{3,2},{4,5},{5,4},{6,7},{7,6},{8,9},{9,8},{10,11... | collective-permute-start | bytes 835592 | tf_op jit(solution)/shard_map/ppermute | solution.py:617
  3.0 13.8 %collective-permute-start = (bf16[136,1024]{1,0:T(8,128)(2,1)}, bf16[136,1024]{1,0:T(8,128)(2,1)S(1)}, u32[]{:S(2)}, u32[]{:S(2)}) collective-permute-start(bf16[136,1024]{1,0:T(8,128)(2,1)} %get-tuple-element.38.refs_0_), channel_id=1, source_target_pairs={{0,4},{1,5},{2,0},{3,1},{4,6},{5,7},{6,2},{7,3},{8,12},{9,13},{10,... | collective-permute-start | bytes 835592 | tf_op jit(solution)/shard_map/ppermute | solution.py:667
  6.6 23.3 %collective-permute-start.6 = (bf16[136,1024]{1,0:T(8,128)(2,1)}, bf16[136,1024]{1,0:T(8,128)(2,1)S(1)}, u32[]{:S(2)}, u32[]{:S(2)}) collective-permute-start(bf16[136,1024]{1,0:T(8,128)(2,1)} %get-tuple-element.39.refs_1_), channel_id=1, source_target_pairs={{0,1},{1,0},{2,3},{3,2},{4,5},{5,4},{6,7},{7,6},{8,9},{9,8},{10,11... | collective-permute-start | bytes 835592 | tf_op jit(solution)/shard_map/ppermute | solution.py:617
  6.8 13.0 %collective-permute-start.1 = (bf16[136,1024]{1,0:T(8,128)(2,1)}, bf16[136,1024]{1,0:T(8,128)(2,1)S(1)}, u32[]{:S(2)}, u32[]{:S(2)}) collective-permute-start(bf16[136,1024]{1,0:T(8,128)(2,1)} %get-tuple-element.39.refs_1_), channel_id=1, source_target_pairs={{0,4},{1,5},{2,0},{3,1},{4,6},{5,7},{6,2},{7,3},{8,12},{9,13},{10,... | collective-permute-start | bytes 835592 | tf_op jit(solution)/shard_map/ppermute | solution.py:667
  13.1 26.0 %all-to-all-start = ((bf16[4,328,512]{2,1,0:T(8,128)(2,1)}), bf16[4,328,512]{2,1,0:T(8,128)(2,1)S(1)}, u32[]{:S(2)}, u32[]{:S(2)}) async-start(bf16[4,328,512]{2,1,0:T(8,128)(2,1)} %pad_maximum_fusion.1), calls=%async_computation | async-start | bytes 2686976 | tf_op jit(solution)/shard_map/all_to_all | solution.py:629
  16.8 22.4 %copy-start.3 = (bf16[136,1024]{1,0:T(8,128)(2,1)}, bf16[136,1024]{1,0:T(8,128)(2,1)S(1)}, u32[]{:S(2)}) copy-start(bf16[136,1024]{1,0:T(8,128)(2,1)S(1)} %collective-permute-done.refs_2_) | copy-start | bytes 835588
  16.8 6.4 %collective-permute-start.4 = (bf16[136,1024]{1,0:T(8,128)(2,1)S(1)}, bf16[136,1024]{1,0:T(8,128)(2,1)S(1)}, u32[]{:S(2)}, u32[]{:S(2)}) collective-permute-start(bf16[136,1024]{1,0:T(8,128)(2,1)S(1)} %collective-permute-done.refs_2_), channel_id=1, source_target_pairs={{0,1},{1,0},{2,3},{3,2},{4,5},{5,4},{6,7},{7,6},{8,9},{9,8},{10,11... | collective-permute-start | bytes 835592 | tf_op jit(solution)/shard_map/ppermute | solution.py:617
  16.8 9.5 %collective-permute-start.2 = (bf16[136,1024]{1,0:T(8,128)(2,1)S(1)}, bf16[136,1024]{1,0:T(8,128)(2,1)S(1)}, u32[]{:S(2)}, u32[]{:S(2)}) collective-permute-start(bf16[136,1024]{1,0:T(8,128)(2,1)S(1)} %collective-permute-done.refs_2_), channel_id=1, source_target_pairs={{0,4},{1,5},{2,0},{3,1},{4,6},{5,7},{6,2},{7,3},{8,12},{9,13},{10,... | collective-permute-start | bytes 835592 | tf_op jit(solution)/shard_map/ppermute | solution.py:667
  19.8 19.3 %copy-start.4 = (bf16[136,1024]{1,0:T(8,128)(2,1)}, bf16[136,1024]{1,0:T(8,128)(2,1)S(1)}, u32[]{:S(2)}) copy-start(bf16[136,1024]{1,0:T(8,128)(2,1)S(1)} %collective-permute-done.1.refs_3_) | copy-start | bytes 835588
  19.8 10.0 %collective-permute-start.7 = (bf16[136,1024]{1,0:T(8,128)(2,1)S(1)}, bf16[136,1024]{1,0:T(8,128)(2,1)S(1)}, u32[]{:S(2)}, u32[]{:S(2)}) collective-permute-start(bf16[136,1024]{1,0:T(8,128)(2,1)S(1)} %collective-permute-done.1.refs_3_), channel_id=1, source_target_pairs={{0,1},{1,0},{2,3},{3,2},{4,5},{5,4},{6,7},{7,6},{8,9},{9,8},{10,11... | collective-permute-start | bytes 835592 | tf_op jit(solution)/shard_map/ppermute | solution.py:617
  19.8 12.5 %collective-permute-start.5 = (bf16[136,1024]{1,0:T(8,128)(2,1)S(1)}, bf16[136,1024]{1,0:T(8,128)(2,1)S(1)}, u32[]{:S(2)}, u32[]{:S(2)}) collective-permute-start(bf16[136,1024]{1,0:T(8,128)(2,1)S(1)} %collective-permute-done.1.refs_3_), channel_id=1, source_target_pairs={{0,4},{1,5},{2,0},{3,1},{4,6},{5,7},{6,2},{7,3},{8,12},{9,13},{10,... | collective-permute-start | bytes 835592 | tf_op jit(solution)/shard_map/ppermute | solution.py:667
  26.4 14.6 %copy-start.5 = (bf16[136,1024]{1,0:T(8,128)(2,1)}, bf16[136,1024]{1,0:T(8,128)(2,1)S(1)}, u32[]{:S(2)}) copy-start(bf16[136,1024]{1,0:T(8,128)(2,1)S(1)} %collective-permute-done.2.refs_4_) | copy-start | bytes 835588
  26.4 11.9 %collective-permute-start.8 = (bf16[136,1024]{1,0:T(8,128)(2,1)S(1)}, bf16[136,1024]{1,0:T(8,128)(2,1)S(1)}, u32[]{:S(2)}, u32[]{:S(2)}) collective-permute-start(bf16[136,1024]{1,0:T(8,128)(2,1)S(1)} %collective-permute-done.2.refs_4_), channel_id=1, source_target_pairs={{0,4},{1,5},{2,0},{3,1},{4,6},{5,7},{6,2},{7,3},{8,12},{9,13},{10,... | collective-permute-start | bytes 835592 | tf_op jit(solution)/shard_map/ppermute | solution.py:667
  29.8 15.6 %collective-permute-start.11 = (bf16[136,1024]{1,0:T(8,128)(2,1)S(1)}, bf16[136,1024]{1,0:T(8,128)(2,1)}, u32[]{:S(2)}, u32[]{:S(2)}) collective-permute-start(bf16[136,1024]{1,0:T(8,128)(2,1)S(1)} %collective-permute-done.2.refs_4_), channel_id=1, source_target_pairs={{0,1},{1,0},{2,3},{3,2},{4,5},{5,4},{6,7},{7,6},{8,9},{9,8},{10,11... | collective-permute-start | bytes 835592 | tf_op jit(solution)/shard_map/ppermute | solution.py:617
  29.8 8.5 %copy-start.13 = (bf16[136,1024]{1,0:T(8,128)(2,1)}, bf16[136,1024]{1,0:T(8,128)(2,1)S(1)}, u32[]{:S(2)}) copy-start(bf16[136,1024]{1,0:T(8,128)(2,1)S(1)} %collective-permute-done.7.refs_11_) | copy-start | bytes 835588
  32.3 8.7 %copy-start.6 = (bf16[136,1024]{1,0:T(8,128)(2,1)}, bf16[136,1024]{1,0:T(8,128)(2,1)S(1)}, u32[]{:S(2)}) copy-start(bf16[136,1024]{1,0:T(8,128)(2,1)S(1)} %collective-permute-done.5.refs_5_) | copy-start | bytes 835588
  32.3 13.0 %collective-permute-start.12 = (bf16[136,1024]{1,0:T(8,128)(2,1)S(1)}, bf16[136,1024]{1,0:T(8,128)(2,1)}, u32[]{:S(2)}, u32[]{:S(2)}) collective-permute-start(bf16[136,1024]{1,0:T(8,128)(2,1)S(1)} %collective-permute-done.5.refs_5_), channel_id=1, source_target_pairs={{0,1},{1,0},{2,3},{3,2},{4,5},{5,4},{6,7},{7,6},{8,9},{9,8},{10,11... | collective-permute-start | bytes 835592 | tf_op jit(solution)/shard_map/ppermute | solution.py:617
  32.3 11.5 %collective-permute-start.9 = (bf16[136,1024]{1,0:T(8,128)(2,1)S(1)}, bf16[136,1024]{1,0:T(8,128)(2,1)S(1)}, u32[]{:S(2)}, u32[]{:S(2)}) collective-permute-start(bf16[136,1024]{1,0:T(8,128)(2,1)S(1)} %collective-permute-done.5.refs_5_), channel_id=1, source_target_pairs={{0,4},{1,5},{2,0},{3,1},{4,6},{5,7},{6,2},{7,3},{8,12},{9,13},{10,... | collective-permute-start | bytes 835592 | tf_op jit(solution)/shard_map/ppermute | solution.py:667
  39.1 4.8 %copy-start = (bf16[4,328,512]{2,1,0:T(8,128)(2,1)}, bf16[4,328,512]{2,1,0:T(8,128)(2,1)S(1)}, u32[]{:S(2)}) copy-start(bf16[4,328,512]{2,1,0:T(8,128)(2,1)S(1)} %all-to-all-done.refs_0_) | copy-start | bytes 4030468
  39.1 4.8 %copy-start.9 = (bf16[1,136,512]{2,1,0:T(8,128)(2,1)S(1)}, bf16[1,136,512]{2,1,0:T(8,128)(2,1)}, u32[]{:S(2)}) copy-start(bf16[1,136,512]{2,1,0:T(8,128)(2,1)} %get-tuple-element.86) | copy-start | bytes 417796
  39.1 4.8 %copy-start.10 = (bf16[1,136,512]{2,1,0:T(8,128)(2,1)S(1)}, bf16[1,136,512]{2,1,0:T(8,128)(2,1)}, u32[]{:S(2)}) copy-start(bf16[1,136,512]{2,1,0:T(8,128)(2,1)} %get-tuple-element.87) | copy-start | bytes 417796
  39.2 7.6 %collective-permute-start.10 = (bf16[4,136,512]{2,1,0:T(8,128)(2,1)S(1)}, bf16[4,136,512]{2,1,0:T(8,128)(2,1)}, u32[]{:S(2)}, u32[]{:S(2)}) collective-permute-start(bf16[4,136,512]{2,1,0:T(8,128)(2,1)S(1)} %slice.106), channel_id=1, source_target_pairs={{0,1},{1,0},{2,3},{3,2},{4,5},{5,4},{6,7},{7,6},{8,9},{9,8},{10,11... | collective-permute-start | bytes 1671176 | tf_op jit(solution)/shard_map/ppermute | solution.py:617
  41.0 4.4 %collective-permute-start.13 = (bf16[136,1024]{1,0:T(8,128)(2,1)S(1)}, bf16[136,1024]{1,0:T(8,128)(2,1)S(1)}, u32[]{:S(2)}, u32[]{:S(2)}) collective-permute-start(bf16[136,1024]{1,0:T(8,128)(2,1)S(1)} %collective-permute-done.8.refs_6_), channel_id=1, source_target_pairs={{0,1},{1,0},{2,3},{3,2},{4,5},{5,4},{6,7},{7,6},{8,9},{9,8},{10,11... | collective-permute-start | bytes 835592 | tf_op jit(solution)/shard_map/ppermute | solution.py:617
  43.8 1.6 %collective-permute-start.14 = (bf16[136,1024]{1,0:T(8,128)(2,1)S(1)}, bf16[136,1024]{1,0:T(8,128)(2,1)S(1)}, u32[]{:S(2)}, u32[]{:S(2)}) collective-permute-start(bf16[136,1024]{1,0:T(8,128)(2,1)S(1)} %collective-permute-done.9.refs_7_), channel_id=1, source_target_pairs={{0,1},{1,0},{2,3},{3,2},{4,5},{5,4},{6,7},{7,6},{8,9},{9,8},{10,11... | collective-permute-start | bytes 835592 | tf_op jit(solution)/shard_map/ppermute | solution.py:617
  46.8 25.1 %all-to-all-start.1 = ((bf16[4,3,136,512]{3,2,1,0:T(8,128)(2,1)}), bf16[4,3,136,512]{3,2,1,0:T(8,128)(2,1)S(1)}, u32[]{:S(2)}, u32[]{:S(2)}) async-start(bf16[4,3,136,512]{3,2,1,0:T(8,128)(2,1)} %pad_maximum_fusion), calls=%async_computation.1 | async-start | bytes 3342336 | tf_op jit(solution)/shard_map/all_to_all | solution.py:629
  71.9 8.3 %copy-start.2 = (bf16[4,3,136,512]{3,2,1,0:T(8,128)(2,1)}, bf16[4,3,136,512]{3,2,1,0:T(8,128)(2,1)S(1)}, u32[]{:S(2)}) copy-start(bf16[4,3,136,512]{3,2,1,0:T(8,128)(2,1)S(1)} %all-to-all-done.1.refs_2_) | copy-start | bytes 5013508
  71.9 4.4 %collective-permute-start.15 = (bf16[4,3,136,512]{3,2,1,0:T(8,128)(2,1)S(1)}, bf16[4,3,136,512]{3,2,1,0:T(8,128)(2,1)}, u32[]{:S(2)}, u32[]{:S(2)}) collective-permute-start(bf16[4,3,136,512]{3,2,1,0:T(8,128)(2,1)S(1)} %all-to-all-done.1.refs_2_), channel_id=1, source_target_pairs={{0,1},{1,0},{2,3},{3,2},{4,5},{5,4},{6,7},{7,6},{8,9},{9,8},{10,11... | collective-permute-start | bytes 5013512 | tf_op jit(solution)/shard_map/ppermute | solution.py:617
  71.9 15.4 %collective-permute-start.16 = (bf16[16,64,96]{2,1,0:T(8,128)(2,1)}, bf16[16,64,96]{2,1,0:T(8,128)(2,1)S(1)}, u32[]{:S(2)}, u32[]{:S(2)}) collective-permute-start(bf16[16,64,96]{2,1,0:T(8,128)(2,1)} %get-tuple-element.60), channel_id=1, source_target_pairs={{0,8},{8,16},{16,24},{24,0},{1,9},{9,17},{17,25},{25,1},{2,10},{10... | collective-permute-start | bytes 589832 | tf_op jit(solution)/shard_map/ppermute | solution.py:612
  73.3 14.0 %collective-permute-start.17 = (bf16[16,64,96]{2,1,0:T(8,128)(2,1)}, bf16[16,64,96]{2,1,0:T(8,128)(2,1)S(1)}, u32[]{:S(2)}, u32[]{:S(2)}) collective-permute-start(bf16[16,64,96]{2,1,0:T(8,128)(2,1)} %get-tuple-element.61), channel_id=1, source_target_pairs={{0,16},{8,24},{16,0},{24,8},{1,17},{9,25},{17,1},{25,9},{2,18},{10... | collective-permute-start | bytes 589832 | tf_op jit(solution)/shard_map/ppermute | solution.py:612
  73.9 13.5 %collective-permute-start.18 = (bf16[16,64,96]{2,1,0:T(8,128)(2,1)}, bf16[16,64,96]{2,1,0:T(8,128)(2,1)S(1)}, u32[]{:S(2)}, u32[]{:S(2)}) collective-permute-start(bf16[16,64,96]{2,1,0:T(8,128)(2,1)} %get-tuple-element.62), channel_id=1, source_target_pairs={{0,24},{8,0},{16,8},{24,16},{1,25},{9,1},{17,9},{25,17},{2,26},{10... | collective-permute-start | bytes 589832 | tf_op jit(solution)/shard_map/ppermute | solution.py:612
  76.3 11.1 %all-to-all-start.2 = ((f32[8,8,128]{2,1,0:T(8,128)}), f32[8,8,128]{2,1,0:T(8,128)S(1)}, u32[]{:S(2)}, u32[]{:S(2)}) async-start(f32[8,8,128]{2,1,0:T(8,128)} %get-tuple-element.59), calls=%async_computation.2 | async-start | bytes 65536 | tf_op jit(solution)/shard_map/all_to_all | solution.py:720
  80.2 7.9 %copy-start.16 = (bf16[16,64,96]{2,1,0:T(8,128)(2,1)S(1)}, bf16[16,64,96]{2,1,0:T(8,128)(2,1)}, u32[]{:S(2)}) copy-start(bf16[16,64,96]{2,1,0:T(8,128)(2,1)} %get-tuple-element.67) | copy-start | bytes 589828
  (7 other events, 10.3 us)

commit v14 on v13

--- a/solution.py
+++ b/solution.py
@@ -713,7 +713,7 @@
         name="expert_rows",
     )(*pieces, hidden, u, frozen_down_weight, amap, adapter_output_map)
 
-    columns, parts, routed = lax.optimization_barrier((columns, parts, routed))
+    columns, _, _ = lax.optimization_barrier((columns, parts, routed))
     swapped = swap_partners(columns)
     arrived = [shift_groups(parts[s], s) for s in others]
     swapped, routed = lax.optimization_barrier((swapped, routed))

time: 89.4 us -> 89.4 us (level)
  no operation moved by 1% of the time
where the time goes in v14:
time: 89.4 us; the launch traced here: 89 us
  starting transfers between devices  31.4 us (35%)
  Pallas kernels  27.8 us (31%)
  waiting for transfers between devices  14.4 us (16%)
  local copies, waits for them, and re-layouts  6.35 us (7%)
  other arithmetic  6.25 us (7%)
  matrix products  1.91 us (2%)
  between operations  0.93 us (1%)
    pallas_call x1, Pallas kernels, local_by_tokens(): pl.pallas_call(functools.partial(expert_kernel, capacity, group_count, so...  18.8 us
    ppermute x6, starting transfers between devices, local_by_tokens(): near.append([lax.ppermute(piece, 'expert', ring) for piece in near[step]])  14.3 us
    ppermute x6, waiting for transfers between devices, local_by_tokens(): near.append([lax.ppermute(piece, 'expert', ring) for piece in near[step]])  12.1 us
    all_to_all x2, starting transfers between devices, across_groups(): return lax.all_to_all(array, 'dp', split_axis=0, concat_axis=0, tiled=True)  7.85 us
    pallas_call x1, Pallas kernels, local_by_tokens(): pl.pallas_call(functools.partial(adapter_kernel, capacity, micro, span, t...  7.09 us
    ppermute x3, starting transfers between devices, shift_groups(): lax.ppermute(array, 'dp', [(d, (d + by) % group_count) for d in range(gro...  4.39 us
    all_to_all x1, starting transfers between devices, local_by_tokens(): lax.all_to_all(routed, 'expert', split_axis=0, concat_axis=0, tiled=True)  3.85 us
    another operation x3, other arithmetic, exchange_columns(): jnp.stack([jnp.stack([columns(pieces, g) for pieces in chosen]) for g in...  3.21 us
  transfers between devices with their start and end apart: 22, of which 7 were waited for; matrix products, arithmetic and copies ran while one was open for 12% of the time, Pallas kernels for 29%

profile of v14, /device:TPU:0, one launch (start us, length us, event | category | flops | bytes accessed | tf_op | source)
XLA Modules:
  0.0 89.0 jit_solution(7396849265345782792)
XLA Ops:
  0.6 1.9 %ring_payload.1 = (bf16[136,1024]{1,0:T(8,128)(2,1)}, bf16[136,1024]{1,0:T(8,128)(2,1)}) custom-call(bf16[128,2048]{1,0:T(8,128)(2,1)} %dy_ref.1, s32[8,128]{1,0:T(8,128)} %bitcast.56, bf16[8,128]{1,0:T(8,128)(2,1)} %bitcast.58), custom_call_target="tpu_custom_call" | custom-call | tf_op jit(solution)/shard_map/ring_payload/pallas_call | solution.py:635
  3.0 3.6 %collective-permute-start = (bf16[136,1024]{1,0:T(8,128)(2,1)}, bf16[136,1024]{1,0:T(8,128)(2,1)S(1)}, u32[]{:S(2)}, u32[]{:S(2)}) collective-permute-start(bf16[136,1024]{1,0:T(8,128)(2,1)} %get-tuple-element.33.refs_0_), channel_id=1, source_target_pairs={{0,4},{1,5},{2,0},{3,1},{4,6},{5,7},{6,2},{7,3},{8,12},{9,13},{10,... | collective-permute-start | bytes 835592 | tf_op jit(solution)/shard_map/ppermute | solution.py:667
  6.8 1.6 %collective-permute-start.1 = (bf16[136,1024]{1,0:T(8,128)(2,1)}, bf16[136,1024]{1,0:T(8,128)(2,1)S(1)}, u32[]{:S(2)}, u32[]{:S(2)}) collective-permute-start(bf16[136,1024]{1,0:T(8,128)(2,1)} %get-tuple-element.34.refs_1_), channel_id=1, source_target_pairs={{0,4},{1,5},{2,0},{3,1},{4,6},{5,7},{6,2},{7,3},{8,12},{9,13},{10,... | collective-permute-start | bytes 835592 | tf_op jit(solution)/shard_map/ppermute | solution.py:667
  8.4 1.1 %fusion.6 = (bf16[136,512]{1,0:T(8,128)(2,1)S(1)}, bf16[136,512]{1,0:T(8,128)(2,1)S(1)}, bf16[136,512]{1,0:T(8,128)(2,1)S(1)}, bf16[136,512]{1,0:T(8,128)(2,1)S(1)}) fusion(bf16[136,1024]{1,0:T(8,128)(2,1)} %get-tuple-element.33.refs_0_, bf16[136,1024]{1,0:T(8,128)(2,1)} %get-tuple-element.34.refs_1_), kind=kLoop, calls=%fused_computation.34 | loop fusion | bytes 1114112 | tf_op jit(solution)/shard_map/slice | solution.py:652
  9.5 1.9 %convolution_convert_fusion = bf16[16,2,40,64]{3,2,1,0:T(8,128)(2,1)S(1)} fusion(bf16[2,16,40,384]{3,2,1,0:T(8,128)(2,1)} %refs_16_.1, bf16[16,384,64]{1,2,0:T(8,128)(2,1)} %param.12), kind=kOutput, calls=%fused_computation.2 | convolution fusion | flops 62996480 | bytes 1933312 | tf_op jit(solution)/shard_map/mesk,exk->emsx/dot_general | solution.py:604
  11.8 1.2 %pad_maximum_fusion.1 = bf16[4,328,512]{2,1,0:T(8,128)(2,1)} fusion(bf16[1,328,512]{2,1,0:T(8,128)(2,1)S(1)} %get-tuple-element.83, bf16[1,328,512]{2,1,0:T(8,128)(2,1)S(1)} %get-tuple-element.82, bf16[1,328,512]{2,1,0:T(8,128)(2,1)S(1)} %get-tuple-element.81, bf16[1,328,512]{2,1,0:T(8,128)(2,1)S(1)} %get-tuple-element.80), kind=kLoop, calls=%fused_computation.1 | loop fusion | flops 2015232 | bytes 2686976 | tf_op jit(solution)/shard_map/stack | solution.py:649
  13.1 3.7 %all-to-all-start = ((bf16[4,328,512]{2,1,0:T(8,128)(2,1)}), bf16[4,328,512]{2,1,0:T(8,128)(2,1)S(1)}, u32[]{:S(2)}, u32[]{:S(2)}) async-start(bf16[4,328,512]{2,1,0:T(8,128)(2,1)} %pad_maximum_fusion.1), calls=%async_computation | async-start | bytes 2686976 | tf_op jit(solution)/shard_map/all_to_all | solution.py:629
  17.2 0.7 slice_bitcast_fusion.7
  17.9 1.9 %collective-permute-done.1.refs_3_ = bf16[136,1024]{1,0:T(8,128)(2,1)S(1)} collective-permute-done((bf16[136,1024]{1,0:T(8,128)(2,1)}, bf16[136,1024]{1,0:T(8,128)(2,1)S(1)}, u32[]{:S(2)}, u32[]{:S(2)}) %collective-permute-start.1) | collective-permute-done | bytes 278560 | tf_op jit(solution)/shard_map/ppermute | solution.py:667
  19.8 3.3 %collective-permute-start.5 = (bf16[136,1024]{1,0:T(8,128)(2,1)S(1)}, bf16[136,1024]{1,0:T(8,128)(2,1)S(1)}, u32[]{:S(2)}, u32[]{:S(2)}) collective-permute-start(bf16[136,1024]{1,0:T(8,128)(2,1)S(1)} %collective-permute-done.1.refs_3_), channel_id=1, source_target_pairs={{0,4},{1,5},{2,0},{3,1},{4,6},{5,7},{6,2},{7,3},{8,12},{9,13},{10,... | collective-permute-start | bytes 835592 | tf_op jit(solution)/shard_map/ppermute | solution.py:667
  23.2 0.7 copy-done.12
  23.9 2.5 %collective-permute-done.2.refs_4_ = bf16[136,1024]{1,0:T(8,128)(2,1)S(1)} collective-permute-done((bf16[136,1024]{1,0:T(8,128)(2,1)S(1)}, bf16[136,1024]{1,0:T(8,128)(2,1)S(1)}, u32[]{:S(2)}, u32[]{:S(2)}) %collective-permute-start.2) | collective-permute-done | bytes 278560 | tf_op jit(solution)/shard_map/ppermute | solution.py:667
  26.4 2.7 %collective-permute-start.8 = (bf16[136,1024]{1,0:T(8,128)(2,1)S(1)}, bf16[136,1024]{1,0:T(8,128)(2,1)S(1)}, u32[]{:S(2)}, u32[]{:S(2)}) collective-permute-start(bf16[136,1024]{1,0:T(8,128)(2,1)S(1)} %collective-permute-done.2.refs_4_), channel_id=1, source_target_pairs={{0,4},{1,5},{2,0},{3,1},{4,6},{5,7},{6,2},{7,3},{8,12},{9,13},{10,... | collective-permute-start | bytes 835592 | tf_op jit(solution)/shard_map/ppermute | solution.py:667
  29.1 0.7 slice_bitcast_fusion.11
  29.8 2.5 %collective-permute-done.5.refs_5_ = bf16[136,1024]{1,0:T(8,128)(2,1)S(1)} collective-permute-done((bf16[136,1024]{1,0:T(8,128)(2,1)S(1)}, bf16[136,1024]{1,0:T(8,128)(2,1)S(1)}, u32[]{:S(2)}, u32[]{:S(2)}) %collective-permute-start.5) | collective-permute-done | bytes 278560 | tf_op jit(solution)/shard_map/ppermute | solution.py:667
  32.3 2.8 %collective-permute-start.9 = (bf16[136,1024]{1,0:T(8,128)(2,1)S(1)}, bf16[136,1024]{1,0:T(8,128)(2,1)S(1)}, u32[]{:S(2)}, u32[]{:S(2)}) collective-permute-start(bf16[136,1024]{1,0:T(8,128)(2,1)S(1)} %collective-permute-done.5.refs_5_), channel_id=1, source_target_pairs={{0,4},{1,5},{2,0},{3,1},{4,6},{5,7},{6,2},{7,3},{8,12},{9,13},{10,... | collective-permute-start | bytes 835592 | tf_op jit(solution)/shard_map/ppermute | solution.py:667
  35.1 0.7 slice_bitcast_fusion.9
  35.8 2.5 %collective-permute-done.8.refs_6_ = bf16[136,1024]{1,0:T(8,128)(2,1)S(1)} collective-permute-done((bf16[136,1024]{1,0:T(8,128)(2,1)S(1)}, bf16[136,1024]{1,0:T(8,128)(2,1)S(1)}, u32[]{:S(2)}, u32[]{:S(2)}) %collective-permute-start.8) | collective-permute-done | bytes 278560 | tf_op jit(solution)/shard_map/ppermute | solution.py:667
  38.3 0.8 slice_bitcast_fusion.6
  39.2 1.7 %maximum_bitcast_fusion = (bf16[1,3,136,512]{3,2,1,0:T(8,128)(2,1)S(1)}, bf16[1,3,136,512]{3,2,1,0:T(8,128)(2,1)S(1)}) fusion(bf16[1,136,512]{2,1,0:T(8,128)(2,1)} %get-tuple-element.72, bf16[1,136,512]{2,1,0:T(8,128)(2,1)} %get-tuple-element.70, bf16[1,136,512]{2,1,0:T(8,128)(2,1)S(1)} %get-tuple-element.68, bf16[1,136,512]{2,1,0:T(8,128)(2,1)} %get-tuple-element.73, ...), kind=kLoop, calls=%fused_computation.10 | loop fusion | flops 835584 | bytes 1671168 | tf_op jit(solution)/shard_map/stack | solution.py:624
  41.1 2.7 %collective-permute-done.9.refs_7_ = bf16[136,1024]{1,0:T(8,128)(2,1)S(1)} collective-permute-done((bf16[136,1024]{1,0:T(8,128)(2,1)S(1)}, bf16[136,1024]{1,0:T(8,128)(2,1)S(1)}, u32[]{:S(2)}, u32[]{:S(2)}) %collective-permute-start.9) | collective-permute-done | bytes 278560 | tf_op jit(solution)/shard_map/ppermute | solution.py:667
  44.0 1.4 %pad_maximum_fusion = bf16[4,3,136,512]{3,2,1,0:T(8,128)(2,1)} fusion(bf16[1,3,136,512]{3,2,1,0:T(8,128)(2,1)S(1)} %get-tuple-element.91, bf16[1,3,136,512]{3,2,1,0:T(8,128)(2,1)S(1)} %get-tuple-element.90, bf16[1,3,136,512]{3,2,1,0:T(8,128)(2,1)S(1)} %get-tuple-element.93, bf16[1,3,136,512]{3,2,1,0:T(8,128)(2,1)S(1)} %get-tuple-element.92), kind=kLoop, calls=%fused_computation | loop fusion | flops 2506752 | bytes 3342336 | tf_op jit(solution)/shard_map/stack | solution.py:624
  45.4 0.7 copy-done.14
  46.1 0.7 copy-done.15
  46.8 4.1 %all-to-all-start.1 = ((bf16[4,3,136,512]{3,2,1,0:T(8,128)(2,1)}), bf16[4,3,136,512]{3,2,1,0:T(8,128)(2,1)S(1)}, u32[]{:S(2)}, u32[]{:S(2)}) async-start(bf16[4,3,136,512]{3,2,1,0:T(8,128)(2,1)} %pad_maximum_fusion), calls=%async_computation.1 | async-start | bytes 3342336 | tf_op jit(solution)/shard_map/all_to_all | solution.py:629
  50.9 18.8 %expert_rows.1 = (bf16[2,16,40,384]{3,2,1,0:T(8,128)(2,1)}, f32[8,8,128]{2,1,0:T(8,128)}, bf16[16,64,96]{2,1,0:T(8,128)(2,1)}, bf16[16,64,96]{2,1,0:T(8,128)(2,1...) custom-call(bf16[136,1024]{1,0:T(8,128)(2,1)} %get-tuple-element.33.refs_0_, ...), custom_call_target="tpu_custom_call" | custom-call | flops 6039797760 | bytes 33554432 | tf_op jit(solution)/shard_map/expert_rows/pallas_call | solution.py:680
  69.8 2.1 %all-to-all-done.1.refs_2_ = bf16[4,3,136,512]{3,2,1,0:T(8,128)(2,1)S(1)} async-done(((bf16[4,3,136,512]{3,2,1,0:T(8,128)(2,1)}), bf16[4,3,136,512]{3,2,1,0:T(8,128)(2,1)S(1)}, u32[]{:S(2)}, u32[]{:S(2)}) %all-to-all-start.1) | async-done | bytes 1671200 | tf_op jit(solution)/shard_map/all_to_all | solution.py:629
  71.9 1.4 %collective-permute-start.16 = (bf16[16,64,96]{2,1,0:T(8,128)(2,1)}, bf16[16,64,96]{2,1,0:T(8,128)(2,1)S(1)}, u32[]{:S(2)}, u32[]{:S(2)}) collective-permute-start(bf16[16,64,96]{2,1,0:T(8,128)(2,1)} %get-tuple-element.48), channel_id=1, source_target_pairs={{0,8},{8,16},{16,24},{24,0},{1,9},{9,17},{17,25},{25,1},{2,10},{10... | collective-permute-start | bytes 589832 | tf_op jit(solution)/shard_map/ppermute | solution.py:612
  73.9 2.4 %collective-permute-start.18 = (bf16[16,64,96]{2,1,0:T(8,128)(2,1)}, bf16[16,64,96]{2,1,0:T(8,128)(2,1)S(1)}, u32[]{:S(2)}, u32[]{:S(2)}) collective-permute-start(bf16[16,64,96]{2,1,0:T(8,128)(2,1)} %get-tuple-element.50), channel_id=1, source_target_pairs={{0,24},{8,0},{16,8},{24,16},{1,25},{9,1},{17,9},{25,17},{2,26},{10... | collective-permute-start | bytes 589832 | tf_op jit(solution)/shard_map/ppermute | solution.py:612
  76.3 3.9 %all-to-all-start.2 = ((f32[8,8,128]{2,1,0:T(8,128)}), f32[8,8,128]{2,1,0:T(8,128)S(1)}, u32[]{:S(2)}, u32[]{:S(2)}) async-start(f32[8,8,128]{2,1,0:T(8,128)} %get-tuple-element.53), calls=%async_computation.2 | async-start | bytes 65536 | tf_op jit(solution)/shard_map/all_to_all | solution.py:720
  80.2 7.1 %adapter_columns.1 = f32[16,64,512]{2,1,0:T(8,128)} custom-call(bf16[4,328,512]{2,1,0:T(8,128)(2,1)} %copy-done, bf16[4,136,512]{2,1,0:T(8,128)(2,1)} %collective-permute-done.10.refs_1_, bf16[4,3,136,512]{3,2,1,0:T(8,128)(2,1)} %copy-done.2, bf16[4,3,136,512]{3,2,1,0:T(8,128)(2,1)} %collective-permute-done.15.refs_3_), custom_call_target="tpu_custom_call" | custom-call | flops 3623878656 | bytes 6291456 | tf_op jit(solution)/shard_map/adapter_columns/pallas_call | solution.py:722
  88.0 1.0 %convert_add_fusion = f32[16,64,96]{2,1,0:T(8,128)} fusion(bf16[16,64,96]{2,1,0:T(8,128)(2,1)S(1)} %collective-permute-done.18, bf16[16,64,96]{2,1,0:T(8,128)(2,1)S(1)} %collective-permute-done.17, bf16[16,64,96]{2,1,0:T(8,128)(2,1)S(1)} %collective-permute-done.16, bf16[16,64,96]{2,1,0:T(8,128)(2,1)S(1)} %copy-done.16), kind=kLoop, calls=%fused_computation.5 | loop fusion | flops 688128 | bytes 1179648 | tf_op jit(solution)/shard_map/add | solution.py:749
  (69 shorter events, 3.2 us)
Async XLA Ops:
  2.5 17.3 %collective-permute-start.3 = (bf16[136,1024]{1,0:T(8,128)(2,1)}, bf16[136,1024]{1,0:T(8,128)(2,1)}, u32[]{:S(2)}, u32[]{:S(2)}) collective-permute-start(bf16[136,1024]{1,0:T(8,128)(2,1)} %get-tuple-element.33.refs_0_), channel_id=1, source_target_pairs={{0,1},{1,0},{2,3},{3,2},{4,5},{5,4},{6,7},{7,6},{8,9},{9,8},{10,11... | collective-permute-start | bytes 835592 | tf_op jit(solution)/shard_map/ppermute | solution.py:617
  3.0 13.8 %collective-permute-start = (bf16[136,1024]{1,0:T(8,128)(2,1)}, bf16[136,1024]{1,0:T(8,128)(2,1)S(1)}, u32[]{:S(2)}, u32[]{:S(2)}) collective-permute-start(bf16[136,1024]{1,0:T(8,128)(2,1)} %get-tuple-element.33.refs_0_), channel_id=1, source_target_pairs={{0,4},{1,5},{2,0},{3,1},{4,6},{5,7},{6,2},{7,3},{8,12},{9,13},{10,... | collective-permute-start | bytes 835592 | tf_op jit(solution)/shard_map/ppermute | solution.py:667
  6.6 23.3 %collective-permute-start.6 = (bf16[136,1024]{1,0:T(8,128)(2,1)}, bf16[136,1024]{1,0:T(8,128)(2,1)S(1)}, u32[]{:S(2)}, u32[]{:S(2)}) collective-permute-start(bf16[136,1024]{1,0:T(8,128)(2,1)} %get-tuple-element.34.refs_1_), channel_id=1, source_target_pairs={{0,1},{1,0},{2,3},{3,2},{4,5},{5,4},{6,7},{7,6},{8,9},{9,8},{10,11... | collective-permute-start | bytes 835592 | tf_op jit(solution)/shard_map/ppermute | solution.py:617
  6.8 13.0 %collective-permute-start.1 = (bf16[136,1024]{1,0:T(8,128)(2,1)}, bf16[136,1024]{1,0:T(8,128)(2,1)S(1)}, u32[]{:S(2)}, u32[]{:S(2)}) collective-permute-start(bf16[136,1024]{1,0:T(8,128)(2,1)} %get-tuple-element.34.refs_1_), channel_id=1, source_target_pairs={{0,4},{1,5},{2,0},{3,1},{4,6},{5,7},{6,2},{7,3},{8,12},{9,13},{10,... | collective-permute-start | bytes 835592 | tf_op jit(solution)/shard_map/ppermute | solution.py:667
  13.1 26.0 %all-to-all-start = ((bf16[4,328,512]{2,1,0:T(8,128)(2,1)}), bf16[4,328,512]{2,1,0:T(8,128)(2,1)S(1)}, u32[]{:S(2)}, u32[]{:S(2)}) async-start(bf16[4,328,512]{2,1,0:T(8,128)(2,1)} %pad_maximum_fusion.1), calls=%async_computation | async-start | bytes 2686976 | tf_op jit(solution)/shard_map/all_to_all | solution.py:629
  16.8 22.4 %copy-start.3 = (bf16[136,1024]{1,0:T(8,128)(2,1)}, bf16[136,1024]{1,0:T(8,128)(2,1)S(1)}, u32[]{:S(2)}) copy-start(bf16[136,1024]{1,0:T(8,128)(2,1)S(1)} %collective-permute-done.refs_2_) | copy-start | bytes 835588
  16.8 6.4 %collective-permute-start.4 = (bf16[136,1024]{1,0:T(8,128)(2,1)S(1)}, bf16[136,1024]{1,0:T(8,128)(2,1)S(1)}, u32[]{:S(2)}, u32[]{:S(2)}) collective-permute-start(bf16[136,1024]{1,0:T(8,128)(2,1)S(1)} %collective-permute-done.refs_2_), channel_id=1, source_target_pairs={{0,1},{1,0},{2,3},{3,2},{4,5},{5,4},{6,7},{7,6},{8,9},{9,8},{10,11... | collective-permute-start | bytes 835592 | tf_op jit(solution)/shard_map/ppermute | solution.py:617
  16.8 9.5 %collective-permute-start.2 = (bf16[136,1024]{1,0:T(8,128)(2,1)S(1)}, bf16[136,1024]{1,0:T(8,128)(2,1)S(1)}, u32[]{:S(2)}, u32[]{:S(2)}) collective-permute-start(bf16[136,1024]{1,0:T(8,128)(2,1)S(1)} %collective-permute-done.refs_2_), channel_id=1, source_target_pairs={{0,4},{1,5},{2,0},{3,1},{4,6},{5,7},{6,2},{7,3},{8,12},{9,13},{10,... | collective-permute-start | bytes 835592 | tf_op jit(solution)/shard_map/ppermute | solution.py:667
  19.8 19.3 %copy-start.4 = (bf16[136,1024]{1,0:T(8,128)(2,1)}, bf16[136,1024]{1,0:T(8,128)(2,1)S(1)}, u32[]{:S(2)}) copy-start(bf16[136,1024]{1,0:T(8,128)(2,1)S(1)} %collective-permute-done.1.refs_3_) | copy-start | bytes 835588
  19.8 10.0 %collective-permute-start.7 = (bf16[136,1024]{1,0:T(8,128)(2,1)S(1)}, bf16[136,1024]{1,0:T(8,128)(2,1)S(1)}, u32[]{:S(2)}, u32[]{:S(2)}) collective-permute-start(bf16[136,1024]{1,0:T(8,128)(2,1)S(1)} %collective-permute-done.1.refs_3_), channel_id=1, source_target_pairs={{0,1},{1,0},{2,3},{3,2},{4,5},{5,4},{6,7},{7,6},{8,9},{9,8},{10,11... | collective-permute-start | bytes 835592 | tf_op jit(solution)/shard_map/ppermute | solution.py:617
  19.8 12.5 %collective-permute-start.5 = (bf16[136,1024]{1,0:T(8,128)(2,1)S(1)}, bf16[136,1024]{1,0:T(8,128)(2,1)S(1)}, u32[]{:S(2)}, u32[]{:S(2)}) collective-permute-start(bf16[136,1024]{1,0:T(8,128)(2,1)S(1)} %collective-permute-done.1.refs_3_), channel_id=1, source_target_pairs={{0,4},{1,5},{2,0},{3,1},{4,6},{5,7},{6,2},{7,3},{8,12},{9,13},{10,... | collective-permute-start | bytes 835592 | tf_op jit(solution)/shard_map/ppermute | solution.py:667
  26.4 14.6 %copy-start.5 = (bf16[136,1024]{1,0:T(8,128)(2,1)}, bf16[136,1024]{1,0:T(8,128)(2,1)S(1)}, u32[]{:S(2)}) copy-start(bf16[136,1024]{1,0:T(8,128)(2,1)S(1)} %collective-permute-done.2.refs_4_) | copy-start | bytes 835588
  26.4 11.9 %collective-permute-start.8 = (bf16[136,1024]{1,0:T(8,128)(2,1)S(1)}, bf16[136,1024]{1,0:T(8,128)(2,1)S(1)}, u32[]{:S(2)}, u32[]{:S(2)}) collective-permute-start(bf16[136,1024]{1,0:T(8,128)(2,1)S(1)} %collective-permute-done.2.refs_4_), channel_id=1, source_target_pairs={{0,4},{1,5},{2,0},{3,1},{4,6},{5,7},{6,2},{7,3},{8,12},{9,13},{10,... | collective-permute-start | bytes 835592 | tf_op jit(solution)/shard_map/ppermute | solution.py:667
  29.8 15.6 %collective-permute-start.11 = (bf16[136,1024]{1,0:T(8,128)(2,1)S(1)}, bf16[136,1024]{1,0:T(8,128)(2,1)}, u32[]{:S(2)}, u32[]{:S(2)}) collective-permute-start(bf16[136,1024]{1,0:T(8,128)(2,1)S(1)} %collective-permute-done.2.refs_4_), channel_id=1, source_target_pairs={{0,1},{1,0},{2,3},{3,2},{4,5},{5,4},{6,7},{7,6},{8,9},{9,8},{10,11... | collective-permute-start | bytes 835592 | tf_op jit(solution)/shard_map/ppermute | solution.py:617
  29.8 8.5 %copy-start.13 = (bf16[136,1024]{1,0:T(8,128)(2,1)}, bf16[136,1024]{1,0:T(8,128)(2,1)S(1)}, u32[]{:S(2)}) copy-start(bf16[136,1024]{1,0:T(8,128)(2,1)S(1)} %collective-permute-done.7.refs_11_) | copy-start | bytes 835588
  32.3 8.7 %copy-start.6 = (bf16[136,1024]{1,0:T(8,128)(2,1)}, bf16[136,1024]{1,0:T(8,128)(2,1)S(1)}, u32[]{:S(2)}) copy-start(bf16[136,1024]{1,0:T(8,128)(2,1)S(1)} %collective-permute-done.5.refs_5_) | copy-start | bytes 835588
  32.3 13.0 %collective-permute-start.12 = (bf16[136,1024]{1,0:T(8,128)(2,1)S(1)}, bf16[136,1024]{1,0:T(8,128)(2,1)}, u32[]{:S(2)}, u32[]{:S(2)}) collective-permute-start(bf16[136,1024]{1,0:T(8,128)(2,1)S(1)} %collective-permute-done.5.refs_5_), channel_id=1, source_target_pairs={{0,1},{1,0},{2,3},{3,2},{4,5},{5,4},{6,7},{7,6},{8,9},{9,8},{10,11... | collective-permute-start | bytes 835592 | tf_op jit(solution)/shard_map/ppermute | solution.py:617
  32.3 11.5 %collective-permute-start.9 = (bf16[136,1024]{1,0:T(8,128)(2,1)S(1)}, bf16[136,1024]{1,0:T(8,128)(2,1)S(1)}, u32[]{:S(2)}, u32[]{:S(2)}) collective-permute-start(bf16[136,1024]{1,0:T(8,128)(2,1)S(1)} %collective-permute-done.5.refs_5_), channel_id=1, source_target_pairs={{0,4},{1,5},{2,0},{3,1},{4,6},{5,7},{6,2},{7,3},{8,12},{9,13},{10,... | collective-permute-start | bytes 835592 | tf_op jit(solution)/shard_map/ppermute | solution.py:667
  39.1 4.8 %copy-start = (bf16[4,328,512]{2,1,0:T(8,128)(2,1)}, bf16[4,328,512]{2,1,0:T(8,128)(2,1)S(1)}, u32[]{:S(2)}) copy-start(bf16[4,328,512]{2,1,0:T(8,128)(2,1)S(1)} %all-to-all-done.refs_0_) | copy-start | bytes 4030468
  39.1 4.8 %copy-start.9 = (bf16[1,136,512]{2,1,0:T(8,128)(2,1)S(1)}, bf16[1,136,512]{2,1,0:T(8,128)(2,1)}, u32[]{:S(2)}) copy-start(bf16[1,136,512]{2,1,0:T(8,128)(2,1)} %get-tuple-element.76) | copy-start | bytes 417796
  39.1 4.8 %copy-start.10 = (bf16[1,136,512]{2,1,0:T(8,128)(2,1)S(1)}, bf16[1,136,512]{2,1,0:T(8,128)(2,1)}, u32[]{:S(2)}) copy-start(bf16[1,136,512]{2,1,0:T(8,128)(2,1)} %get-tuple-element.77) | copy-start | bytes 417796
  39.2 7.6 %collective-permute-start.10 = (bf16[4,136,512]{2,1,0:T(8,128)(2,1)S(1)}, bf16[4,136,512]{2,1,0:T(8,128)(2,1)}, u32[]{:S(2)}, u32[]{:S(2)}) collective-permute-start(bf16[4,136,512]{2,1,0:T(8,128)(2,1)S(1)} %slice.106), channel_id=1, source_target_pairs={{0,1},{1,0},{2,3},{3,2},{4,5},{5,4},{6,7},{7,6},{8,9},{9,8},{10,11... | collective-permute-start | bytes 1671176 | tf_op jit(solution)/shard_map/ppermute | solution.py:617
  41.0 4.4 %collective-permute-start.13 = (bf16[136,1024]{1,0:T(8,128)(2,1)S(1)}, bf16[136,1024]{1,0:T(8,128)(2,1)S(1)}, u32[]{:S(2)}, u32[]{:S(2)}) collective-permute-start(bf16[136,1024]{1,0:T(8,128)(2,1)S(1)} %collective-permute-done.8.refs_6_), channel_id=1, source_target_pairs={{0,1},{1,0},{2,3},{3,2},{4,5},{5,4},{6,7},{7,6},{8,9},{9,8},{10,11... | collective-permute-start | bytes 835592 | tf_op jit(solution)/shard_map/ppermute | solution.py:617
  43.8 1.6 %collective-permute-start.14 = (bf16[136,1024]{1,0:T(8,128)(2,1)S(1)}, bf16[136,1024]{1,0:T(8,128)(2,1)S(1)}, u32[]{:S(2)}, u32[]{:S(2)}) collective-permute-start(bf16[136,1024]{1,0:T(8,128)(2,1)S(1)} %collective-permute-done.9.refs_7_), channel_id=1, source_target_pairs={{0,1},{1,0},{2,3},{3,2},{4,5},{5,4},{6,7},{7,6},{8,9},{9,8},{10,11... | collective-permute-start | bytes 835592 | tf_op jit(solution)/shard_map/ppermute | solution.py:617
  46.8 25.1 %all-to-all-start.1 = ((bf16[4,3,136,512]{3,2,1,0:T(8,128)(2,1)}), bf16[4,3,136,512]{3,2,1,0:T(8,128)(2,1)S(1)}, u32[]{:S(2)}, u32[]{:S(2)}) async-start(bf16[4,3,136,512]{3,2,1,0:T(8,128)(2,1)} %pad_maximum_fusion), calls=%async_computation.1 | async-start | bytes 3342336 | tf_op jit(solution)/shard_map/all_to_all | solution.py:629
  71.9 8.3 %copy-start.2 = (bf16[4,3,136,512]{3,2,1,0:T(8,128)(2,1)}, bf16[4,3,136,512]{3,2,1,0:T(8,128)(2,1)S(1)}, u32[]{:S(2)}) copy-start(bf16[4,3,136,512]{3,2,1,0:T(8,128)(2,1)S(1)} %all-to-all-done.1.refs_2_) | copy-start | bytes 5013508
  71.9 4.4 %collective-permute-start.15 = (bf16[4,3,136,512]{3,2,1,0:T(8,128)(2,1)S(1)}, bf16[4,3,136,512]{3,2,1,0:T(8,128)(2,1)}, u32[]{:S(2)}, u32[]{:S(2)}) collective-permute-start(bf16[4,3,136,512]{3,2,1,0:T(8,128)(2,1)S(1)} %all-to-all-done.1.refs_2_), channel_id=1, source_target_pairs={{0,1},{1,0},{2,3},{3,2},{4,5},{5,4},{6,7},{7,6},{8,9},{9,8},{10,11... | collective-permute-start | bytes 5013512 | tf_op jit(solution)/shard_map/ppermute | solution.py:617
  71.9 15.4 %collective-permute-start.16 = (bf16[16,64,96]{2,1,0:T(8,128)(2,1)}, bf16[16,64,96]{2,1,0:T(8,128)(2,1)S(1)}, u32[]{:S(2)}, u32[]{:S(2)}) collective-permute-start(bf16[16,64,96]{2,1,0:T(8,128)(2,1)} %get-tuple-element.48), channel_id=1, source_target_pairs={{0,8},{8,16},{16,24},{24,0},{1,9},{9,17},{17,25},{25,1},{2,10},{10... | collective-permute-start | bytes 589832 | tf_op jit(solution)/shard_map/ppermute | solution.py:612
  73.3 14.0 %collective-permute-start.17 = (bf16[16,64,96]{2,1,0:T(8,128)(2,1)}, bf16[16,64,96]{2,1,0:T(8,128)(2,1)S(1)}, u32[]{:S(2)}, u32[]{:S(2)}) collective-permute-start(bf16[16,64,96]{2,1,0:T(8,128)(2,1)} %get-tuple-element.49), channel_id=1, source_target_pairs={{0,16},{8,24},{16,0},{24,8},{1,17},{9,25},{17,1},{25,9},{2,18},{10... | collective-permute-start | bytes 589832 | tf_op jit(solution)/shard_map/ppermute | solution.py:612
  73.9 13.5 %collective-permute-start.18 = (bf16[16,64,96]{2,1,0:T(8,128)(2,1)}, bf16[16,64,96]{2,1,0:T(8,128)(2,1)S(1)}, u32[]{:S(2)}, u32[]{:S(2)}) collective-permute-start(bf16[16,64,96]{2,1,0:T(8,128)(2,1)} %get-tuple-element.50), channel_id=1, source_target_pairs={{0,24},{8,0},{16,8},{24,16},{1,25},{9,1},{17,9},{25,17},{2,26},{10... | collective-permute-start | bytes 589832 | tf_op jit(solution)/shard_map/ppermute | solution.py:612
  76.3 11.1 %all-to-all-start.2 = ((f32[8,8,128]{2,1,0:T(8,128)}), f32[8,8,128]{2,1,0:T(8,128)S(1)}, u32[]{:S(2)}, u32[]{:S(2)}) async-start(f32[8,8,128]{2,1,0:T(8,128)} %get-tuple-element.53), calls=%async_computation.2 | async-start | bytes 65536 | tf_op jit(solution)/shard_map/all_to_all | solution.py:720
  80.2 7.9 %copy-start.16 = (bf16[16,64,96]{2,1,0:T(8,128)(2,1)S(1)}, bf16[16,64,96]{2,1,0:T(8,128)(2,1)}, u32[]{:S(2)}) copy-start(bf16[16,64,96]{2,1,0:T(8,128)(2,1)} %get-tuple-element.47) | copy-start | bytes 589828
  (7 other events, 10.3 us)
